TPU v7x, 256 devices: a whole 4x4x8 slice. The times are simulated.
256 devices in a mesh: fft: 64 (over x, z, core), band: 4 (over y).
Axes of the slice: x: 4, y: 4, z: 8, core: 2. Of those that a mesh axis runs over, the one named last changes fastest.
Arguments:
- psi_g: float32 [4, 2, 192, 36864], P('band', None, 'fft'), may hold values from -24 to 24
- vloc: float32 [192, 36864], P('fft'), may hold values from -6 to 6
- beta: float32 [32768, 8, 128], P(('fft', 'band')), may hold values from -0.1875 to 0.1875
- blk_slot: int32 [32768], P(('fft', 'band')), may hold values from 0 to 192, as said below
- blk_tile: int32 [32768], P(('fft', 'band')), may hold values from 0 to 863, as said below
- dmat: float32 [4096, 8, 8], P('fft'), may hold values from -12 to 12
Outputs:
- hpsi_g: float32 [4, 2, 192, 36864], P('band', None, 'fft')
Inputs may be any that keep to these rules, and one draw needn't show every extreme that they name: Blocks come slab by slab, 512 to a slab. blk_slot // 64 is 0, 1 or 2 for an atom homed on the slab below (periodically), on the block's own slab, or on the slab above; 192 marks an empty block. `blk_tile`: blocks of atoms homed on the slab below lie in their slab's first 288 tiles; those of atoms homed on the slab above in its last 288 tiles.
All inputs are finite; a program needn't handle non-finite values.
Results may differ from a plain program's by a relative error of at most 0.00007.
Values sent between devices are 32-bit elements; how exact they have to be, the bound alone decides.
No kernel may reach another device: no remote copies, remote signals or barrier semaphores. Data moves between devices by JAX's collectives and lax.ppermute only.
A program may use at most 64 MiB of HBM per device.

v0:
```python
import functools

import jax
import jax.numpy as jnp
import ml_dtypes
import numpy as np
from jax import lax
from jax.experimental import pallas as pl
from jax.experimental.pallas import tpu as pltpu
from jax.sharding import PartitionSpec as P

N = 192
R2 = 48 * 48
BF = jnp.bfloat16
F32 = jnp.float32
VMEM_LIMIT = 48 * 1024 * 1024


def trig(freqs, points):
    angle = 2.0 * np.pi * (np.outer(freqs, points) % N) / N
    return np.cos(angle) / np.sqrt(N), np.sin(angle) / np.sqrt(N)


def pair_of(table):
    table = np.asarray(table, np.float32)
    high = table.astype(ml_dtypes.bfloat16)
    low = (table - high.astype(np.float32)).astype(ml_dtypes.bfloat16)
    return high, low


KZ = np.concatenate([np.arange(64), np.arange(128, 192)])
SIGNED = np.concatenate([np.arange(64), np.arange(-64, 0)])
YS = [2 * np.arange(96), 2 * np.arange(96) + 1]


@functools.cache
def tables():
    t = {}
    blocks = []
    for zi in range(3):
        c, s = trig(3 * np.arange(64) + zi, KZ)
        blocks += [np.concatenate([c, -s], 1), np.concatenate([s, c], 1)]
    t["wz"] = pair_of(np.concatenate(blocks, 0))
    c, s = trig(np.concatenate(YS), SIGNED)
    t["ey"] = pair_of(
        np.concatenate([np.concatenate([c, -s], 1), np.concatenate([s, c], 1)], 0)
    )
    c, s = trig(SIGNED, np.arange(N))
    gap = np.zeros((128, 64))
    even = [np.concatenate([v, gap], 1) for v in (c, s, -s, c)]
    odd = [np.concatenate([gap, v], 1) for v in (c, s, -s, c)]
    t["xe"] = pair_of(np.block([[even[0], even[1]], [even[2], even[3]]]))
    t["xo"] = pair_of(np.block([[odd[0], odd[1]], [odd[2], odd[3]]]))
    parts = {}
    for name, table in (("c", c), ("s", s)):
        parts[name] = (
            np.concatenate([table, gap], 1),
            np.concatenate([gap, table], 1),
        )

    def forward_x(which):
        cc, ss = parts["c"][which], parts["s"][which]
        rows = []
        for first, second in ((cc, ss), (-ss, cc)):
            rows.append(
                np.concatenate(
                    [first[:, :128], second[:, :128], first[:, 128:], second[:, 128:]], 1
                )
            )
        return np.concatenate(rows, 0)

    t["fe"] = pair_of(forward_x(0))
    t["fo"] = pair_of(forward_x(1))
    c, s = trig(np.concatenate(YS), SIGNED)
    t["fy"] = pair_of(
        np.concatenate([np.concatenate([c, -s], 1), np.concatenate([s, c], 1)], 0)
    )
    blocks = []
    for zi in range(3):
        c, s = trig(3 * np.arange(64) + zi, KZ)
        blocks += [np.concatenate([c, -s], 1), np.concatenate([s, c], 1)]
    t["fz"] = pair_of(np.concatenate(blocks, 0))
    u = np.zeros((128, 384), np.float32)
    for zi in range(3):
        for p in range(128):
            u[32 * zi + 8 * (p >= 64) + p % 8, 128 * zi + p] = 1.0
    t["u"] = u.astype(ml_dtypes.bfloat16)
    t["ut"] = np.concatenate([u[:, 128 * zi : 128 * zi + 128].T for zi in range(3)], 0).astype(
        ml_dtypes.bfloat16
    )
    return t


def split(x):
    high = x.astype(BF)
    return high, (x - high.astype(F32)).astype(BF)


def mm(a, b):
    return jnp.dot(a, b, preferred_element_type=F32)


def mm_nt(a, b):
    return lax.dot_general(a, b, (((1,), (1,)), ((), ())), preferred_element_type=F32)


def three(product, a, b):
    return product(a[0], b[0]) + (product(a[0], b[1]) + product(a[1], b[0]))


def iota(shape, dim):
    return lax.broadcasted_iota(jnp.int32, shape, dim)


def masks_sp():
    s, p = iota((64, 128), 0), iota((64, 128), 1)
    ky = jnp.where(p < 64, p, p - 128)
    away = 64 - jnp.abs(ky)
    inside = ky * ky + s * s <= R2
    clash = away * away + (64 - s) * (64 - s) <= R2
    other = (p - 64) * (p - 64) + (64 - s) * (64 - s) <= R2
    return inside & ~clash, inside & clash, other


def line_places(r, s):
    plane, rest = r // 128, r % 128
    ky = 2 * (rest % 64 - 24) + rest // 64
    here = jnp.where(plane == 0, s, 64 - s)
    away = 64 - jnp.abs(ky)
    inside = ky * ky + here * here <= R2
    clash = (away * away + (64 - s) * (64 - s) <= R2) & (plane == 0)
    place = jnp.where(plane == 0, jnp.where(ky < 0, ky + 128, ky), ky + 64)
    main = jnp.where(inside & ~clash, place, -1)
    spare = jnp.where(inside & clash, jnp.where(ky < 0, 8, 0) + (ky + 64) % 8, -1)
    return main, spare


def one_hot(condition):
    return jnp.where(condition, 1.0, 0.0).astype(BF)


def sphere_rows(plane, parity, s):
    m, lane = iota((64, 128), 0), iota((64, 128), 1)
    ky = 2 * (m - 24) + parity
    kz = jnp.where(lane < 64, lane, lane - 128)
    kx = s - 64 * plane
    return ky * ky + kz * kz + kx * kx <= R2


def kernel_z_inverse(psi, wz_h, wz_l, send, buf, sems):
    s = lax.axis_index("fft")
    copies = []
    for plane in range(2):
        base = 1152 * plane
        for k, (src, dst, rows) in enumerate(((432, 0, 144), (0, 144, 152))):
            copies.append(
                pltpu.make_async_copy(
                    psi.at[pl.ds(base + src, rows)],
                    buf.at[plane, pl.ds(dst, rows)],
                    sems.at[2 * plane + k],
                )
            )
    for copy in copies:
        copy.start()
    r = iota((1, 256), 1)
    main, spare = line_places(r, s)
    j = iota((128, 256), 0)
    pack = jnp.concatenate(
        [one_hot(j == main), one_hot((j % 32 == spare) & (j < 96))], axis=0
    )
    for copy in copies:
        copy.wait()
    lane = iota((64, 128), 1)
    rows = []
    for plane in range(2):
        lines = [[], []]
        for c in range(2):
            t = [buf[plane, pl.ds(2 * k + c, 64, stride=6), :] for k in range(3)]
            middle = pltpu.roll(t[1], 64, 1)
            even = jnp.where(lane < 64, t[0], middle)
            odd = jnp.where(lane < 64, middle, t[2])
            lines[0].append(jnp.where(sphere_rows(plane, 0, s), even, 0.0))
            lines[1].append(jnp.where(sphere_rows(plane, 1, s), odd, 0.0))
        rows += [jnp.concatenate(lines[0], 1), jnp.concatenate(lines[1], 1)]
    high, low = split(jnp.concatenate(rows, 0))
    packed = (mm(pack, high).astype(BF), mm(pack, low).astype(BF))
    out = three(mm_nt, (wz_h[...], wz_l[...]), packed)
    for c in range(2):
        block = [out[(2 * zi + c) * 64 : (2 * zi + c) * 64 + 64] for zi in range(3)]
        for zi in range(3):
            send[pl.ds(4 * c + zi, 64, stride=8), :] = block[zi][:, :128]
        send[pl.ds(4 * c + 3, 64, stride=8), :] = jnp.where(
            lane < 32, block[0][:, 128:], jnp.where(lane < 64, block[1][:, 128:], block[2][:, 128:])
        )


def block_ids(betas, row):
    return jnp.concatenate([b[1024 + row : 1025 + row, :] for b in betas], 1)


def as_column(ids):
    return jnp.broadcast_to(ids, (8, 512)).T[:, 0:1]


def slot_hot(betas):
    return one_hot(as_column(block_ids(betas, 0)).astype(jnp.int32) == iota((512, 256), 1))


def kernel_field(
    recv, ey_h, ey_l, xe_h, xe_l, xo_h, xo_l, u, vloc, dmat, b0, b1, b2, b3,
    local, near, far, rows_h, rows_l, field_rows,
):
    main, spare, other = masks_sp()
    spread = []
    for c in range(2):
        high, low = split(recv[pl.ds(4 * c + 3, 64, stride=8), :])
        spread.append(mm(high, u[...]) + mm(low, u[...]))
    lines = []
    for zi in range(3):
        first, second = [], []
        for c in range(2):
            got = recv[pl.ds(4 * c + zi, 64, stride=8), :]
            extra = spread[c][:, 128 * zi : 128 * zi + 128]
            first.append(jnp.where(main, got, jnp.where(spare, extra, 0.0)))
            second.append(pltpu.roll(jnp.where(other, got, 0.0), 64, 1))
        lines += [jnp.concatenate(first, 1), jnp.concatenate(second, 1)]
    g = three(mm_nt, (ey_h[...], ey_l[...]), split(jnp.concatenate(lines, 0)))
    out = []
    for parity, table in ((0, (xe_h, xe_l)), (1, (xo_h, xo_l))):
        a = 96 * parity
        block = jnp.concatenate(
            [
                jnp.concatenate(
                    [
                        g[a : a + 96, 128 * zi : 128 * zi + 128],
                        g[192 + a : 288 + a, 128 * zi : 128 * zi + 128],
                    ],
                    1,
                )
                for zi in range(3)
            ],
            0,
        )
        out.append(three(mm, split(block), (table[0][...], table[1][...])))
    even, odd = out
    for c in range(2):
        a = 256 * c
        kinds = (
            even[:, a : a + 128],
            even[:, a + 128 : a + 256] + odd[:, a : a + 128],
            odd[:, a + 128 : a + 256],
        )
        for k, tile in enumerate(kinds):
            span = pl.ds(288 * k, 288)
            lanes = pl.ds(128 * c, 128)
            local[span, lanes] = tile * vloc[span, :]
            high, low = split(tile)
            rows_h[span, lanes] = high
            rows_l[span, lanes] = low
    rows_h[864:896, :] = jnp.zeros((32, 256), BF)
    rows_l[864:896, :] = jnp.zeros((32, 256), BF)

    betas = (b0, b1, b2, b3)
    tile_of = as_column(block_ids(betas, 1)).astype(jnp.int32)
    pick = one_hot(tile_of == iota((512, 896), 1))
    field_rows[...] = mm(pick, rows_h[...]) + mm(pick, rows_l[...])
    lane = iota((128, 128), 1)
    sums = []
    for k, beta in enumerate(betas):
        total = jnp.zeros((128, 128), F32)
        for j in range(8):
            projector = beta[pl.ds(j, 128, stride=8), :]
            for c in range(2):
                value = field_rows[128 * k : 128 * k + 128, 128 * c : 128 * c + 128] * projector
                total = jnp.where(
                    lane == 8 * c + j, jnp.sum(value, axis=1, keepdims=True), total
                )
        sums.append(total.T[:16])
    high, low = split(jnp.concatenate(sums, 1))
    slots = slot_hot(betas)
    coef = mm(high, slots) + mm(low, slots)
    coef = jnp.where(iota((16, 256), 1) < 192, coef, 0.0)
    near[0:64, :] = jnp.concatenate([dmat[...], jnp.zeros((64, 64), F32)], 1)
    near[64:80, :] = coef[:, :128]
    near[80:96, :] = coef[:, 128:]
    far[0:16, :] = coef[:, :128]
    far[16:32, :] = coef[:, 128:]


def kernel_back(
    local, near, below, above, below2, above2, b0, b1, b2, b3,
    fe_h, fe_l, fo_h, fo_l, fy_h, fy_l, ut, send, scr, rows,
):
    lane = iota((16, 128), 1)

    def half(ref, k):
        return ref[64 + 16 * k : 80 + 16 * k, :]

    def shifted(low, high, up):
        low, high = pltpu.roll(low, 64, 1), pltpu.roll(high, 64, 1)
        if up:
            return jnp.where(lane < 64, 0.0, low), jnp.where(lane < 64, low, high)
        return jnp.where(lane < 64, low, high), jnp.where(lane < 64, high, 0.0)

    from_below = shifted(half(below, 0), half(below, 1), False)
    from_above = shifted(half(above, 0), half(above, 1), True)
    tot = [
        half(near, 0) + from_below[0] + from_above[0] + below2[16:32, :],
        half(near, 1) + from_below[1] + from_above[1] + above2[0:16, :],
    ]
    tot[1] = jnp.where(lane < 64, tot[1], 0.0)
    wide = iota((64, 128), 1)
    coupling = [
        jnp.where(wide < 64, below[0:64, :], pltpu.roll(near[0:64, :], 64, 1)),
        jnp.where(wide < 64, above[0:64, :], 0.0),
    ]
    for h in range(2):
        for c in range(2):
            coef = tot[h][8 * c : 8 * c + 8, :]
            for j in range(8):
                row = jnp.sum(coupling[h][8 * j : 8 * j + 8, :] * coef, axis=0, keepdims=True)
                scr[8 * c + j : 8 * c + j + 1, 128 * h : 128 * h + 128] = row
    betas = (b0, b1, b2, b3)
    slots = slot_hot(betas)
    high, low = split(scr[...])
    weight = mm_nt(slots, high) + mm_nt(slots, low)
    for k, beta in enumerate(betas):
        span = slice(128 * k, 128 * k + 128)
        terms = [jnp.zeros((128, 128), F32), jnp.zeros((128, 128), F32)]
        for j in range(8):
            projector = beta[pl.ds(j, 128, stride=8), :]
            for c in range(2):
                terms[c] = terms[c] + projector * weight[span, 8 * c + j : 8 * c + j + 1]
        for c in range(2):
            high, low = split(terms[c])
            rows[span, 128 * c : 128 * c + 128] = high
            rows[span, 256 + 128 * c : 384 + 128 * c] = low
    tile_of = block_ids(betas, 1).astype(jnp.int32)
    put = one_hot(iota((864, 512), 0) == tile_of)
    both = mm(put, rows[...])
    applied = local[...] + (both[:, :256] + both[:, 256:])
    app = split(applied)
    main, spare, _ = masks_sp()
    spares = [jnp.zeros((64, 128), F32), jnp.zeros((64, 128), F32)]
    for zi in range(3):
        kinds = [
            [a[288 * k + 96 * zi : 288 * k + 96 * zi + 96] for a in app] for k in range(3)
        ]
        h = jnp.zeros((128, 256), F32)
        for parity, table in ((0, (fe_h, fe_l)), (1, (fo_h, fo_l))):
            lines = [
                jnp.concatenate([kinds[parity][i], kinds[parity + 1][i]], 1) for i in range(2)
            ]
            g = split(three(mm_nt, (table[0][...], table[1][...]), lines))
            for c in range(2):
                part = [v[128 * c : 128 * c + 128] for v in g]
                at = slice(192 * c + 96 * parity, 192 * c + 96 * parity + 96)
                h = h + three(mm, part, (fy_h[at, :], fy_l[at, :]))
        for c in range(2):
            first = h[:64, 128 * c : 128 * c + 128]
            second = pltpu.roll(h[64:, 128 * c : 128 * c + 128], 64, 1)
            send[pl.ds(4 * c + zi, 64, stride=8), :] = jnp.where(main, first, second)
            high, low = split(jnp.where(spare, first, 0.0))
            move = ut[128 * zi : 128 * zi + 128, :]
            spares[c] = spares[c] + (mm(high, move) + mm(low, move))
    for c in range(2):
        send[pl.ds(4 * c + 3, 64, stride=8), :] = spares[c]


def kernel_z_forward(recv, fz_h, fz_l, out):
    s = lax.axis_index("fft")
    out[...] = jnp.zeros((1728, 128), F32)
    r = iota((256, 1), 0)
    main, spare = line_places(r, s)
    lane = iota((256, 128), 1)
    keep = one_hot(lane == main)
    highs, lows = [], []
    for zi in range(3):
        unpack = jnp.concatenate(
            [keep, one_hot((lane == spare + 32 * zi) & (spare >= 0))], 1
        )
        lines = jnp.concatenate(
            [
                jnp.concatenate(
                    [
                        recv[pl.ds(4 * c + zi, 64, stride=8), :],
                        recv[pl.ds(4 * c + 3, 64, stride=8), :],
                    ],
                    1,
                )
                for c in range(2)
            ],
            0,
        )
        high, low = split(lines)
        columns = mm_nt(unpack, jnp.concatenate([high, low], 0))
        highs.append(columns[:, :128].astype(BF))
        lows.append(columns[:, 128:].astype(BF))
    z = three(
        mm, (jnp.concatenate(highs, 1), jnp.concatenate(lows, 1)), (fz_h[...], fz_l[...])
    )
    low_lane = iota((64, 128), 1) < 64
    for plane in range(2):
        for c in range(2):
            block = z[128 * plane : 128 * plane + 128, 128 * c : 128 * c + 128]
            even = jnp.where(sphere_rows(plane, 0, s), block[:64], 0.0)
            odd = jnp.where(sphere_rows(plane, 1, s), block[64:], 0.0)
            kinds = (
                jnp.where(low_lane, even, 0.0),
                pltpu.roll(jnp.where(low_lane, odd, even), 64, 1),
                jnp.where(low_lane, 0.0, odd),
            )
            for k, tile in enumerate(kinds):
                at = 1152 * plane + 2 * k + c
                out[pl.ds(at, 32, stride=6), :] = tile[24:56]
                out[pl.ds(at + 432, 24, stride=6), :] = tile[:24]


def call(kernel, name, out_shape, args, scratch=(), anywhere=()):
    specs = [
        pl.BlockSpec(memory_space=pl.ANY if k in anywhere else pltpu.VMEM)
        for k in range(len(args))
    ]
    shapes = [jax.ShapeDtypeStruct(shape, F32) for shape in out_shape]
    out = pl.pallas_call(
        kernel,
        name=name,
        out_shape=shapes,
        in_specs=specs,
        out_specs=[pl.BlockSpec(memory_space=pltpu.VMEM)] * len(shapes),
        scratch_shapes=list(scratch),
        compiler_params=pltpu.CompilerParams(vmem_limit_bytes=VMEM_LIMIT),
    )(*args)
    return out


def body(psi_g, vloc, beta, blk_slot, blk_tile, dmat):
    t = {
        name: tuple(jnp.asarray(v) for v in value) if isinstance(value, tuple) else jnp.asarray(value)
        for name, value in tables().items()
    }
    tile_row = (blk_tile % 3) * 288 + blk_tile // 3
    ids = jnp.concatenate(
        [blk_slot[None], tile_row[None], jnp.zeros((6, 128), jnp.int32)], 0
    ).astype(F32)
    own = jnp.concatenate([beta, ids[None]], 0).reshape(1032, 128)
    betas = [own] + [
        lax.ppermute(own, "band", [(i, (i + k) % 4) for i in range(4)]) for k in (1, 3, 2)
    ]

    psi = psi_g[0].transpose(1, 0, 2).reshape(3, 2, 288, 128).transpose(0, 2, 1, 3)
    psi = psi.reshape(1728, 128)
    (send,) = call(
        kernel_z_inverse,
        "z_inverse",
        [(512, 128)],
        (psi, *t["wz"]),
        [pltpu.VMEM((2, 384, 128), F32), pltpu.SemaphoreType.DMA((4,))],
        anywhere=(0,),
    )

    def exchange(x):
        x = lax.all_to_all(x.reshape(64, 8, 128), "fft", 0, 0, tiled=True)
        return x.reshape(512, 128)

    recv = exchange(send)
    vloc_rows = vloc.reshape(3, 96, 3, 128).transpose(2, 0, 1, 3).reshape(864, 128)
    dmat_rows = dmat.transpose(1, 2, 0).reshape(64, 64)
    local, near, far = call(
        kernel_field,
        "field",
        [(864, 256), (96, 128), (32, 128)],
        (recv, *t["ey"], *t["xe"], *t["xo"], t["u"], vloc_rows, dmat_rows, *betas),
        [pltpu.VMEM((896, 256), BF), pltpu.VMEM((896, 256), BF), pltpu.VMEM((512, 256), F32)],
    )

    def moved(x, step):
        return lax.ppermute(x, "fft", [(i, (i + step) % 64) for i in range(64)])

    sides = (moved(near, 1), moved(near, -1), moved(far, 2), moved(far, -2))
    (send,) = call(
        kernel_back,
        "back",
        [(512, 128)],
        (local, near, *sides, *betas, *t["fe"], *t["fo"], *t["fy"], t["ut"]),
        [pltpu.VMEM((16, 256), F32), pltpu.VMEM((512, 512), BF)],
    )
    (out,) = call(kernel_z_forward, "z_forward", [(1728, 128)], (exchange(send), *t["fz"]))
    out = out.reshape(3, 288, 2, 128).transpose(0, 2, 1, 3).reshape(3, 2, N * N)
    return out.transpose(1, 0, 2)[None]


def solution(mesh):
    in_specs = (
        P("band", None, "fft", None),
        P("fft", None),
        P(("fft", "band"), None, None),
        P(("fft", "band")),
        P(("fft", "band")),
        P("fft", None, None),
    )
    out_specs = P("band", None, "fft", None)
    return jax.shard_map(body, mesh=mesh, in_specs=in_specs, out_specs=out_specs, check_vma=False)
```

profile of v0, /device:TPU:1, one launch (start us, length us, event | category | flops | bytes accessed | tf_op | source)
XLA Modules:
  0.0 79.2 jit_solution(18114391436145794978)
XLA Ops:
  0.0 0.8 fusion.2
  0.8 0.1 pad.4.clone
  0.8 0.7 add_convert_fusion
  1.6 1.1 %maximum_bitcast_fusion.b0 = f32[1032,128]{1,0:T(8,128)S(1)} fusion(f32[1,8,128]{2,1,0:T(8,128)S(1)} %add_convert_fusion, f32[128,8,128]{2,1,0:T(8,128)} %param.26), kind=kLoop, calls=%fused_computation | loop fusion | flops 132096 | bytes 1056768 | tf_op jit(solution)/shard_map/reshape | solution.py:446
  2.7 3.8 %collective-permute-start.2 = (f32[1032,128]{1,0:T(8,128)S(1)}, f32[1032,128]{1,0:T(8,128)S(1)}, u32[]{:S(2)}, u32[]{:S(2)}) collective-permute-start(f32[1032,128]{1,0:T(8,128)S(1)} %maximum_bitcast_fusion.b0), channel_id=1, source_target_pairs={{0,2},{1,3},{2,0},{3,1},{4,6},{5,7},{6,4},{7,5},{8,10},{9,11},{10,... | collective-permute-start | bytes 1585160 | tf_op jit(solution)/shard_map/ppermute | solution.py:448
  6.5 0.8 collective-permute-start.1
  7.3 0.7 collective-permute-start
  8.0 0.9 %copy-done.4 = bf16[384,256]{1,0:T(8,128)(2,1)S(1)} copy-done((bf16[384,256]{1,0:T(8,128)(2,1)S(1)}, bf16[384,256]{1,0:T(8,128)(2,1)}, u32[]{:S(2)}) %copy-start.4) | copy-done | bytes 196632
  8.9 1.8 %z_inverse.1 = f32[512,128]{1,0:T(8,128)} custom-call(f32[1728,128]{1,0:T(8,128)S(1)} %bitcast.36, bf16[384,256]{1,0:T(8,128)(2,1)S(1)} %copy-done.4, bf16[384,256]{1,0:T(8,128)(2,1)S(1)} %copy-done.3), custom_call_target="tpu_custom_call" | custom-call | tf_op jit(solution)/shard_map/z_inverse/pallas_call | solution.py:425
  10.6 13.0 %all-to-all-start = ((f32[64,8,128]{2,1,0:T(8,128)}), f32[64,8,128]{2,1,0:T(8,128)S(1)}, u32[]{:S(2)}, u32[]{:S(2)}) async-start(f32[64,8,128]{2,1,0:T(8,128)} %bitcast.5), calls=%async_computation | async-start | bytes 524288 | tf_op jit(solution)/shard_map/all_to_all | solution.py:463
  23.7 1.2 %reshape.78 = f32[3,96,3,128]{3,2,1,0:T(4,128)} reshape(f32[3,36864]{1,0:T(4,128)S(1)} %copy-done.17) | data formatting | bytes 884736 | tf_op jit(solution)/shard_map/reshape | solution.py:467
  24.9 1.2 %copy.28 = f32[3,3,96,128]{3,2,1,0:T(8,128)S(1)} copy(f32[3,3,96,128]{3,0,2,1:T(4,128)} %bitcast.38) | data formatting | bytes 884736 | tf_op jit(solution)/shard_map/transpose | solution.py:467
  26.1 9.6 %all-to-all-done = f32[64,8,128]{2,1,0:T(8,128)S(1)} async-done(((f32[64,8,128]{2,1,0:T(8,128)}), f32[64,8,128]{2,1,0:T(8,128)S(1)}, u32[]{:S(2)}, u32[]{:S(2)}) %all-to-all-start) | async-done | bytes 262176 | tf_op jit(solution)/shard_map/all_to_all | solution.py:463
  35.7 0.0 collective-permute-done.2.b3
  35.7 0.0 collective-permute-done.1.b2
  35.7 0.0 collective-permute-done.b1
  35.7 0.0 copy-start.10
  35.7 0.9 %copy-done.10 = bf16[256,512]{1,0:T(8,128)(2,1)S(1)} copy-done((bf16[256,512]{1,0:T(8,128)(2,1)S(1)}, bf16[256,512]{1,0:T(8,128)(2,1)}, u32[]{:S(2)}) %copy-start.10) | copy-done | bytes 262168
  36.7 0.9 %copy-done.11 = bf16[256,512]{1,0:T(8,128)(2,1)S(1)} copy-done((bf16[256,512]{1,0:T(8,128)(2,1)S(1)}, bf16[256,512]{1,0:T(8,128)(2,1)}, u32[]{:S(2)}) %copy-start.11) | copy-done | bytes 262168
  37.6 0.9 %copy-done.12 = bf16[256,512]{1,0:T(8,128)(2,1)S(1)} copy-done((bf16[256,512]{1,0:T(8,128)(2,1)S(1)}, bf16[256,512]{1,0:T(8,128)(2,1)}, u32[]{:S(2)}) %copy-start.12) | copy-done | bytes 262168
  38.6 0.9 %copy-done.13 = bf16[256,512]{1,0:T(8,128)(2,1)S(1)} copy-done((bf16[256,512]{1,0:T(8,128)(2,1)S(1)}, bf16[256,512]{1,0:T(8,128)(2,1)}, u32[]{:S(2)}) %copy-start.13) | copy-done | bytes 262168
  39.5 0.0 copy-start.14
  39.5 3.6 %field.1 = (f32[864,256]{1,0:T(8,128)S(1)}, f32[96,128]{1,0:T(8,128)S(1)}, f32[32,128]{1,0:T(8,128)S(1)}) custom-call(f32[512,128]{1,0:T(8,128)S(1)} %bitcast.33, bf16[384,256]{1,0:T(8,128)(2,1)S(1)} %copy-done.2, bf16[384,256]{1,0:T(8,128)(2,1)S(1)} %copy-done.1, bf16[256,512]{1,0:T(8,128)(2,1)S(1)} %copy-done.13, bf16[256,512]{1,0:T(8,128)(2,1)S(1)} %copy-done.12, ...), custom_call_target="tpu_custom_call" | custom-call | tf_op jit(solution)/shard_map/field/pallas_call | solution.py:425
  43.2 0.5 collective-permute-start.4
  43.7 1.3 %collective-permute-start.3 = (f32[96,128]{1,0:T(8,128)S(1)}, f32[96,128]{1,0:T(8,128)S(1)}, u32[]{:S(2)}, u32[]{:S(2)}) collective-permute-start(f32[96,128]{1,0:T(8,128)S(1)} %get-tuple-element.9.near), channel_id=1, source_target_pairs={{0,4},{4,8},{8,12},{12,16},{16,20},{20,24},{24,28},{28,32},{32,36}... | collective-permute-start | bytes 147464 | tf_op jit(solution)/shard_map/ppermute | solution.py:478
  44.9 5.7 %collective-permute-start.6 = (f32[32,128]{1,0:T(8,128)S(1)}, f32[32,128]{1,0:T(8,128)S(1)}, u32[]{:S(2)}, u32[]{:S(2)}) collective-permute-start(f32[32,128]{1,0:T(8,128)S(1)} %get-tuple-element.10), channel_id=1, source_target_pairs={{0,248},{4,252},{8,0},{12,4},{16,8},{20,12},{24,16},{28,20},{32,24... | collective-permute-start | bytes 49160 | tf_op jit(solution)/shard_map/ppermute | solution.py:478
  50.7 0.0 collective-permute-start.5
  50.7 0.9 %collective-permute-done.6.above2 = f32[32,128]{1,0:T(8,128)S(1)} collective-permute-done((f32[32,128]{1,0:T(8,128)S(1)}, f32[32,128]{1,0:T(8,128)S(1)}, u32[]{:S(2)}, u32[]{:S(2)}) %collective-permute-start.6) | collective-permute-done | bytes 16416 | tf_op jit(solution)/shard_map/ppermute | solution.py:478
  51.5 5.0 %collective-permute-done.5.below2 = f32[32,128]{1,0:T(8,128)S(1)} collective-permute-done((f32[32,128]{1,0:T(8,128)S(1)}, f32[32,128]{1,0:T(8,128)S(1)}, u32[]{:S(2)}, u32[]{:S(2)}) %collective-permute-start.5) | collective-permute-done | bytes 16416 | tf_op jit(solution)/shard_map/ppermute | solution.py:478
  56.6 6.5 %back.1 = f32[512,128]{1,0:T(8,128)S(1)} custom-call(f32[864,256]{1,0:T(8,128)S(1)} %get-tuple-element.8.local, f32[96,128]{1,0:T(8,128)S(1)} %get-tuple-element.9.near, f32[96,128]{1,0:T(8,128)S(1)} %collective-permute-done.3.below, f32[96,128]{1,0:T(8,128)S(1)} %collective-permute-done.4.above, f32[32,128]{1,0:T(8,128)S(1)} %collective-permute-done.5.below2, ...), custom_call_target="tpu_custom_call" | custom-call | tf_op jit(solution)/shard_map/back/pallas_call | solution.py:425
  63.1 14.2 %all_to_all.10 = f32[64,8,128]{2,1,0:T(8,128)S(1)} all-to-all(f32[64,8,128]{2,1,0:T(8,128)S(1)} %bitcast.34), channel_id=1, replica_groups=mesh['fft'=64,'band'=4] {'fft'}, dimensions={0} | all-to-all | bytes 524288 | tf_op jit(solution)/shard_map/all_to_all | solution.py:463
  77.4 1.8 %z_forward.1 = f32[1728,128]{1,0:T(8,128)} custom-call(f32[512,128]{1,0:T(8,128)S(1)} %bitcast.35, bf16[384,256]{1,0:T(8,128)(2,1)S(1)} %copy-done.5, bf16[384,256]{1,0:T(8,128)(2,1)S(1)} %copy-done.3), custom_call_target="tpu_custom_call" | custom-call | tf_op jit(solution)/shard_map/z_forward/pallas_call | solution.py:425
  (32 shorter events, 0.1 us)
Async XLA Ops:
  0.0 8.0 %copy-start.3 = (bf16[384,256]{1,0:T(8,128)(2,1)S(1)}, bf16[384,256]{1,0:T(8,128)(2,1)}, u32[]{:S(2)}) copy-start(bf16[384,256]{1,0:T(8,128)(2,1)} %constant.52.clone.wz_l.fz_l) | copy-start | bytes 589828
  0.0 8.0 %copy-start = (f32[1,2,3,36864]{3,1,2,0:T(2,128)S(1)}, f32[1,2,3,36864]{3,1,2,0:T(2,128)}, u32[]{:S(2)}) copy-start(f32[1,2,3,36864]{3,1,2,0:T(2,128)} %param.24) | copy-start | bytes 2654212
  2.7 33.0 %collective-permute-start.2 = (f32[1032,128]{1,0:T(8,128)S(1)}, f32[1032,128]{1,0:T(8,128)S(1)}, u32[]{:S(2)}, u32[]{:S(2)}) collective-permute-start(f32[1032,128]{1,0:T(8,128)S(1)} %maximum_bitcast_fusion.b0), channel_id=1, source_target_pairs={{0,2},{1,3},{2,0},{3,1},{4,6},{5,7},{6,4},{7,5},{8,10},{9,11},{10,... | collective-permute-start | bytes 1585160 | tf_op jit(solution)/shard_map/ppermute | solution.py:448
  6.5 29.2 %collective-permute-start.1 = (f32[1032,128]{1,0:T(8,128)S(1)}, f32[1032,128]{1,0:T(8,128)S(1)}, u32[]{:S(2)}, u32[]{:S(2)}) collective-permute-start(f32[1032,128]{1,0:T(8,128)S(1)} %maximum_bitcast_fusion.b0), channel_id=1, source_target_pairs={{0,3},{1,0},{2,1},{3,2},{4,7},{5,4},{6,5},{7,6},{8,11},{9,8},{10,9... | collective-permute-start | bytes 1585160 | tf_op jit(solution)/shard_map/ppermute | solution.py:448
  7.3 28.4 %collective-permute-start = (f32[1032,128]{1,0:T(8,128)S(1)}, f32[1032,128]{1,0:T(8,128)S(1)}, u32[]{:S(2)}, u32[]{:S(2)}) collective-permute-start(f32[1032,128]{1,0:T(8,128)S(1)} %maximum_bitcast_fusion.b0), channel_id=1, source_target_pairs={{0,1},{1,2},{2,3},{3,0},{4,5},{5,6},{6,7},{7,4},{8,9},{9,10},{10,1... | collective-permute-start | bytes 1585160 | tf_op jit(solution)/shard_map/ppermute | solution.py:448
  8.0 0.9 %copy-start.4 = (bf16[384,256]{1,0:T(8,128)(2,1)S(1)}, bf16[384,256]{1,0:T(8,128)(2,1)}, u32[]{:S(2)}) copy-start(bf16[384,256]{1,0:T(8,128)(2,1)} %constant.51.clone.wz_h.fz_h) | copy-start | bytes 589828
  8.9 14.8 %copy-start.17 = (f32[3,36864]{1,0:T(4,128)S(1)}, f32[3,36864]{1,0:T(4,128)}, u32[]{:S(2)}) copy-start(f32[3,36864]{1,0:T(4,128)} %param.25) | copy-start | bytes 1327108
  10.6 25.0 %all-to-all-start = ((f32[64,8,128]{2,1,0:T(8,128)}), f32[64,8,128]{2,1,0:T(8,128)S(1)}, u32[]{:S(2)}, u32[]{:S(2)}) async-start(f32[64,8,128]{2,1,0:T(8,128)} %bitcast.5), calls=%async_computation | async-start | bytes 524288 | tf_op jit(solution)/shard_map/all_to_all | solution.py:463
  24.9 10.8 %copy-start.1 = (bf16[384,256]{1,0:T(8,128)(2,1)S(1)}, bf16[384,256]{1,0:T(8,128)(2,1)}, u32[]{:S(2)}) copy-start(bf16[384,256]{1,0:T(8,128)(2,1)} %constant.54.clone.ey_l.fy_l) | copy-start | bytes 589828
  24.9 10.8 %copy-start.2 = (bf16[384,256]{1,0:T(8,128)(2,1)S(1)}, bf16[384,256]{1,0:T(8,128)(2,1)}, u32[]{:S(2)}) copy-start(bf16[384,256]{1,0:T(8,128)(2,1)} %constant.53.clone.ey_h.fy_h) | copy-start | bytes 589828
  24.9 10.8 %copy-start.15 = (bf16[128,384]{1,0:T(8,128)(2,1)S(1)}, bf16[128,384]{1,0:T(8,128)(2,1)}, u32[]{:S(2)}) copy-start(bf16[128,384]{1,0:T(8,128)(2,1)} %constant.63.clone.u) | copy-start | bytes 294916
  24.9 10.8 %copy-start.16 = (f32[64,8,8]{0,2,1:T(8,128)S(1)}, f32[64,8,8]{0,2,1:T(8,128)}, u32[]{:S(2)}) copy-start(f32[64,8,8]{0,2,1:T(8,128)} %param.29) | copy-start | bytes 49156
  35.7 1.0 %copy-start.10 = (bf16[256,512]{1,0:T(8,128)(2,1)S(1)}, bf16[256,512]{1,0:T(8,128)(2,1)}, u32[]{:S(2)}) copy-start(bf16[256,512]{1,0:T(8,128)(2,1)} %constant.58.clone.xo_l) | copy-start | bytes 786436
  36.7 0.9 %copy-start.11 = (bf16[256,512]{1,0:T(8,128)(2,1)S(1)}, bf16[256,512]{1,0:T(8,128)(2,1)}, u32[]{:S(2)}) copy-start(bf16[256,512]{1,0:T(8,128)(2,1)} %constant.57.clone.xo_h) | copy-start | bytes 786436
  37.6 0.9 %copy-start.12 = (bf16[256,512]{1,0:T(8,128)(2,1)S(1)}, bf16[256,512]{1,0:T(8,128)(2,1)}, u32[]{:S(2)}) copy-start(bf16[256,512]{1,0:T(8,128)(2,1)} %constant.56.clone.xe_l) | copy-start | bytes 786436
  38.6 0.9 %copy-start.13 = (bf16[256,512]{1,0:T(8,128)(2,1)S(1)}, bf16[256,512]{1,0:T(8,128)(2,1)}, u32[]{:S(2)}) copy-start(bf16[256,512]{1,0:T(8,128)(2,1)} %constant.55.clone.xe_h) | copy-start | bytes 786436
  39.5 17.1 %copy-start.6 = (bf16[256,512]{1,0:T(8,128)(2,1)S(1)}, bf16[256,512]{1,0:T(8,128)(2,1)}, u32[]{:S(2)}) copy-start(bf16[256,512]{1,0:T(8,128)(2,1)} %constant.62.clone.fo_l) | copy-start | bytes 786436
  39.5 17.1 %copy-start.7 = (bf16[256,512]{1,0:T(8,128)(2,1)S(1)}, bf16[256,512]{1,0:T(8,128)(2,1)}, u32[]{:S(2)}) copy-start(bf16[256,512]{1,0:T(8,128)(2,1)} %constant.61.clone.fo_h) | copy-start | bytes 786436
  39.5 17.1 %copy-start.8 = (bf16[256,512]{1,0:T(8,128)(2,1)S(1)}, bf16[256,512]{1,0:T(8,128)(2,1)}, u32[]{:S(2)}) copy-start(bf16[256,512]{1,0:T(8,128)(2,1)} %constant.60.clone.fe_l) | copy-start | bytes 786436
  39.5 17.1 %copy-start.9 = (bf16[256,512]{1,0:T(8,128)(2,1)S(1)}, bf16[256,512]{1,0:T(8,128)(2,1)}, u32[]{:S(2)}) copy-start(bf16[256,512]{1,0:T(8,128)(2,1)} %constant.59.clone.fe_h) | copy-start | bytes 786436
  39.5 17.1 %copy-start.14 = (bf16[384,128]{1,0:T(8,128)(2,1)S(1)}, bf16[384,128]{1,0:T(8,128)(2,1)}, u32[]{:S(2)}) copy-start(bf16[384,128]{1,0:T(8,128)(2,1)} %constant.64.clone.ut) | copy-start | bytes 294916
  43.2 13.4 %collective-permute-start.4 = (f32[96,128]{1,0:T(8,128)S(1)}, f32[96,128]{1,0:T(8,128)S(1)}, u32[]{:S(2)}, u32[]{:S(2)}) collective-permute-start(f32[96,128]{1,0:T(8,128)S(1)} %get-tuple-element.9.near), channel_id=1, source_target_pairs={{0,252},{4,0},{8,4},{12,8},{16,12},{20,16},{24,20},{28,24},{32,28}... | collective-permute-start | bytes 147464 | tf_op jit(solution)/shard_map/ppermute | solution.py:478
  43.7 12.9 %collective-permute-start.3 = (f32[96,128]{1,0:T(8,128)S(1)}, f32[96,128]{1,0:T(8,128)S(1)}, u32[]{:S(2)}, u32[]{:S(2)}) collective-permute-start(f32[96,128]{1,0:T(8,128)S(1)} %get-tuple-element.9.near), channel_id=1, source_target_pairs={{0,4},{4,8},{8,12},{12,16},{16,20},{20,24},{24,28},{28,32},{32,36}... | collective-permute-start | bytes 147464 | tf_op jit(solution)/shard_map/ppermute | solution.py:478
  44.9 6.6 %collective-permute-start.6 = (f32[32,128]{1,0:T(8,128)S(1)}, f32[32,128]{1,0:T(8,128)S(1)}, u32[]{:S(2)}, u32[]{:S(2)}) collective-permute-start(f32[32,128]{1,0:T(8,128)S(1)} %get-tuple-element.10), channel_id=1, source_target_pairs={{0,248},{4,252},{8,0},{12,4},{16,8},{20,12},{24,16},{28,20},{32,24... | collective-permute-start | bytes 49160 | tf_op jit(solution)/shard_map/ppermute | solution.py:478
  50.7 5.9 %collective-permute-start.5 = (f32[32,128]{1,0:T(8,128)S(1)}, f32[32,128]{1,0:T(8,128)S(1)}, u32[]{:S(2)}, u32[]{:S(2)}) collective-permute-start(f32[32,128]{1,0:T(8,128)S(1)} %get-tuple-element.10), channel_id=1, source_target_pairs={{0,8},{4,12},{8,16},{12,20},{16,24},{20,28},{24,32},{28,36},{32,40... | collective-permute-start | bytes 49160 | tf_op jit(solution)/shard_map/ppermute | solution.py:478
  63.1 14.2 %copy-start.5 = (bf16[384,256]{1,0:T(8,128)(2,1)S(1)}, bf16[384,256]{1,0:T(8,128)(2,1)}, u32[]{:S(2)}) copy-start(bf16[384,256]{1,0:T(8,128)(2,1)} %constant.51.clone.wz_h.fz_h) | copy-start | bytes 589828
where the time goes:
time: 79.6 us; the launch traced here: 79.2 us
  starting transfers between devices  25.8 us (32%)
  waiting for transfers between devices  15.5 us (19%)
  blocking collectives  14.2 us (18%)
  Pallas kernels  13.7 us (17%)
  local copies, waits for them, and re-layouts  7.23 us (9%)
  other arithmetic  2.56 us (3%)
    all_to_all x1, blocking collectives, exchange(): x = lax.all_to_all(x.reshape(64, 8, 128), 'fft', 0, 0, tiled=True)  14.2 us
    pallas_call x4, Pallas kernels, call(): pl.pallas_call(kernel, name=name, out_shape=shapes, in_specs=specs, out_s...  13.7 us
    all_to_all x1, starting transfers between devices, exchange(): x = lax.all_to_all(x.reshape(64, 8, 128), 'fft', 0, 0, tiled=True)  13 us
    all_to_all x1, waiting for transfers between devices, exchange(): x = lax.all_to_all(x.reshape(64, 8, 128), 'fft', 0, 0, tiled=True)  9.58 us
    ppermute x4, starting transfers between devices, moved(): return lax.ppermute(x, 'fft', [(i, (i + step) % 64) for i in range(64)])  7.49 us
    ppermute x4, waiting for transfers between devices, moved(): return lax.ppermute(x, 'fft', [(i, (i + step) % 64) for i in range(64)])  5.91 us
    ppermute x3, starting transfers between devices, body(): lax.ppermute(own, 'band', [(i, (i + k) % 4) for i in range(4)])  5.3 us
    unnamed x36, local copies, waits for them, and re-layouts  4.77 us
  transfers between devices with their start and end apart: 8, of which 3 were waited for; matrix products, arithmetic and copies ran while one was open for 3% of the time, Pallas kernels for 2%

commit v1 on v0

--- a/solution.py
+++ b/solution.py
@@ -25,7 +25,7 @@
     table = np.asarray(table, np.float32)
     high = table.astype(ml_dtypes.bfloat16)
     low = (table - high.astype(np.float32)).astype(ml_dtypes.bfloat16)
-    return high, low
+    return np.concatenate([high, low], 0)
 
 
 KZ = np.concatenate([np.arange(64), np.arange(128, 192)])
@@ -49,8 +49,13 @@
     gap = np.zeros((128, 64))
     even = [np.concatenate([v, gap], 1) for v in (c, s, -s, c)]
     odd = [np.concatenate([gap, v], 1) for v in (c, s, -s, c)]
-    t["xe"] = pair_of(np.block([[even[0], even[1]], [even[2], even[3]]]))
-    t["xo"] = pair_of(np.block([[odd[0], odd[1]], [odd[2], odd[3]]]))
+    t["ix"] = np.concatenate(
+        [
+            pair_of(np.block([[even[0], even[1]], [even[2], even[3]]])),
+            pair_of(np.block([[odd[0], odd[1]], [odd[2], odd[3]]])),
+        ],
+        0,
+    )
     parts = {}
     for name, table in (("c", c), ("s", s)):
         parts[name] = (
@@ -69,8 +74,7 @@
             )
         return np.concatenate(rows, 0)
 
-    t["fe"] = pair_of(forward_x(0))
-    t["fo"] = pair_of(forward_x(1))
+    t["fx"] = np.concatenate([pair_of(forward_x(0)), pair_of(forward_x(1))], 0)
     c, s = trig(np.concatenate(YS), SIGNED)
     t["fy"] = pair_of(
         np.concatenate([np.concatenate([c, -s], 1), np.concatenate([s, c], 1)], 0)
@@ -147,9 +151,16 @@
     return ky * ky + kz * kz + kx * kx <= R2
 
 
-def kernel_z_inverse(psi, wz_h, wz_l, send, buf, sems):
+def kernel_z_inverse(psi, wz_in, beta, slot, tile, send, own, buf, wz, ids, sems):
     s = lax.axis_index("fft")
-    copies = []
+    ids[...] = jnp.zeros((8, 128), F32)
+    ids[0:1, :] = slot[...].astype(F32)
+    ids[1:2, :] = ((tile[...] % 3) * 288 + tile[...] // 3).astype(F32)
+    later = [
+        pltpu.make_async_copy(beta, own.at[pl.ds(0, 1024)], sems.at[5]),
+        pltpu.make_async_copy(ids, own.at[pl.ds(1024, 8)], sems.at[6]),
+    ]
+    copies = [pltpu.make_async_copy(wz_in, wz, sems.at[4])]
     for plane in range(2):
         base = 1152 * plane
         for k, (src, dst, rows) in enumerate(((432, 0, 144), (0, 144, 152))):
@@ -160,7 +171,7 @@
                     sems.at[2 * plane + k],
                 )
             )
-    for copy in copies:
+    for copy in copies[1:] + copies[:1] + later:
         copy.start()
     r = iota((1, 256), 1)
     main, spare = line_places(r, s)
@@ -184,7 +195,7 @@
         rows += [jnp.concatenate(lines[0], 1), jnp.concatenate(lines[1], 1)]
     high, low = split(jnp.concatenate(rows, 0))
     packed = (mm(pack, high).astype(BF), mm(pack, low).astype(BF))
-    out = three(mm_nt, (wz_h[...], wz_l[...]), packed)
+    out = three(mm_nt, (wz[0:384, :], wz[384:768, :]), packed)
     for c in range(2):
         block = [out[(2 * zi + c) * 64 : (2 * zi + c) * 64 + 64] for zi in range(3)]
         for zi in range(3):
@@ -192,6 +203,8 @@
         send[pl.ds(4 * c + 3, 64, stride=8), :] = jnp.where(
             lane < 32, block[0][:, 128:], jnp.where(lane < 64, block[1][:, 128:], block[2][:, 128:])
         )
+    for copy in later:
+        copy.wait()
 
 
 def block_ids(betas, row):
@@ -207,9 +220,11 @@
 
 
 def kernel_field(
-    recv, ey_h, ey_l, xe_h, xe_l, xo_h, xo_l, u, vloc, dmat, b0, b1, b2, b3,
-    local, near, far, rows_h, rows_l, field_rows,
+    recv, ey, ix_in, u, dmat, b0, b1, b2, b3,
+    field, near, far, rows_h, rows_l, field_rows, ix, sem,
 ):
+    copy = pltpu.make_async_copy(ix_in, ix, sem)
+    copy.start()
     main, spare, other = masks_sp()
     spread = []
     for c in range(2):
@@ -224,10 +239,12 @@
             first.append(jnp.where(main, got, jnp.where(spare, extra, 0.0)))
             second.append(pltpu.roll(jnp.where(other, got, 0.0), 64, 1))
         lines += [jnp.concatenate(first, 1), jnp.concatenate(second, 1)]
-    g = three(mm_nt, (ey_h[...], ey_l[...]), split(jnp.concatenate(lines, 0)))
+    g = three(mm_nt, (ey[0:384, :], ey[384:768, :]), split(jnp.concatenate(lines, 0)))
+    copy.wait()
     out = []
-    for parity, table in ((0, (xe_h, xe_l)), (1, (xo_h, xo_l))):
+    for parity in range(2):
         a = 96 * parity
+        table = [ix[512 * parity + 256 * i : 512 * parity + 256 * i + 256, :] for i in range(2)]
         block = jnp.concatenate(
             [
                 jnp.concatenate(
@@ -241,7 +258,7 @@
             ],
             0,
         )
-        out.append(three(mm, split(block), (table[0][...], table[1][...])))
+        out.append(three(mm, split(block), table))
     even, odd = out
     for c in range(2):
         a = 256 * c
@@ -253,7 +270,7 @@
         for k, tile in enumerate(kinds):
             span = pl.ds(288 * k, 288)
             lanes = pl.ds(128 * c, 128)
-            local[span, lanes] = tile * vloc[span, :]
+            field[span, lanes] = tile
             high, low = split(tile)
             rows_h[span, lanes] = high
             rows_l[span, lanes] = low
@@ -288,9 +305,18 @@
 
 
 def kernel_back(
-    local, near, below, above, below2, above2, b0, b1, b2, b3,
-    fe_h, fe_l, fo_h, fo_l, fy_h, fy_l, ut, send, scr, rows,
+    field, near, below, above, below2, above2, b0, b1, b2, b3,
+    vloc_in, fx_in, fy_in, ut_in, send, scr, rows, vloc, fx, fy, ut, sems,
 ):
+    copies = [
+        pltpu.make_async_copy(vloc_in.at[:, zi, :], vloc.at[zi], sems.at[zi]) for zi in range(3)
+    ] + [
+        pltpu.make_async_copy(fx_in, fx, sems.at[3]),
+        pltpu.make_async_copy(fy_in, fy, sems.at[4]),
+        pltpu.make_async_copy(ut_in, ut, sems.at[5]),
+    ]
+    for copy in copies:
+        copy.start()
     lane = iota((16, 128), 1)
 
     def half(ref, k):
@@ -338,24 +364,30 @@
     tile_of = block_ids(betas, 1).astype(jnp.int32)
     put = one_hot(iota((864, 512), 0) == tile_of)
     both = mm(put, rows[...])
-    applied = local[...] + (both[:, :256] + both[:, 256:])
-    app = split(applied)
+    nonloc = both[:, :256] + both[:, 256:]
+    for copy in copies:
+        copy.wait()
     main, spare, _ = masks_sp()
     spares = [jnp.zeros((64, 128), F32), jnp.zeros((64, 128), F32)]
     for zi in range(3):
-        kinds = [
-            [a[288 * k + 96 * zi : 288 * k + 96 * zi + 96] for a in app] for k in range(3)
-        ]
+        kinds = []
+        for k in range(3):
+            at = slice(288 * k + 96 * zi, 288 * k + 96 * zi + 96)
+            factor = vloc[zi, pl.ds(k, 96, stride=3), :]
+            kinds.append(
+                split(field[at, :] * jnp.concatenate([factor, factor], 1) + nonloc[at, :])
+            )
         h = jnp.zeros((128, 256), F32)
-        for parity, table in ((0, (fe_h, fe_l)), (1, (fo_h, fo_l))):
+        for parity in range(2):
+            table = [fx[512 * parity + 256 * i : 512 * parity + 256 * i + 256, :] for i in range(2)]
             lines = [
                 jnp.concatenate([kinds[parity][i], kinds[parity + 1][i]], 1) for i in range(2)
             ]
-            g = split(three(mm_nt, (table[0][...], table[1][...]), lines))
+            g = split(three(mm_nt, table, lines))
             for c in range(2):
                 part = [v[128 * c : 128 * c + 128] for v in g]
-                at = slice(192 * c + 96 * parity, 192 * c + 96 * parity + 96)
-                h = h + three(mm, part, (fy_h[at, :], fy_l[at, :]))
+                at = 192 * c + 96 * parity
+                h = h + three(mm, part, (fy[at : at + 96, :], fy[384 + at : 480 + at, :]))
         for c in range(2):
             first = h[:64, 128 * c : 128 * c + 128]
             second = pltpu.roll(h[64:, 128 * c : 128 * c + 128], 64, 1)
@@ -367,7 +399,7 @@
         send[pl.ds(4 * c + 3, 64, stride=8), :] = spares[c]
 
 
-def kernel_z_forward(recv, fz_h, fz_l, out):
+def kernel_z_forward(recv, fz, out):
     s = lax.axis_index("fft")
     out[...] = jnp.zeros((1728, 128), F32)
     r = iota((256, 1), 0)
@@ -397,7 +429,7 @@
         highs.append(columns[:, :128].astype(BF))
         lows.append(columns[:, 128:].astype(BF))
     z = three(
-        mm, (jnp.concatenate(highs, 1), jnp.concatenate(lows, 1)), (fz_h[...], fz_l[...])
+        mm, (jnp.concatenate(highs, 1), jnp.concatenate(lows, 1)), (fz[0:384, :], fz[384:768, :])
     )
     low_lane = iota((64, 128), 1) < 64
     for plane in range(2):
@@ -416,7 +448,9 @@
                 out[pl.ds(at + 432, 24, stride=6), :] = tile[:24]
 
 
-def call(kernel, name, out_shape, args, scratch=(), anywhere=()):
+def call(
+    kernel, name, out_shape, args, scratch=(), anywhere=(), anywhere_out=(), limit=VMEM_LIMIT
+):
     specs = [
         pl.BlockSpec(memory_space=pl.ANY if k in anywhere else pltpu.VMEM)
         for k in range(len(args))
@@ -427,51 +461,61 @@
         name=name,
         out_shape=shapes,
         in_specs=specs,
-        out_specs=[pl.BlockSpec(memory_space=pltpu.VMEM)] * len(shapes),
+        out_specs=[
+            pl.BlockSpec(memory_space=pl.ANY if k in anywhere_out else pltpu.VMEM)
+            for k in range(len(shapes))
+        ],
         scratch_shapes=list(scratch),
-        compiler_params=pltpu.CompilerParams(vmem_limit_bytes=VMEM_LIMIT),
+        compiler_params=pltpu.CompilerParams(vmem_limit_bytes=limit),
     )(*args)
     return out
 
 
 def body(psi_g, vloc, beta, blk_slot, blk_tile, dmat):
     t = {
-        name: tuple(jnp.asarray(v) for v in value) if isinstance(value, tuple) else jnp.asarray(value)
-        for name, value in tables().items()
+        name: jnp.asarray(value) for name, value in tables().items()
     }
-    tile_row = (blk_tile % 3) * 288 + blk_tile // 3
-    ids = jnp.concatenate(
-        [blk_slot[None], tile_row[None], jnp.zeros((6, 128), jnp.int32)], 0
-    ).astype(F32)
-    own = jnp.concatenate([beta, ids[None]], 0).reshape(1032, 128)
+    psi = psi_g[0].transpose(1, 0, 2).reshape(3, 2, 288, 128).transpose(0, 2, 1, 3)
+    psi = psi.reshape(1728, 128)
+    send, own = call(
+        kernel_z_inverse,
+        "z_inverse",
+        [(512, 128), (1032, 128)],
+        (psi, t["wz"], beta.reshape(1024, 128), blk_slot[None], blk_tile[None]),
+        [
+            pltpu.VMEM((2, 384, 128), F32),
+            pltpu.VMEM((768, 256), BF),
+            pltpu.VMEM((8, 128), F32),
+            pltpu.SemaphoreType.DMA((7,)),
+        ],
+        anywhere=(0, 1, 2),
+        anywhere_out=(1,),
+        limit=60 * 1024 * 1024,
+    )
     betas = [own] + [
         lax.ppermute(own, "band", [(i, (i + k) % 4) for i in range(4)]) for k in (1, 3, 2)
     ]
 
-    psi = psi_g[0].transpose(1, 0, 2).reshape(3, 2, 288, 128).transpose(0, 2, 1, 3)
-    psi = psi.reshape(1728, 128)
-    (send,) = call(
-        kernel_z_inverse,
-        "z_inverse",
-        [(512, 128)],
-        (psi, *t["wz"]),
-        [pltpu.VMEM((2, 384, 128), F32), pltpu.SemaphoreType.DMA((4,))],
-        anywhere=(0,),
-    )
-
     def exchange(x):
         x = lax.all_to_all(x.reshape(64, 8, 128), "fft", 0, 0, tiled=True)
         return x.reshape(512, 128)
 
     recv = exchange(send)
-    vloc_rows = vloc.reshape(3, 96, 3, 128).transpose(2, 0, 1, 3).reshape(864, 128)
+    vloc_tiles = vloc.reshape(3, 288, 128).transpose(1, 0, 2)
     dmat_rows = dmat.transpose(1, 2, 0).reshape(64, 64)
-    local, near, far = call(
+    field, near, far = call(
         kernel_field,
         "field",
         [(864, 256), (96, 128), (32, 128)],
-        (recv, *t["ey"], *t["xe"], *t["xo"], t["u"], vloc_rows, dmat_rows, *betas),
-        [pltpu.VMEM((896, 256), BF), pltpu.VMEM((896, 256), BF), pltpu.VMEM((512, 256), F32)],
+        (recv, t["ey"], t["ix"], t["u"], dmat_rows, *betas),
+        [
+            pltpu.VMEM((896, 256), BF),
+            pltpu.VMEM((896, 256), BF),
+            pltpu.VMEM((512, 256), F32),
+            pltpu.VMEM((1024, 512), BF),
+            pltpu.SemaphoreType.DMA,
+        ],
+        anywhere=(2,),
     )
 
     def moved(x, step):
@@ -482,10 +526,19 @@
         kernel_back,
         "back",
         [(512, 128)],
-        (local, near, *sides, *betas, *t["fe"], *t["fo"], *t["fy"], t["ut"]),
-        [pltpu.VMEM((16, 256), F32), pltpu.VMEM((512, 512), BF)],
-    )
-    (out,) = call(kernel_z_forward, "z_forward", [(1728, 128)], (exchange(send), *t["fz"]))
+        (field, near, *sides, *betas, vloc_tiles, t["fx"], t["fy"], t["ut"]),
+        [
+            pltpu.VMEM((16, 256), F32),
+            pltpu.VMEM((512, 512), BF),
+            pltpu.VMEM((3, 288, 128), F32),
+            pltpu.VMEM((1024, 512), BF),
+            pltpu.VMEM((768, 256), BF),
+            pltpu.VMEM((384, 128), BF),
+            pltpu.SemaphoreType.DMA((6,)),
+        ],
+        anywhere=(10, 11, 12, 13),
+    )
+    (out,) = call(kernel_z_forward, "z_forward", [(1728, 128)], (exchange(send), t["fz"]))
     out = out.reshape(3, 288, 2, 128).transpose(0, 2, 1, 3).reshape(3, 2, N * N)
     return out.transpose(1, 0, 2)[None]
 

time: 79.6 us -> 93.1 us (1.17)
  blocking collectives: 14.2 us -> 39.2 us
  Pallas kernels: 13.7 us -> 31.7 us
  starting transfers between devices: 25.8 us -> 15.8 us
  waiting for transfers between devices: 15.5 us -> 5.92 us
  local copies, waits for them, and re-layouts: 7.23 us -> 0.05 us
  other arithmetic: 2.56 us -> 0 us
    all_to_all x1 -> x2, blocking collectives: 14.2 us -> 39.2 us  [exchange(): x = lax.all_to_all(x.reshape(64, 8, 128), 'fft', 0, 0, tiled=True)]
    pallas_call x4, Pallas kernels: 13.7 us -> 31.7 us  [call(): pl.pallas_call(kernel, name=name, out_shape=shapes, in_specs=specs, out_s...]
    all_to_all x1 -> x0, starting transfers between devices: 13 us -> none  [exchange(): x = lax.all_to_all(x.reshape(64, 8, 128), 'fft', 0, 0, tiled=True)]
    all_to_all x1 -> x0, waiting for transfers between devices: 9.58 us -> none  [exchange(): x = lax.all_to_all(x.reshape(64, 8, 128), 'fft', 0, 0, tiled=True)]
    unnamed x36 -> x18, local copies, waits for them, and re-layouts: 4.77 us -> 0.05 us
    ppermute x4, starting transfers between devices: 7.49 us -> 10.5 us  [moved(): return lax.ppermute(x, 'fft', [(i, (i + step) % 64) for i in range(64)])]
    reshape x1 -> x0, local copies, waits for them, and re-layouts: 1.23 us -> none  [body(): vloc.reshape(3, 96, 3, 128).transpose(2, 0, 1, 3).reshape(864, 128)]
    transpose x1 -> x0, local copies, waits for them, and re-layouts: 1.15 us -> none  [body(): vloc.reshape(3, 96, 3, 128).transpose(2, 0, 1, 3).reshape(864, 128)]
  transfers between devices with their start and end apart: 8 -> 7, of which waited for: 3 -> 2; matrix products, arithmetic and copies ran while one was open for 3% -> 0% of each run, Pallas kernels for 2% -> 0%
where the time goes in v1:
time: 93.1 us; the launch traced here: 92.8 us
  blocking collectives  39.2 us (42%)
  Pallas kernels  31.7 us (34%)
  starting transfers between devices  15.8 us (17%)
  waiting for transfers between devices  5.92 us (6%)
    all_to_all x2, blocking collectives, exchange(): x = lax.all_to_all(x.reshape(64, 8, 128), 'fft', 0, 0, tiled=True)  39.2 us
    pallas_call x4, Pallas kernels, call(): pl.pallas_call(kernel, name=name, out_shape=shapes, in_specs=specs, out_s...  31.7 us
    ppermute x4, starting transfers between devices, moved(): return lax.ppermute(x, 'fft', [(i, (i + step) % 64) for i in range(64)])  10.5 us
    ppermute x4, waiting for transfers between devices, moved(): return lax.ppermute(x, 'fft', [(i, (i + step) % 64) for i in range(64)])  5.91 us
    ppermute x3, starting transfers between devices, body(): lax.ppermute(own, 'band', [(i, (i + k) % 4) for i in range(4)])  5.3 us
  transfers between devices with their start and end apart: 7, of which 2 were waited for; matrix products, arithmetic and copies ran while one was open for 0% of the time, Pallas kernels for 0%

profile of v1, /device:TPU:1, one launch (start us, length us, event | category | flops | bytes accessed | tf_op | source)
XLA Modules:
  0.0 92.8 jit_solution(16338766762010403786)
XLA Ops:
  0.0 0.0 copy-start.8
  0.0 18.5 %z_inverse.1 = (f32[512,128]{1,0:T(8,128)}, f32[1032,128]{1,0:T(8,128)}) custom-call(f32[1728,128]{1,0:T(8,128)} %bitcast.36, bf16[768,256]{1,0:T(8,128)(2,1)} %constant.12.clone.wz_in.fz, f32[1024,128]{1,0:T(8,128)} %bitcast.37, s32[1,128]{1,0:T(1,128)} %bitcast.39, s32[1,128]{1,0:T(1,128)} %bitcast.40), custom_call_target="tpu_custom_call" | custom-call | tf_op jit(solution)/shard_map/z_inverse/pallas_call | solution.py:459
  18.6 0.0 copy-start
  18.6 3.8 %collective-permute-start.2 = (f32[1032,128]{1,0:T(8,128)}, f32[1032,128]{1,0:T(8,128)S(1)}, u32[]{:S(2)}, u32[]{:S(2)}) collective-permute-start(f32[1032,128]{1,0:T(8,128)} %get-tuple-element.11.b0), channel_id=1, source_target_pairs={{0,2},{1,3},{2,0},{3,1},{4,6},{5,7},{6,4},{7,5},{8,10},{9,11},{10,... | collective-permute-start | bytes 1585160 | tf_op jit(solution)/shard_map/ppermute | solution.py:496
  22.4 0.8 collective-permute-start.1
  23.2 0.7 collective-permute-start
  23.9 25.0 %all_to_all.10 = f32[64,8,128]{2,1,0:T(8,128)S(1)} all-to-all(f32[64,8,128]{2,1,0:T(8,128)} %bitcast.38), channel_id=1, replica_groups=mesh['fft'=64,'band'=4] {'fft'}, dimensions={0} | all-to-all | bytes 524288 | tf_op jit(solution)/shard_map/all_to_all | solution.py:500
  48.9 0.0 collective-permute-done.2.b3
  48.9 0.0 collective-permute-done.1.b2
  48.9 0.0 collective-permute-done.b1
  48.9 0.0 copy-done.2
  48.9 0.0 copy-done.4
  48.9 0.0 copy-done.7
  48.9 0.0 copy-done.8
  48.9 0.0 copy-done
  48.9 0.0 copy-start.3
  48.9 0.0 copy-start.5
  49.0 0.0 copy-start.6
  49.0 3.9 %field.1 = (f32[864,256]{1,0:T(8,128)S(1)}, f32[96,128]{1,0:T(8,128)S(1)}, f32[32,128]{1,0:T(8,128)S(1)}) custom-call(f32[512,128]{1,0:T(8,128)S(1)} %bitcast.33, bf16[768,256]{1,0:T(8,128)(2,1)S(1)} %copy-done.2, bf16[1024,512]{1,0:T(8,128)(2,1)S(1)} %copy-done.4, bf16[128,384]{1,0:T(8,128)(2,1)S(1)} %copy-done.7, f32[64,64]{1,0:T(8,128)S(1)} %bitcast.35, ...), custom_call_target="tpu_custom_call" | custom-call | tf_op jit(solution)/shard_map/field/pallas_call | solution.py:459
  52.9 0.5 collective-permute-start.4
  53.4 1.3 %collective-permute-start.3 = (f32[96,128]{1,0:T(8,128)S(1)}, f32[96,128]{1,0:T(8,128)S(1)}, u32[]{:S(2)}, u32[]{:S(2)}) collective-permute-start(f32[96,128]{1,0:T(8,128)S(1)} %get-tuple-element.13.near), channel_id=1, source_target_pairs={{0,4},{4,8},{8,12},{12,16},{16,20},{20,24},{24,28},{28,32},{32,36}... | collective-permute-start | bytes 147464 | tf_op jit(solution)/shard_map/ppermute | solution.py:522
  54.7 8.6 %collective-permute-start.6 = (f32[32,128]{1,0:T(8,128)S(1)}, f32[32,128]{1,0:T(8,128)S(1)}, u32[]{:S(2)}, u32[]{:S(2)}) collective-permute-start(f32[32,128]{1,0:T(8,128)S(1)} %get-tuple-element.14), channel_id=1, source_target_pairs={{0,248},{4,252},{8,0},{12,4},{16,8},{20,12},{24,16},{28,20},{32,24... | collective-permute-start | bytes 49160 | tf_op jit(solution)/shard_map/ppermute | solution.py:522
  63.4 0.0 collective-permute-start.5
  63.4 0.9 collective-permute-done.6.above2
  64.3 5.0 %collective-permute-done.5.below2 = f32[32,128]{1,0:T(8,128)S(1)} collective-permute-done((f32[32,128]{1,0:T(8,128)S(1)}, f32[32,128]{1,0:T(8,128)S(1)}, u32[]{:S(2)}, u32[]{:S(2)}) %collective-permute-start.5) | collective-permute-done | bytes 16416 | tf_op jit(solution)/shard_map/ppermute | solution.py:522
  69.3 0.0 collective-permute-done.4.above
  69.3 0.0 collective-permute-done.3.below
  69.3 0.0 copy-done.3
  69.3 7.4 %back.1 = f32[512,128]{1,0:T(8,128)S(1)} custom-call(f32[864,256]{1,0:T(8,128)S(1)} %get-tuple-element.12.field, f32[96,128]{1,0:T(8,128)S(1)} %get-tuple-element.13.near, f32[96,128]{1,0:T(8,128)S(1)} %collective-permute-done.3.below, f32[96,128]{1,0:T(8,128)S(1)} %collective-permute-done.4.above, f32[32,128]{1,0:T(8,128)S(1)} %collective-permute-done.5.below2, ...), custom_call_target="tpu_custom_call" | custom-call | tf_op jit(solution)/shard_map/back/pallas_call | solution.py:459
  76.8 0.0 copy-start.1
  76.8 14.2 %all_to_all.11 = f32[64,8,128]{2,1,0:T(8,128)S(1)} all-to-all(f32[64,8,128]{2,1,0:T(8,128)S(1)} %bitcast.31), channel_id=1, replica_groups=mesh['fft'=64,'band'=4] {'fft'}, dimensions={0} | all-to-all | bytes 524288 | tf_op jit(solution)/shard_map/all_to_all | solution.py:500
  91.0 1.8 %z_forward.1 = f32[1728,128]{1,0:T(8,128)} custom-call(f32[512,128]{1,0:T(8,128)S(1)} %bitcast.32, bf16[768,256]{1,0:T(8,128)(2,1)S(1)} %copy-done.1), custom_call_target="tpu_custom_call" | custom-call | tf_op jit(solution)/shard_map/z_forward/pallas_call | solution.py:459
  (6 shorter events, 0.0 us)
Async XLA Ops:
  0.0 48.9 %copy-start.2 = (bf16[768,256]{1,0:T(8,128)(2,1)S(1)}, bf16[768,256]{1,0:T(8,128)(2,1)}, u32[]{:S(2)}) copy-start(bf16[768,256]{1,0:T(8,128)(2,1)} %constant.13.clone.ey.fy_in) | copy-start | bytes 1179652
  0.0 48.9 %copy-start.4 = (bf16[1024,512]{1,0:T(8,128)(2,1)S(1)}, bf16[1024,512]{1,0:T(8,128)(2,1)}, u32[]{:S(2)}) copy-start(bf16[1024,512]{1,0:T(8,128)(2,1)} %constant.14.clone.ix_in) | copy-start | bytes 3145732
  0.0 48.9 %copy-start.7 = (bf16[128,384]{1,0:T(8,128)(2,1)S(1)}, bf16[128,384]{1,0:T(8,128)(2,1)}, u32[]{:S(2)}) copy-start(bf16[128,384]{1,0:T(8,128)(2,1)} %constant.16.clone.u) | copy-start | bytes 294916
  0.0 48.9 %copy-start.8 = (f32[64,8,8]{0,2,1:T(8,128)S(1)}, f32[64,8,8]{0,2,1:T(8,128)}, u32[]{:S(2)}) copy-start(f32[64,8,8]{0,2,1:T(8,128)} %param.19) | copy-start | bytes 49156
  18.6 30.4 %copy-start = (f32[1032,128]{1,0:T(8,128)S(1)}, f32[1032,128]{1,0:T(8,128)}, u32[]{:S(2)}) copy-start(f32[1032,128]{1,0:T(8,128)} %get-tuple-element.11.b0) | copy-start | bytes 1585156
  18.6 30.3 %collective-permute-start.2 = (f32[1032,128]{1,0:T(8,128)}, f32[1032,128]{1,0:T(8,128)S(1)}, u32[]{:S(2)}, u32[]{:S(2)}) collective-permute-start(f32[1032,128]{1,0:T(8,128)} %get-tuple-element.11.b0), channel_id=1, source_target_pairs={{0,2},{1,3},{2,0},{3,1},{4,6},{5,7},{6,4},{7,5},{8,10},{9,11},{10,... | collective-permute-start | bytes 1585160 | tf_op jit(solution)/shard_map/ppermute | solution.py:496
  22.4 26.5 %collective-permute-start.1 = (f32[1032,128]{1,0:T(8,128)}, f32[1032,128]{1,0:T(8,128)S(1)}, u32[]{:S(2)}, u32[]{:S(2)}) collective-permute-start(f32[1032,128]{1,0:T(8,128)} %get-tuple-element.11.b0), channel_id=1, source_target_pairs={{0,3},{1,0},{2,1},{3,2},{4,7},{5,4},{6,5},{7,6},{8,11},{9,8},{10,9... | collective-permute-start | bytes 1585160 | tf_op jit(solution)/shard_map/ppermute | solution.py:496
  23.2 25.7 %collective-permute-start = (f32[1032,128]{1,0:T(8,128)}, f32[1032,128]{1,0:T(8,128)S(1)}, u32[]{:S(2)}, u32[]{:S(2)}) collective-permute-start(f32[1032,128]{1,0:T(8,128)} %get-tuple-element.11.b0), channel_id=1, source_target_pairs={{0,1},{1,2},{2,3},{3,0},{4,5},{5,6},{6,7},{7,4},{8,9},{9,10},{10,1... | collective-permute-start | bytes 1585160 | tf_op jit(solution)/shard_map/ppermute | solution.py:496
  48.9 20.4 %copy-start.3 = (bf16[1024,512]{1,0:T(8,128)(2,1)S(1)}, bf16[1024,512]{1,0:T(8,128)(2,1)}, u32[]{:S(2)}) copy-start(bf16[1024,512]{1,0:T(8,128)(2,1)} %constant.15.clone.fx_in) | copy-start | bytes 3145732
  48.9 20.4 %copy-start.5 = (f32[3,36864]{1,0:T(4,128)S(1)}, f32[3,36864]{1,0:T(4,128)}, u32[]{:S(2)}) copy-start(f32[3,36864]{1,0:T(4,128)} %param.15) | copy-start | bytes 1327108
  49.0 20.4 %copy-start.6 = (bf16[384,128]{1,0:T(8,128)(2,1)S(1)}, bf16[384,128]{1,0:T(8,128)(2,1)}, u32[]{:S(2)}) copy-start(bf16[384,128]{1,0:T(8,128)(2,1)} %constant.17.clone.ut_in) | copy-start | bytes 294916
  52.9 16.4 %collective-permute-start.4 = (f32[96,128]{1,0:T(8,128)S(1)}, f32[96,128]{1,0:T(8,128)S(1)}, u32[]{:S(2)}, u32[]{:S(2)}) collective-permute-start(f32[96,128]{1,0:T(8,128)S(1)} %get-tuple-element.13.near), channel_id=1, source_target_pairs={{0,252},{4,0},{8,4},{12,8},{16,12},{20,16},{24,20},{28,24},{32,28}... | collective-permute-start | bytes 147464 | tf_op jit(solution)/shard_map/ppermute | solution.py:522
  53.4 15.9 %collective-permute-start.3 = (f32[96,128]{1,0:T(8,128)S(1)}, f32[96,128]{1,0:T(8,128)S(1)}, u32[]{:S(2)}, u32[]{:S(2)}) collective-permute-start(f32[96,128]{1,0:T(8,128)S(1)} %get-tuple-element.13.near), channel_id=1, source_target_pairs={{0,4},{4,8},{8,12},{12,16},{16,20},{20,24},{24,28},{28,32},{32,36}... | collective-permute-start | bytes 147464 | tf_op jit(solution)/shard_map/ppermute | solution.py:522
  54.7 9.5 %collective-permute-start.6 = (f32[32,128]{1,0:T(8,128)S(1)}, f32[32,128]{1,0:T(8,128)S(1)}, u32[]{:S(2)}, u32[]{:S(2)}) collective-permute-start(f32[32,128]{1,0:T(8,128)S(1)} %get-tuple-element.14), channel_id=1, source_target_pairs={{0,248},{4,252},{8,0},{12,4},{16,8},{20,12},{24,16},{28,20},{32,24... | collective-permute-start | bytes 49160 | tf_op jit(solution)/shard_map/ppermute | solution.py:522
  63.4 5.9 %collective-permute-start.5 = (f32[32,128]{1,0:T(8,128)S(1)}, f32[32,128]{1,0:T(8,128)S(1)}, u32[]{:S(2)}, u32[]{:S(2)}) collective-permute-start(f32[32,128]{1,0:T(8,128)S(1)} %get-tuple-element.14), channel_id=1, source_target_pairs={{0,8},{4,12},{8,16},{12,20},{16,24},{20,28},{24,32},{28,36},{32,40... | collective-permute-start | bytes 49160 | tf_op jit(solution)/shard_map/ppermute | solution.py:522
  76.8 14.2 %copy-start.1 = (bf16[768,256]{1,0:T(8,128)(2,1)S(1)}, bf16[768,256]{1,0:T(8,128)(2,1)}, u32[]{:S(2)}) copy-start(bf16[768,256]{1,0:T(8,128)(2,1)} %constant.12.clone.wz_in.fz) | copy-start | bytes 1179652

commit v2 on v1

--- a/solution.py
+++ b/solution.py
@@ -57,27 +57,20 @@
         0,
     )
     parts = {}
+    c, s = trig(np.arange(N), SIGNED)
+    gap = np.zeros((64, 128))
     for name, table in (("c", c), ("s", s)):
-        parts[name] = (
-            np.concatenate([table, gap], 1),
-            np.concatenate([gap, table], 1),
-        )
+        parts[name] = (np.concatenate([table, gap], 0), np.concatenate([gap, table], 0))
 
     def forward_x(which):
         cc, ss = parts["c"][which], parts["s"][which]
-        rows = []
-        for first, second in ((cc, ss), (-ss, cc)):
-            rows.append(
-                np.concatenate(
-                    [first[:, :128], second[:, :128], first[:, 128:], second[:, 128:]], 1
-                )
-            )
-        return np.concatenate(rows, 0)
+        first, second = np.concatenate([cc, -ss], 1), np.concatenate([ss, cc], 1)
+        return np.concatenate([first[:128], second[:128], first[128:], second[128:]], 0)
 
     t["fx"] = np.concatenate([pair_of(forward_x(0)), pair_of(forward_x(1))], 0)
-    c, s = trig(np.concatenate(YS), SIGNED)
+    c, s = trig(SIGNED, np.concatenate(YS))
     t["fy"] = pair_of(
-        np.concatenate([np.concatenate([c, -s], 1), np.concatenate([s, c], 1)], 0)
+        np.concatenate([np.concatenate([c, s], 1), np.concatenate([-s, c], 1)], 0)
     )
     blocks = []
     for zi in range(3):
@@ -151,15 +144,12 @@
     return ky * ky + kz * kz + kx * kx <= R2
 
 
-def kernel_z_inverse(psi, wz_in, beta, slot, tile, send, own, buf, wz, ids, sems):
+def kernel_z_inverse(psi, wz_in, beta, slot, tile, send, own, buf, wz, sems):
     s = lax.axis_index("fft")
-    ids[...] = jnp.zeros((8, 128), F32)
-    ids[0:1, :] = slot[...].astype(F32)
-    ids[1:2, :] = ((tile[...] % 3) * 288 + tile[...] // 3).astype(F32)
-    later = [
-        pltpu.make_async_copy(beta, own.at[pl.ds(0, 1024)], sems.at[5]),
-        pltpu.make_async_copy(ids, own.at[pl.ds(1024, 8)], sems.at[6]),
-    ]
+    own[1024:1025, :] = slot[...].astype(F32)
+    own[1025:1026, :] = ((tile[...] % 3) * 288 + tile[...] // 3).astype(F32)
+    own[1026:1032, :] = jnp.zeros((6, 128), F32)
+    later = [pltpu.make_async_copy(beta, own.at[pl.ds(0, 1024)], sems.at[5])]
     copies = [pltpu.make_async_copy(wz_in, wz, sems.at[4])]
     for plane in range(2):
         base = 1152 * plane
@@ -367,30 +357,41 @@
     nonloc = both[:, :256] + both[:, 256:]
     for copy in copies:
         copy.wait()
+    kinds = []
+    for k in range(3):
+        factor = jnp.concatenate([vloc[zi, pl.ds(k, 96, stride=3), :] for zi in range(3)], 0)
+        at = slice(288 * k, 288 * k + 288)
+        kinds.append(split(field[at, :] * jnp.concatenate([factor, factor], 1) + nonloc[at, :]))
+    g = []
+    for parity in range(2):
+        table = [fx[1024 * parity + 512 * i : 1024 * parity + 512 * i + 512, :] for i in range(2)]
+        lines = [jnp.concatenate([kinds[parity][i], kinds[parity + 1][i]], 1) for i in range(2)]
+        g.append(split(three(mm, lines, table)))
+    lines = [
+        jnp.concatenate(
+            [
+                jnp.concatenate(
+                    [
+                        g[parity][i][96 * zi : 96 * zi + 96, 128 * c : 128 * c + 128]
+                        for zi in range(3)
+                    ],
+                    1,
+                )
+                for c in range(2)
+                for parity in range(2)
+            ],
+            0,
+        )
+        for i in range(2)
+    ]
+    h = three(mm, (fy[0:256, :], fy[256:512, :]), lines)
     main, spare, _ = masks_sp()
     spares = [jnp.zeros((64, 128), F32), jnp.zeros((64, 128), F32)]
     for zi in range(3):
-        kinds = []
-        for k in range(3):
-            at = slice(288 * k + 96 * zi, 288 * k + 96 * zi + 96)
-            factor = vloc[zi, pl.ds(k, 96, stride=3), :]
-            kinds.append(
-                split(field[at, :] * jnp.concatenate([factor, factor], 1) + nonloc[at, :])
-            )
-        h = jnp.zeros((128, 256), F32)
-        for parity in range(2):
-            table = [fx[512 * parity + 256 * i : 512 * parity + 256 * i + 256, :] for i in range(2)]
-            lines = [
-                jnp.concatenate([kinds[parity][i], kinds[parity + 1][i]], 1) for i in range(2)
-            ]
-            g = split(three(mm_nt, table, lines))
-            for c in range(2):
-                part = [v[128 * c : 128 * c + 128] for v in g]
-                at = 192 * c + 96 * parity
-                h = h + three(mm, part, (fy[at : at + 96, :], fy[384 + at : 480 + at, :]))
         for c in range(2):
-            first = h[:64, 128 * c : 128 * c + 128]
-            second = pltpu.roll(h[64:, 128 * c : 128 * c + 128], 64, 1)
+            turned = h[128 * c : 128 * c + 128, 128 * zi : 128 * zi + 128].T
+            first = turned[:64]
+            second = pltpu.roll(turned[64:], 64, 1)
             send[pl.ds(4 * c + zi, 64, stride=8), :] = jnp.where(main, first, second)
             high, low = split(jnp.where(spare, first, 0.0))
             move = ut[128 * zi : 128 * zi + 128, :]
@@ -448,9 +449,7 @@
                 out[pl.ds(at + 432, 24, stride=6), :] = tile[:24]
 
 
-def call(
-    kernel, name, out_shape, args, scratch=(), anywhere=(), anywhere_out=(), limit=VMEM_LIMIT
-):
+def call(kernel, name, out_shape, args, scratch=(), anywhere=(), limit=VMEM_LIMIT):
     specs = [
         pl.BlockSpec(memory_space=pl.ANY if k in anywhere else pltpu.VMEM)
         for k in range(len(args))
@@ -461,10 +460,7 @@
         name=name,
         out_shape=shapes,
         in_specs=specs,
-        out_specs=[
-            pl.BlockSpec(memory_space=pl.ANY if k in anywhere_out else pltpu.VMEM)
-            for k in range(len(shapes))
-        ],
+        out_specs=[pl.BlockSpec(memory_space=pltpu.VMEM)] * len(shapes),
         scratch_shapes=list(scratch),
         compiler_params=pltpu.CompilerParams(vmem_limit_bytes=limit),
     )(*args)
@@ -485,11 +481,9 @@
         [
             pltpu.VMEM((2, 384, 128), F32),
             pltpu.VMEM((768, 256), BF),
-            pltpu.VMEM((8, 128), F32),
-            pltpu.SemaphoreType.DMA((7,)),
+            pltpu.SemaphoreType.DMA((6,)),
         ],
         anywhere=(0, 1, 2),
-        anywhere_out=(1,),
         limit=60 * 1024 * 1024,
     )
     betas = [own] + [
@@ -531,8 +525,8 @@
             pltpu.VMEM((16, 256), F32),
             pltpu.VMEM((512, 512), BF),
             pltpu.VMEM((3, 288, 128), F32),
-            pltpu.VMEM((1024, 512), BF),
-            pltpu.VMEM((768, 256), BF),
+            pltpu.VMEM((2048, 256), BF),
+            pltpu.VMEM((512, 384), BF),
             pltpu.VMEM((384, 128), BF),
             pltpu.SemaphoreType.DMA((6,)),
         ],

time: 93.1 us -> 76.4 us (0.82)
  Pallas kernels: 31.7 us -> 15 us
    pallas_call x4, Pallas kernels: 31.7 us -> 15 us  [call(): pl.pallas_call(kernel, name=name, out_shape=shapes, in_specs=specs, out_s...]
where the time goes in v2:
time: 76.4 us; the launch traced here: 76.2 us
  blocking collectives  39.2 us (51%)
  starting transfers between devices  15.8 us (21%)
  Pallas kernels  15 us (20%)
  waiting for transfers between devices  5.92 us (8%)
    all_to_all x2, blocking collectives, exchange(): x = lax.all_to_all(x.reshape(64, 8, 128), 'fft', 0, 0, tiled=True)  39.2 us
    pallas_call x4, Pallas kernels, call(): pl.pallas_call(kernel, name=name, out_shape=shapes, in_specs=specs, out_s...  15 us
    ppermute x4, starting transfers between devices, moved(): return lax.ppermute(x, 'fft', [(i, (i + step) % 64) for i in range(64)])  10.5 us
    ppermute x4, waiting for transfers between devices, moved(): return lax.ppermute(x, 'fft', [(i, (i + step) % 64) for i in range(64)])  5.91 us
    ppermute x3, starting transfers between devices, body(): lax.ppermute(own, 'band', [(i, (i + k) % 4) for i in range(4)])  5.3 us
  transfers between devices with their start and end apart: 7, of which 2 were waited for; matrix products, arithmetic and copies ran while one was open for 0% of the time, Pallas kernels for 0%

profile of v2, /device:TPU:1, one launch (start us, length us, event | category | flops | bytes accessed | tf_op | source)
XLA Modules:
  0.0 76.2 jit_solution(14176787620460961869)
XLA Ops:
  0.0 0.0 copy-start.9
  0.0 3.5 %z_inverse.1 = (f32[512,128]{1,0:T(8,128)}, f32[1032,128]{1,0:T(8,128)}) custom-call(f32[1728,128]{1,0:T(8,128)} %bitcast.36, bf16[768,256]{1,0:T(8,128)(2,1)} %constant.14.clone.wz_in.fz, f32[1024,128]{1,0:T(8,128)} %bitcast.37, s32[1,128]{1,0:T(1,128)} %bitcast.39, s32[1,128]{1,0:T(1,128)} %bitcast.40), custom_call_target="tpu_custom_call" | custom-call | tf_op jit(solution)/shard_map/z_inverse/pallas_call | solution.py:458
  3.5 0.0 copy-start
  3.5 3.8 %collective-permute-start.2 = (f32[1032,128]{1,0:T(8,128)}, f32[1032,128]{1,0:T(8,128)S(1)}, u32[]{:S(2)}, u32[]{:S(2)}) collective-permute-start(f32[1032,128]{1,0:T(8,128)} %get-tuple-element.11.b0), channel_id=1, source_target_pairs={{0,2},{1,3},{2,0},{3,1},{4,6},{5,7},{6,4},{7,5},{8,10},{9,11},{10,... | collective-permute-start | bytes 1585160 | tf_op jit(solution)/shard_map/ppermute | solution.py:490
  7.4 0.8 %collective-permute-start.1 = (f32[1032,128]{1,0:T(8,128)}, f32[1032,128]{1,0:T(8,128)S(1)}, u32[]{:S(2)}, u32[]{:S(2)}) collective-permute-start(f32[1032,128]{1,0:T(8,128)} %get-tuple-element.11.b0), channel_id=1, source_target_pairs={{0,3},{1,0},{2,1},{3,2},{4,7},{5,4},{6,5},{7,6},{8,11},{9,8},{10,9... | collective-permute-start | bytes 1585160 | tf_op jit(solution)/shard_map/ppermute | solution.py:490
  8.1 0.7 collective-permute-start
  8.8 25.0 %all_to_all.10 = f32[64,8,128]{2,1,0:T(8,128)S(1)} all-to-all(f32[64,8,128]{2,1,0:T(8,128)} %bitcast.38), channel_id=1, replica_groups=mesh['fft'=64,'band'=4] {'fft'}, dimensions={0} | all-to-all | bytes 524288 | tf_op jit(solution)/shard_map/all_to_all | solution.py:494
  33.8 0.0 collective-permute-done.2.b3
  33.8 0.0 collective-permute-done.1.b2
  33.8 0.0 collective-permute-done.b1
  33.8 0.0 copy-done.3
  33.9 0.0 copy-done.6
  33.9 0.0 copy-done.8
  33.9 0.0 copy-done.9
  33.9 0.0 copy-done
  33.9 0.0 copy-start.2
  33.9 0.0 copy-start.4
  33.9 0.0 copy-start.5
  33.9 0.0 copy-start.7
  33.9 3.9 %field.1 = (f32[864,256]{1,0:T(8,128)S(1)}, f32[96,128]{1,0:T(8,128)S(1)}, f32[32,128]{1,0:T(8,128)S(1)}) custom-call(f32[512,128]{1,0:T(8,128)S(1)} %bitcast.33, bf16[768,256]{1,0:T(8,128)(2,1)S(1)} %copy-done.6, bf16[1024,512]{1,0:T(8,128)(2,1)S(1)} %copy-done.3, bf16[128,384]{1,0:T(8,128)(2,1)S(1)} %copy-done.8, f32[64,64]{1,0:T(8,128)S(1)} %bitcast.35, ...), custom_call_target="tpu_custom_call" | custom-call | tf_op jit(solution)/shard_map/field/pallas_call | solution.py:458
  37.9 0.5 collective-permute-start.4
  38.4 1.3 %collective-permute-start.3 = (f32[96,128]{1,0:T(8,128)S(1)}, f32[96,128]{1,0:T(8,128)S(1)}, u32[]{:S(2)}, u32[]{:S(2)}) collective-permute-start(f32[96,128]{1,0:T(8,128)S(1)} %get-tuple-element.13.near), channel_id=1, source_target_pairs={{0,4},{4,8},{8,12},{12,16},{16,20},{20,24},{24,28},{28,32},{32,36}... | collective-permute-start | bytes 147464 | tf_op jit(solution)/shard_map/ppermute | solution.py:516
  39.7 8.6 %collective-permute-start.6 = (f32[32,128]{1,0:T(8,128)S(1)}, f32[32,128]{1,0:T(8,128)S(1)}, u32[]{:S(2)}, u32[]{:S(2)}) collective-permute-start(f32[32,128]{1,0:T(8,128)S(1)} %get-tuple-element.14), channel_id=1, source_target_pairs={{0,248},{4,252},{8,0},{12,4},{16,8},{20,12},{24,16},{28,20},{32,24... | collective-permute-start | bytes 49160 | tf_op jit(solution)/shard_map/ppermute | solution.py:516
  48.3 0.0 collective-permute-start.5
  48.4 0.9 %collective-permute-done.6.above2 = f32[32,128]{1,0:T(8,128)S(1)} collective-permute-done((f32[32,128]{1,0:T(8,128)S(1)}, f32[32,128]{1,0:T(8,128)S(1)}, u32[]{:S(2)}, u32[]{:S(2)}) %collective-permute-start.6) | collective-permute-done | bytes 16416 | tf_op jit(solution)/shard_map/ppermute | solution.py:516
  49.2 5.0 %collective-permute-done.5.below2 = f32[32,128]{1,0:T(8,128)S(1)} collective-permute-done((f32[32,128]{1,0:T(8,128)S(1)}, f32[32,128]{1,0:T(8,128)S(1)}, u32[]{:S(2)}, u32[]{:S(2)}) %collective-permute-start.5) | collective-permute-done | bytes 16416 | tf_op jit(solution)/shard_map/ppermute | solution.py:516
  54.3 0.0 collective-permute-done.4.above
  54.3 0.0 collective-permute-done.3.below
  54.3 5.8 %back.1 = f32[512,128]{1,0:T(8,128)S(1)} custom-call(f32[864,256]{1,0:T(8,128)S(1)} %get-tuple-element.12.field, f32[96,128]{1,0:T(8,128)S(1)} %get-tuple-element.13.near, f32[96,128]{1,0:T(8,128)S(1)} %collective-permute-done.3.below, f32[96,128]{1,0:T(8,128)S(1)} %collective-permute-done.4.above, f32[32,128]{1,0:T(8,128)S(1)} %collective-permute-done.5.below2, ...), custom_call_target="tpu_custom_call" | custom-call | tf_op jit(solution)/shard_map/back/pallas_call | solution.py:458
  60.1 0.0 copy-start.1
  60.1 14.2 %all_to_all.11 = f32[64,8,128]{2,1,0:T(8,128)S(1)} all-to-all(f32[64,8,128]{2,1,0:T(8,128)S(1)} %bitcast.31), channel_id=1, replica_groups=mesh['fft'=64,'band'=4] {'fft'}, dimensions={0} | all-to-all | bytes 524288 | tf_op jit(solution)/shard_map/all_to_all | solution.py:494
  74.3 1.8 %z_forward.1 = f32[1728,128]{1,0:T(8,128)} custom-call(f32[512,128]{1,0:T(8,128)S(1)} %bitcast.32, bf16[768,256]{1,0:T(8,128)(2,1)S(1)} %copy-done.1), custom_call_target="tpu_custom_call" | custom-call | tf_op jit(solution)/shard_map/z_forward/pallas_call | solution.py:458
  (8 shorter events, 0.0 us)
Async XLA Ops:
  0.0 33.8 %copy-start.3 = (bf16[1024,512]{1,0:T(8,128)(2,1)S(1)}, bf16[1024,512]{1,0:T(8,128)(2,1)}, u32[]{:S(2)}) copy-start(bf16[1024,512]{1,0:T(8,128)(2,1)} %constant.16.clone.ix_in) | copy-start | bytes 3145732
  0.0 33.9 %copy-start.6 = (bf16[768,256]{1,0:T(8,128)(2,1)S(1)}, bf16[768,256]{1,0:T(8,128)(2,1)}, u32[]{:S(2)}) copy-start(bf16[768,256]{1,0:T(8,128)(2,1)} %constant.15.clone.ey) | copy-start | bytes 1179652
  0.0 33.9 %copy-start.8 = (bf16[128,384]{1,0:T(8,128)(2,1)S(1)}, bf16[128,384]{1,0:T(8,128)(2,1)}, u32[]{:S(2)}) copy-start(bf16[128,384]{1,0:T(8,128)(2,1)} %constant.19.clone.u) | copy-start | bytes 294916
  0.0 33.9 %copy-start.9 = (f32[64,8,8]{0,2,1:T(8,128)S(1)}, f32[64,8,8]{0,2,1:T(8,128)}, u32[]{:S(2)}) copy-start(f32[64,8,8]{0,2,1:T(8,128)} %param.19) | copy-start | bytes 49156
  3.5 30.4 %copy-start = (f32[1032,128]{1,0:T(8,128)S(1)}, f32[1032,128]{1,0:T(8,128)}, u32[]{:S(2)}) copy-start(f32[1032,128]{1,0:T(8,128)} %get-tuple-element.11.b0) | copy-start | bytes 1585156
  3.5 30.3 %collective-permute-start.2 = (f32[1032,128]{1,0:T(8,128)}, f32[1032,128]{1,0:T(8,128)S(1)}, u32[]{:S(2)}, u32[]{:S(2)}) collective-permute-start(f32[1032,128]{1,0:T(8,128)} %get-tuple-element.11.b0), channel_id=1, source_target_pairs={{0,2},{1,3},{2,0},{3,1},{4,6},{5,7},{6,4},{7,5},{8,10},{9,11},{10,... | collective-permute-start | bytes 1585160 | tf_op jit(solution)/shard_map/ppermute | solution.py:490
  7.4 26.5 %collective-permute-start.1 = (f32[1032,128]{1,0:T(8,128)}, f32[1032,128]{1,0:T(8,128)S(1)}, u32[]{:S(2)}, u32[]{:S(2)}) collective-permute-start(f32[1032,128]{1,0:T(8,128)} %get-tuple-element.11.b0), channel_id=1, source_target_pairs={{0,3},{1,0},{2,1},{3,2},{4,7},{5,4},{6,5},{7,6},{8,11},{9,8},{10,9... | collective-permute-start | bytes 1585160 | tf_op jit(solution)/shard_map/ppermute | solution.py:490
  8.1 25.7 %collective-permute-start = (f32[1032,128]{1,0:T(8,128)}, f32[1032,128]{1,0:T(8,128)S(1)}, u32[]{:S(2)}, u32[]{:S(2)}) collective-permute-start(f32[1032,128]{1,0:T(8,128)} %get-tuple-element.11.b0), channel_id=1, source_target_pairs={{0,1},{1,2},{2,3},{3,0},{4,5},{5,6},{6,7},{7,4},{8,9},{9,10},{10,1... | collective-permute-start | bytes 1585160 | tf_op jit(solution)/shard_map/ppermute | solution.py:490
  33.9 20.4 %copy-start.2 = (bf16[2048,256]{1,0:T(8,128)(2,1)S(1)}, bf16[2048,256]{1,0:T(8,128)(2,1)}, u32[]{:S(2)}) copy-start(bf16[2048,256]{1,0:T(8,128)(2,1)} %constant.17.clone.fx_in) | copy-start | bytes 3145732
  33.9 20.4 %copy-start.4 = (f32[3,36864]{1,0:T(4,128)S(1)}, f32[3,36864]{1,0:T(4,128)}, u32[]{:S(2)}) copy-start(f32[3,36864]{1,0:T(4,128)} %param.15) | copy-start | bytes 1327108
  33.9 20.4 %copy-start.5 = (bf16[512,384]{1,0:T(8,128)(2,1)S(1)}, bf16[512,384]{1,0:T(8,128)(2,1)}, u32[]{:S(2)}) copy-start(bf16[512,384]{1,0:T(8,128)(2,1)} %constant.18.clone.fy_in) | copy-start | bytes 1179652
  33.9 20.4 %copy-start.7 = (bf16[384,128]{1,0:T(8,128)(2,1)S(1)}, bf16[384,128]{1,0:T(8,128)(2,1)}, u32[]{:S(2)}) copy-start(bf16[384,128]{1,0:T(8,128)(2,1)} %constant.20.clone.ut_in) | copy-start | bytes 294916
  37.9 16.4 %collective-permute-start.4 = (f32[96,128]{1,0:T(8,128)S(1)}, f32[96,128]{1,0:T(8,128)S(1)}, u32[]{:S(2)}, u32[]{:S(2)}) collective-permute-start(f32[96,128]{1,0:T(8,128)S(1)} %get-tuple-element.13.near), channel_id=1, source_target_pairs={{0,252},{4,0},{8,4},{12,8},{16,12},{20,16},{24,20},{28,24},{32,28}... | collective-permute-start | bytes 147464 | tf_op jit(solution)/shard_map/ppermute | solution.py:516
  38.4 15.9 %collective-permute-start.3 = (f32[96,128]{1,0:T(8,128)S(1)}, f32[96,128]{1,0:T(8,128)S(1)}, u32[]{:S(2)}, u32[]{:S(2)}) collective-permute-start(f32[96,128]{1,0:T(8,128)S(1)} %get-tuple-element.13.near), channel_id=1, source_target_pairs={{0,4},{4,8},{8,12},{12,16},{16,20},{20,24},{24,28},{28,32},{32,36}... | collective-permute-start | bytes 147464 | tf_op jit(solution)/shard_map/ppermute | solution.py:516
  39.7 9.5 %collective-permute-start.6 = (f32[32,128]{1,0:T(8,128)S(1)}, f32[32,128]{1,0:T(8,128)S(1)}, u32[]{:S(2)}, u32[]{:S(2)}) collective-permute-start(f32[32,128]{1,0:T(8,128)S(1)} %get-tuple-element.14), channel_id=1, source_target_pairs={{0,248},{4,252},{8,0},{12,4},{16,8},{20,12},{24,16},{28,20},{32,24... | collective-permute-start | bytes 49160 | tf_op jit(solution)/shard_map/ppermute | solution.py:516
  48.3 5.9 %collective-permute-start.5 = (f32[32,128]{1,0:T(8,128)S(1)}, f32[32,128]{1,0:T(8,128)S(1)}, u32[]{:S(2)}, u32[]{:S(2)}) collective-permute-start(f32[32,128]{1,0:T(8,128)S(1)} %get-tuple-element.14), channel_id=1, source_target_pairs={{0,8},{4,12},{8,16},{12,20},{16,24},{20,28},{24,32},{28,36},{32,40... | collective-permute-start | bytes 49160 | tf_op jit(solution)/shard_map/ppermute | solution.py:516
  60.1 14.2 %copy-start.1 = (bf16[768,256]{1,0:T(8,128)(2,1)S(1)}, bf16[768,256]{1,0:T(8,128)(2,1)}, u32[]{:S(2)}) copy-start(bf16[768,256]{1,0:T(8,128)(2,1)} %constant.14.clone.wz_in.fz) | copy-start | bytes 1179652

commit v3 on v2

--- a/solution.py
+++ b/solution.py
@@ -144,13 +144,9 @@
     return ky * ky + kz * kz + kx * kx <= R2
 
 
-def kernel_z_inverse(psi, wz_in, beta, slot, tile, send, own, buf, wz, sems):
+def kernel_z_inverse(psi, wz_in, send, buf, wz, sems):
     s = lax.axis_index("fft")
-    own[1024:1025, :] = slot[...].astype(F32)
-    own[1025:1026, :] = ((tile[...] % 3) * 288 + tile[...] // 3).astype(F32)
-    own[1026:1032, :] = jnp.zeros((6, 128), F32)
-    later = [pltpu.make_async_copy(beta, own.at[pl.ds(0, 1024)], sems.at[5])]
-    copies = [pltpu.make_async_copy(wz_in, wz, sems.at[4])]
+    copies = []
     for plane in range(2):
         base = 1152 * plane
         for k, (src, dst, rows) in enumerate(((432, 0, 144), (0, 144, 152))):
@@ -161,18 +157,18 @@
                     sems.at[2 * plane + k],
                 )
             )
-    for copy in copies[1:] + copies[:1] + later:
+    copies.append(pltpu.make_async_copy(wz_in, wz, sems.at[4]))
+    for copy in copies:
         copy.start()
-    r = iota((1, 256), 1)
-    main, spare = line_places(r, s)
+    main, spare = line_places(iota((1, 256), 1), s)
     j = iota((128, 256), 0)
     pack = jnp.concatenate(
         [one_hot(j == main), one_hot((j % 32 == spare) & (j < 96))], axis=0
     )
-    for copy in copies:
-        copy.wait()
     lane = iota((64, 128), 1)
     rows = []
+    for copy in copies[:4]:
+        copy.wait()
     for plane in range(2):
         lines = [[], []]
         for c in range(2):
@@ -185,6 +181,7 @@
         rows += [jnp.concatenate(lines[0], 1), jnp.concatenate(lines[1], 1)]
     high, low = split(jnp.concatenate(rows, 0))
     packed = (mm(pack, high).astype(BF), mm(pack, low).astype(BF))
+    copies[4].wait()
     out = three(mm_nt, (wz[0:384, :], wz[384:768, :]), packed)
     for c in range(2):
         block = [out[(2 * zi + c) * 64 : (2 * zi + c) * 64 + 64] for zi in range(3)]
@@ -193,28 +190,19 @@
         send[pl.ds(4 * c + 3, 64, stride=8), :] = jnp.where(
             lane < 32, block[0][:, 128:], jnp.where(lane < 64, block[1][:, 128:], block[2][:, 128:])
         )
-    for copy in later:
-        copy.wait()
-
-
-def block_ids(betas, row):
-    return jnp.concatenate([b[1024 + row : 1025 + row, :] for b in betas], 1)
+
+
+def tile_rows(tiles):
+    return (tiles % 3) * 288 + tiles // 3
 
 
 def as_column(ids):
-    return jnp.broadcast_to(ids, (8, 512)).T[:, 0:1]
-
-
-def slot_hot(betas):
-    return one_hot(as_column(block_ids(betas, 0)).astype(jnp.int32) == iota((512, 256), 1))
+    return jnp.broadcast_to(ids.astype(F32), (8, 512)).T[:, 0:1].astype(jnp.int32)
 
 
 def kernel_field(
-    recv, ey, ix_in, u, dmat, b0, b1, b2, b3,
-    field, near, far, rows_h, rows_l, field_rows, ix, sem,
+    recv, ey, ix, u, field, rows_h, rows_l,
 ):
-    copy = pltpu.make_async_copy(ix_in, ix, sem)
-    copy.start()
     main, spare, other = masks_sp()
     spread = []
     for c in range(2):
@@ -230,7 +218,6 @@
             second.append(pltpu.roll(jnp.where(other, got, 0.0), 64, 1))
         lines += [jnp.concatenate(first, 1), jnp.concatenate(second, 1)]
     g = three(mm_nt, (ey[0:384, :], ey[384:768, :]), split(jnp.concatenate(lines, 0)))
-    copy.wait()
     out = []
     for parity in range(2):
         a = 96 * parity
@@ -267,8 +254,10 @@
     rows_h[864:896, :] = jnp.zeros((32, 256), BF)
     rows_l[864:896, :] = jnp.zeros((32, 256), BF)
 
+
+def kernel_project(rows_h, rows_l, dmat, ids, b0, b1, b2, b3, near, far, slots_out, field_rows):
     betas = (b0, b1, b2, b3)
-    tile_of = as_column(block_ids(betas, 1)).astype(jnp.int32)
+    tile_of = as_column(tile_rows(ids[1:2, :]))
     pick = one_hot(tile_of == iota((512, 896), 1))
     field_rows[...] = mm(pick, rows_h[...]) + mm(pick, rows_l[...])
     lane = iota((128, 128), 1)
@@ -284,7 +273,8 @@
                 )
         sums.append(total.T[:16])
     high, low = split(jnp.concatenate(sums, 1))
-    slots = slot_hot(betas)
+    slots = one_hot(as_column(ids[0:1, :]) == iota((512, 256), 1))
+    slots_out[...] = slots
     coef = mm(high, slots) + mm(low, slots)
     coef = jnp.where(iota((16, 256), 1) < 192, coef, 0.0)
     near[0:64, :] = jnp.concatenate([dmat[...], jnp.zeros((64, 64), F32)], 1)
@@ -294,8 +284,12 @@
     far[16:32, :] = coef[:, 128:]
 
 
+def kernel_put(ids, put):
+    put[...] = one_hot(iota((864, 512), 0) == tile_rows(ids[1:2, :]))
+
+
 def kernel_back(
-    field, near, below, above, below2, above2, b0, b1, b2, b3,
+    field, near, below, above, below2, above2, slots, put, b0, b1, b2, b3,
     vloc_in, fx_in, fy_in, ut_in, send, scr, rows, vloc, fx, fy, ut, sems,
 ):
     copies = [
@@ -337,23 +331,21 @@
                 row = jnp.sum(coupling[h][8 * j : 8 * j + 8, :] * coef, axis=0, keepdims=True)
                 scr[8 * c + j : 8 * c + j + 1, 128 * h : 128 * h + 128] = row
     betas = (b0, b1, b2, b3)
-    slots = slot_hot(betas)
     high, low = split(scr[...])
-    weight = mm_nt(slots, high) + mm_nt(slots, low)
+    weight = mm_nt(slots[...], high) + mm_nt(slots[...], low)
+    high, low = split(weight)
+    weight = jnp.concatenate([high, low], 1)
     for k, beta in enumerate(betas):
         span = slice(128 * k, 128 * k + 128)
-        terms = [jnp.zeros((128, 128), F32), jnp.zeros((128, 128), F32)]
+        terms = jnp.zeros((128, 256), F32)
         for j in range(8):
+            wide = one_hot(iota((32, 256), 0) % 16 == 8 * (iota((32, 256), 1) // 128) + j)
             projector = beta[pl.ds(j, 128, stride=8), :]
-            for c in range(2):
-                terms[c] = terms[c] + projector * weight[span, 8 * c + j : 8 * c + j + 1]
-        for c in range(2):
-            high, low = split(terms[c])
-            rows[span, 128 * c : 128 * c + 128] = high
-            rows[span, 256 + 128 * c : 384 + 128 * c] = low
-    tile_of = block_ids(betas, 1).astype(jnp.int32)
-    put = one_hot(iota((864, 512), 0) == tile_of)
-    both = mm(put, rows[...])
+            terms = terms + mm(weight[span], wide) * jnp.concatenate([projector, projector], 1)
+        high, low = split(terms)
+        rows[span, 0:256] = high
+        rows[span, 256:512] = low
+    both = mm(put[...], rows[...])
     nonloc = both[:, :256] + both[:, 256:]
     for copy in copies:
         copy.wait()
@@ -449,19 +441,26 @@
                 out[pl.ds(at + 432, 24, stride=6), :] = tile[:24]
 
 
-def call(kernel, name, out_shape, args, scratch=(), anywhere=(), limit=VMEM_LIMIT):
+def call(kernel, name, out_shape, args, scratch=(), anywhere=(), anywhere_out=(), limit=VMEM_LIMIT, cost=None):
     specs = [
         pl.BlockSpec(memory_space=pl.ANY if k in anywhere else pltpu.VMEM)
         for k in range(len(args))
     ]
-    shapes = [jax.ShapeDtypeStruct(shape, F32) for shape in out_shape]
+    shapes = [
+        jax.ShapeDtypeStruct(*shape) if isinstance(shape[0], tuple) else jax.ShapeDtypeStruct(shape, F32)
+        for shape in out_shape
+    ]
     out = pl.pallas_call(
         kernel,
         name=name,
         out_shape=shapes,
         in_specs=specs,
-        out_specs=[pl.BlockSpec(memory_space=pltpu.VMEM)] * len(shapes),
+        out_specs=[
+            pl.BlockSpec(memory_space=pl.ANY if k in anywhere_out else pltpu.VMEM)
+            for k in range(len(shapes))
+        ],
         scratch_shapes=list(scratch),
+        cost_estimate=cost,
         compiler_params=pltpu.CompilerParams(vmem_limit_bytes=limit),
     )(*args)
     return out
@@ -473,22 +472,26 @@
     }
     psi = psi_g[0].transpose(1, 0, 2).reshape(3, 2, 288, 128).transpose(0, 2, 1, 3)
     psi = psi.reshape(1728, 128)
-    send, own = call(
+    def gathered(x):
+        return [x] + [
+            lax.ppermute(x, "band", [(i, (i + k) % 4) for i in range(4)]) for k in (1, 3, 2)
+        ]
+
+    betas = gathered(beta.reshape(1024, 128))
+    ids = jnp.concatenate(gathered(jnp.stack([blk_slot, blk_tile])), 1)
+    (send,) = call(
         kernel_z_inverse,
         "z_inverse",
-        [(512, 128), (1032, 128)],
-        (psi, t["wz"], beta.reshape(1024, 128), blk_slot[None], blk_tile[None]),
+        [(512, 128)],
+        (psi, t["wz"]),
         [
             pltpu.VMEM((2, 384, 128), F32),
             pltpu.VMEM((768, 256), BF),
-            pltpu.SemaphoreType.DMA((6,)),
+            pltpu.SemaphoreType.DMA((5,)),
         ],
-        anywhere=(0, 1, 2),
+        anywhere=(0, 1),
         limit=60 * 1024 * 1024,
     )
-    betas = [own] + [
-        lax.ppermute(own, "band", [(i, (i + k) % 4) for i in range(4)]) for k in (1, 3, 2)
-    ]
 
     def exchange(x):
         x = lax.all_to_all(x.reshape(64, 8, 128), "fft", 0, 0, tiled=True)
@@ -497,30 +500,36 @@
     recv = exchange(send)
     vloc_tiles = vloc.reshape(3, 288, 128).transpose(1, 0, 2)
     dmat_rows = dmat.transpose(1, 2, 0).reshape(64, 64)
-    field, near, far = call(
+    field, rows_h, rows_l = call(
         kernel_field,
         "field",
-        [(864, 256), (96, 128), (32, 128)],
-        (recv, t["ey"], t["ix"], t["u"], dmat_rows, *betas),
-        [
-            pltpu.VMEM((896, 256), BF),
-            pltpu.VMEM((896, 256), BF),
-            pltpu.VMEM((512, 256), F32),
-            pltpu.VMEM((1024, 512), BF),
-            pltpu.SemaphoreType.DMA,
-        ],
-        anywhere=(2,),
+        [(864, 256), ((896, 256), BF), ((896, 256), BF)],
+        (recv, t["ey"], t["ix"], t["u"]),
+    )
+    near, far, slots = call(
+        kernel_project,
+        "project",
+        [(96, 128), (32, 128), ((512, 256), BF)],
+        (rows_h, rows_l, dmat_rows, ids, *betas),
+        [pltpu.VMEM((512, 256), F32)],
     )
 
     def moved(x, step):
         return lax.ppermute(x, "fft", [(i, (i + step) % 64) for i in range(64)])
 
     sides = (moved(near, 1), moved(near, -1), moved(far, 2), moved(far, -2))
+    (put,) = call(
+        kernel_put,
+        "put",
+        [((864, 512), BF)],
+        (ids,),
+        cost=pl.CostEstimate(flops=2000000, bytes_accessed=3000000, transcendentals=0),
+    )
     (send,) = call(
         kernel_back,
         "back",
         [(512, 128)],
-        (field, near, *sides, *betas, vloc_tiles, t["fx"], t["fy"], t["ut"]),
+        (field, near, *sides, slots, put, *betas, vloc_tiles, t["fx"], t["fy"], t["ut"]),
         [
             pltpu.VMEM((16, 256), F32),
             pltpu.VMEM((512, 512), BF),
@@ -530,7 +539,7 @@
             pltpu.VMEM((384, 128), BF),
             pltpu.SemaphoreType.DMA((6,)),
         ],
-        anywhere=(10, 11, 12, 13),
+        anywhere=(12, 13, 14, 15),
     )
     (out,) = call(kernel_z_forward, "z_forward", [(1728, 128)], (exchange(send), t["fz"]))
     out = out.reshape(3, 288, 2, 128).transpose(0, 2, 1, 3).reshape(3, 2, N * N)

time: 76.4 us -> 75.1 us (0.983)
  starting transfers between devices: 15.8 us -> 31.1 us
  blocking collectives: 39.2 us -> 24.1 us
  Pallas kernels: 15 us -> 12.8 us
    all_to_all x2 -> x1, blocking collectives: 39.2 us -> 24.1 us  [exchange(): x = lax.all_to_all(x.reshape(64, 8, 128), 'fft', 0, 0, tiled=True)]
    all_to_all x0 -> x1, starting transfers between devices: none -> 13.1 us  [exchange(): x = lax.all_to_all(x.reshape(64, 8, 128), 'fft', 0, 0, tiled=True)]
    ppermute x3 -> x6, starting transfers between devices: 5.3 us -> 11.5 us  [gathered(): lax.ppermute(x, 'band', [(i, (i + k) % 4) for i in range(4)])]
    ppermute x4, waiting for transfers between devices: 5.91 us -> 0.96 us  [moved(): return lax.ppermute(x, 'fft', [(i, (i + step) % 64) for i in range(64)])]
    ppermute x4, starting transfers between devices: 10.5 us -> 6.47 us  [moved(): return lax.ppermute(x, 'fft', [(i, (i + step) % 64) for i in range(64)])]
    ppermute x3 -> x6, waiting for transfers between devices: 0.01 us -> 2.61 us  [gathered(): lax.ppermute(x, 'band', [(i, (i + k) % 4) for i in range(4)])]
    all_to_all x0 -> x1, waiting for transfers between devices: none -> 2.4 us  [exchange(): x = lax.all_to_all(x.reshape(64, 8, 128), 'fft', 0, 0, tiled=True)]
    pallas_call x4 -> x6, Pallas kernels: 15 us -> 12.8 us  [call(): pl.pallas_call(kernel, name=name, out_shape=shapes, in_specs=specs, out_s...]
  transfers between devices with their start and end apart: 7 -> 11, of which waited for: 2 -> 4; matrix products, arithmetic and copies ran while one was open for 0% -> 0% of each run, Pallas kernels for 0% -> 5%
where the time goes in v3:
time: 75.1 us; the launch traced here: 74.9 us
  starting transfers between devices  31.1 us (41%)
  blocking collectives  24.1 us (32%)
  Pallas kernels  12.8 us (17%)
  waiting for transfers between devices  5.97 us (8%)
    all_to_all x1, blocking collectives, exchange(): x = lax.all_to_all(x.reshape(64, 8, 128), 'fft', 0, 0, tiled=True)  24.1 us
    all_to_all x1, starting transfers between devices, exchange(): x = lax.all_to_all(x.reshape(64, 8, 128), 'fft', 0, 0, tiled=True)  13.1 us
    pallas_call x6, Pallas kernels, call(): pl.pallas_call(kernel, name=name, out_shape=shapes, in_specs=specs, out_s...  12.8 us
    ppermute x6, starting transfers between devices, gathered(): lax.ppermute(x, 'band', [(i, (i + k) % 4) for i in range(4)])  11.5 us
    ppermute x4, starting transfers between devices, moved(): return lax.ppermute(x, 'fft', [(i, (i + step) % 64) for i in range(64)])  6.47 us
    ppermute x6, waiting for transfers between devices, gathered(): lax.ppermute(x, 'band', [(i, (i + k) % 4) for i in range(4)])  2.61 us
    all_to_all x1, waiting for transfers between devices, exchange(): x = lax.all_to_all(x.reshape(64, 8, 128), 'fft', 0, 0, tiled=True)  2.4 us
  transfers between devices with their start and end apart: 11, of which 4 were waited for; matrix products, arithmetic and copies ran while one was open for 0% of the time, Pallas kernels for 5%

profile of v3, /device:TPU:1, one launch (start us, length us, event | category | flops | bytes accessed | tf_op | source)
XLA Modules:
  0.0 74.9 jit_solution(15796486800542870975)
XLA Ops:
  0.0 2.1 %collective-permute-start.3 = (f32[1024,128]{1,0:T(8,128)}, f32[1024,128]{1,0:T(8,128)S(1)}, u32[]{:S(2)}, u32[]{:S(2)}) collective-permute-start(f32[1024,128]{1,0:T(8,128)} %bitcast.31), channel_id=1, source_target_pairs={{0,1},{1,2},{2,3},{3,0},{4,5},{5,6},{6,7},{7,4},{8,9},{9,10},{10,1... | collective-permute-start | bytes 1572872 | tf_op jit(solution)/shard_map/ppermute | solution.py:477
  2.1 1.5 %collective-permute-start.4 = (f32[1024,128]{1,0:T(8,128)}, f32[1024,128]{1,0:T(8,128)S(1)}, u32[]{:S(2)}, u32[]{:S(2)}) collective-permute-start(f32[1024,128]{1,0:T(8,128)} %bitcast.32), channel_id=1, source_target_pairs={{0,3},{1,0},{2,1},{3,2},{4,7},{5,4},{6,5},{7,6},{8,11},{9,8},{10,9... | collective-permute-start | bytes 1572872 | tf_op jit(solution)/shard_map/ppermute | solution.py:477
  3.6 1.6 %collective-permute-start.5 = (f32[1024,128]{1,0:T(8,128)}, f32[1024,128]{1,0:T(8,128)S(1)}, u32[]{:S(2)}, u32[]{:S(2)}) collective-permute-start(f32[1024,128]{1,0:T(8,128)} %bitcast.33), channel_id=1, source_target_pairs={{0,2},{1,3},{2,0},{3,1},{4,6},{5,7},{6,4},{7,5},{8,10},{9,11},{10,... | collective-permute-start | bytes 1572872 | tf_op jit(solution)/shard_map/ppermute | solution.py:477
  5.2 2.4 %z_inverse.1 = f32[512,128]{1,0:T(8,128)} custom-call(f32[1728,128]{1,0:T(8,128)} %bitcast.42, bf16[768,256]{1,0:T(8,128)(2,1)} %constant.14.clone.wz_in.fz), custom_call_target="tpu_custom_call" | custom-call | tf_op jit(solution)/shard_map/z_inverse/pallas_call | solution.py:453
  7.6 0.0 copy-start.5
  7.7 0.0 copy-start.6
  7.7 13.1 %all-to-all-start = ((f32[64,8,128]{2,1,0:T(8,128)}), f32[64,8,128]{2,1,0:T(8,128)S(1)}, u32[]{:S(2)}, u32[]{:S(2)}) async-start(f32[64,8,128]{2,1,0:T(8,128)} %bitcast.41), calls=%async_computation | async-start | bytes 524288 | tf_op jit(solution)/shard_map/all_to_all | solution.py:497
  20.8 0.0 copy-start.9
  20.8 0.0 copy-start.10
  20.8 0.6 copy-done.9
  21.5 0.0 copy-done.10
  21.5 0.5 collective-permute-start
  22.0 2.3 %collective-permute-start.1 = (s32[2,128]{1,0:T(2,128)S(1)}, s32[2,128]{1,0:T(2,128)S(1)}, u32[]{:S(2)}, u32[]{:S(2)}) collective-permute-start(s32[2,128]{1,0:T(2,128)S(1)} %pad_add_fusion.1), channel_id=1, source_target_pairs={{0,3},{1,0},{2,1},{3,2},{4,7},{5,4},{6,5},{7,6},{8,11},{9,8},{10,9... | collective-permute-start | bytes 3080 | tf_op jit(solution)/shard_map/ppermute | solution.py:477
  24.2 1.4 %collective-permute-done = s32[2,128]{1,0:T(2,128)S(1)} collective-permute-done((s32[2,128]{1,0:T(2,128)S(1)}, s32[2,128]{1,0:T(2,128)S(1)}, u32[]{:S(2)}, u32[]{:S(2)}) %collective-permute-start) | collective-permute-done | bytes 1056 | tf_op jit(solution)/shard_map/ppermute | solution.py:477
  25.6 3.6 %collective-permute-start.2 = (s32[2,128]{1,0:T(2,128)S(1)}, s32[2,128]{1,0:T(2,128)S(1)}, u32[]{:S(2)}, u32[]{:S(2)}) collective-permute-start(s32[2,128]{1,0:T(2,128)S(1)} %pad_add_fusion.1), channel_id=1, source_target_pairs={{0,2},{1,3},{2,0},{3,1},{4,6},{5,7},{6,4},{7,5},{8,10},{9,11},{10,... | collective-permute-start | bytes 3080 | tf_op jit(solution)/shard_map/ppermute | solution.py:477
  29.2 1.2 %collective-permute-done.2 = s32[2,128]{1,0:T(2,128)S(1)} collective-permute-done((s32[2,128]{1,0:T(2,128)S(1)}, s32[2,128]{1,0:T(2,128)S(1)}, u32[]{:S(2)}, u32[]{:S(2)}) %collective-permute-start.2) | collective-permute-done | bytes 1056 | tf_op jit(solution)/shard_map/ppermute | solution.py:477
  30.4 2.4 %all-to-all-done = f32[64,8,128]{2,1,0:T(8,128)S(1)} async-done(((f32[64,8,128]{2,1,0:T(8,128)}), f32[64,8,128]{2,1,0:T(8,128)S(1)}, u32[]{:S(2)}, u32[]{:S(2)}) %all-to-all-start) | async-done | bytes 262176 | tf_op jit(solution)/shard_map/all_to_all | solution.py:497
  32.8 0.0 copy-start
  32.8 0.0 copy-start.8
  32.9 1.3 %field.1 = (f32[864,256]{1,0:T(8,128)S(1)}, bf16[896,256]{1,0:T(8,128)(2,1)S(1)}, bf16[896,256]{1,0:T(8,128)(2,1)S(1)}) custom-call(f32[512,128]{1,0:T(8,128)S(1)} %bitcast.36, bf16[768,256]{1,0:T(8,128)(2,1)S(1)} %copy-done.5, bf16[1024,512]{1,0:T(8,128)(2,1)S(1)} %copy-done.2, bf16[128,384]{1,0:T(8,128)(2,1)S(1)} %copy-done.6), custom_call_target="tpu_custom_call" | custom-call | tf_op jit(solution)/shard_map/field/pallas_call | solution.py:453
  34.1 0.0 collective-permute-done.3.b1
  34.2 0.0 copy-start.4
  34.2 2.5 %project.1 = (f32[96,128]{1,0:T(8,128)S(1)}, f32[32,128]{1,0:T(8,128)S(1)}, bf16[512,256]{1,0:T(8,128)(2,1)S(1)}) custom-call(bf16[896,256]{1,0:T(8,128)(2,1)S(1)} %get-tuple-element.12.rows_h, bf16[896,256]{1,0:T(8,128)(2,1)S(1)} %get-tuple-element.13.rows_l, f32[64,64]{1,0:T(8,128)S(1)} %bitcast.40, s32[2,512]{1,0:T(2,128)S(1)} %pad_add_fusion.ids, ...), custom_call_target="tpu_custom_call" | custom-call | tf_op jit(solution)/shard_map/project/pallas_call | solution.py:453
  36.7 1.4 %collective-permute-start.6 = (f32[96,128]{1,0:T(8,128)S(1)}, f32[96,128]{1,0:T(8,128)S(1)}, u32[]{:S(2)}, u32[]{:S(2)}) collective-permute-start(f32[96,128]{1,0:T(8,128)S(1)} %get-tuple-element.14.near), channel_id=1, source_target_pairs={{0,4},{4,8},{8,12},{12,16},{16,20},{20,24},{24,28},{28,32},{32,36}... | collective-permute-start | bytes 147464 | tf_op jit(solution)/shard_map/ppermute | solution.py:518
  38.1 1.2 %collective-permute-start.8 = (f32[32,128]{1,0:T(8,128)S(1)}, f32[32,128]{1,0:T(8,128)S(1)}, u32[]{:S(2)}, u32[]{:S(2)}) collective-permute-start(f32[32,128]{1,0:T(8,128)S(1)} %get-tuple-element.15), channel_id=1, source_target_pairs={{0,8},{4,12},{8,16},{12,20},{16,24},{20,28},{24,32},{28,36},{32,40... | collective-permute-start | bytes 49160 | tf_op jit(solution)/shard_map/ppermute | solution.py:518
  39.2 3.9 %collective-permute-start.9 = (f32[32,128]{1,0:T(8,128)S(1)}, f32[32,128]{1,0:T(8,128)S(1)}, u32[]{:S(2)}, u32[]{:S(2)}) collective-permute-start(f32[32,128]{1,0:T(8,128)S(1)} %get-tuple-element.15), channel_id=1, source_target_pairs={{0,248},{4,252},{8,0},{12,4},{16,8},{20,12},{24,16},{28,20},{32,24... | collective-permute-start | bytes 49160 | tf_op jit(solution)/shard_map/ppermute | solution.py:518
  43.1 0.2 put.1
  43.3 1.0 %collective-permute-done.8.below2 = f32[32,128]{1,0:T(8,128)S(1)} collective-permute-done((f32[32,128]{1,0:T(8,128)S(1)}, f32[32,128]{1,0:T(8,128)S(1)}, u32[]{:S(2)}, u32[]{:S(2)}) %collective-permute-start.8) | collective-permute-done | bytes 16416 | tf_op jit(solution)/shard_map/ppermute | solution.py:518
  44.3 4.6 %back.1 = f32[512,128]{1,0:T(8,128)S(1)} custom-call(f32[864,256]{1,0:T(8,128)S(1)} %get-tuple-element.11.field, f32[96,128]{1,0:T(8,128)S(1)} %get-tuple-element.14.near, f32[96,128]{1,0:T(8,128)S(1)} %collective-permute-done.6.below, f32[96,128]{1,0:T(8,128)S(1)} %collective-permute-done.7.above, f32[32,128]{1,0:T(8,128)S(1)} %collective-permute-done.8.below2, ...), custom_call_target="tpu_custom_call" | custom-call | tf_op jit(solution)/shard_map/back/pallas_call | solution.py:453
  48.9 0.0 copy-start.1
  49.0 24.1 %all_to_all.10 = f32[64,8,128]{2,1,0:T(8,128)S(1)} all-to-all(f32[64,8,128]{2,1,0:T(8,128)S(1)} %bitcast.37), channel_id=1, replica_groups=mesh['fft'=64,'band'=4] {'fft'}, dimensions={0} | all-to-all | bytes 524288 | tf_op jit(solution)/shard_map/all_to_all | solution.py:497
  73.1 1.8 %z_forward.1 = f32[1728,128]{1,0:T(8,128)} custom-call(f32[512,128]{1,0:T(8,128)S(1)} %bitcast.38, bf16[768,256]{1,0:T(8,128)(2,1)S(1)} %copy-done.1), custom_call_target="tpu_custom_call" | custom-call | tf_op jit(solution)/shard_map/z_forward/pallas_call | solution.py:453
  (21 shorter events, 0.1 us)
Async XLA Ops:
  0.0 32.8 %copy-start.2 = (bf16[1024,512]{1,0:T(8,128)(2,1)S(1)}, bf16[1024,512]{1,0:T(8,128)(2,1)}, u32[]{:S(2)}) copy-start(bf16[1024,512]{1,0:T(8,128)(2,1)} %constant.16.clone.ix) | copy-start | bytes 3145732
  0.0 34.1 %collective-permute-start.3 = (f32[1024,128]{1,0:T(8,128)}, f32[1024,128]{1,0:T(8,128)S(1)}, u32[]{:S(2)}, u32[]{:S(2)}) collective-permute-start(f32[1024,128]{1,0:T(8,128)} %bitcast.31), channel_id=1, source_target_pairs={{0,1},{1,2},{2,3},{3,0},{4,5},{5,6},{6,7},{7,4},{8,9},{9,10},{10,1... | collective-permute-start | bytes 1572872 | tf_op jit(solution)/shard_map/ppermute | solution.py:477
  2.1 32.0 %collective-permute-start.4 = (f32[1024,128]{1,0:T(8,128)}, f32[1024,128]{1,0:T(8,128)S(1)}, u32[]{:S(2)}, u32[]{:S(2)}) collective-permute-start(f32[1024,128]{1,0:T(8,128)} %bitcast.32), channel_id=1, source_target_pairs={{0,3},{1,0},{2,1},{3,2},{4,7},{5,4},{6,5},{7,6},{8,11},{9,8},{10,9... | collective-permute-start | bytes 1572872 | tf_op jit(solution)/shard_map/ppermute | solution.py:477
  3.6 30.5 %collective-permute-start.5 = (f32[1024,128]{1,0:T(8,128)}, f32[1024,128]{1,0:T(8,128)S(1)}, u32[]{:S(2)}, u32[]{:S(2)}) collective-permute-start(f32[1024,128]{1,0:T(8,128)} %bitcast.33), channel_id=1, source_target_pairs={{0,2},{1,3},{2,0},{3,1},{4,6},{5,7},{6,4},{7,5},{8,10},{9,11},{10,... | collective-permute-start | bytes 1572872 | tf_op jit(solution)/shard_map/ppermute | solution.py:477
  7.6 25.2 %copy-start.5 = (bf16[768,256]{1,0:T(8,128)(2,1)S(1)}, bf16[768,256]{1,0:T(8,128)(2,1)}, u32[]{:S(2)}) copy-start(bf16[768,256]{1,0:T(8,128)(2,1)} %constant.15.clone.ey) | copy-start | bytes 1179652
  7.7 25.2 %copy-start.6 = (bf16[128,384]{1,0:T(8,128)(2,1)S(1)}, bf16[128,384]{1,0:T(8,128)(2,1)}, u32[]{:S(2)}) copy-start(bf16[128,384]{1,0:T(8,128)(2,1)} %constant.19.clone.u) | copy-start | bytes 294916
  7.7 25.1 %all-to-all-start = ((f32[64,8,128]{2,1,0:T(8,128)}), f32[64,8,128]{2,1,0:T(8,128)S(1)}, u32[]{:S(2)}, u32[]{:S(2)}) async-start(f32[64,8,128]{2,1,0:T(8,128)} %bitcast.41), calls=%async_computation | async-start | bytes 524288 | tf_op jit(solution)/shard_map/all_to_all | solution.py:497
  20.8 0.7 copy-start.9
  20.8 0.7 copy-start.10
  21.5 4.1 %collective-permute-start = (s32[2,128]{1,0:T(2,128)S(1)}, s32[2,128]{1,0:T(2,128)S(1)}, u32[]{:S(2)}, u32[]{:S(2)}) collective-permute-start(s32[2,128]{1,0:T(2,128)S(1)} %pad_add_fusion.1), channel_id=1, source_target_pairs={{0,1},{1,2},{2,3},{3,0},{4,5},{5,6},{6,7},{7,4},{8,9},{9,10},{10,1... | collective-permute-start | bytes 3080 | tf_op jit(solution)/shard_map/ppermute | solution.py:477
  22.0 7.2 %collective-permute-start.1 = (s32[2,128]{1,0:T(2,128)S(1)}, s32[2,128]{1,0:T(2,128)S(1)}, u32[]{:S(2)}, u32[]{:S(2)}) collective-permute-start(s32[2,128]{1,0:T(2,128)S(1)} %pad_add_fusion.1), channel_id=1, source_target_pairs={{0,3},{1,0},{2,1},{3,2},{4,7},{5,4},{6,5},{7,6},{8,11},{9,8},{10,9... | collective-permute-start | bytes 3080 | tf_op jit(solution)/shard_map/ppermute | solution.py:477
  25.6 4.8 %collective-permute-start.2 = (s32[2,128]{1,0:T(2,128)S(1)}, s32[2,128]{1,0:T(2,128)S(1)}, u32[]{:S(2)}, u32[]{:S(2)}) collective-permute-start(s32[2,128]{1,0:T(2,128)S(1)} %pad_add_fusion.1), channel_id=1, source_target_pairs={{0,2},{1,3},{2,0},{3,1},{4,6},{5,7},{6,4},{7,5},{8,10},{9,11},{10,... | collective-permute-start | bytes 3080 | tf_op jit(solution)/shard_map/ppermute | solution.py:477
  32.8 1.3 %copy-start = (f32[128,8,128]{2,1,0:T(8,128)S(1)}, f32[128,8,128]{2,1,0:T(8,128)}, u32[]{:S(2)}) copy-start(f32[128,8,128]{2,1,0:T(8,128)} %param.16) | copy-start | bytes 1572868
  32.8 1.3 %copy-start.8 = (f32[64,8,8]{0,2,1:T(8,128)S(1)}, f32[64,8,8]{0,2,1:T(8,128)}, u32[]{:S(2)}) copy-start(f32[64,8,8]{0,2,1:T(8,128)} %param.19) | copy-start | bytes 49156
  34.2 10.1 %copy-start.4 = (bf16[512,384]{1,0:T(8,128)(2,1)S(1)}, bf16[512,384]{1,0:T(8,128)(2,1)}, u32[]{:S(2)}) copy-start(bf16[512,384]{1,0:T(8,128)(2,1)} %constant.18.clone.fy_in) | copy-start | bytes 1179652
  36.7 7.6 %copy-start.3 = (f32[3,36864]{1,0:T(4,128)S(1)}, f32[3,36864]{1,0:T(4,128)}, u32[]{:S(2)}) copy-start(f32[3,36864]{1,0:T(4,128)} %param.15) | copy-start | bytes 1327108
  36.7 7.6 %collective-permute-start.6 = (f32[96,128]{1,0:T(8,128)S(1)}, f32[96,128]{1,0:T(8,128)S(1)}, u32[]{:S(2)}, u32[]{:S(2)}) collective-permute-start(f32[96,128]{1,0:T(8,128)S(1)} %get-tuple-element.14.near), channel_id=1, source_target_pairs={{0,4},{4,8},{8,12},{12,16},{16,20},{20,24},{24,28},{28,32},{32,36}... | collective-permute-start | bytes 147464 | tf_op jit(solution)/shard_map/ppermute | solution.py:518
  38.1 6.2 %collective-permute-start.7 = (f32[96,128]{1,0:T(8,128)S(1)}, f32[96,128]{1,0:T(8,128)S(1)}, u32[]{:S(2)}, u32[]{:S(2)}) collective-permute-start(f32[96,128]{1,0:T(8,128)S(1)} %get-tuple-element.14.near), channel_id=1, source_target_pairs={{0,252},{4,0},{8,4},{12,8},{16,12},{20,16},{24,20},{28,24},{32,28}... | collective-permute-start | bytes 147464 | tf_op jit(solution)/shard_map/ppermute | solution.py:518
  38.1 6.2 %copy-start.7 = (bf16[384,128]{1,0:T(8,128)(2,1)S(1)}, bf16[384,128]{1,0:T(8,128)(2,1)}, u32[]{:S(2)}) copy-start(bf16[384,128]{1,0:T(8,128)(2,1)} %constant.20.clone.ut_in) | copy-start | bytes 294916
  38.1 6.2 %collective-permute-start.8 = (f32[32,128]{1,0:T(8,128)S(1)}, f32[32,128]{1,0:T(8,128)S(1)}, u32[]{:S(2)}, u32[]{:S(2)}) collective-permute-start(f32[32,128]{1,0:T(8,128)S(1)} %get-tuple-element.15), channel_id=1, source_target_pairs={{0,8},{4,12},{8,16},{12,20},{16,24},{20,28},{24,32},{28,36},{32,40... | collective-permute-start | bytes 49160 | tf_op jit(solution)/shard_map/ppermute | solution.py:518
  39.2 5.0 %collective-permute-start.9 = (f32[32,128]{1,0:T(8,128)S(1)}, f32[32,128]{1,0:T(8,128)S(1)}, u32[]{:S(2)}, u32[]{:S(2)}) collective-permute-start(f32[32,128]{1,0:T(8,128)S(1)} %get-tuple-element.15), channel_id=1, source_target_pairs={{0,248},{4,252},{8,0},{12,4},{16,8},{20,12},{24,16},{28,20},{32,24... | collective-permute-start | bytes 49160 | tf_op jit(solution)/shard_map/ppermute | solution.py:518
  48.9 24.1 %copy-start.1 = (bf16[768,256]{1,0:T(8,128)(2,1)S(1)}, bf16[768,256]{1,0:T(8,128)(2,1)}, u32[]{:S(2)}) copy-start(bf16[768,256]{1,0:T(8,128)(2,1)} %constant.14.clone.wz_in.fz) | copy-start | bytes 1179652

commit v4 on v3

--- a/solution.py
+++ b/solution.py
@@ -197,7 +197,7 @@
 
 
 def as_column(ids):
-    return jnp.broadcast_to(ids.astype(F32), (8, 512)).T[:, 0:1].astype(jnp.int32)
+    return jnp.broadcast_to(ids.astype(F32), (8, ids.shape[1])).T[:, 0:1].astype(jnp.int32)
 
 
 def kernel_field(
@@ -255,10 +255,9 @@
     rows_l[864:896, :] = jnp.zeros((32, 256), BF)
 
 
-def kernel_project(rows_h, rows_l, dmat, ids, b0, b1, b2, b3, near, far, slots_out, field_rows):
-    betas = (b0, b1, b2, b3)
-    tile_of = as_column(tile_rows(ids[1:2, :]))
-    pick = one_hot(tile_of == iota((512, 896), 1))
+def project(quarters, rows_h, rows_l, tile_of, slots, betas, field_rows):
+    count = 128 * quarters
+    pick = one_hot(as_column(tile_of) == iota((count, 896), 1))
     field_rows[...] = mm(pick, rows_h[...]) + mm(pick, rows_l[...])
     lane = iota((128, 128), 1)
     sums = []
@@ -273,9 +272,22 @@
                 )
         sums.append(total.T[:16])
     high, low = split(jnp.concatenate(sums, 1))
+    return mm(high, slots) + mm(low, slots)
+
+
+def kernel_project(rows_h, rows_l, i0, i1, i2, i3, b0, b1, b2, coef, slots_out, tiles_out, field_rows):
+    ids = jnp.concatenate([i0[...], i1[...], i2[...], i3[...]], 1)
+    tile_of = tile_rows(ids[1:2, :])
+    tiles_out[...] = tile_of
     slots = one_hot(as_column(ids[0:1, :]) == iota((512, 256), 1))
     slots_out[...] = slots
-    coef = mm(high, slots) + mm(low, slots)
+    coef[...] = project(3, rows_h, rows_l, tile_of[:, :384], slots[:384], (b0, b1, b2), field_rows)
+
+
+def kernel_project_last(rows_h, rows_l, tiles, slots, dmat, coef_in, b3, near, far, field_rows):
+    coef = coef_in[...] + project(
+        1, rows_h, rows_l, tiles[:, 384:], slots[384:512, :], (b3,), field_rows
+    )
     coef = jnp.where(iota((16, 256), 1) < 192, coef, 0.0)
     near[0:64, :] = jnp.concatenate([dmat[...], jnp.zeros((64, 64), F32)], 1)
     near[64:80, :] = coef[:, :128]
@@ -284,8 +296,8 @@
     far[16:32, :] = coef[:, 128:]
 
 
-def kernel_put(ids, put):
-    put[...] = one_hot(iota((864, 512), 0) == tile_rows(ids[1:2, :]))
+def kernel_put(tiles, put):
+    put[...] = one_hot(iota((864, 512), 0) == tiles[...])
 
 
 def kernel_back(
@@ -392,9 +404,16 @@
         send[pl.ds(4 * c + 3, 64, stride=8), :] = spares[c]
 
 
-def kernel_z_forward(recv, fz, out):
+def kernel_z_forward(recv, fz, result, out, sems):
     s = lax.axis_index("fft")
     out[...] = jnp.zeros((1728, 128), F32)
+    spans = [(152, 280), (576, 576), (1304, 280), (0, 152), (432, 144), (1152, 152), (1584, 144)]
+    copies = [
+        pltpu.make_async_copy(out.at[pl.ds(*span)], result.at[pl.ds(*span)], sems.at[k])
+        for k, span in enumerate(spans)
+    ]
+    for copy in copies[:3]:
+        copy.start()
     r = iota((256, 1), 0)
     main, spare = line_places(r, s)
     lane = iota((256, 128), 1)
@@ -437,8 +456,12 @@
             )
             for k, tile in enumerate(kinds):
                 at = 1152 * plane + 2 * k + c
-                out[pl.ds(at, 32, stride=6), :] = tile[24:56]
+                out[pl.ds(at, 25, stride=6), :] = tile[24:49]
                 out[pl.ds(at + 432, 24, stride=6), :] = tile[:24]
+        copies[3 + 2 * plane].start()
+        copies[4 + 2 * plane].start()
+    for copy in copies:
+        copy.wait()
 
 
 def call(kernel, name, out_shape, args, scratch=(), anywhere=(), anywhere_out=(), limit=VMEM_LIMIT, cost=None):
@@ -478,7 +501,7 @@
         ]
 
     betas = gathered(beta.reshape(1024, 128))
-    ids = jnp.concatenate(gathered(jnp.stack([blk_slot, blk_tile])), 1)
+    ids = gathered(jnp.stack([blk_slot, blk_tile]))
     (send,) = call(
         kernel_z_inverse,
         "z_inverse",
@@ -492,6 +515,7 @@
         anywhere=(0, 1),
         limit=60 * 1024 * 1024,
     )
+    send, *ids = lax.optimization_barrier((send, *ids))
 
     def exchange(x):
         x = lax.all_to_all(x.reshape(64, 8, 128), "fft", 0, 0, tiled=True)
@@ -506,12 +530,19 @@
         [(864, 256), ((896, 256), BF), ((896, 256), BF)],
         (recv, t["ey"], t["ix"], t["u"]),
     )
-    near, far, slots = call(
+    coef, slots, tiles = call(
         kernel_project,
         "project",
-        [(96, 128), (32, 128), ((512, 256), BF)],
-        (rows_h, rows_l, dmat_rows, ids, *betas),
-        [pltpu.VMEM((512, 256), F32)],
+        [(16, 256), ((512, 256), BF), ((1, 512), jnp.int32)],
+        (rows_h, rows_l, *ids, *betas[:3]),
+        [pltpu.VMEM((384, 256), F32)],
+    )
+    near, far = call(
+        kernel_project_last,
+        "project_last",
+        [(96, 128), (32, 128)],
+        (rows_h, rows_l, tiles, slots, dmat_rows, coef, betas[3]),
+        [pltpu.VMEM((128, 256), F32)],
     )
 
     def moved(x, step):
@@ -522,7 +553,7 @@
         kernel_put,
         "put",
         [((864, 512), BF)],
-        (ids,),
+        (tiles,),
         cost=pl.CostEstimate(flops=2000000, bytes_accessed=3000000, transcendentals=0),
     )
     (send,) = call(
@@ -541,7 +572,8 @@
         ],
         anywhere=(12, 13, 14, 15),
     )
-    (out,) = call(kernel_z_forward, "z_forward", [(1728, 128)], (exchange(send), t["fz"]))
+    (out,) = call(kernel_z_forward, "z_forward", [(1728, 128)], (exchange(send), t["fz"]),
+        [pltpu.VMEM((1728, 128), F32), pltpu.SemaphoreType.DMA((7,))], anywhere_out=(0,))
     out = out.reshape(3, 288, 2, 128).transpose(0, 2, 1, 3).reshape(3, 2, N * N)
     return out.transpose(1, 0, 2)[None]
 

time: 75.1 us -> 94.4 us (1.26)
  waiting for transfers between devices: 5.97 us -> 23 us
  blocking collectives: 24.1 us -> 40.7 us
  starting transfers between devices: 31.1 us -> 16.3 us
    all_to_all x1 -> x2, blocking collectives: 24.1 us -> 40.7 us  [exchange(): x = lax.all_to_all(x.reshape(64, 8, 128), 'fft', 0, 0, tiled=True)]
    ppermute x6, waiting for transfers between devices: 2.61 us -> 17.3 us  [gathered(): lax.ppermute(x, 'band', [(i, (i + k) % 4) for i in range(4)])]
    all_to_all x1 -> x0, starting transfers between devices: 13.1 us -> none  [exchange(): x = lax.all_to_all(x.reshape(64, 8, 128), 'fft', 0, 0, tiled=True)]
    ppermute x4, waiting for transfers between devices: 0.96 us -> 5.75 us  [moved(): return lax.ppermute(x, 'fft', [(i, (i + step) % 64) for i in range(64)])]
    all_to_all x1 -> x0, waiting for transfers between devices: 2.4 us -> none  [exchange(): x = lax.all_to_all(x.reshape(64, 8, 128), 'fft', 0, 0, tiled=True)]
    ppermute x6, starting transfers between devices: 11.5 us -> 9.7 us  [gathered(): lax.ppermute(x, 'band', [(i, (i + k) % 4) for i in range(4)])]
    pallas_call x6 -> x7, Pallas kernels: 12.8 us -> 13.1 us  [call(): pl.pallas_call(kernel, name=name, out_shape=shapes, in_specs=specs, out_s...]
  transfers between devices with their start and end apart: 11 -> 10, of which waited for: 4 -> 3; matrix products, arithmetic and copies ran while one was open for 0% -> 1% of each run, Pallas kernels for 5% -> 6%
where the time goes in v4:
time: 94.4 us; the launch traced here: 94.2 us
  blocking collectives  40.7 us (43%)
  waiting for transfers between devices  23 us (24%)
  starting transfers between devices  16.3 us (17%)
  Pallas kernels  13.1 us (14%)
    all_to_all x2, blocking collectives, exchange(): x = lax.all_to_all(x.reshape(64, 8, 128), 'fft', 0, 0, tiled=True)  40.7 us
    ppermute x6, waiting for transfers between devices, gathered(): lax.ppermute(x, 'band', [(i, (i + k) % 4) for i in range(4)])  17.3 us
    pallas_call x7, Pallas kernels, call(): pl.pallas_call(kernel, name=name, out_shape=shapes, in_specs=specs, out_s...  13.1 us
    ppermute x6, starting transfers between devices, gathered(): lax.ppermute(x, 'band', [(i, (i + k) % 4) for i in range(4)])  9.7 us
    ppermute x4, starting transfers between devices, moved(): return lax.ppermute(x, 'fft', [(i, (i + step) % 64) for i in range(64)])  6.62 us
    ppermute x4, waiting for transfers between devices, moved(): return lax.ppermute(x, 'fft', [(i, (i + step) % 64) for i in range(64)])  5.75 us
  transfers between devices with their start and end apart: 10, of which 3 were waited for; matrix products, arithmetic and copies ran while one was open for 1% of the time, Pallas kernels for 6%

profile of v4, /device:TPU:1, one launch (start us, length us, event | category | flops | bytes accessed | tf_op | source)
XLA Modules:
  0.0 94.2 jit_solution(10881297125579113615)
XLA Ops:
  0.0 3.7 %collective-permute-start.5 = (f32[1024,128]{1,0:T(8,128)}, f32[1024,128]{1,0:T(8,128)S(1)}, u32[]{:S(2)}, u32[]{:S(2)}) collective-permute-start(f32[1024,128]{1,0:T(8,128)} %bitcast.31), channel_id=1, source_target_pairs={{0,2},{1,3},{2,0},{3,1},{4,6},{5,7},{6,4},{7,5},{8,10},{9,11},{10,... | collective-permute-start | bytes 1572872 | tf_op jit(solution)/shard_map/ppermute | solution.py:500
  3.7 0.8 collective-permute-start.4
  4.5 0.7 collective-permute-start.3
  5.2 0.7 pad_add_fusion.i0
  5.9 0.7 collective-permute-start.2
  6.6 2.1 %collective-permute-start.1 = (s32[2,128]{1,0:T(2,128)S(1)}, s32[2,128]{1,0:T(2,128)S(1)}, u32[]{:S(2)}, u32[]{:S(2)}) collective-permute-start(s32[2,128]{1,0:T(2,128)S(1)} %pad_add_fusion.i0), channel_id=1, source_target_pairs={{0,3},{1,0},{2,1},{3,2},{4,7},{5,4},{6,5},{7,6},{8,11},{9,8},{10,9... | collective-permute-start | bytes 3080 | tf_op jit(solution)/shard_map/ppermute | solution.py:500
  8.7 17.2 %collective-permute-done.2.i3 = s32[2,128]{1,0:T(2,128)S(1)} collective-permute-done((s32[2,128]{1,0:T(2,128)S(1)}, s32[2,128]{1,0:T(2,128)S(1)}, u32[]{:S(2)}, u32[]{:S(2)}) %collective-permute-start.2) | collective-permute-done | bytes 1056 | tf_op jit(solution)/shard_map/ppermute | solution.py:500
  25.9 1.7 %collective-permute-start = (s32[2,128]{1,0:T(2,128)S(1)}, s32[2,128]{1,0:T(2,128)S(1)}, u32[]{:S(2)}, u32[]{:S(2)}) collective-permute-start(s32[2,128]{1,0:T(2,128)S(1)} %pad_add_fusion.i0), channel_id=1, source_target_pairs={{0,1},{1,2},{2,3},{3,0},{4,5},{5,6},{6,7},{7,4},{8,9},{9,10},{10,1... | collective-permute-start | bytes 3080 | tf_op jit(solution)/shard_map/ppermute | solution.py:500
  27.6 2.4 %z_inverse.1 = f32[512,128]{1,0:T(8,128)} custom-call(f32[1728,128]{1,0:T(8,128)} %bitcast.42, bf16[768,256]{1,0:T(8,128)(2,1)} %constant.14.clone.wz_in.fz), custom_call_target="tpu_custom_call" | custom-call | tf_op jit(solution)/shard_map/z_inverse/pallas_call | solution.py:476
  30.1 0.0 copy-start.5
  30.1 0.0 collective-permute-done.i1
  30.1 0.0 copy-start.6
  30.1 26.5 %all_to_all.10 = f32[64,8,128]{2,1,0:T(8,128)S(1)} all-to-all(f32[64,8,128]{2,1,0:T(8,128)} %bitcast.41), channel_id=1, replica_groups=mesh['fft'=64,'band'=4] {'fft'}, dimensions={0} | all-to-all | bytes 524288 | tf_op jit(solution)/shard_map/all_to_all | solution.py:521
  56.6 0.0 copy-start
  56.6 1.3 %field.1 = (f32[864,256]{1,0:T(8,128)S(1)}, bf16[896,256]{1,0:T(8,128)(2,1)S(1)}, bf16[896,256]{1,0:T(8,128)(2,1)S(1)}) custom-call(f32[512,128]{1,0:T(8,128)S(1)} %bitcast.37, bf16[768,256]{1,0:T(8,128)(2,1)S(1)} %copy-done.5, bf16[1024,512]{1,0:T(8,128)(2,1)S(1)} %copy-done.2, bf16[128,384]{1,0:T(8,128)(2,1)S(1)} %copy-done.6), custom_call_target="tpu_custom_call" | custom-call | tf_op jit(solution)/shard_map/field/pallas_call | solution.py:476
  57.9 0.0 copy-start.8
  57.9 2.0 %project.1 = (f32[16,256]{1,0:T(8,128)S(1)}, bf16[512,256]{1,0:T(8,128)(2,1)S(1)}, s32[1,512]{1,0:T(1,128)S(1)}) custom-call(bf16[896,256]{1,0:T(8,128)(2,1)S(1)} %get-tuple-element.20.rows_h, bf16[896,256]{1,0:T(8,128)(2,1)S(1)} %get-tuple-element.21.rows_l, s32[2,128]{1,0:T(2,128)S(1)} %pad_add_fusion.i0, s32[2,128]{1,0:T(2,128)S(1)} %collective-permute-done.i1, ...), custom_call_target="tpu_custom_call" | custom-call | tf_op jit(solution)/shard_map/project/pallas_call | solution.py:476
  60.0 0.0 collective-permute-done.5.b3
  60.0 0.0 copy-start.4
  60.0 0.9 project_last.1
  60.9 0.5 collective-permute-start.7
  61.4 1.3 %collective-permute-start.6 = (f32[96,128]{1,0:T(8,128)S(1)}, f32[96,128]{1,0:T(8,128)S(1)}, u32[]{:S(2)}, u32[]{:S(2)}) collective-permute-start(f32[96,128]{1,0:T(8,128)S(1)} %get-tuple-element.29.near), channel_id=1, source_target_pairs={{0,4},{4,8},{8,12},{12,16},{16,20},{20,24},{24,28},{28,32},{32,36}... | collective-permute-start | bytes 147464 | tf_op jit(solution)/shard_map/ppermute | solution.py:549
  62.7 4.9 %collective-permute-start.9 = (f32[32,128]{1,0:T(8,128)S(1)}, f32[32,128]{1,0:T(8,128)S(1)}, u32[]{:S(2)}, u32[]{:S(2)}) collective-permute-start(f32[32,128]{1,0:T(8,128)S(1)} %get-tuple-element.30), channel_id=1, source_target_pairs={{0,248},{4,252},{8,0},{12,4},{16,8},{20,12},{24,16},{28,20},{32,24... | collective-permute-start | bytes 49160 | tf_op jit(solution)/shard_map/ppermute | solution.py:549
  67.5 0.0 collective-permute-start.8
  67.5 0.2 put.1
  67.7 0.7 collective-permute-done.9.above2
  68.4 5.0 %collective-permute-done.8.below2 = f32[32,128]{1,0:T(8,128)S(1)} collective-permute-done((f32[32,128]{1,0:T(8,128)S(1)}, f32[32,128]{1,0:T(8,128)S(1)}, u32[]{:S(2)}, u32[]{:S(2)}) %collective-permute-start.8) | collective-permute-done | bytes 16416 | tf_op jit(solution)/shard_map/ppermute | solution.py:549
  73.4 0.0 collective-permute-done.7.above
  73.5 4.6 %back.1 = f32[512,128]{1,0:T(8,128)S(1)} custom-call(f32[864,256]{1,0:T(8,128)S(1)} %get-tuple-element.19.field, f32[96,128]{1,0:T(8,128)S(1)} %get-tuple-element.29.near, f32[96,128]{1,0:T(8,128)S(1)} %collective-permute-done.6.below, f32[96,128]{1,0:T(8,128)S(1)} %collective-permute-done.7.above, f32[32,128]{1,0:T(8,128)S(1)} %collective-permute-done.8.below2, ...), custom_call_target="tpu_custom_call" | custom-call | tf_op jit(solution)/shard_map/back/pallas_call | solution.py:476
  78.1 0.0 copy-start.1
  78.1 14.2 %all_to_all.11 = f32[64,8,128]{2,1,0:T(8,128)S(1)} all-to-all(f32[64,8,128]{2,1,0:T(8,128)S(1)} %bitcast.36), channel_id=1, replica_groups=mesh['fft'=64,'band'=4] {'fft'}, dimensions={0} | all-to-all | bytes 524288 | tf_op jit(solution)/shard_map/all_to_all | solution.py:521
  92.4 1.7 %z_forward.1 = f32[1728,128]{1,0:T(8,128)} custom-call(f32[512,128]{1,0:T(8,128)S(1)} %bitcast.38, bf16[768,256]{1,0:T(8,128)(2,1)S(1)} %copy-done.1), custom_call_target="tpu_custom_call" | custom-call | tf_op jit(solution)/shard_map/z_forward/pallas_call | solution.py:476
  (16 shorter events, 0.0 us)
Async XLA Ops:
  0.0 56.6 %copy-start.2 = (bf16[1024,512]{1,0:T(8,128)(2,1)S(1)}, bf16[1024,512]{1,0:T(8,128)(2,1)}, u32[]{:S(2)}) copy-start(bf16[1024,512]{1,0:T(8,128)(2,1)} %constant.16.clone.ix) | copy-start | bytes 3145732
  0.0 60.0 %collective-permute-start.5 = (f32[1024,128]{1,0:T(8,128)}, f32[1024,128]{1,0:T(8,128)S(1)}, u32[]{:S(2)}, u32[]{:S(2)}) collective-permute-start(f32[1024,128]{1,0:T(8,128)} %bitcast.31), channel_id=1, source_target_pairs={{0,2},{1,3},{2,0},{3,1},{4,6},{5,7},{6,4},{7,5},{8,10},{9,11},{10,... | collective-permute-start | bytes 1572872 | tf_op jit(solution)/shard_map/ppermute | solution.py:500
  3.7 54.1 %collective-permute-start.4 = (f32[1024,128]{1,0:T(8,128)}, f32[1024,128]{1,0:T(8,128)S(1)}, u32[]{:S(2)}, u32[]{:S(2)}) collective-permute-start(f32[1024,128]{1,0:T(8,128)} %bitcast.32), channel_id=1, source_target_pairs={{0,3},{1,0},{2,1},{3,2},{4,7},{5,4},{6,5},{7,6},{8,11},{9,8},{10,9... | collective-permute-start | bytes 1572872 | tf_op jit(solution)/shard_map/ppermute | solution.py:500
  4.5 53.4 %collective-permute-start.3 = (f32[1024,128]{1,0:T(8,128)}, f32[1024,128]{1,0:T(8,128)S(1)}, u32[]{:S(2)}, u32[]{:S(2)}) collective-permute-start(f32[1024,128]{1,0:T(8,128)} %bitcast.33), channel_id=1, source_target_pairs={{0,1},{1,2},{2,3},{3,0},{4,5},{5,6},{6,7},{7,4},{8,9},{9,10},{10,1... | collective-permute-start | bytes 1572872 | tf_op jit(solution)/shard_map/ppermute | solution.py:500
  5.9 20.0 %collective-permute-start.2 = (s32[2,128]{1,0:T(2,128)S(1)}, s32[2,128]{1,0:T(2,128)S(1)}, u32[]{:S(2)}, u32[]{:S(2)}) collective-permute-start(s32[2,128]{1,0:T(2,128)S(1)} %pad_add_fusion.i0), channel_id=1, source_target_pairs={{0,2},{1,3},{2,0},{3,1},{4,6},{5,7},{6,4},{7,5},{8,10},{9,11},{10,... | collective-permute-start | bytes 3080 | tf_op jit(solution)/shard_map/ppermute | solution.py:500
  6.6 23.5 %collective-permute-start.1 = (s32[2,128]{1,0:T(2,128)S(1)}, s32[2,128]{1,0:T(2,128)S(1)}, u32[]{:S(2)}, u32[]{:S(2)}) collective-permute-start(s32[2,128]{1,0:T(2,128)S(1)} %pad_add_fusion.i0), channel_id=1, source_target_pairs={{0,3},{1,0},{2,1},{3,2},{4,7},{5,4},{6,5},{7,6},{8,11},{9,8},{10,9... | collective-permute-start | bytes 3080 | tf_op jit(solution)/shard_map/ppermute | solution.py:500
  25.9 4.2 %collective-permute-start = (s32[2,128]{1,0:T(2,128)S(1)}, s32[2,128]{1,0:T(2,128)S(1)}, u32[]{:S(2)}, u32[]{:S(2)}) collective-permute-start(s32[2,128]{1,0:T(2,128)S(1)} %pad_add_fusion.i0), channel_id=1, source_target_pairs={{0,1},{1,2},{2,3},{3,0},{4,5},{5,6},{6,7},{7,4},{8,9},{9,10},{10,1... | collective-permute-start | bytes 3080 | tf_op jit(solution)/shard_map/ppermute | solution.py:500
  30.1 26.5 %copy-start.5 = (bf16[768,256]{1,0:T(8,128)(2,1)S(1)}, bf16[768,256]{1,0:T(8,128)(2,1)}, u32[]{:S(2)}) copy-start(bf16[768,256]{1,0:T(8,128)(2,1)} %constant.15.clone.ey) | copy-start | bytes 1179652
  30.1 26.5 %copy-start.6 = (bf16[128,384]{1,0:T(8,128)(2,1)S(1)}, bf16[128,384]{1,0:T(8,128)(2,1)}, u32[]{:S(2)}) copy-start(bf16[128,384]{1,0:T(8,128)(2,1)} %constant.19.clone.u) | copy-start | bytes 294916
  56.6 1.3 %copy-start = (f32[128,8,128]{2,1,0:T(8,128)S(1)}, f32[128,8,128]{2,1,0:T(8,128)}, u32[]{:S(2)}) copy-start(f32[128,8,128]{2,1,0:T(8,128)} %param.16) | copy-start | bytes 1572868
  57.9 2.1 %copy-start.8 = (f32[64,8,8]{0,2,1:T(8,128)S(1)}, f32[64,8,8]{0,2,1:T(8,128)}, u32[]{:S(2)}) copy-start(f32[64,8,8]{0,2,1:T(8,128)} %param.19) | copy-start | bytes 49156
  60.0 13.5 %copy-start.4 = (bf16[512,384]{1,0:T(8,128)(2,1)S(1)}, bf16[512,384]{1,0:T(8,128)(2,1)}, u32[]{:S(2)}) copy-start(bf16[512,384]{1,0:T(8,128)(2,1)} %constant.18.clone.fy_in) | copy-start | bytes 1179652
  60.9 12.5 %copy-start.3 = (f32[3,36864]{1,0:T(4,128)S(1)}, f32[3,36864]{1,0:T(4,128)}, u32[]{:S(2)}) copy-start(f32[3,36864]{1,0:T(4,128)} %param.15) | copy-start | bytes 1327108
  60.9 12.5 %collective-permute-start.7 = (f32[96,128]{1,0:T(8,128)S(1)}, f32[96,128]{1,0:T(8,128)S(1)}, u32[]{:S(2)}, u32[]{:S(2)}) collective-permute-start(f32[96,128]{1,0:T(8,128)S(1)} %get-tuple-element.29.near), channel_id=1, source_target_pairs={{0,252},{4,0},{8,4},{12,8},{16,12},{20,16},{24,20},{28,24},{32,28}... | collective-permute-start | bytes 147464 | tf_op jit(solution)/shard_map/ppermute | solution.py:549
  61.4 12.1 %collective-permute-start.6 = (f32[96,128]{1,0:T(8,128)S(1)}, f32[96,128]{1,0:T(8,128)S(1)}, u32[]{:S(2)}, u32[]{:S(2)}) collective-permute-start(f32[96,128]{1,0:T(8,128)S(1)} %get-tuple-element.29.near), channel_id=1, source_target_pairs={{0,4},{4,8},{8,12},{12,16},{16,20},{20,24},{24,28},{28,32},{32,36}... | collective-permute-start | bytes 147464 | tf_op jit(solution)/shard_map/ppermute | solution.py:549
  62.7 10.8 %copy-start.7 = (bf16[384,128]{1,0:T(8,128)(2,1)S(1)}, bf16[384,128]{1,0:T(8,128)(2,1)}, u32[]{:S(2)}) copy-start(bf16[384,128]{1,0:T(8,128)(2,1)} %constant.20.clone.ut_in) | copy-start | bytes 294916
  62.7 5.7 %collective-permute-start.9 = (f32[32,128]{1,0:T(8,128)S(1)}, f32[32,128]{1,0:T(8,128)S(1)}, u32[]{:S(2)}, u32[]{:S(2)}) collective-permute-start(f32[32,128]{1,0:T(8,128)S(1)} %get-tuple-element.30), channel_id=1, source_target_pairs={{0,248},{4,252},{8,0},{12,4},{16,8},{20,12},{24,16},{28,20},{32,24... | collective-permute-start | bytes 49160 | tf_op jit(solution)/shard_map/ppermute | solution.py:549
  67.5 5.9 %collective-permute-start.8 = (f32[32,128]{1,0:T(8,128)S(1)}, f32[32,128]{1,0:T(8,128)S(1)}, u32[]{:S(2)}, u32[]{:S(2)}) collective-permute-start(f32[32,128]{1,0:T(8,128)S(1)} %get-tuple-element.30), channel_id=1, source_target_pairs={{0,8},{4,12},{8,16},{12,20},{16,24},{20,28},{24,32},{28,36},{32,40... | collective-permute-start | bytes 49160 | tf_op jit(solution)/shard_map/ppermute | solution.py:549
  78.1 14.2 %copy-start.1 = (bf16[768,256]{1,0:T(8,128)(2,1)S(1)}, bf16[768,256]{1,0:T(8,128)(2,1)}, u32[]{:S(2)}) copy-start(bf16[768,256]{1,0:T(8,128)(2,1)} %constant.14.clone.wz_in.fz) | copy-start | bytes 1179652

commit v5 on v4

--- a/solution.py
+++ b/solution.py
@@ -275,33 +275,62 @@
     return mm(high, slots) + mm(low, slots)
 
 
-def kernel_project(rows_h, rows_l, i0, i1, i2, i3, b0, b1, b2, coef, slots_out, tiles_out, field_rows):
-    ids = jnp.concatenate([i0[...], i1[...], i2[...], i3[...]], 1)
-    tile_of = tile_rows(ids[1:2, :])
+def ids_of(betas, row):
+    return jnp.concatenate([b[1024 + row : 1025 + row, :] for b in betas], 1).astype(jnp.int32)
+
+
+def kernel_project(rows_h, rows_l, b0, b1, b2, coef, slots_out, tiles_out, field_rows):
+    betas = (b0, b1, b2)
+    tile_of = tile_rows(ids_of(betas, 1))
     tiles_out[...] = tile_of
-    slots = one_hot(as_column(ids[0:1, :]) == iota((512, 256), 1))
+    slots = one_hot(as_column(ids_of(betas, 0)) == iota((384, 256), 1))
     slots_out[...] = slots
-    coef[...] = project(3, rows_h, rows_l, tile_of[:, :384], slots[:384], (b0, b1, b2), field_rows)
-
-
-def kernel_project_last(rows_h, rows_l, tiles, slots, dmat, coef_in, b3, near, far, field_rows):
-    coef = coef_in[...] + project(
-        1, rows_h, rows_l, tiles[:, 384:], slots[384:512, :], (b3,), field_rows
-    )
+    coef[...] = project(3, rows_h, rows_l, tile_of, slots, betas, field_rows)
+
+
+def kernel_project_last(rows_h, rows_l, dmat, coef_in, b3, near, slots_out, tiles_out, field_rows):
+    tile_of = tile_rows(ids_of((b3,), 1))
+    tiles_out[...] = tile_of
+    slots = one_hot(as_column(ids_of((b3,), 0)) == iota((128, 256), 1))
+    slots_out[...] = slots
+    coef = coef_in[...] + project(1, rows_h, rows_l, tile_of, slots, (b3,), field_rows)
     coef = jnp.where(iota((16, 256), 1) < 192, coef, 0.0)
     near[0:64, :] = jnp.concatenate([dmat[...], jnp.zeros((64, 64), F32)], 1)
     near[64:80, :] = coef[:, :128]
     near[80:96, :] = coef[:, 128:]
-    far[0:16, :] = coef[:, :128]
-    far[16:32, :] = coef[:, 128:]
-
-
-def kernel_put(tiles, put):
-    put[...] = one_hot(iota((864, 512), 0) == tiles[...])
+
+
+def chip_of(own, other):
+    f = lax.axis_index("fft")
+    core = f % 2
+    own, other = own[...], other[...]
+    return (
+        core,
+        (f // 2) % 2 == 0,
+        jnp.where(core == 0, own, other),
+        jnp.where(core == 0, other, own),
+    )
+
+
+def kernel_merge(own, other, first, second):
+    _, even, a, b = chip_of(own, other)
+    low_lane = iota((16, 128), 1) < 64
+    turned = pltpu.roll(b[64:80], 64, 1)
+    up = jnp.where(low_lane, a[80:96] + turned, pltpu.roll(b[80:96], 64, 1))
+    down = jnp.where(low_lane, a[64:80], a[64:80] + turned)
+    up = jnp.concatenate([b[0:64], up], 0)
+    down = jnp.concatenate([a[0:64], down], 0)
+    first[...] = jnp.where(even, up, down)
+    second[...] = jnp.where(even, down, up)
+
+
+def kernel_put(tiles, tiles_last, put):
+    tile_of = jnp.concatenate([tiles[...], tiles_last[...]], 1)
+    put[...] = one_hot(iota((864, 512), 0) == tile_of)
 
 
 def kernel_back(
-    field, near, below, above, below2, above2, slots, put, b0, b1, b2, b3,
+    field, own, other, first, second, slots, slots_last, put, b0, b1, b2, b3,
     vloc_in, fx_in, fy_in, ut_in, send, scr, rows, vloc, fx, fy, ut, sems,
 ):
     copies = [
@@ -313,28 +342,19 @@
     ]
     for copy in copies:
         copy.start()
-    lane = iota((16, 128), 1)
-
-    def half(ref, k):
-        return ref[64 + 16 * k : 80 + 16 * k, :]
-
-    def shifted(low, high, up):
-        low, high = pltpu.roll(low, 64, 1), pltpu.roll(high, 64, 1)
-        if up:
-            return jnp.where(lane < 64, 0.0, low), jnp.where(lane < 64, low, high)
-        return jnp.where(lane < 64, low, high), jnp.where(lane < 64, high, 0.0)
-
-    from_below = shifted(half(below, 0), half(below, 1), False)
-    from_above = shifted(half(above, 0), half(above, 1), True)
+    core, even, a, b = chip_of(own, other)
+    above = jnp.where(even, first[...], second[...])
+    below = jnp.where(even, second[...], first[...])
+    low_lane = iota((16, 128), 1) < 64
+    turned = pltpu.roll(b[64:80], 64, 1)
     tot = [
-        half(near, 0) + from_below[0] + from_above[0] + below2[16:32, :],
-        half(near, 1) + from_below[1] + from_above[1] + above2[0:16, :],
+        below[64:80] + jnp.where(low_lane, a[64:80], a[64:80] + turned),
+        above[64:80] + jnp.where(low_lane, a[80:96] + turned, pltpu.roll(b[80:96], 64, 1)),
     ]
-    tot[1] = jnp.where(lane < 64, tot[1], 0.0)
-    wide = iota((64, 128), 1)
+    wide = iota((64, 128), 1) < 64
     coupling = [
-        jnp.where(wide < 64, below[0:64, :], pltpu.roll(near[0:64, :], 64, 1)),
-        jnp.where(wide < 64, above[0:64, :], 0.0),
+        jnp.where(wide, below[0:64], pltpu.roll(a[0:64], 64, 1)),
+        jnp.where(wide, b[0:64], pltpu.roll(above[0:64], 64, 1)),
     ]
     for h in range(2):
         for c in range(2):
@@ -343,8 +363,14 @@
                 row = jnp.sum(coupling[h][8 * j : 8 * j + 8, :] * coef, axis=0, keepdims=True)
                 scr[8 * c + j : 8 * c + j + 1, 128 * h : 128 * h + 128] = row
     betas = (b0, b1, b2, b3)
-    high, low = split(scr[...])
-    weight = mm_nt(slots[...], high) + mm_nt(slots[...], low)
+    left, right = scr[:, :128], scr[:, 128:]
+    left_turned, right_turned = pltpu.roll(left, 64, 1), pltpu.roll(right, 64, 1)
+    left = jnp.where(core == 0, left, jnp.where(low_lane, left_turned, right_turned))
+    right = jnp.where(low_lane, jnp.where(core == 0, right, right_turned), 0.0)
+    high, low = split(jnp.concatenate([left, right], 1))
+    weight = jnp.concatenate(
+        [mm_nt(hot[...], high) + mm_nt(hot[...], low) for hot in (slots, slots_last)], 0
+    )
     high, low = split(weight)
     weight = jnp.concatenate([high, low], 1)
     for k, beta in enumerate(betas):
@@ -500,8 +526,9 @@
             lax.ppermute(x, "band", [(i, (i + k) % 4) for i in range(4)]) for k in (1, 3, 2)
         ]
 
-    betas = gathered(beta.reshape(1024, 128))
-    ids = gathered(jnp.stack([blk_slot, blk_tile]))
+    ids = jnp.concatenate([blk_slot[None], blk_tile[None], jnp.zeros((6, 128), jnp.int32)], 0)
+    own = jnp.concatenate([beta, ids.astype(F32)[None]], 0).reshape(1032, 128)
+    betas = gathered(own)
     (send,) = call(
         kernel_z_inverse,
         "z_inverse",
@@ -515,7 +542,6 @@
         anywhere=(0, 1),
         limit=60 * 1024 * 1024,
     )
-    send, *ids = lax.optimization_barrier((send, *ids))
 
     def exchange(x):
         x = lax.all_to_all(x.reshape(64, 8, 128), "fft", 0, 0, tiled=True)
@@ -533,34 +559,33 @@
     coef, slots, tiles = call(
         kernel_project,
         "project",
-        [(16, 256), ((512, 256), BF), ((1, 512), jnp.int32)],
-        (rows_h, rows_l, *ids, *betas[:3]),
+        [(16, 256), ((384, 256), BF), ((1, 384), jnp.int32)],
+        (rows_h, rows_l, *betas[:3]),
         [pltpu.VMEM((384, 256), F32)],
     )
-    near, far = call(
+    near, slots_last, tiles_last = call(
         kernel_project_last,
         "project_last",
-        [(96, 128), (32, 128)],
-        (rows_h, rows_l, tiles, slots, dmat_rows, coef, betas[3]),
+        [(96, 128), ((128, 256), BF), ((1, 128), jnp.int32)],
+        (rows_h, rows_l, dmat_rows, coef, betas[3]),
         [pltpu.VMEM((128, 256), F32)],
     )
-
-    def moved(x, step):
-        return lax.ppermute(x, "fft", [(i, (i + step) % 64) for i in range(64)])
-
-    sides = (moved(near, 1), moved(near, -1), moved(far, 2), moved(far, -2))
+    other = lax.ppermute(near, "fft", [(i, i ^ 1) for i in range(64)])
+    first, second = call(kernel_merge, "merge", [(80, 128), (80, 128)], (near, other))
+    first = lax.ppermute(first, "fft", [(i, i ^ 2) for i in range(64)])
+    second = lax.ppermute(second, "fft", [(i, (((i + 2) % 64) ^ 2) - 2 & 63) for i in range(64)])
     (put,) = call(
         kernel_put,
         "put",
         [((864, 512), BF)],
-        (tiles,),
+        (tiles, tiles_last),
         cost=pl.CostEstimate(flops=2000000, bytes_accessed=3000000, transcendentals=0),
     )
     (send,) = call(
         kernel_back,
         "back",
         [(512, 128)],
-        (field, near, *sides, slots, put, *betas, vloc_tiles, t["fx"], t["fy"], t["ut"]),
+        (field, near, other, first, second, slots, slots_last, put, *betas, vloc_tiles, t["fx"], t["fy"], t["ut"]),
         [
             pltpu.VMEM((16, 256), F32),
             pltpu.VMEM((512, 512), BF),

time: 94.4 us -> 73.6 us (0.78)
  waiting for transfers between devices: 23 us -> 3.55 us
  starting transfers between devices: 16.3 us -> 10.2 us
  blocking collectives: 40.7 us -> 44.3 us
    ppermute x6 -> x3, waiting for transfers between devices: 17.3 us -> 0.01 us  [gathered(): lax.ppermute(x, 'band', [(i, (i + k) % 4) for i in range(4)])]
    ppermute x6 -> x3, starting transfers between devices: 9.7 us -> 5.29 us  [gathered(): lax.ppermute(x, 'band', [(i, (i + k) % 4) for i in range(4)])]
    all_to_all x2, blocking collectives: 40.7 us -> 44.3 us  [exchange(): x = lax.all_to_all(x.reshape(64, 8, 128), 'fft', 0, 0, tiled=True)]
    ppermute x4 -> x3, waiting for transfers between devices: 5.75 us -> 3.54 us  [the longest x1 2.66 us: body(): lax.ppermute(second, 'fft', [(i, ((i + 2) % 64 ^ 2) - 2 & 63) for i in ra...]
    ppermute x4 -> x3, starting transfers between devices: 6.62 us -> 4.92 us  [the longest x1 3.33 us: body(): lax.ppermute(second, 'fft', [(i, ((i + 2) % 64 ^ 2) - 2 & 63) for i in ra...]
    reshape x0 -> x1, other arithmetic: none -> 1.08 us  [body(): own = jnp.concatenate([beta, ids.astype(F32)[None]], 0).reshape(1032, 128)]
    pallas_call x7 -> x8, Pallas kernels: 13.1 us -> 13.2 us  [call(): pl.pallas_call(kernel, name=name, out_shape=shapes, in_specs=specs, out_s...]
  transfers between devices with their start and end apart: 10 -> 6, of which waited for: 3 -> 2; matrix products, arithmetic and copies ran while one was open for 1% -> 0% of each run, Pallas kernels for 6% -> 8%
where the time goes in v5:
time: 73.6 us; the launch traced here: 73.3 us
  blocking collectives  44.3 us (60%)
  Pallas kernels  13.2 us (18%)
  starting transfers between devices  10.2 us (14%)
  waiting for transfers between devices  3.55 us (5%)
  other arithmetic  1.15 us (2%)
  local copies, waits for them, and re-layouts  0.8 us (1%)
    all_to_all x2, blocking collectives, exchange(): x = lax.all_to_all(x.reshape(64, 8, 128), 'fft', 0, 0, tiled=True)  44.3 us
    pallas_call x8, Pallas kernels, call(): pl.pallas_call(kernel, name=name, out_shape=shapes, in_specs=specs, out_s...  13.2 us
    ppermute x3, starting transfers between devices, gathered(): lax.ppermute(x, 'band', [(i, (i + k) % 4) for i in range(4)])  5.29 us
    ppermute x1, starting transfers between devices, body(): lax.ppermute(second, 'fft', [(i, ((i + 2) % 64 ^ 2) - 2 & 63) for i in ra...  3.33 us
    ppermute x1, waiting for transfers between devices, body(): lax.ppermute(second, 'fft', [(i, ((i + 2) % 64 ^ 2) - 2 & 63) for i in ra...  2.66 us
  transfers between devices with their start and end apart: 6, of which 2 were waited for; matrix products, arithmetic and copies ran while one was open for 0% of the time, Pallas kernels for 8%

profile of v5, /device:TPU:1, one launch (start us, length us, event | category | flops | bytes accessed | tf_op | source)
XLA Modules:
  0.0 73.3 jit_solution(17529599631198481405)
XLA Ops:
  0.0 0.1 pad.4.clone
  0.1 0.7 copy-done.8
  0.7 0.0 copy-done.9
  0.8 0.1 add_convert_fusion
  0.8 1.1 %maximum_bitcast_fusion.b0 = f32[1032,128]{1,0:T(8,128)S(1)} fusion(f32[1,8,128]{2,1,0:T(8,128)S(1)} %add_convert_fusion, f32[128,8,128]{2,1,0:T(8,128)} %param.16), kind=kLoop, calls=%fused_computation | loop fusion | flops 132096 | bytes 1056768 | tf_op jit(solution)/shard_map/reshape | solution.py:530
  1.9 0.0 copy-start.1
  1.9 3.6 %collective-permute-start.1 = (f32[1032,128]{1,0:T(8,128)S(1)}, f32[1032,128]{1,0:T(8,128)S(1)}, u32[]{:S(2)}, u32[]{:S(2)}) collective-permute-start(f32[1032,128]{1,0:T(8,128)S(1)} %maximum_bitcast_fusion.b0), channel_id=1, source_target_pairs={{0,3},{1,0},{2,1},{3,2},{4,7},{5,4},{6,5},{7,6},{8,11},{9,8},{10,9... | collective-permute-start | bytes 1585160 | tf_op jit(solution)/shard_map/ppermute | solution.py:526
  5.6 0.0 collective-permute-start
  5.6 1.6 %collective-permute-start.2 = (f32[1032,128]{1,0:T(8,128)S(1)}, f32[1032,128]{1,0:T(8,128)S(1)}, u32[]{:S(2)}, u32[]{:S(2)}) collective-permute-start(f32[1032,128]{1,0:T(8,128)S(1)} %maximum_bitcast_fusion.b0), channel_id=1, source_target_pairs={{0,2},{1,3},{2,0},{3,1},{4,6},{5,7},{6,4},{7,5},{8,10},{9,11},{10,... | collective-permute-start | bytes 1585160 | tf_op jit(solution)/shard_map/ppermute | solution.py:526
  7.2 2.4 %z_inverse.1 = f32[512,128]{1,0:T(8,128)} custom-call(f32[1728,128]{1,0:T(8,128)} %bitcast.38, bf16[768,256]{1,0:T(8,128)(2,1)} %constant.16.clone.wz_in.fz), custom_call_target="tpu_custom_call" | custom-call | tf_op jit(solution)/shard_map/z_inverse/pallas_call | solution.py:502
  9.6 0.0 copy-start.4
  9.7 0.0 copy-start.5
  9.7 25.1 %all_to_all.10 = f32[64,8,128]{2,1,0:T(8,128)S(1)} all-to-all(f32[64,8,128]{2,1,0:T(8,128)} %bitcast.37), channel_id=1, replica_groups=mesh['fft'=64,'band'=4] {'fft'}, dimensions={0} | all-to-all | bytes 524288 | tf_op jit(solution)/shard_map/all_to_all | solution.py:547
  34.8 1.3 %field.1 = (f32[864,256]{1,0:T(8,128)S(1)}, bf16[896,256]{1,0:T(8,128)(2,1)S(1)}, bf16[896,256]{1,0:T(8,128)(2,1)S(1)}) custom-call(f32[512,128]{1,0:T(8,128)S(1)} %bitcast.33, bf16[768,256]{1,0:T(8,128)(2,1)S(1)} %copy-done.4, bf16[1024,512]{1,0:T(8,128)(2,1)S(1)} %copy-done.1, bf16[128,384]{1,0:T(8,128)(2,1)S(1)} %copy-done.5), custom_call_target="tpu_custom_call" | custom-call | tf_op jit(solution)/shard_map/field/pallas_call | solution.py:502
  36.1 0.0 collective-permute-done.1.b2
  36.1 0.0 collective-permute-done.b1
  36.1 0.0 copy-start.7
  36.1 2.0 %project.1 = (f32[16,256]{1,0:T(8,128)S(1)}, bf16[384,256]{1,0:T(8,128)(2,1)S(1)}, s32[1,384]{1,0:T(1,128)S(1)}) custom-call(bf16[896,256]{1,0:T(8,128)(2,1)S(1)} %get-tuple-element.17.rows_h, bf16[896,256]{1,0:T(8,128)(2,1)S(1)} %get-tuple-element.18.rows_l, f32[1032,128]{1,0:T(8,128)S(1)} %maximum_bitcast_fusion.b0, ...), custom_call_target="tpu_custom_call" | custom-call | tf_op jit(solution)/shard_map/project/pallas_call | solution.py:502
  38.1 0.0 collective-permute-done.2.b3
  38.1 0.0 copy-start.6
  38.1 1.0 %project_last.1 = (f32[96,128]{1,0:T(8,128)S(1)}, bf16[128,256]{1,0:T(8,128)(2,1)S(1)}, s32[1,128]{1,0:T(1,128)S(1)}) custom-call(bf16[896,256]{1,0:T(8,128)(2,1)S(1)} %get-tuple-element.17.rows_h, bf16[896,256]{1,0:T(8,128)(2,1)S(1)} %get-tuple-element.18.rows_l, f32[64,64]{1,0:T(8,128)S(1)} %bitcast.36, f32[16,256]{1,0:T(8,128)S(1)} %get-tuple-element.19.coef_in, ...), custom_call_target="tpu_custom_call" | custom-call | tf_op jit(solution)/shard_map/project_last/pallas_call | solution.py:502
  39.1 0.4 collective-permute-start.3
  39.6 0.9 %collective-permute-done.3.other = f32[96,128]{1,0:T(8,128)S(1)} collective-permute-done((f32[96,128]{1,0:T(8,128)S(1)}, f32[96,128]{1,0:T(8,128)S(1)}, u32[]{:S(2)}, u32[]{:S(2)}) %collective-permute-start.3) | collective-permute-done | bytes 49184 | tf_op jit(solution)/shard_map/ppermute | solution.py:573
  40.4 0.1 merge.1
  40.5 1.1 %collective-permute-start.4 = (f32[80,128]{1,0:T(8,128)S(1)}, f32[80,128]{1,0:T(8,128)S(1)}, u32[]{:S(2)}, u32[]{:S(2)}) collective-permute-start(f32[80,128]{1,0:T(8,128)S(1)} %get-tuple-element.21), channel_id=1, source_target_pairs={{0,8},{4,12},{8,0},{12,4},{16,24},{20,28},{24,16},{28,20},{32,40},... | collective-permute-start | bytes 122888 | tf_op jit(solution)/shard_map/ppermute | solution.py:575
  41.7 3.3 %collective-permute-start.5 = (f32[80,128]{1,0:T(8,128)S(1)}, f32[80,128]{1,0:T(8,128)S(1)}, u32[]{:S(2)}, u32[]{:S(2)}) collective-permute-start(f32[80,128]{1,0:T(8,128)S(1)} %get-tuple-element.22), channel_id=1, source_target_pairs={{0,248},{4,252},{8,16},{12,20},{16,8},{20,12},{24,32},{28,36},{32,... | collective-permute-start | bytes 122888 | tf_op jit(solution)/shard_map/ppermute | solution.py:576
  45.0 0.2 put.1
  45.2 2.7 %collective-permute-done.5.second = f32[80,128]{1,0:T(8,128)S(1)} collective-permute-done((f32[80,128]{1,0:T(8,128)S(1)}, f32[80,128]{1,0:T(8,128)S(1)}, u32[]{:S(2)}, u32[]{:S(2)}) %collective-permute-start.5) | collective-permute-done | bytes 40992 | tf_op jit(solution)/shard_map/ppermute | solution.py:576
  47.8 4.7 %back.1 = f32[512,128]{1,0:T(8,128)S(1)} custom-call(f32[864,256]{1,0:T(8,128)S(1)} %get-tuple-element.16.field, f32[96,128]{1,0:T(8,128)S(1)} %get-tuple-element.20.own, f32[96,128]{1,0:T(8,128)S(1)} %collective-permute-done.3.other, f32[80,128]{1,0:T(8,128)S(1)} %collective-permute-done.4.first, f32[80,128]{1,0:T(8,128)S(1)} %collective-permute-done.5.second, ...), custom_call_target="tpu_custom_call" | custom-call | tf_op jit(solution)/shard_map/back/pallas_call | solution.py:502
  52.5 0.0 copy-start
  52.5 19.2 %all_to_all.11 = f32[64,8,128]{2,1,0:T(8,128)S(1)} all-to-all(f32[64,8,128]{2,1,0:T(8,128)S(1)} %bitcast.32), channel_id=1, replica_groups=mesh['fft'=64,'band'=4] {'fft'}, dimensions={0} | all-to-all | bytes 524288 | tf_op jit(solution)/shard_map/all_to_all | solution.py:547
  71.7 1.7 %z_forward.1 = f32[1728,128]{1,0:T(8,128)} custom-call(f32[512,128]{1,0:T(8,128)S(1)} %bitcast.34, bf16[768,256]{1,0:T(8,128)(2,1)S(1)} %copy-done), custom_call_target="tpu_custom_call" | custom-call | tf_op jit(solution)/shard_map/z_forward/pallas_call | solution.py:502
  (14 shorter events, 0.0 us)
Async XLA Ops:
  0.1 0.7 copy-start.8
  0.1 0.7 copy-start.9
  1.9 32.9 %copy-start.1 = (bf16[1024,512]{1,0:T(8,128)(2,1)S(1)}, bf16[1024,512]{1,0:T(8,128)(2,1)}, u32[]{:S(2)}) copy-start(bf16[1024,512]{1,0:T(8,128)(2,1)} %constant.18.clone.ix) | copy-start | bytes 3145732
  1.9 34.2 %collective-permute-start.1 = (f32[1032,128]{1,0:T(8,128)S(1)}, f32[1032,128]{1,0:T(8,128)S(1)}, u32[]{:S(2)}, u32[]{:S(2)}) collective-permute-start(f32[1032,128]{1,0:T(8,128)S(1)} %maximum_bitcast_fusion.b0), channel_id=1, source_target_pairs={{0,3},{1,0},{2,1},{3,2},{4,7},{5,4},{6,5},{7,6},{8,11},{9,8},{10,9... | collective-permute-start | bytes 1585160 | tf_op jit(solution)/shard_map/ppermute | solution.py:526
  5.6 30.5 %collective-permute-start = (f32[1032,128]{1,0:T(8,128)S(1)}, f32[1032,128]{1,0:T(8,128)S(1)}, u32[]{:S(2)}, u32[]{:S(2)}) collective-permute-start(f32[1032,128]{1,0:T(8,128)S(1)} %maximum_bitcast_fusion.b0), channel_id=1, source_target_pairs={{0,1},{1,2},{2,3},{3,0},{4,5},{5,6},{6,7},{7,4},{8,9},{9,10},{10,1... | collective-permute-start | bytes 1585160 | tf_op jit(solution)/shard_map/ppermute | solution.py:526
  5.6 32.6 %collective-permute-start.2 = (f32[1032,128]{1,0:T(8,128)S(1)}, f32[1032,128]{1,0:T(8,128)S(1)}, u32[]{:S(2)}, u32[]{:S(2)}) collective-permute-start(f32[1032,128]{1,0:T(8,128)S(1)} %maximum_bitcast_fusion.b0), channel_id=1, source_target_pairs={{0,2},{1,3},{2,0},{3,1},{4,6},{5,7},{6,4},{7,5},{8,10},{9,11},{10,... | collective-permute-start | bytes 1585160 | tf_op jit(solution)/shard_map/ppermute | solution.py:526
  9.6 25.2 %copy-start.4 = (bf16[768,256]{1,0:T(8,128)(2,1)S(1)}, bf16[768,256]{1,0:T(8,128)(2,1)}, u32[]{:S(2)}) copy-start(bf16[768,256]{1,0:T(8,128)(2,1)} %constant.17.clone.ey) | copy-start | bytes 1179652
  9.7 25.2 %copy-start.5 = (bf16[128,384]{1,0:T(8,128)(2,1)S(1)}, bf16[128,384]{1,0:T(8,128)(2,1)}, u32[]{:S(2)}) copy-start(bf16[128,384]{1,0:T(8,128)(2,1)} %constant.21.clone.u) | copy-start | bytes 294916
  36.1 2.0 %copy-start.7 = (f32[64,8,8]{0,2,1:T(8,128)S(1)}, f32[64,8,8]{0,2,1:T(8,128)}, u32[]{:S(2)}) copy-start(f32[64,8,8]{0,2,1:T(8,128)} %param.19) | copy-start | bytes 49156
  38.1 9.7 %copy-start.6 = (bf16[384,128]{1,0:T(8,128)(2,1)S(1)}, bf16[384,128]{1,0:T(8,128)(2,1)}, u32[]{:S(2)}) copy-start(bf16[384,128]{1,0:T(8,128)(2,1)} %constant.22.clone.ut_in) | copy-start | bytes 294916
  39.1 8.7 %copy-start.2 = (f32[3,36864]{1,0:T(4,128)S(1)}, f32[3,36864]{1,0:T(4,128)}, u32[]{:S(2)}) copy-start(f32[3,36864]{1,0:T(4,128)} %param.15) | copy-start | bytes 1327108
  39.1 1.3 %collective-permute-start.3 = (f32[96,128]{1,0:T(8,128)S(1)}, f32[96,128]{1,0:T(8,128)S(1)}, u32[]{:S(2)}, u32[]{:S(2)}) collective-permute-start(f32[96,128]{1,0:T(8,128)S(1)} %get-tuple-element.20.own), channel_id=1, source_target_pairs={{0,4},{4,0},{8,12},{12,8},{16,20},{20,16},{24,28},{28,24},{32,36},... | collective-permute-start | bytes 147464 | tf_op jit(solution)/shard_map/ppermute | solution.py:573
  40.5 4.6 %collective-permute-start.4 = (f32[80,128]{1,0:T(8,128)S(1)}, f32[80,128]{1,0:T(8,128)S(1)}, u32[]{:S(2)}, u32[]{:S(2)}) collective-permute-start(f32[80,128]{1,0:T(8,128)S(1)} %get-tuple-element.21), channel_id=1, source_target_pairs={{0,8},{4,12},{8,0},{12,4},{16,24},{20,28},{24,16},{28,20},{32,40},... | collective-permute-start | bytes 122888 | tf_op jit(solution)/shard_map/ppermute | solution.py:575
  41.7 6.2 %collective-permute-start.5 = (f32[80,128]{1,0:T(8,128)S(1)}, f32[80,128]{1,0:T(8,128)S(1)}, u32[]{:S(2)}, u32[]{:S(2)}) collective-permute-start(f32[80,128]{1,0:T(8,128)S(1)} %get-tuple-element.22), channel_id=1, source_target_pairs={{0,248},{4,252},{8,16},{12,20},{16,8},{20,12},{24,32},{28,36},{32,... | collective-permute-start | bytes 122888 | tf_op jit(solution)/shard_map/ppermute | solution.py:576
  45.0 2.8 %copy-start.3 = (bf16[512,384]{1,0:T(8,128)(2,1)S(1)}, bf16[512,384]{1,0:T(8,128)(2,1)}, u32[]{:S(2)}) copy-start(bf16[512,384]{1,0:T(8,128)(2,1)} %constant.20.clone.fy_in) | copy-start | bytes 1179652
  52.5 19.2 %copy-start = (bf16[768,256]{1,0:T(8,128)(2,1)S(1)}, bf16[768,256]{1,0:T(8,128)(2,1)}, u32[]{:S(2)}) copy-start(bf16[768,256]{1,0:T(8,128)(2,1)} %constant.16.clone.wz_in.fz) | copy-start | bytes 1179652

commit v6 on v5

--- a/solution.py
+++ b/solution.py
@@ -80,7 +80,7 @@
     u = np.zeros((128, 384), np.float32)
     for zi in range(3):
         for p in range(128):
-            u[32 * zi + 8 * (p >= 64) + p % 8, 128 * zi + p] = 1.0
+            u[16 * zi + 8 * (p >= 64) + p % 8, 128 * zi + p] = 1.0
     t["u"] = u.astype(ml_dtypes.bfloat16)
     t["ut"] = np.concatenate([u[:, 128 * zi : 128 * zi + 128].T for zi in range(3)], 0).astype(
         ml_dtypes.bfloat16
@@ -163,7 +163,7 @@
     main, spare = line_places(iota((1, 256), 1), s)
     j = iota((128, 256), 0)
     pack = jnp.concatenate(
-        [one_hot(j == main), one_hot((j % 32 == spare) & (j < 96))], axis=0
+        [one_hot(j == main), one_hot((j % 16 == spare) & (j % 64 < 48))], axis=0
     )
     lane = iota((64, 128), 1)
     rows = []
@@ -183,13 +183,13 @@
     packed = (mm(pack, high).astype(BF), mm(pack, low).astype(BF))
     copies[4].wait()
     out = three(mm_nt, (wz[0:384, :], wz[384:768, :]), packed)
+    spares = out[0:64, 128:]
     for c in range(2):
-        block = [out[(2 * zi + c) * 64 : (2 * zi + c) * 64 + 64] for zi in range(3)]
         for zi in range(3):
-            send[pl.ds(4 * c + zi, 64, stride=8), :] = block[zi][:, :128]
-        send[pl.ds(4 * c + 3, 64, stride=8), :] = jnp.where(
-            lane < 32, block[0][:, 128:], jnp.where(lane < 64, block[1][:, 128:], block[2][:, 128:])
-        )
+            block = out[(2 * zi + c) * 64 : (2 * zi + c) * 64 + 64]
+            send[pl.ds(3 * c + zi, 64, stride=7), :] = block[:, :128]
+            spares = jnp.where(lane // 16 == 4 * c + zi, block[:, 128:], spares)
+    send[pl.ds(6, 64, stride=7), :] = spares
 
 
 def tile_rows(tiles):
@@ -206,13 +206,14 @@
     main, spare, other = masks_sp()
     spread = []
     for c in range(2):
-        high, low = split(recv[pl.ds(4 * c + 3, 64, stride=8), :])
+        got = recv[pl.ds(6, 64, stride=7), :]
+        high, low = split(pltpu.roll(got, 64, 1) if c else got)
         spread.append(mm(high, u[...]) + mm(low, u[...]))
     lines = []
     for zi in range(3):
         first, second = [], []
         for c in range(2):
-            got = recv[pl.ds(4 * c + zi, 64, stride=8), :]
+            got = recv[pl.ds(3 * c + zi, 64, stride=7), :]
             extra = spread[c][:, 128 * zi : 128 * zi + 128]
             first.append(jnp.where(main, got, jnp.where(spare, extra, 0.0)))
             second.append(pltpu.roll(jnp.where(other, got, 0.0), 64, 1))
@@ -422,12 +423,11 @@
             turned = h[128 * c : 128 * c + 128, 128 * zi : 128 * zi + 128].T
             first = turned[:64]
             second = pltpu.roll(turned[64:], 64, 1)
-            send[pl.ds(4 * c + zi, 64, stride=8), :] = jnp.where(main, first, second)
+            send[pl.ds(3 * c + zi, 64, stride=7), :] = jnp.where(main, first, second)
             high, low = split(jnp.where(spare, first, 0.0))
             move = ut[128 * zi : 128 * zi + 128, :]
             spares[c] = spares[c] + (mm(high, move) + mm(low, move))
-    for c in range(2):
-        send[pl.ds(4 * c + 3, 64, stride=8), :] = spares[c]
+    send[pl.ds(6, 64, stride=7), :] = spares[0] + pltpu.roll(spares[1], 64, 1)
 
 
 def kernel_z_forward(recv, fz, result, out, sems):
@@ -444,17 +444,19 @@
     main, spare = line_places(r, s)
     lane = iota((256, 128), 1)
     keep = one_hot(lane == main)
+    spares = recv[pl.ds(6, 64, stride=7), :]
+    spares = (spares, pltpu.roll(spares, 64, 1))
     highs, lows = [], []
     for zi in range(3):
         unpack = jnp.concatenate(
-            [keep, one_hot((lane == spare + 32 * zi) & (spare >= 0))], 1
+            [keep, one_hot((lane == spare + 16 * zi) & (spare >= 0))], 1
         )
         lines = jnp.concatenate(
             [
                 jnp.concatenate(
                     [
-                        recv[pl.ds(4 * c + zi, 64, stride=8), :],
-                        recv[pl.ds(4 * c + 3, 64, stride=8), :],
+                        recv[pl.ds(3 * c + zi, 64, stride=7), :],
+                        spares[c],
                     ],
                     1,
                 )
@@ -528,11 +530,10 @@
 
     ids = jnp.concatenate([blk_slot[None], blk_tile[None], jnp.zeros((6, 128), jnp.int32)], 0)
     own = jnp.concatenate([beta, ids.astype(F32)[None]], 0).reshape(1032, 128)
-    betas = gathered(own)
     (send,) = call(
         kernel_z_inverse,
         "z_inverse",
-        [(512, 128)],
+        [(448, 128)],
         (psi, t["wz"]),
         [
             pltpu.VMEM((2, 384, 128), F32),
@@ -542,10 +543,12 @@
         anywhere=(0, 1),
         limit=60 * 1024 * 1024,
     )
+    own, send = lax.optimization_barrier((own, send))
+    betas = gathered(own)
 
     def exchange(x):
-        x = lax.all_to_all(x.reshape(64, 8, 128), "fft", 0, 0, tiled=True)
-        return x.reshape(512, 128)
+        x = lax.all_to_all(x.reshape(64, 1, 896), "fft", 0, 0, tiled=True)
+        return x.reshape(448, 128)
 
     recv = exchange(send)
     vloc_tiles = vloc.reshape(3, 288, 128).transpose(1, 0, 2)
@@ -584,7 +587,7 @@
     (send,) = call(
         kernel_back,
         "back",
-        [(512, 128)],
+        [(448, 128)],
         (field, near, other, first, second, slots, slots_last, put, *betas, vloc_tiles, t["fx"], t["fy"], t["ut"]),
         [
             pltpu.VMEM((16, 256), F32),

time: 73.6 us -> 73.5 us (level)
  starting transfers between devices: 10.2 us -> 13.6 us
  waiting for transfers between devices: 3.55 us -> 2.1 us
  other arithmetic: 1.15 us -> 0.11 us
    ppermute x1, starting transfers between devices: 3.33 us -> 6.38 us  [body(): lax.ppermute(second, 'fft', [(i, ((i + 2) % 64 ^ 2) - 2 & 63) for i in ra...]
    ppermute x1, waiting for transfers between devices: 2.66 us -> 1.21 us  [body(): lax.ppermute(second, 'fft', [(i, ((i + 2) % 64 ^ 2) - 2 & 63) for i in ra...]
    reshape x1, other arithmetic: 1.08 us -> 0.04 us  [body(): own = jnp.concatenate([beta, ids.astype(F32)[None]], 0).reshape(1032, 128)]
  transfers between devices with their start and end apart: 6 -> 6, of which waited for: 2 -> 2; matrix products, arithmetic and copies ran while one was open for 0% -> 0% of each run, Pallas kernels for 8% -> 5%
where the time goes in v6:
time: 73.5 us; the launch traced here: 73.3 us
  blocking collectives  43.9 us (60%)
  starting transfers between devices  13.6 us (19%)
  Pallas kernels  13.4 us (18%)
  waiting for transfers between devices  2.1 us (3%)
    all_to_all x2, blocking collectives, exchange(): x = lax.all_to_all(x.reshape(64, 1, 896), 'fft', 0, 0, tiled=True)  43.9 us
    pallas_call x8, Pallas kernels, call(): pl.pallas_call(kernel, name=name, out_shape=shapes, in_specs=specs, out_s...  13.4 us
    ppermute x1, starting transfers between devices, body(): lax.ppermute(second, 'fft', [(i, ((i + 2) % 64 ^ 2) - 2 & 63) for i in ra...  6.38 us
    ppermute x3, starting transfers between devices, gathered(): lax.ppermute(x, 'band', [(i, (i + k) % 4) for i in range(4)])  5.29 us
    ppermute x1, starting transfers between devices, body(): first = lax.ppermute(first, 'fft', [(i, i ^ 2) for i in range(64)])  1.57 us
  transfers between devices with their start and end apart: 6, of which 2 were waited for; matrix products, arithmetic and copies ran while one was open for 0% of the time, Pallas kernels for 5%

profile of v6, /device:TPU:1, one launch (start us, length us, event | category | flops | bytes accessed | tf_op | source)
XLA Modules:
  0.0 73.3 jit_solution(360799503620412855)
XLA Ops:
  0.0 0.1 pad.4.clone
  0.1 2.5 %z_inverse.1 = f32[448,128]{1,0:T(8,128)} custom-call(f32[1728,128]{1,0:T(8,128)} %bitcast.38, bf16[768,256]{1,0:T(8,128)(2,1)} %constant.16.clone.wz_in.fz), custom_call_target="tpu_custom_call" | custom-call | tf_op jit(solution)/shard_map/z_inverse/pallas_call | solution.py:504
  2.6 0.0 copy-start.1
  2.6 0.0 copy-done.9
  2.6 0.0 copy-done.10
  2.6 0.1 add_convert_fusion
  2.7 0.0 copy-start.4
  2.7 3.6 %collective-permute-start.1 = (f32[1032,128]{1,0:T(8,128)S(1)}, f32[1032,128]{1,0:T(8,128)S(1)}, u32[]{:S(2)}, u32[]{:S(2)}) collective-permute-start(f32[1032,128]{1,0:T(8,128)S(1)} %maximum_bitcast_fusion.b0), channel_id=1, source_target_pairs={{0,3},{1,0},{2,1},{3,2},{4,7},{5,4},{6,5},{7,6},{8,11},{9,8},{10,9... | collective-permute-start | bytes 1585160 | tf_op jit(solution)/shard_map/ppermute | solution.py:528
  6.4 0.0 collective-permute-start
  6.4 1.6 %collective-permute-start.2 = (f32[1032,128]{1,0:T(8,128)S(1)}, f32[1032,128]{1,0:T(8,128)S(1)}, u32[]{:S(2)}, u32[]{:S(2)}) collective-permute-start(f32[1032,128]{1,0:T(8,128)S(1)} %maximum_bitcast_fusion.b0), channel_id=1, source_target_pairs={{0,2},{1,3},{2,0},{3,1},{4,6},{5,7},{6,4},{7,5},{8,10},{9,11},{10,... | collective-permute-start | bytes 1585160 | tf_op jit(solution)/shard_map/ppermute | solution.py:528
  8.0 24.1 %all_to_all.10 = f32[64,1,896]{2,1,0:T(1,128)S(1)} all-to-all(f32[64,1,896]{2,1,0:T(1,128)} %bitcast.37), channel_id=1, replica_groups=mesh['fft'=64,'band'=4] {'fft'}, dimensions={0} | all-to-all | bytes 458752 | tf_op jit(solution)/shard_map/all_to_all | solution.py:550
  32.1 1.3 %field.1 = (f32[864,256]{1,0:T(8,128)S(1)}, bf16[896,256]{1,0:T(8,128)(2,1)S(1)}, bf16[896,256]{1,0:T(8,128)(2,1)S(1)}) custom-call(f32[448,128]{1,0:T(8,128)S(1)} %bitcast.32, bf16[768,256]{1,0:T(8,128)(2,1)S(1)} %copy-done.4, bf16[1024,512]{1,0:T(8,128)(2,1)S(1)} %copy-done.1, bf16[128,384]{1,0:T(8,128)(2,1)S(1)} %copy-done.5), custom_call_target="tpu_custom_call" | custom-call | tf_op jit(solution)/shard_map/field/pallas_call | solution.py:504
  33.5 0.0 collective-permute-done.1.b2
  33.5 0.0 collective-permute-done.b1
  33.5 0.0 copy-start.7
  33.5 2.0 %project.1 = (f32[16,256]{1,0:T(8,128)S(1)}, bf16[384,256]{1,0:T(8,128)(2,1)S(1)}, s32[1,384]{1,0:T(1,128)S(1)}) custom-call(bf16[896,256]{1,0:T(8,128)(2,1)S(1)} %get-tuple-element.20.rows_h, bf16[896,256]{1,0:T(8,128)(2,1)S(1)} %get-tuple-element.21.rows_l, f32[1032,128]{1,0:T(8,128)S(1)} %maximum_bitcast_fusion.b0, ...), custom_call_target="tpu_custom_call" | custom-call | tf_op jit(solution)/shard_map/project/pallas_call | solution.py:504
  35.5 0.0 collective-permute-done.2.b3
  35.5 0.0 copy-start.6
  35.5 1.0 %project_last.1 = (f32[96,128]{1,0:T(8,128)S(1)}, bf16[128,256]{1,0:T(8,128)(2,1)S(1)}, s32[1,128]{1,0:T(1,128)S(1)}) custom-call(bf16[896,256]{1,0:T(8,128)(2,1)S(1)} %get-tuple-element.20.rows_h, bf16[896,256]{1,0:T(8,128)(2,1)S(1)} %get-tuple-element.21.rows_l, f32[64,64]{1,0:T(8,128)S(1)} %bitcast.36, f32[16,256]{1,0:T(8,128)S(1)} %get-tuple-element.23.coef_in, ...), custom_call_target="tpu_custom_call" | custom-call | tf_op jit(solution)/shard_map/project_last/pallas_call | solution.py:504
  36.5 0.4 collective-permute-start.3
  36.9 0.9 %collective-permute-done.3.other = f32[96,128]{1,0:T(8,128)S(1)} collective-permute-done((f32[96,128]{1,0:T(8,128)S(1)}, f32[96,128]{1,0:T(8,128)S(1)}, u32[]{:S(2)}, u32[]{:S(2)}) %collective-permute-start.3) | collective-permute-done | bytes 49184 | tf_op jit(solution)/shard_map/ppermute | solution.py:576
  37.8 0.1 merge.1
  37.8 1.6 %collective-permute-start.4 = (f32[80,128]{1,0:T(8,128)S(1)}, f32[80,128]{1,0:T(8,128)S(1)}, u32[]{:S(2)}, u32[]{:S(2)}) collective-permute-start(f32[80,128]{1,0:T(8,128)S(1)} %get-tuple-element.25), channel_id=1, source_target_pairs={{0,8},{4,12},{8,0},{12,4},{16,24},{20,28},{24,16},{28,20},{32,40},... | collective-permute-start | bytes 122888 | tf_op jit(solution)/shard_map/ppermute | solution.py:578
  39.4 6.4 %collective-permute-start.5 = (f32[80,128]{1,0:T(8,128)S(1)}, f32[80,128]{1,0:T(8,128)S(1)}, u32[]{:S(2)}, u32[]{:S(2)}) collective-permute-start(f32[80,128]{1,0:T(8,128)S(1)} %get-tuple-element.26), channel_id=1, source_target_pairs={{0,248},{4,252},{8,16},{12,20},{16,8},{20,12},{24,32},{28,36},{32,... | collective-permute-start | bytes 122888 | tf_op jit(solution)/shard_map/ppermute | solution.py:579
  45.8 0.2 put.1
  46.0 0.0 collective-permute-done.4.first
  46.0 1.2 %collective-permute-done.5.second = f32[80,128]{1,0:T(8,128)S(1)} collective-permute-done((f32[80,128]{1,0:T(8,128)S(1)}, f32[80,128]{1,0:T(8,128)S(1)}, u32[]{:S(2)}, u32[]{:S(2)}) %collective-permute-start.5) | collective-permute-done | bytes 40992 | tf_op jit(solution)/shard_map/ppermute | solution.py:579
  47.2 0.0 copy-done.2
  47.2 4.7 %back.1 = f32[448,128]{1,0:T(8,128)S(1)} custom-call(f32[864,256]{1,0:T(8,128)S(1)} %get-tuple-element.19.field, f32[96,128]{1,0:T(8,128)S(1)} %get-tuple-element.24.own, f32[96,128]{1,0:T(8,128)S(1)} %collective-permute-done.3.other, f32[80,128]{1,0:T(8,128)S(1)} %collective-permute-done.4.first, f32[80,128]{1,0:T(8,128)S(1)} %collective-permute-done.5.second, ...), custom_call_target="tpu_custom_call" | custom-call | tf_op jit(solution)/shard_map/back/pallas_call | solution.py:504
  51.9 0.0 copy-start
  52.0 19.7 %all_to_all.11 = f32[64,1,896]{2,1,0:T(1,128)S(1)} all-to-all(f32[64,1,896]{2,1,0:T(1,128)S(1)} %bitcast.33), channel_id=1, replica_groups=mesh['fft'=64,'band'=4] {'fft'}, dimensions={0} | all-to-all | bytes 458752 | tf_op jit(solution)/shard_map/all_to_all | solution.py:550
  71.7 1.6 %z_forward.1 = f32[1728,128]{1,0:T(8,128)} custom-call(f32[448,128]{1,0:T(8,128)S(1)} %bitcast.34, bf16[768,256]{1,0:T(8,128)(2,1)S(1)} %copy-done), custom_call_target="tpu_custom_call" | custom-call | tf_op jit(solution)/shard_map/z_forward/pallas_call | solution.py:504
  (16 shorter events, 0.1 us)
Async XLA Ops:
  0.1 2.5 %copy-start.9 = (s32[128]{0:T(128)S(1)}, s32[128]{0:T(128)}, u32[]{:S(2)}) copy-start(s32[128]{0:T(128)} %param.18) | copy-start | bytes 1540
  0.1 2.5 %copy-start.10 = (s32[128]{0:T(128)S(1)}, s32[128]{0:T(128)}, u32[]{:S(2)}) copy-start(s32[128]{0:T(128)} %param.17) | copy-start | bytes 1540
  0.1 2.6 %copy-start.8 = (f32[128,8,128]{2,1,0:T(8,128)S(1)}, f32[128,8,128]{2,1,0:T(8,128)}, u32[]{:S(2)}) copy-start(f32[128,8,128]{2,1,0:T(8,128)} %param.16) | copy-start | bytes 1572868
  0.1 32.1 %copy-start.5 = (bf16[128,384]{1,0:T(8,128)(2,1)S(1)}, bf16[128,384]{1,0:T(8,128)(2,1)}, u32[]{:S(2)}) copy-start(bf16[128,384]{1,0:T(8,128)(2,1)} %constant.21.clone.u) | copy-start | bytes 294916
  2.6 29.6 %copy-start.1 = (bf16[1024,512]{1,0:T(8,128)(2,1)S(1)}, bf16[1024,512]{1,0:T(8,128)(2,1)}, u32[]{:S(2)}) copy-start(bf16[1024,512]{1,0:T(8,128)(2,1)} %constant.18.clone.ix) | copy-start | bytes 3145732
  2.7 29.4 %copy-start.4 = (bf16[768,256]{1,0:T(8,128)(2,1)S(1)}, bf16[768,256]{1,0:T(8,128)(2,1)}, u32[]{:S(2)}) copy-start(bf16[768,256]{1,0:T(8,128)(2,1)} %constant.17.clone.ey) | copy-start | bytes 1179652
  2.7 30.7 %collective-permute-start.1 = (f32[1032,128]{1,0:T(8,128)S(1)}, f32[1032,128]{1,0:T(8,128)S(1)}, u32[]{:S(2)}, u32[]{:S(2)}) collective-permute-start(f32[1032,128]{1,0:T(8,128)S(1)} %maximum_bitcast_fusion.b0), channel_id=1, source_target_pairs={{0,3},{1,0},{2,1},{3,2},{4,7},{5,4},{6,5},{7,6},{8,11},{9,8},{10,9... | collective-permute-start | bytes 1585160 | tf_op jit(solution)/shard_map/ppermute | solution.py:528
  6.4 27.1 %collective-permute-start = (f32[1032,128]{1,0:T(8,128)S(1)}, f32[1032,128]{1,0:T(8,128)S(1)}, u32[]{:S(2)}, u32[]{:S(2)}) collective-permute-start(f32[1032,128]{1,0:T(8,128)S(1)} %maximum_bitcast_fusion.b0), channel_id=1, source_target_pairs={{0,1},{1,2},{2,3},{3,0},{4,5},{5,6},{6,7},{7,4},{8,9},{9,10},{10,1... | collective-permute-start | bytes 1585160 | tf_op jit(solution)/shard_map/ppermute | solution.py:528
  6.4 29.1 %collective-permute-start.2 = (f32[1032,128]{1,0:T(8,128)S(1)}, f32[1032,128]{1,0:T(8,128)S(1)}, u32[]{:S(2)}, u32[]{:S(2)}) collective-permute-start(f32[1032,128]{1,0:T(8,128)S(1)} %maximum_bitcast_fusion.b0), channel_id=1, source_target_pairs={{0,2},{1,3},{2,0},{3,1},{4,6},{5,7},{6,4},{7,5},{8,10},{9,11},{10,... | collective-permute-start | bytes 1585160 | tf_op jit(solution)/shard_map/ppermute | solution.py:528
  33.5 2.0 %copy-start.7 = (f32[64,8,8]{0,2,1:T(8,128)S(1)}, f32[64,8,8]{0,2,1:T(8,128)}, u32[]{:S(2)}) copy-start(f32[64,8,8]{0,2,1:T(8,128)} %param.19) | copy-start | bytes 49156
  35.5 11.7 %copy-start.6 = (bf16[384,128]{1,0:T(8,128)(2,1)S(1)}, bf16[384,128]{1,0:T(8,128)(2,1)}, u32[]{:S(2)}) copy-start(bf16[384,128]{1,0:T(8,128)(2,1)} %constant.22.clone.ut_in) | copy-start | bytes 294916
  36.5 10.7 %copy-start.2 = (f32[3,36864]{1,0:T(4,128)S(1)}, f32[3,36864]{1,0:T(4,128)}, u32[]{:S(2)}) copy-start(f32[3,36864]{1,0:T(4,128)} %param.15) | copy-start | bytes 1327108
  36.5 1.3 %collective-permute-start.3 = (f32[96,128]{1,0:T(8,128)S(1)}, f32[96,128]{1,0:T(8,128)S(1)}, u32[]{:S(2)}, u32[]{:S(2)}) collective-permute-start(f32[96,128]{1,0:T(8,128)S(1)} %get-tuple-element.24.own), channel_id=1, source_target_pairs={{0,4},{4,0},{8,12},{12,8},{16,20},{20,16},{24,28},{28,24},{32,36},... | collective-permute-start | bytes 147464 | tf_op jit(solution)/shard_map/ppermute | solution.py:576
  37.8 8.1 %collective-permute-start.4 = (f32[80,128]{1,0:T(8,128)S(1)}, f32[80,128]{1,0:T(8,128)S(1)}, u32[]{:S(2)}, u32[]{:S(2)}) collective-permute-start(f32[80,128]{1,0:T(8,128)S(1)} %get-tuple-element.25), channel_id=1, source_target_pairs={{0,8},{4,12},{8,0},{12,4},{16,24},{20,28},{24,16},{28,20},{32,40},... | collective-permute-start | bytes 122888 | tf_op jit(solution)/shard_map/ppermute | solution.py:578
  39.4 7.8 %collective-permute-start.5 = (f32[80,128]{1,0:T(8,128)S(1)}, f32[80,128]{1,0:T(8,128)S(1)}, u32[]{:S(2)}, u32[]{:S(2)}) collective-permute-start(f32[80,128]{1,0:T(8,128)S(1)} %get-tuple-element.26), channel_id=1, source_target_pairs={{0,248},{4,252},{8,16},{12,20},{16,8},{20,12},{24,32},{28,36},{32,... | collective-permute-start | bytes 122888 | tf_op jit(solution)/shard_map/ppermute | solution.py:579
  45.8 1.4 %copy-start.3 = (bf16[512,384]{1,0:T(8,128)(2,1)S(1)}, bf16[512,384]{1,0:T(8,128)(2,1)}, u32[]{:S(2)}) copy-start(bf16[512,384]{1,0:T(8,128)(2,1)} %constant.20.clone.fy_in) | copy-start | bytes 1179652
  51.9 19.7 %copy-start = (bf16[768,256]{1,0:T(8,128)(2,1)S(1)}, bf16[768,256]{1,0:T(8,128)(2,1)}, u32[]{:S(2)}) copy-start(bf16[768,256]{1,0:T(8,128)(2,1)} %constant.16.clone.wz_in.fz) | copy-start | bytes 1179652

commit v7 on v6

--- a/solution.py
+++ b/solution.py
@@ -525,7 +525,7 @@
     psi = psi.reshape(1728, 128)
     def gathered(x):
         return [x] + [
-            lax.ppermute(x, "band", [(i, (i + k) % 4) for i in range(4)]) for k in (1, 3, 2)
+            lax.ppermute(x, "band", [(i, (i + k) % 4) for i in range(4)]) for k in (3, 2, 1)
         ]
 
     ids = jnp.concatenate([blk_slot[None], blk_tile[None], jnp.zeros((6, 128), jnp.int32)], 0)
@@ -543,7 +543,6 @@
         anywhere=(0, 1),
         limit=60 * 1024 * 1024,
     )
-    own, send = lax.optimization_barrier((own, send))
     betas = gathered(own)
 
     def exchange(x):

time: 73.5 us -> 70.8 us (0.963)
  starting transfers between devices: 13.6 us -> 9 us
  waiting for transfers between devices: 2.1 us -> 5.16 us
  blocking collectives: 43.9 us -> 41 us
  other arithmetic: 0.11 us -> 1.15 us
    ppermute x1, starting transfers between devices: 6.38 us -> 1.73 us  [body(): lax.ppermute(second, 'fft', [(i, ((i + 2) % 64 ^ 2) - 2 & 63) for i in ra...]
    ppermute x1, waiting for transfers between devices: 1.21 us -> 4.27 us  [body(): lax.ppermute(second, 'fft', [(i, ((i + 2) % 64 ^ 2) - 2 & 63) for i in ra...]
    all_to_all x2, blocking collectives: 43.9 us -> 41 us  [exchange(): x = lax.all_to_all(x.reshape(64, 1, 896), 'fft', 0, 0, tiled=True)]
    reshape x1, other arithmetic: 0.04 us -> 1.08 us  [body(): own = jnp.concatenate([beta, ids.astype(F32)[None]], 0).reshape(1032, 128)]
  transfers between devices with their start and end apart: 6 -> 6, of which waited for: 2 -> 2; matrix products, arithmetic and copies ran while one was open for 0% -> 0% of each run, Pallas kernels for 5% -> 8%
where the time goes in v7:
time: 70.8 us; the launch traced here: 70.5 us
  blocking collectives  41 us (58%)
  Pallas kernels  13.3 us (19%)
  starting transfers between devices  9 us (13%)
  waiting for transfers between devices  5.16 us (7%)
  other arithmetic  1.15 us (2%)
  local copies, waits for them, and re-layouts  0.8 us (1%)
    all_to_all x2, blocking collectives, exchange(): x = lax.all_to_all(x.reshape(64, 1, 896), 'fft', 0, 0, tiled=True)  41 us
    pallas_call x8, Pallas kernels, call(): pl.pallas_call(kernel, name=name, out_shape=shapes, in_specs=specs, out_s...  13.3 us
    ppermute x3, starting transfers between devices, gathered(): lax.ppermute(x, 'band', [(i, (i + k) % 4) for i in range(4)])  5.3 us
    ppermute x1, waiting for transfers between devices, body(): lax.ppermute(second, 'fft', [(i, ((i + 2) % 64 ^ 2) - 2 & 63) for i in ra...  4.27 us
    ppermute x1, starting transfers between devices, body(): lax.ppermute(second, 'fft', [(i, ((i + 2) % 64 ^ 2) - 2 & 63) for i in ra...  1.73 us
    ppermute x1, starting transfers between devices, body(): first = lax.ppermute(first, 'fft', [(i, i ^ 2) for i in range(64)])  1.56 us
  transfers between devices with their start and end apart: 6, of which 2 were waited for; matrix products, arithmetic and copies ran while one was open for 0% of the time, Pallas kernels for 8%

profile of v7, /device:TPU:1, one launch (start us, length us, event | category | flops | bytes accessed | tf_op | source)
XLA Modules:
  0.0 70.5 jit_solution(16042609217643413266)
XLA Ops:
  0.0 0.1 pad.4.clone
  0.1 0.7 copy-done.8
  0.7 0.0 copy-done.9
  0.8 0.1 add_convert_fusion
  0.8 1.1 %maximum_bitcast_fusion.b0 = f32[1032,128]{1,0:T(8,128)S(1)} fusion(f32[1,8,128]{2,1,0:T(8,128)S(1)} %add_convert_fusion, f32[128,8,128]{2,1,0:T(8,128)} %param.16), kind=kLoop, calls=%fused_computation | loop fusion | flops 132096 | bytes 1056768 | tf_op jit(solution)/shard_map/reshape | solution.py:532
  1.9 0.0 copy-start.1
  1.9 3.8 %collective-permute-start.1 = (f32[1032,128]{1,0:T(8,128)S(1)}, f32[1032,128]{1,0:T(8,128)S(1)}, u32[]{:S(2)}, u32[]{:S(2)}) collective-permute-start(f32[1032,128]{1,0:T(8,128)S(1)} %maximum_bitcast_fusion.b0), channel_id=1, source_target_pairs={{0,2},{1,3},{2,0},{3,1},{4,6},{5,7},{6,4},{7,5},{8,10},{9,11},{10,... | collective-permute-start | bytes 1585160 | tf_op jit(solution)/shard_map/ppermute | solution.py:528
  5.7 0.8 %collective-permute-start = (f32[1032,128]{1,0:T(8,128)S(1)}, f32[1032,128]{1,0:T(8,128)S(1)}, u32[]{:S(2)}, u32[]{:S(2)}) collective-permute-start(f32[1032,128]{1,0:T(8,128)S(1)} %maximum_bitcast_fusion.b0), channel_id=1, source_target_pairs={{0,3},{1,0},{2,1},{3,2},{4,7},{5,4},{6,5},{7,6},{8,11},{9,8},{10,9... | collective-permute-start | bytes 1585160 | tf_op jit(solution)/shard_map/ppermute | solution.py:528
  6.5 0.7 collective-permute-start.2
  7.2 2.4 %z_inverse.1 = f32[448,128]{1,0:T(8,128)} custom-call(f32[1728,128]{1,0:T(8,128)} %bitcast.38, bf16[768,256]{1,0:T(8,128)(2,1)} %constant.16.clone.wz_in.fz), custom_call_target="tpu_custom_call" | custom-call | tf_op jit(solution)/shard_map/z_inverse/pallas_call | solution.py:504
  9.7 0.0 copy-start.4
  9.7 24.3 %all_to_all.10 = f32[64,1,896]{2,1,0:T(1,128)S(1)} all-to-all(f32[64,1,896]{2,1,0:T(1,128)} %bitcast.37), channel_id=1, replica_groups=mesh['fft'=64,'band'=4] {'fft'}, dimensions={0} | all-to-all | bytes 458752 | tf_op jit(solution)/shard_map/all_to_all | solution.py:549
  34.0 1.3 %field.1 = (f32[864,256]{1,0:T(8,128)S(1)}, bf16[896,256]{1,0:T(8,128)(2,1)S(1)}, bf16[896,256]{1,0:T(8,128)(2,1)S(1)}) custom-call(f32[448,128]{1,0:T(8,128)S(1)} %bitcast.32, bf16[768,256]{1,0:T(8,128)(2,1)S(1)} %copy-done.4, bf16[1024,512]{1,0:T(8,128)(2,1)S(1)} %copy-done.1, bf16[128,384]{1,0:T(8,128)(2,1)S(1)} %copy-done.5), custom_call_target="tpu_custom_call" | custom-call | tf_op jit(solution)/shard_map/field/pallas_call | solution.py:504
  35.3 0.0 collective-permute-done.1.b2
  35.3 0.0 collective-permute-done.b1
  35.3 0.0 copy-start.7
  35.3 2.0 %project.1 = (f32[16,256]{1,0:T(8,128)S(1)}, bf16[384,256]{1,0:T(8,128)(2,1)S(1)}, s32[1,384]{1,0:T(1,128)S(1)}) custom-call(bf16[896,256]{1,0:T(8,128)(2,1)S(1)} %get-tuple-element.17.rows_h, bf16[896,256]{1,0:T(8,128)(2,1)S(1)} %get-tuple-element.18.rows_l, f32[1032,128]{1,0:T(8,128)S(1)} %maximum_bitcast_fusion.b0, ...), custom_call_target="tpu_custom_call" | custom-call | tf_op jit(solution)/shard_map/project/pallas_call | solution.py:504
  37.3 0.0 collective-permute-done.2.b3
  37.3 0.0 copy-start.6
  37.3 1.0 %project_last.1 = (f32[96,128]{1,0:T(8,128)S(1)}, bf16[128,256]{1,0:T(8,128)(2,1)S(1)}, s32[1,128]{1,0:T(1,128)S(1)}) custom-call(bf16[896,256]{1,0:T(8,128)(2,1)S(1)} %get-tuple-element.17.rows_h, bf16[896,256]{1,0:T(8,128)(2,1)S(1)} %get-tuple-element.18.rows_l, f32[64,64]{1,0:T(8,128)S(1)} %bitcast.36, f32[16,256]{1,0:T(8,128)S(1)} %get-tuple-element.19.coef_in, ...), custom_call_target="tpu_custom_call" | custom-call | tf_op jit(solution)/shard_map/project_last/pallas_call | solution.py:504
  38.3 0.4 collective-permute-start.3
  38.7 0.9 %collective-permute-done.3.other = f32[96,128]{1,0:T(8,128)S(1)} collective-permute-done((f32[96,128]{1,0:T(8,128)S(1)}, f32[96,128]{1,0:T(8,128)S(1)}, u32[]{:S(2)}, u32[]{:S(2)}) %collective-permute-start.3) | collective-permute-done | bytes 49184 | tf_op jit(solution)/shard_map/ppermute | solution.py:575
  39.6 0.1 merge.1
  39.7 1.6 %collective-permute-start.4 = (f32[80,128]{1,0:T(8,128)S(1)}, f32[80,128]{1,0:T(8,128)S(1)}, u32[]{:S(2)}, u32[]{:S(2)}) collective-permute-start(f32[80,128]{1,0:T(8,128)S(1)} %get-tuple-element.21), channel_id=1, source_target_pairs={{0,8},{4,12},{8,0},{12,4},{16,24},{20,28},{24,16},{28,20},{32,40},... | collective-permute-start | bytes 122888 | tf_op jit(solution)/shard_map/ppermute | solution.py:577
  41.2 1.7 %collective-permute-start.5 = (f32[80,128]{1,0:T(8,128)S(1)}, f32[80,128]{1,0:T(8,128)S(1)}, u32[]{:S(2)}, u32[]{:S(2)}) collective-permute-start(f32[80,128]{1,0:T(8,128)S(1)} %get-tuple-element.22), channel_id=1, source_target_pairs={{0,248},{4,252},{8,16},{12,20},{16,8},{20,12},{24,32},{28,36},{32,... | collective-permute-start | bytes 122888 | tf_op jit(solution)/shard_map/ppermute | solution.py:578
  43.0 0.2 put.1
  43.1 0.0 collective-permute-done.4.first
  43.1 4.3 %collective-permute-done.5.second = f32[80,128]{1,0:T(8,128)S(1)} collective-permute-done((f32[80,128]{1,0:T(8,128)S(1)}, f32[80,128]{1,0:T(8,128)S(1)}, u32[]{:S(2)}, u32[]{:S(2)}) %collective-permute-start.5) | collective-permute-done | bytes 40992 | tf_op jit(solution)/shard_map/ppermute | solution.py:578
  47.4 4.7 %back.1 = f32[448,128]{1,0:T(8,128)S(1)} custom-call(f32[864,256]{1,0:T(8,128)S(1)} %get-tuple-element.16.field, f32[96,128]{1,0:T(8,128)S(1)} %get-tuple-element.20.own, f32[96,128]{1,0:T(8,128)S(1)} %collective-permute-done.3.other, f32[80,128]{1,0:T(8,128)S(1)} %collective-permute-done.4.first, f32[80,128]{1,0:T(8,128)S(1)} %collective-permute-done.5.second, ...), custom_call_target="tpu_custom_call" | custom-call | tf_op jit(solution)/shard_map/back/pallas_call | solution.py:504
  52.2 0.0 copy-start
  52.2 16.7 %all_to_all.11 = f32[64,1,896]{2,1,0:T(1,128)S(1)} all-to-all(f32[64,1,896]{2,1,0:T(1,128)S(1)} %bitcast.33), channel_id=1, replica_groups=mesh['fft'=64,'band'=4] {'fft'}, dimensions={0} | all-to-all | bytes 458752 | tf_op jit(solution)/shard_map/all_to_all | solution.py:549
  68.9 1.6 %z_forward.1 = f32[1728,128]{1,0:T(8,128)} custom-call(f32[448,128]{1,0:T(8,128)S(1)} %bitcast.34, bf16[768,256]{1,0:T(8,128)(2,1)S(1)} %copy-done), custom_call_target="tpu_custom_call" | custom-call | tf_op jit(solution)/shard_map/z_forward/pallas_call | solution.py:504
  (14 shorter events, 0.0 us)
Async XLA Ops:
  0.1 0.7 copy-start.8
  0.1 0.7 copy-start.9
  1.9 32.0 %copy-start.1 = (bf16[1024,512]{1,0:T(8,128)(2,1)S(1)}, bf16[1024,512]{1,0:T(8,128)(2,1)}, u32[]{:S(2)}) copy-start(bf16[1024,512]{1,0:T(8,128)(2,1)} %constant.18.clone.ix) | copy-start | bytes 3145732
  1.9 33.4 %collective-permute-start.1 = (f32[1032,128]{1,0:T(8,128)S(1)}, f32[1032,128]{1,0:T(8,128)S(1)}, u32[]{:S(2)}, u32[]{:S(2)}) collective-permute-start(f32[1032,128]{1,0:T(8,128)S(1)} %maximum_bitcast_fusion.b0), channel_id=1, source_target_pairs={{0,2},{1,3},{2,0},{3,1},{4,6},{5,7},{6,4},{7,5},{8,10},{9,11},{10,... | collective-permute-start | bytes 1585160 | tf_op jit(solution)/shard_map/ppermute | solution.py:528
  5.7 29.5 %collective-permute-start = (f32[1032,128]{1,0:T(8,128)S(1)}, f32[1032,128]{1,0:T(8,128)S(1)}, u32[]{:S(2)}, u32[]{:S(2)}) collective-permute-start(f32[1032,128]{1,0:T(8,128)S(1)} %maximum_bitcast_fusion.b0), channel_id=1, source_target_pairs={{0,3},{1,0},{2,1},{3,2},{4,7},{5,4},{6,5},{7,6},{8,11},{9,8},{10,9... | collective-permute-start | bytes 1585160 | tf_op jit(solution)/shard_map/ppermute | solution.py:528
  6.5 30.8 %collective-permute-start.2 = (f32[1032,128]{1,0:T(8,128)S(1)}, f32[1032,128]{1,0:T(8,128)S(1)}, u32[]{:S(2)}, u32[]{:S(2)}) collective-permute-start(f32[1032,128]{1,0:T(8,128)S(1)} %maximum_bitcast_fusion.b0), channel_id=1, source_target_pairs={{0,1},{1,2},{2,3},{3,0},{4,5},{5,6},{6,7},{7,4},{8,9},{9,10},{10,1... | collective-permute-start | bytes 1585160 | tf_op jit(solution)/shard_map/ppermute | solution.py:528
  7.2 26.7 %copy-start.5 = (bf16[128,384]{1,0:T(8,128)(2,1)S(1)}, bf16[128,384]{1,0:T(8,128)(2,1)}, u32[]{:S(2)}) copy-start(bf16[128,384]{1,0:T(8,128)(2,1)} %constant.21.clone.u) | copy-start | bytes 294916
  9.7 24.3 %copy-start.4 = (bf16[768,256]{1,0:T(8,128)(2,1)S(1)}, bf16[768,256]{1,0:T(8,128)(2,1)}, u32[]{:S(2)}) copy-start(bf16[768,256]{1,0:T(8,128)(2,1)} %constant.17.clone.ey) | copy-start | bytes 1179652
  35.3 2.0 %copy-start.7 = (f32[64,8,8]{0,2,1:T(8,128)S(1)}, f32[64,8,8]{0,2,1:T(8,128)}, u32[]{:S(2)}) copy-start(f32[64,8,8]{0,2,1:T(8,128)} %param.19) | copy-start | bytes 49156
  37.3 10.1 %copy-start.6 = (bf16[384,128]{1,0:T(8,128)(2,1)S(1)}, bf16[384,128]{1,0:T(8,128)(2,1)}, u32[]{:S(2)}) copy-start(bf16[384,128]{1,0:T(8,128)(2,1)} %constant.22.clone.ut_in) | copy-start | bytes 294916
  38.3 9.1 %copy-start.2 = (f32[3,36864]{1,0:T(4,128)S(1)}, f32[3,36864]{1,0:T(4,128)}, u32[]{:S(2)}) copy-start(f32[3,36864]{1,0:T(4,128)} %param.15) | copy-start | bytes 1327108
  38.3 1.3 %collective-permute-start.3 = (f32[96,128]{1,0:T(8,128)S(1)}, f32[96,128]{1,0:T(8,128)S(1)}, u32[]{:S(2)}, u32[]{:S(2)}) collective-permute-start(f32[96,128]{1,0:T(8,128)S(1)} %get-tuple-element.20.own), channel_id=1, source_target_pairs={{0,4},{4,0},{8,12},{12,8},{16,20},{20,16},{24,28},{28,24},{32,36},... | collective-permute-start | bytes 147464 | tf_op jit(solution)/shard_map/ppermute | solution.py:575
  39.7 3.5 %collective-permute-start.4 = (f32[80,128]{1,0:T(8,128)S(1)}, f32[80,128]{1,0:T(8,128)S(1)}, u32[]{:S(2)}, u32[]{:S(2)}) collective-permute-start(f32[80,128]{1,0:T(8,128)S(1)} %get-tuple-element.21), channel_id=1, source_target_pairs={{0,8},{4,12},{8,0},{12,4},{16,24},{20,28},{24,16},{28,20},{32,40},... | collective-permute-start | bytes 122888 | tf_op jit(solution)/shard_map/ppermute | solution.py:577
  41.2 6.2 %collective-permute-start.5 = (f32[80,128]{1,0:T(8,128)S(1)}, f32[80,128]{1,0:T(8,128)S(1)}, u32[]{:S(2)}, u32[]{:S(2)}) collective-permute-start(f32[80,128]{1,0:T(8,128)S(1)} %get-tuple-element.22), channel_id=1, source_target_pairs={{0,248},{4,252},{8,16},{12,20},{16,8},{20,12},{24,32},{28,36},{32,... | collective-permute-start | bytes 122888 | tf_op jit(solution)/shard_map/ppermute | solution.py:578
  43.0 4.5 %copy-start.3 = (bf16[512,384]{1,0:T(8,128)(2,1)S(1)}, bf16[512,384]{1,0:T(8,128)(2,1)}, u32[]{:S(2)}) copy-start(bf16[512,384]{1,0:T(8,128)(2,1)} %constant.20.clone.fy_in) | copy-start | bytes 1179652
  52.2 16.7 %copy-start = (bf16[768,256]{1,0:T(8,128)(2,1)S(1)}, bf16[768,256]{1,0:T(8,128)(2,1)}, u32[]{:S(2)}) copy-start(bf16[768,256]{1,0:T(8,128)(2,1)} %constant.16.clone.wz_in.fz) | copy-start | bytes 1179652

commit v8 on v7

--- a/solution.py
+++ b/solution.py
@@ -331,7 +331,7 @@
 
 
 def kernel_back(
-    field, own, other, first, second, slots, slots_last, put, b0, b1, b2, b3,
+    field, own, other, second, first, slots, slots_last, put, b0, b1, b2, b3,
     vloc_in, fx_in, fy_in, ut_in, send, scr, rows, vloc, fx, fy, ut, sems,
 ):
     copies = [
@@ -543,6 +543,7 @@
         anywhere=(0, 1),
         limit=60 * 1024 * 1024,
     )
+    own, send = lax.optimization_barrier((own, send))
     betas = gathered(own)
 
     def exchange(x):
@@ -587,7 +588,7 @@
         kernel_back,
         "back",
         [(448, 128)],
-        (field, near, other, first, second, slots, slots_last, put, *betas, vloc_tiles, t["fx"], t["fy"], t["ut"]),
+        (field, near, other, second, first, slots, slots_last, put, *betas, vloc_tiles, t["fx"], t["fy"], t["ut"]),
         [
             pltpu.VMEM((16, 256), F32),
             pltpu.VMEM((512, 512), BF),

time: 70.8 us -> 70.5 us (level)
  starting transfers between devices: 9 us -> 10.9 us
  waiting for transfers between devices: 5.16 us -> 3.57 us
  blocking collectives: 41 us -> 42.1 us
  other arithmetic: 1.15 us -> 0.11 us
    ppermute x1, starting transfers between devices: 1.73 us -> 5.18 us  [body(): lax.ppermute(second, 'fft', [(i, ((i + 2) % 64 ^ 2) - 2 & 63) for i in ra...]
    ppermute x1, waiting for transfers between devices: 4.27 us -> 1.22 us  [body(): lax.ppermute(second, 'fft', [(i, ((i + 2) % 64 ^ 2) - 2 & 63) for i in ra...]
    ppermute x1, starting transfers between devices: 1.56 us -> 0.01 us  [body(): first = lax.ppermute(first, 'fft', [(i, i ^ 2) for i in range(64)])]
    ppermute x1, waiting for transfers between devices: 0.01 us -> 1.46 us  [body(): first = lax.ppermute(first, 'fft', [(i, i ^ 2) for i in range(64)])]
    all_to_all x2, blocking collectives: 41 us -> 42.1 us  [exchange(): x = lax.all_to_all(x.reshape(64, 1, 896), 'fft', 0, 0, tiled=True)]
    reshape x1, other arithmetic: 1.08 us -> 0.04 us  [body(): own = jnp.concatenate([beta, ids.astype(F32)[None]], 0).reshape(1032, 128)]
  transfers between devices with their start and end apart: 6 -> 6, of which waited for: 2 -> 3; matrix products, arithmetic and copies ran while one was open for 0% -> 0% of each run, Pallas kernels for 8% -> 5%
where the time goes in v8:
time: 70.5 us; the launch traced here: 70.3 us
  blocking collectives  42.1 us (60%)
  Pallas kernels  13.4 us (19%)
  starting transfers between devices  10.9 us (15%)
  waiting for transfers between devices  3.57 us (5%)
    all_to_all x2, blocking collectives, exchange(): x = lax.all_to_all(x.reshape(64, 1, 896), 'fft', 0, 0, tiled=True)  42.1 us
    pallas_call x8, Pallas kernels, call(): pl.pallas_call(kernel, name=name, out_shape=shapes, in_specs=specs, out_s...  13.4 us
    ppermute x3, starting transfers between devices, gathered(): lax.ppermute(x, 'band', [(i, (i + k) % 4) for i in range(4)])  5.3 us
    ppermute x1, starting transfers between devices, body(): lax.ppermute(second, 'fft', [(i, ((i + 2) % 64 ^ 2) - 2 & 63) for i in ra...  5.18 us
    ppermute x1, waiting for transfers between devices, body(): first = lax.ppermute(first, 'fft', [(i, i ^ 2) for i in range(64)])  1.46 us
  transfers between devices with their start and end apart: 6, of which 3 were waited for; matrix products, arithmetic and copies ran while one was open for 0% of the time, Pallas kernels for 5%

profile of v8, /device:TPU:1, one launch (start us, length us, event | category | flops | bytes accessed | tf_op | source)
XLA Modules:
  0.0 70.3 jit_solution(10763378086529237778)
XLA Ops:
  0.0 0.1 pad.4.clone
  0.1 2.5 %z_inverse.1 = f32[448,128]{1,0:T(8,128)} custom-call(f32[1728,128]{1,0:T(8,128)} %bitcast.38, bf16[768,256]{1,0:T(8,128)(2,1)} %constant.16.clone.wz_in.fz), custom_call_target="tpu_custom_call" | custom-call | tf_op jit(solution)/shard_map/z_inverse/pallas_call | solution.py:504
  2.6 0.0 copy-start.1
  2.6 0.0 copy-done.9
  2.6 0.1 add_convert_fusion
  2.7 0.0 copy-start.4
  2.7 3.8 %collective-permute-start.1 = (f32[1032,128]{1,0:T(8,128)S(1)}, f32[1032,128]{1,0:T(8,128)S(1)}, u32[]{:S(2)}, u32[]{:S(2)}) collective-permute-start(f32[1032,128]{1,0:T(8,128)S(1)} %maximum_bitcast_fusion.b0), channel_id=1, source_target_pairs={{0,2},{1,3},{2,0},{3,1},{4,6},{5,7},{6,4},{7,5},{8,10},{9,11},{10,... | collective-permute-start | bytes 1585160 | tf_op jit(solution)/shard_map/ppermute | solution.py:528
  6.6 0.8 %collective-permute-start = (f32[1032,128]{1,0:T(8,128)S(1)}, f32[1032,128]{1,0:T(8,128)S(1)}, u32[]{:S(2)}, u32[]{:S(2)}) collective-permute-start(f32[1032,128]{1,0:T(8,128)S(1)} %maximum_bitcast_fusion.b0), channel_id=1, source_target_pairs={{0,3},{1,0},{2,1},{3,2},{4,7},{5,4},{6,5},{7,6},{8,11},{9,8},{10,9... | collective-permute-start | bytes 1585160 | tf_op jit(solution)/shard_map/ppermute | solution.py:528
  7.3 0.7 collective-permute-start.2
  8.0 24.1 %all_to_all.10 = f32[64,1,896]{2,1,0:T(1,128)S(1)} all-to-all(f32[64,1,896]{2,1,0:T(1,128)} %bitcast.37), channel_id=1, replica_groups=mesh['fft'=64,'band'=4] {'fft'}, dimensions={0} | all-to-all | bytes 458752 | tf_op jit(solution)/shard_map/all_to_all | solution.py:550
  32.1 0.0 copy-done.5
  32.2 1.3 %field.1 = (f32[864,256]{1,0:T(8,128)S(1)}, bf16[896,256]{1,0:T(8,128)(2,1)S(1)}, bf16[896,256]{1,0:T(8,128)(2,1)S(1)}) custom-call(f32[448,128]{1,0:T(8,128)S(1)} %bitcast.32, bf16[768,256]{1,0:T(8,128)(2,1)S(1)} %copy-done.4, bf16[1024,512]{1,0:T(8,128)(2,1)S(1)} %copy-done.1, bf16[128,384]{1,0:T(8,128)(2,1)S(1)} %copy-done.5), custom_call_target="tpu_custom_call" | custom-call | tf_op jit(solution)/shard_map/field/pallas_call | solution.py:504
  33.5 0.0 collective-permute-done.1.b2
  33.5 0.0 collective-permute-done.b1
  33.5 0.0 copy-start.7
  33.5 2.0 %project.1 = (f32[16,256]{1,0:T(8,128)S(1)}, bf16[384,256]{1,0:T(8,128)(2,1)S(1)}, s32[1,384]{1,0:T(1,128)S(1)}) custom-call(bf16[896,256]{1,0:T(8,128)(2,1)S(1)} %get-tuple-element.20.rows_h, bf16[896,256]{1,0:T(8,128)(2,1)S(1)} %get-tuple-element.21.rows_l, f32[1032,128]{1,0:T(8,128)S(1)} %maximum_bitcast_fusion.b0, ...), custom_call_target="tpu_custom_call" | custom-call | tf_op jit(solution)/shard_map/project/pallas_call | solution.py:504
  35.5 0.0 collective-permute-done.2.b3
  35.5 0.0 copy-start.6
  35.5 1.0 %project_last.1 = (f32[96,128]{1,0:T(8,128)S(1)}, bf16[128,256]{1,0:T(8,128)(2,1)S(1)}, s32[1,128]{1,0:T(1,128)S(1)}) custom-call(bf16[896,256]{1,0:T(8,128)(2,1)S(1)} %get-tuple-element.20.rows_h, bf16[896,256]{1,0:T(8,128)(2,1)S(1)} %get-tuple-element.21.rows_l, f32[64,64]{1,0:T(8,128)S(1)} %bitcast.36, f32[16,256]{1,0:T(8,128)S(1)} %get-tuple-element.23.coef_in, ...), custom_call_target="tpu_custom_call" | custom-call | tf_op jit(solution)/shard_map/project_last/pallas_call | solution.py:504
  36.5 0.4 collective-permute-start.3
  36.9 0.9 %collective-permute-done.3.other = f32[96,128]{1,0:T(8,128)S(1)} collective-permute-done((f32[96,128]{1,0:T(8,128)S(1)}, f32[96,128]{1,0:T(8,128)S(1)}, u32[]{:S(2)}, u32[]{:S(2)}) %collective-permute-start.3) | collective-permute-done | bytes 49184 | tf_op jit(solution)/shard_map/ppermute | solution.py:576
  37.8 0.1 merge.1
  37.9 5.2 %collective-permute-start.4 = (f32[80,128]{1,0:T(8,128)S(1)}, f32[80,128]{1,0:T(8,128)S(1)}, u32[]{:S(2)}, u32[]{:S(2)}) collective-permute-start(f32[80,128]{1,0:T(8,128)S(1)} %get-tuple-element.25), channel_id=1, source_target_pairs={{0,248},{4,252},{8,16},{12,20},{16,8},{20,12},{24,32},{28,36},{32,... | collective-permute-start | bytes 122888 | tf_op jit(solution)/shard_map/ppermute | solution.py:579
  43.0 0.0 collective-permute-start.5
  43.0 0.2 put.1
  43.2 1.2 %collective-permute-done.4.second = f32[80,128]{1,0:T(8,128)S(1)} collective-permute-done((f32[80,128]{1,0:T(8,128)S(1)}, f32[80,128]{1,0:T(8,128)S(1)}, u32[]{:S(2)}, u32[]{:S(2)}) %collective-permute-start.4) | collective-permute-done | bytes 40992 | tf_op jit(solution)/shard_map/ppermute | solution.py:579
  44.4 1.5 %collective-permute-done.5.first = f32[80,128]{1,0:T(8,128)S(1)} collective-permute-done((f32[80,128]{1,0:T(8,128)S(1)}, f32[80,128]{1,0:T(8,128)S(1)}, u32[]{:S(2)}, u32[]{:S(2)}) %collective-permute-start.5) | collective-permute-done | bytes 40992 | tf_op jit(solution)/shard_map/ppermute | solution.py:578
  45.9 0.0 copy-done.3
  45.9 4.7 %back.1 = f32[448,128]{1,0:T(8,128)S(1)} custom-call(f32[864,256]{1,0:T(8,128)S(1)} %get-tuple-element.19.field, f32[96,128]{1,0:T(8,128)S(1)} %get-tuple-element.24.own, f32[96,128]{1,0:T(8,128)S(1)} %collective-permute-done.3.other, f32[80,128]{1,0:T(8,128)S(1)} %collective-permute-done.4.second, f32[80,128]{1,0:T(8,128)S(1)} %collective-permute-done.5.first, ...), custom_call_target="tpu_custom_call" | custom-call | tf_op jit(solution)/shard_map/back/pallas_call | solution.py:504
  50.6 0.0 copy-start
  50.7 18.0 %all_to_all.11 = f32[64,1,896]{2,1,0:T(1,128)S(1)} all-to-all(f32[64,1,896]{2,1,0:T(1,128)S(1)} %bitcast.33), channel_id=1, replica_groups=mesh['fft'=64,'band'=4] {'fft'}, dimensions={0} | all-to-all | bytes 458752 | tf_op jit(solution)/shard_map/all_to_all | solution.py:550
  68.7 1.6 %z_forward.1 = f32[1728,128]{1,0:T(8,128)} custom-call(f32[448,128]{1,0:T(8,128)S(1)} %bitcast.34, bf16[768,256]{1,0:T(8,128)(2,1)S(1)} %copy-done), custom_call_target="tpu_custom_call" | custom-call | tf_op jit(solution)/shard_map/z_forward/pallas_call | solution.py:504
  (16 shorter events, 0.1 us)
Async XLA Ops:
  0.1 2.5 %copy-start.9 = (s32[128]{0:T(128)S(1)}, s32[128]{0:T(128)}, u32[]{:S(2)}) copy-start(s32[128]{0:T(128)} %param.18) | copy-start | bytes 1540
  0.1 2.5 %copy-start.10 = (s32[128]{0:T(128)S(1)}, s32[128]{0:T(128)}, u32[]{:S(2)}) copy-start(s32[128]{0:T(128)} %param.17) | copy-start | bytes 1540
  0.1 2.6 %copy-start.8 = (f32[128,8,128]{2,1,0:T(8,128)S(1)}, f32[128,8,128]{2,1,0:T(8,128)}, u32[]{:S(2)}) copy-start(f32[128,8,128]{2,1,0:T(8,128)} %param.16) | copy-start | bytes 1572868
  0.1 32.1 %copy-start.5 = (bf16[128,384]{1,0:T(8,128)(2,1)S(1)}, bf16[128,384]{1,0:T(8,128)(2,1)}, u32[]{:S(2)}) copy-start(bf16[128,384]{1,0:T(8,128)(2,1)} %constant.21.clone.u) | copy-start | bytes 294916
  2.6 29.6 %copy-start.1 = (bf16[1024,512]{1,0:T(8,128)(2,1)S(1)}, bf16[1024,512]{1,0:T(8,128)(2,1)}, u32[]{:S(2)}) copy-start(bf16[1024,512]{1,0:T(8,128)(2,1)} %constant.18.clone.ix) | copy-start | bytes 3145732
  2.7 29.4 %copy-start.4 = (bf16[768,256]{1,0:T(8,128)(2,1)S(1)}, bf16[768,256]{1,0:T(8,128)(2,1)}, u32[]{:S(2)}) copy-start(bf16[768,256]{1,0:T(8,128)(2,1)} %constant.17.clone.ey) | copy-start | bytes 1179652
  2.7 30.8 %collective-permute-start.1 = (f32[1032,128]{1,0:T(8,128)S(1)}, f32[1032,128]{1,0:T(8,128)S(1)}, u32[]{:S(2)}, u32[]{:S(2)}) collective-permute-start(f32[1032,128]{1,0:T(8,128)S(1)} %maximum_bitcast_fusion.b0), channel_id=1, source_target_pairs={{0,2},{1,3},{2,0},{3,1},{4,6},{5,7},{6,4},{7,5},{8,10},{9,11},{10,... | collective-permute-start | bytes 1585160 | tf_op jit(solution)/shard_map/ppermute | solution.py:528
  6.6 26.9 %collective-permute-start = (f32[1032,128]{1,0:T(8,128)S(1)}, f32[1032,128]{1,0:T(8,128)S(1)}, u32[]{:S(2)}, u32[]{:S(2)}) collective-permute-start(f32[1032,128]{1,0:T(8,128)S(1)} %maximum_bitcast_fusion.b0), channel_id=1, source_target_pairs={{0,3},{1,0},{2,1},{3,2},{4,7},{5,4},{6,5},{7,6},{8,11},{9,8},{10,9... | collective-permute-start | bytes 1585160 | tf_op jit(solution)/shard_map/ppermute | solution.py:528
  7.3 28.2 %collective-permute-start.2 = (f32[1032,128]{1,0:T(8,128)S(1)}, f32[1032,128]{1,0:T(8,128)S(1)}, u32[]{:S(2)}, u32[]{:S(2)}) collective-permute-start(f32[1032,128]{1,0:T(8,128)S(1)} %maximum_bitcast_fusion.b0), channel_id=1, source_target_pairs={{0,1},{1,2},{2,3},{3,0},{4,5},{5,6},{6,7},{7,4},{8,9},{9,10},{10,1... | collective-permute-start | bytes 1585160 | tf_op jit(solution)/shard_map/ppermute | solution.py:528
  33.5 2.0 %copy-start.7 = (f32[64,8,8]{0,2,1:T(8,128)S(1)}, f32[64,8,8]{0,2,1:T(8,128)}, u32[]{:S(2)}) copy-start(f32[64,8,8]{0,2,1:T(8,128)} %param.19) | copy-start | bytes 49156
  35.5 10.4 %copy-start.6 = (bf16[384,128]{1,0:T(8,128)(2,1)S(1)}, bf16[384,128]{1,0:T(8,128)(2,1)}, u32[]{:S(2)}) copy-start(bf16[384,128]{1,0:T(8,128)(2,1)} %constant.22.clone.ut_in) | copy-start | bytes 294916
  36.5 9.4 %copy-start.2 = (f32[3,36864]{1,0:T(4,128)S(1)}, f32[3,36864]{1,0:T(4,128)}, u32[]{:S(2)}) copy-start(f32[3,36864]{1,0:T(4,128)} %param.15) | copy-start | bytes 1327108
  36.5 1.3 %collective-permute-start.3 = (f32[96,128]{1,0:T(8,128)S(1)}, f32[96,128]{1,0:T(8,128)S(1)}, u32[]{:S(2)}, u32[]{:S(2)}) collective-permute-start(f32[96,128]{1,0:T(8,128)S(1)} %get-tuple-element.24.own), channel_id=1, source_target_pairs={{0,4},{4,0},{8,12},{12,8},{16,20},{20,16},{24,28},{28,24},{32,36},... | collective-permute-start | bytes 147464 | tf_op jit(solution)/shard_map/ppermute | solution.py:576
  37.9 6.6 %collective-permute-start.4 = (f32[80,128]{1,0:T(8,128)S(1)}, f32[80,128]{1,0:T(8,128)S(1)}, u32[]{:S(2)}, u32[]{:S(2)}) collective-permute-start(f32[80,128]{1,0:T(8,128)S(1)} %get-tuple-element.25), channel_id=1, source_target_pairs={{0,248},{4,252},{8,16},{12,20},{16,8},{20,12},{24,32},{28,36},{32,... | collective-permute-start | bytes 122888 | tf_op jit(solution)/shard_map/ppermute | solution.py:579
  43.0 2.9 %collective-permute-start.5 = (f32[80,128]{1,0:T(8,128)S(1)}, f32[80,128]{1,0:T(8,128)S(1)}, u32[]{:S(2)}, u32[]{:S(2)}) collective-permute-start(f32[80,128]{1,0:T(8,128)S(1)} %get-tuple-element.26), channel_id=1, source_target_pairs={{0,8},{4,12},{8,0},{12,4},{16,24},{20,28},{24,16},{28,20},{32,40},... | collective-permute-start | bytes 122888 | tf_op jit(solution)/shard_map/ppermute | solution.py:578
  43.0 2.9 %copy-start.3 = (bf16[512,384]{1,0:T(8,128)(2,1)S(1)}, bf16[512,384]{1,0:T(8,128)(2,1)}, u32[]{:S(2)}) copy-start(bf16[512,384]{1,0:T(8,128)(2,1)} %constant.20.clone.fy_in) | copy-start | bytes 1179652
  50.6 18.0 %copy-start = (bf16[768,256]{1,0:T(8,128)(2,1)S(1)}, bf16[768,256]{1,0:T(8,128)(2,1)}, u32[]{:S(2)}) copy-start(bf16[768,256]{1,0:T(8,128)(2,1)} %constant.16.clone.wz_in.fz) | copy-start | bytes 1179652

commit v9 on v8

--- a/solution.py
+++ b/solution.py
@@ -144,22 +144,8 @@
     return ky * ky + kz * kz + kx * kx <= R2
 
 
-def kernel_z_inverse(psi, wz_in, send, buf, wz, sems):
+def kernel_z_inverse(psi, wz, send):
     s = lax.axis_index("fft")
-    copies = []
-    for plane in range(2):
-        base = 1152 * plane
-        for k, (src, dst, rows) in enumerate(((432, 0, 144), (0, 144, 152))):
-            copies.append(
-                pltpu.make_async_copy(
-                    psi.at[pl.ds(base + src, rows)],
-                    buf.at[plane, pl.ds(dst, rows)],
-                    sems.at[2 * plane + k],
-                )
-            )
-    copies.append(pltpu.make_async_copy(wz_in, wz, sems.at[4]))
-    for copy in copies:
-        copy.start()
     main, spare = line_places(iota((1, 256), 1), s)
     j = iota((128, 256), 0)
     pack = jnp.concatenate(
@@ -167,12 +153,20 @@
     )
     lane = iota((64, 128), 1)
     rows = []
-    for copy in copies[:4]:
-        copy.wait()
     for plane in range(2):
         lines = [[], []]
         for c in range(2):
-            t = [buf[plane, pl.ds(2 * k + c, 64, stride=6), :] for k in range(3)]
+            at = 1152 * plane + c
+            t = [
+                jnp.concatenate(
+                    [
+                        psi[pl.ds(at + 432 + 2 * k, 24, stride=6), :],
+                        psi[pl.ds(at + 2 * k, 40, stride=6), :],
+                    ],
+                    0,
+                )
+                for k in range(3)
+            ]
             middle = pltpu.roll(t[1], 64, 1)
             even = jnp.where(lane < 64, t[0], middle)
             odd = jnp.where(lane < 64, middle, t[2])
@@ -181,7 +175,6 @@
         rows += [jnp.concatenate(lines[0], 1), jnp.concatenate(lines[1], 1)]
     high, low = split(jnp.concatenate(rows, 0))
     packed = (mm(pack, high).astype(BF), mm(pack, low).astype(BF))
-    copies[4].wait()
     out = three(mm_nt, (wz[0:384, :], wz[384:768, :]), packed)
     spares = out[0:64, 128:]
     for c in range(2):
@@ -530,20 +523,7 @@
 
     ids = jnp.concatenate([blk_slot[None], blk_tile[None], jnp.zeros((6, 128), jnp.int32)], 0)
     own = jnp.concatenate([beta, ids.astype(F32)[None]], 0).reshape(1032, 128)
-    (send,) = call(
-        kernel_z_inverse,
-        "z_inverse",
-        [(448, 128)],
-        (psi, t["wz"]),
-        [
-            pltpu.VMEM((2, 384, 128), F32),
-            pltpu.VMEM((768, 256), BF),
-            pltpu.SemaphoreType.DMA((5,)),
-        ],
-        anywhere=(0, 1),
-        limit=60 * 1024 * 1024,
-    )
-    own, send = lax.optimization_barrier((own, send))
+    (send,) = call(kernel_z_inverse, "z_inverse", [(448, 128)], (psi, t["wz"]))
     betas = gathered(own)
 
     def exchange(x):

time: 70.5 us -> 69.6 us (0.987)
  Pallas kernels: 13.4 us -> 11.5 us
  local copies, waits for them, and re-layouts: 0.14 us -> 1.96 us
  starting transfers between devices: 10.9 us -> 9.13 us
  other arithmetic: 0.11 us -> 1.2 us
    pallas_call x8, Pallas kernels: 13.4 us -> 11.5 us  [call(): pl.pallas_call(kernel, name=name, out_shape=shapes, in_specs=specs, out_s...]
    unnamed x22, local copies, waits for them, and re-layouts: 0.06 us -> 1.88 us
    ppermute x1, starting transfers between devices: 5.18 us -> 3.43 us  [body(): lax.ppermute(second, 'fft', [(i, ((i + 2) % 64 ^ 2) - 2 & 63) for i in ra...]
    ppermute x1, waiting for transfers between devices: 1.22 us -> 2.6 us  [body(): lax.ppermute(second, 'fft', [(i, ((i + 2) % 64 ^ 2) - 2 & 63) for i in ra...]
    reshape x1, other arithmetic: 0.04 us -> 1.13 us  [body(): own = jnp.concatenate([beta, ids.astype(F32)[None]], 0).reshape(1032, 128)]
    ppermute x1, waiting for transfers between devices: 1.46 us -> 0.37 us  [body(): first = lax.ppermute(first, 'fft', [(i, i ^ 2) for i in range(64)])]
  transfers between devices with their start and end apart: 6 -> 6, of which waited for: 3 -> 3; matrix products, arithmetic and copies ran while one was open for 0% -> 0% of each run, Pallas kernels for 5% -> 6%
where the time goes in v9:
time: 69.6 us; the launch traced here: 69.4 us
  blocking collectives  41.6 us (60%)
  Pallas kernels  11.5 us (17%)
  starting transfers between devices  9.13 us (13%)
  waiting for transfers between devices  3.87 us (6%)
  local copies, waits for them, and re-layouts  1.96 us (3%)
  other arithmetic  1.2 us (2%)
    all_to_all x2, blocking collectives, exchange(): x = lax.all_to_all(x.reshape(64, 1, 896), 'fft', 0, 0, tiled=True)  41.6 us
    pallas_call x8, Pallas kernels, call(): pl.pallas_call(kernel, name=name, out_shape=shapes, in_specs=specs, out_s...  11.5 us
    ppermute x3, starting transfers between devices, gathered(): lax.ppermute(x, 'band', [(i, (i + k) % 4) for i in range(4)])  5.3 us
    ppermute x1, starting transfers between devices, body(): lax.ppermute(second, 'fft', [(i, ((i + 2) % 64 ^ 2) - 2 & 63) for i in ra...  3.43 us
    ppermute x1, waiting for transfers between devices, body(): lax.ppermute(second, 'fft', [(i, ((i + 2) % 64 ^ 2) - 2 & 63) for i in ra...  2.6 us
    unnamed x22, local copies, waits for them, and re-layouts  1.88 us
  transfers between devices with their start and end apart: 6, of which 3 were waited for; matrix products, arithmetic and copies ran while one was open for 0% of the time, Pallas kernels for 6%

profile of v9, /device:TPU:1, one launch (start us, length us, event | category | flops | bytes accessed | tf_op | source)
XLA Modules:
  0.0 69.4 jit_solution(9857477173827315606)
XLA Ops:
  0.0 0.1 pad.4.clone
  0.1 0.7 copy-done.9
  0.7 0.0 copy-done.10
  0.8 0.1 add_convert_fusion
  0.8 1.1 %maximum_bitcast_fusion.b0 = f32[1032,128]{1,0:T(8,128)S(1)} fusion(f32[1,8,128]{2,1,0:T(8,128)S(1)} %add_convert_fusion, f32[128,8,128]{2,1,0:T(8,128)} %param.16), kind=kLoop, calls=%fused_computation | loop fusion | flops 132096 | bytes 1056768 | tf_op jit(solution)/shard_map/reshape | solution.py:525
  2.0 0.0 copy-start.1
  2.0 3.8 %collective-permute-start.1 = (f32[1032,128]{1,0:T(8,128)S(1)}, f32[1032,128]{1,0:T(8,128)S(1)}, u32[]{:S(2)}, u32[]{:S(2)}) collective-permute-start(f32[1032,128]{1,0:T(8,128)S(1)} %maximum_bitcast_fusion.b0), channel_id=1, source_target_pairs={{0,2},{1,3},{2,0},{3,1},{4,6},{5,7},{6,4},{7,5},{8,10},{9,11},{10,... | collective-permute-start | bytes 1585160 | tf_op jit(solution)/shard_map/ppermute | solution.py:521
  5.8 0.8 %collective-permute-start = (f32[1032,128]{1,0:T(8,128)S(1)}, f32[1032,128]{1,0:T(8,128)S(1)}, u32[]{:S(2)}, u32[]{:S(2)}) collective-permute-start(f32[1032,128]{1,0:T(8,128)S(1)} %maximum_bitcast_fusion.b0), channel_id=1, source_target_pairs={{0,3},{1,0},{2,1},{3,2},{4,7},{5,4},{6,5},{7,6},{8,11},{9,8},{10,9... | collective-permute-start | bytes 1585160 | tf_op jit(solution)/shard_map/ppermute | solution.py:521
  6.6 0.7 collective-permute-start.2
  7.3 1.2 %copy-done.2 = f32[1,2,3,36864]{3,1,2,0:T(2,128)S(1)} copy-done((f32[1,2,3,36864]{3,1,2,0:T(2,128)S(1)}, f32[1,2,3,36864]{3,1,2,0:T(2,128)}, u32[]{:S(2)}) %copy-start.2) | copy-done | bytes 884760
  8.4 0.6 z_inverse.1
  9.1 0.0 copy-start.5
  9.1 24.1 %all_to_all.10 = f32[64,1,896]{2,1,0:T(1,128)S(1)} all-to-all(f32[64,1,896]{2,1,0:T(1,128)S(1)} %bitcast.35), channel_id=1, replica_groups=mesh['fft'=64,'band'=4] {'fft'}, dimensions={0} | all-to-all | bytes 458752 | tf_op jit(solution)/shard_map/all_to_all | solution.py:530
  33.1 1.3 %field.1 = (f32[864,256]{1,0:T(8,128)S(1)}, bf16[896,256]{1,0:T(8,128)(2,1)S(1)}, bf16[896,256]{1,0:T(8,128)(2,1)S(1)}) custom-call(f32[448,128]{1,0:T(8,128)S(1)} %bitcast.32, bf16[768,256]{1,0:T(8,128)(2,1)S(1)} %copy-done.5, bf16[1024,512]{1,0:T(8,128)(2,1)S(1)} %copy-done.1, bf16[128,384]{1,0:T(8,128)(2,1)S(1)} %copy-done.6), custom_call_target="tpu_custom_call" | custom-call | tf_op jit(solution)/shard_map/field/pallas_call | solution.py:497
  34.5 0.0 collective-permute-done.1.b2
  34.5 0.0 collective-permute-done.b1
  34.5 0.0 copy-start.8
  34.5 2.0 %project.1 = (f32[16,256]{1,0:T(8,128)S(1)}, bf16[384,256]{1,0:T(8,128)(2,1)S(1)}, s32[1,384]{1,0:T(1,128)S(1)}) custom-call(bf16[896,256]{1,0:T(8,128)(2,1)S(1)} %get-tuple-element.17.rows_h, bf16[896,256]{1,0:T(8,128)(2,1)S(1)} %get-tuple-element.18.rows_l, f32[1032,128]{1,0:T(8,128)S(1)} %maximum_bitcast_fusion.b0, ...), custom_call_target="tpu_custom_call" | custom-call | tf_op jit(solution)/shard_map/project/pallas_call | solution.py:497
  36.5 0.0 collective-permute-done.2.b3
  36.5 0.0 copy-start.7
  36.5 1.0 %project_last.1 = (f32[96,128]{1,0:T(8,128)S(1)}, bf16[128,256]{1,0:T(8,128)(2,1)S(1)}, s32[1,128]{1,0:T(1,128)S(1)}) custom-call(bf16[896,256]{1,0:T(8,128)(2,1)S(1)} %get-tuple-element.17.rows_h, bf16[896,256]{1,0:T(8,128)(2,1)S(1)} %get-tuple-element.18.rows_l, f32[64,64]{1,0:T(8,128)S(1)} %bitcast.38, f32[16,256]{1,0:T(8,128)S(1)} %get-tuple-element.19.coef_in, ...), custom_call_target="tpu_custom_call" | custom-call | tf_op jit(solution)/shard_map/project_last/pallas_call | solution.py:497
  37.5 0.4 collective-permute-start.3
  37.9 0.9 %collective-permute-done.3.other = f32[96,128]{1,0:T(8,128)S(1)} collective-permute-done((f32[96,128]{1,0:T(8,128)S(1)}, f32[96,128]{1,0:T(8,128)S(1)}, u32[]{:S(2)}, u32[]{:S(2)}) %collective-permute-start.3) | collective-permute-done | bytes 49184 | tf_op jit(solution)/shard_map/ppermute | solution.py:556
  38.8 0.1 merge.1
  38.8 3.4 %collective-permute-start.4 = (f32[80,128]{1,0:T(8,128)S(1)}, f32[80,128]{1,0:T(8,128)S(1)}, u32[]{:S(2)}, u32[]{:S(2)}) collective-permute-start(f32[80,128]{1,0:T(8,128)S(1)} %get-tuple-element.21), channel_id=1, source_target_pairs={{0,248},{4,252},{8,16},{12,20},{16,8},{20,12},{24,32},{28,36},{32,... | collective-permute-start | bytes 122888 | tf_op jit(solution)/shard_map/ppermute | solution.py:559
  42.3 0.0 collective-permute-start.5
  42.3 0.2 put.1
  42.4 2.6 %collective-permute-done.4.second = f32[80,128]{1,0:T(8,128)S(1)} collective-permute-done((f32[80,128]{1,0:T(8,128)S(1)}, f32[80,128]{1,0:T(8,128)S(1)}, u32[]{:S(2)}, u32[]{:S(2)}) %collective-permute-start.4) | collective-permute-done | bytes 40992 | tf_op jit(solution)/shard_map/ppermute | solution.py:559
  45.0 0.4 collective-permute-done.5.first
  45.4 4.7 %back.1 = f32[448,128]{1,0:T(8,128)S(1)} custom-call(f32[864,256]{1,0:T(8,128)S(1)} %get-tuple-element.16.field, f32[96,128]{1,0:T(8,128)S(1)} %get-tuple-element.20.own, f32[96,128]{1,0:T(8,128)S(1)} %collective-permute-done.3.other, f32[80,128]{1,0:T(8,128)S(1)} %collective-permute-done.4.second, f32[80,128]{1,0:T(8,128)S(1)} %collective-permute-done.5.first, ...), custom_call_target="tpu_custom_call" | custom-call | tf_op jit(solution)/shard_map/back/pallas_call | solution.py:497
  50.2 17.6 %all_to_all.11 = f32[64,1,896]{2,1,0:T(1,128)S(1)} all-to-all(f32[64,1,896]{2,1,0:T(1,128)S(1)} %bitcast.33), channel_id=1, replica_groups=mesh['fft'=64,'band'=4] {'fft'}, dimensions={0} | all-to-all | bytes 458752 | tf_op jit(solution)/shard_map/all_to_all | solution.py:530
  67.8 1.6 %z_forward.1 = f32[1728,128]{1,0:T(8,128)} custom-call(f32[448,128]{1,0:T(8,128)S(1)} %bitcast.34, bf16[768,256]{1,0:T(8,128)(2,1)S(1)} %copy-done), custom_call_target="tpu_custom_call" | custom-call | tf_op jit(solution)/shard_map/z_forward/pallas_call | solution.py:497
  (16 shorter events, 0.0 us)
Async XLA Ops:
  0.1 0.7 copy-start.9
  0.1 0.7 copy-start.10
  0.8 6.4 %copy-start = (bf16[768,256]{1,0:T(8,128)(2,1)S(1)}, bf16[768,256]{1,0:T(8,128)(2,1)}, u32[]{:S(2)}) copy-start(bf16[768,256]{1,0:T(8,128)(2,1)} %constant.16.clone.wz.fz) | copy-start | bytes 1179652
  2.0 31.2 %copy-start.1 = (bf16[1024,512]{1,0:T(8,128)(2,1)S(1)}, bf16[1024,512]{1,0:T(8,128)(2,1)}, u32[]{:S(2)}) copy-start(bf16[1024,512]{1,0:T(8,128)(2,1)} %constant.18.clone.ix) | copy-start | bytes 3145732
  2.0 32.5 %collective-permute-start.1 = (f32[1032,128]{1,0:T(8,128)S(1)}, f32[1032,128]{1,0:T(8,128)S(1)}, u32[]{:S(2)}, u32[]{:S(2)}) collective-permute-start(f32[1032,128]{1,0:T(8,128)S(1)} %maximum_bitcast_fusion.b0), channel_id=1, source_target_pairs={{0,2},{1,3},{2,0},{3,1},{4,6},{5,7},{6,4},{7,5},{8,10},{9,11},{10,... | collective-permute-start | bytes 1585160 | tf_op jit(solution)/shard_map/ppermute | solution.py:521
  5.8 28.7 %collective-permute-start = (f32[1032,128]{1,0:T(8,128)S(1)}, f32[1032,128]{1,0:T(8,128)S(1)}, u32[]{:S(2)}, u32[]{:S(2)}) collective-permute-start(f32[1032,128]{1,0:T(8,128)S(1)} %maximum_bitcast_fusion.b0), channel_id=1, source_target_pairs={{0,3},{1,0},{2,1},{3,2},{4,7},{5,4},{6,5},{7,6},{8,11},{9,8},{10,9... | collective-permute-start | bytes 1585160 | tf_op jit(solution)/shard_map/ppermute | solution.py:521
  6.6 29.9 %collective-permute-start.2 = (f32[1032,128]{1,0:T(8,128)S(1)}, f32[1032,128]{1,0:T(8,128)S(1)}, u32[]{:S(2)}, u32[]{:S(2)}) collective-permute-start(f32[1032,128]{1,0:T(8,128)S(1)} %maximum_bitcast_fusion.b0), channel_id=1, source_target_pairs={{0,1},{1,2},{2,3},{3,0},{4,5},{5,6},{6,7},{7,4},{8,9},{9,10},{10,1... | collective-permute-start | bytes 1585160 | tf_op jit(solution)/shard_map/ppermute | solution.py:521
  7.3 1.2 %copy-start.2 = (f32[1,2,3,36864]{3,1,2,0:T(2,128)S(1)}, f32[1,2,3,36864]{3,1,2,0:T(2,128)}, u32[]{:S(2)}) copy-start(f32[1,2,3,36864]{3,1,2,0:T(2,128)} %param.14) | copy-start | bytes 2654212
  8.4 24.7 %copy-start.6 = (bf16[128,384]{1,0:T(8,128)(2,1)S(1)}, bf16[128,384]{1,0:T(8,128)(2,1)}, u32[]{:S(2)}) copy-start(bf16[128,384]{1,0:T(8,128)(2,1)} %constant.21.clone.u) | copy-start | bytes 294916
  9.1 24.1 %copy-start.5 = (bf16[768,256]{1,0:T(8,128)(2,1)S(1)}, bf16[768,256]{1,0:T(8,128)(2,1)}, u32[]{:S(2)}) copy-start(bf16[768,256]{1,0:T(8,128)(2,1)} %constant.17.clone.ey) | copy-start | bytes 1179652
  34.5 2.0 %copy-start.8 = (f32[64,8,8]{0,2,1:T(8,128)S(1)}, f32[64,8,8]{0,2,1:T(8,128)}, u32[]{:S(2)}) copy-start(f32[64,8,8]{0,2,1:T(8,128)} %param.19) | copy-start | bytes 49156
  36.5 8.9 %copy-start.7 = (bf16[384,128]{1,0:T(8,128)(2,1)S(1)}, bf16[384,128]{1,0:T(8,128)(2,1)}, u32[]{:S(2)}) copy-start(bf16[384,128]{1,0:T(8,128)(2,1)} %constant.22.clone.ut_in) | copy-start | bytes 294916
  37.5 8.0 %copy-start.3 = (f32[3,36864]{1,0:T(4,128)S(1)}, f32[3,36864]{1,0:T(4,128)}, u32[]{:S(2)}) copy-start(f32[3,36864]{1,0:T(4,128)} %param.15) | copy-start | bytes 1327108
  37.5 1.3 %collective-permute-start.3 = (f32[96,128]{1,0:T(8,128)S(1)}, f32[96,128]{1,0:T(8,128)S(1)}, u32[]{:S(2)}, u32[]{:S(2)}) collective-permute-start(f32[96,128]{1,0:T(8,128)S(1)} %get-tuple-element.20.own), channel_id=1, source_target_pairs={{0,4},{4,0},{8,12},{12,8},{16,20},{20,16},{24,28},{28,24},{32,36},... | collective-permute-start | bytes 147464 | tf_op jit(solution)/shard_map/ppermute | solution.py:556
  38.8 6.2 %collective-permute-start.4 = (f32[80,128]{1,0:T(8,128)S(1)}, f32[80,128]{1,0:T(8,128)S(1)}, u32[]{:S(2)}, u32[]{:S(2)}) collective-permute-start(f32[80,128]{1,0:T(8,128)S(1)} %get-tuple-element.21), channel_id=1, source_target_pairs={{0,248},{4,252},{8,16},{12,20},{16,8},{20,12},{24,32},{28,36},{32,... | collective-permute-start | bytes 122888 | tf_op jit(solution)/shard_map/ppermute | solution.py:559
  42.3 3.1 %collective-permute-start.5 = (f32[80,128]{1,0:T(8,128)S(1)}, f32[80,128]{1,0:T(8,128)S(1)}, u32[]{:S(2)}, u32[]{:S(2)}) collective-permute-start(f32[80,128]{1,0:T(8,128)S(1)} %get-tuple-element.22), channel_id=1, source_target_pairs={{0,8},{4,12},{8,0},{12,4},{16,24},{20,28},{24,16},{28,20},{32,40},... | collective-permute-start | bytes 122888 | tf_op jit(solution)/shard_map/ppermute | solution.py:558
  42.3 3.2 %copy-start.4 = (bf16[512,384]{1,0:T(8,128)(2,1)S(1)}, bf16[512,384]{1,0:T(8,128)(2,1)}, u32[]{:S(2)}) copy-start(bf16[512,384]{1,0:T(8,128)(2,1)} %constant.20.clone.fy_in) | copy-start | bytes 1179652

commit v10 on v9

--- a/solution.py
+++ b/solution.py
@@ -13,7 +13,7 @@
 R2 = 48 * 48
 BF = jnp.bfloat16
 F32 = jnp.float32
-VMEM_LIMIT = 48 * 1024 * 1024
+VMEM_LIMIT = 32 * 1024 * 1024
 
 
 def trig(freqs, points):
@@ -318,24 +318,26 @@
     second[...] = jnp.where(even, down, up)
 
 
-def kernel_put(tiles, tiles_last, put):
+def kernel_put(tiles, tiles_last, vloc_in, put, vloc_out, vloc, sems):
+    copies = [
+        pltpu.make_async_copy(vloc_in.at[:, zi, :], vloc.at[zi], sems.at[zi]) for zi in range(3)
+    ]
+    for copy in copies:
+        copy.start()
     tile_of = jnp.concatenate([tiles[...], tiles_last[...]], 1)
     put[...] = one_hot(iota((864, 512), 0) == tile_of)
+    for copy in copies:
+        copy.wait()
+    for k in range(3):
+        for zi in range(3):
+            at = 288 * k + 96 * zi
+            vloc_out[at : at + 96, :] = vloc[zi, pl.ds(k, 96, stride=3), :]
 
 
 def kernel_back(
     field, own, other, second, first, slots, slots_last, put, b0, b1, b2, b3,
-    vloc_in, fx_in, fy_in, ut_in, send, scr, rows, vloc, fx, fy, ut, sems,
+    vloc, fx, fy, ut, send, scr, rows,
 ):
-    copies = [
-        pltpu.make_async_copy(vloc_in.at[:, zi, :], vloc.at[zi], sems.at[zi]) for zi in range(3)
-    ] + [
-        pltpu.make_async_copy(fx_in, fx, sems.at[3]),
-        pltpu.make_async_copy(fy_in, fy, sems.at[4]),
-        pltpu.make_async_copy(ut_in, ut, sems.at[5]),
-    ]
-    for copy in copies:
-        copy.start()
     core, even, a, b = chip_of(own, other)
     above = jnp.where(even, first[...], second[...])
     below = jnp.where(even, second[...], first[...])
@@ -379,12 +381,10 @@
         rows[span, 256:512] = low
     both = mm(put[...], rows[...])
     nonloc = both[:, :256] + both[:, 256:]
-    for copy in copies:
-        copy.wait()
     kinds = []
     for k in range(3):
-        factor = jnp.concatenate([vloc[zi, pl.ds(k, 96, stride=3), :] for zi in range(3)], 0)
         at = slice(288 * k, 288 * k + 288)
+        factor = vloc[at, :]
         kinds.append(split(field[at, :] * jnp.concatenate([factor, factor], 1) + nonloc[at, :]))
     g = []
     for parity in range(2):
@@ -557,28 +557,24 @@
     first, second = call(kernel_merge, "merge", [(80, 128), (80, 128)], (near, other))
     first = lax.ppermute(first, "fft", [(i, i ^ 2) for i in range(64)])
     second = lax.ppermute(second, "fft", [(i, (((i + 2) % 64) ^ 2) - 2 & 63) for i in range(64)])
-    (put,) = call(
+    put, vloc_rows = call(
         kernel_put,
         "put",
-        [((864, 512), BF)],
-        (tiles, tiles_last),
+        [((864, 512), BF), (864, 128)],
+        (tiles, tiles_last, vloc_tiles),
+        [pltpu.VMEM((3, 288, 128), F32), pltpu.SemaphoreType.DMA((3,))],
+        anywhere=(2,),
         cost=pl.CostEstimate(flops=2000000, bytes_accessed=3000000, transcendentals=0),
     )
     (send,) = call(
         kernel_back,
         "back",
         [(448, 128)],
-        (field, near, other, second, first, slots, slots_last, put, *betas, vloc_tiles, t["fx"], t["fy"], t["ut"]),
+        (field, near, other, second, first, slots, slots_last, put, *betas, vloc_rows, t["fx"], t["fy"], t["ut"]),
         [
             pltpu.VMEM((16, 256), F32),
             pltpu.VMEM((512, 512), BF),
-            pltpu.VMEM((3, 288, 128), F32),
-            pltpu.VMEM((2048, 256), BF),
-            pltpu.VMEM((512, 384), BF),
-            pltpu.VMEM((384, 128), BF),
-            pltpu.SemaphoreType.DMA((6,)),
         ],
-        anywhere=(12, 13, 14, 15),
     )
     (out,) = call(kernel_z_forward, "z_forward", [(1728, 128)], (exchange(send), t["fz"]),
         [pltpu.VMEM((1728, 128), F32), pltpu.SemaphoreType.DMA((7,))], anywhere_out=(0,))

time: 69.6 us -> 68.7 us (0.987)
    unnamed x22 -> x24, local copies, waits for them, and re-layouts: 1.88 us -> 1.89 us
where the time goes in v10:
time: 68.7 us; the launch traced here: 68.4 us
  blocking collectives  41.7 us (61%)
  Pallas kernels  10.9 us (16%)
  starting transfers between devices  9.14 us (13%)
  waiting for transfers between devices  3.49 us (5%)
  local copies, waits for them, and re-layouts  1.97 us (3%)
  other arithmetic  1.2 us (2%)
    all_to_all x2, blocking collectives, exchange(): x = lax.all_to_all(x.reshape(64, 1, 896), 'fft', 0, 0, tiled=True)  41.7 us
    pallas_call x8, Pallas kernels, call(): pl.pallas_call(kernel, name=name, out_shape=shapes, in_specs=specs, out_s...  10.9 us
    ppermute x3, starting transfers between devices, gathered(): lax.ppermute(x, 'band', [(i, (i + k) % 4) for i in range(4)])  5.3 us
    ppermute x1, starting transfers between devices, body(): lax.ppermute(second, 'fft', [(i, ((i + 2) % 64 ^ 2) - 2 & 63) for i in ra...  3.43 us
    ppermute x1, waiting for transfers between devices, body(): lax.ppermute(second, 'fft', [(i, ((i + 2) % 64 ^ 2) - 2 & 63) for i in ra...  2.23 us
    unnamed x24, local copies, waits for them, and re-layouts  1.89 us
  transfers between devices with their start and end apart: 6, of which 3 were waited for; matrix products, arithmetic and copies ran while one was open for 0% of the time, Pallas kernels for 6%

profile of v10, /device:TPU:1, one launch (start us, length us, event | category | flops | bytes accessed | tf_op | source)
XLA Modules:
  0.0 68.4 jit_solution(15572713484887452706)
XLA Ops:
  0.0 0.1 pad.4.clone
  0.1 0.7 copy-done.10
  0.7 0.0 copy-done.11
  0.8 0.1 add_convert_fusion
  0.8 1.1 %maximum_bitcast_fusion.b0 = f32[1032,128]{1,0:T(8,128)S(1)} fusion(f32[1,8,128]{2,1,0:T(8,128)S(1)} %add_convert_fusion, f32[128,8,128]{2,1,0:T(8,128)} %param.16), kind=kLoop, calls=%fused_computation | loop fusion | flops 132096 | bytes 1056768 | tf_op jit(solution)/shard_map/reshape | solution.py:525
  2.0 0.0 copy-start.2
  2.0 3.8 %collective-permute-start.1 = (f32[1032,128]{1,0:T(8,128)S(1)}, f32[1032,128]{1,0:T(8,128)S(1)}, u32[]{:S(2)}, u32[]{:S(2)}) collective-permute-start(f32[1032,128]{1,0:T(8,128)S(1)} %maximum_bitcast_fusion.b0), channel_id=1, source_target_pairs={{0,2},{1,3},{2,0},{3,1},{4,6},{5,7},{6,4},{7,5},{8,10},{9,11},{10,... | collective-permute-start | bytes 1585160 | tf_op jit(solution)/shard_map/ppermute | solution.py:521
  5.8 0.8 %collective-permute-start = (f32[1032,128]{1,0:T(8,128)S(1)}, f32[1032,128]{1,0:T(8,128)S(1)}, u32[]{:S(2)}, u32[]{:S(2)}) collective-permute-start(f32[1032,128]{1,0:T(8,128)S(1)} %maximum_bitcast_fusion.b0), channel_id=1, source_target_pairs={{0,3},{1,0},{2,1},{3,2},{4,7},{5,4},{6,5},{7,6},{8,11},{9,8},{10,9... | collective-permute-start | bytes 1585160 | tf_op jit(solution)/shard_map/ppermute | solution.py:521
  6.6 0.7 %collective-permute-start.2 = (f32[1032,128]{1,0:T(8,128)S(1)}, f32[1032,128]{1,0:T(8,128)S(1)}, u32[]{:S(2)}, u32[]{:S(2)}) collective-permute-start(f32[1032,128]{1,0:T(8,128)S(1)} %maximum_bitcast_fusion.b0), channel_id=1, source_target_pairs={{0,1},{1,2},{2,3},{3,0},{4,5},{5,6},{6,7},{7,4},{8,9},{9,10},{10,1... | collective-permute-start | bytes 1585160 | tf_op jit(solution)/shard_map/ppermute | solution.py:521
  7.3 1.2 %copy-done.3 = f32[1,2,3,36864]{3,1,2,0:T(2,128)S(1)} copy-done((f32[1,2,3,36864]{3,1,2,0:T(2,128)S(1)}, f32[1,2,3,36864]{3,1,2,0:T(2,128)}, u32[]{:S(2)}) %copy-start.3) | copy-done | bytes 884760
  8.4 0.6 z_inverse.1
  9.1 0.0 copy-start.6
  9.1 24.1 %all_to_all.10 = f32[64,1,896]{2,1,0:T(1,128)S(1)} all-to-all(f32[64,1,896]{2,1,0:T(1,128)S(1)} %bitcast.35), channel_id=1, replica_groups=mesh['fft'=64,'band'=4] {'fft'}, dimensions={0} | all-to-all | bytes 458752 | tf_op jit(solution)/shard_map/all_to_all | solution.py:530
  33.1 1.3 %field.1 = (f32[864,256]{1,0:T(8,128)S(1)}, bf16[896,256]{1,0:T(8,128)(2,1)S(1)}, bf16[896,256]{1,0:T(8,128)(2,1)S(1)}) custom-call(f32[448,128]{1,0:T(8,128)S(1)} %bitcast.32, bf16[768,256]{1,0:T(8,128)(2,1)S(1)} %copy-done.6, bf16[1024,512]{1,0:T(8,128)(2,1)S(1)} %copy-done.2, bf16[128,384]{1,0:T(8,128)(2,1)S(1)} %copy-done.7), custom_call_target="tpu_custom_call" | custom-call | tf_op jit(solution)/shard_map/field/pallas_call | solution.py:497
  34.5 0.0 collective-permute-done.b1
  34.5 0.0 copy-start.9
  34.5 0.0 copy-start.4
  34.5 2.0 %project.1 = (f32[16,256]{1,0:T(8,128)S(1)}, bf16[384,256]{1,0:T(8,128)(2,1)S(1)}, s32[1,384]{1,0:T(1,128)S(1)}) custom-call(bf16[896,256]{1,0:T(8,128)(2,1)S(1)} %get-tuple-element.19.rows_h, bf16[896,256]{1,0:T(8,128)(2,1)S(1)} %get-tuple-element.20.rows_l, f32[1032,128]{1,0:T(8,128)S(1)} %maximum_bitcast_fusion.b0, ...), custom_call_target="tpu_custom_call" | custom-call | tf_op jit(solution)/shard_map/project/pallas_call | solution.py:497
  36.5 0.0 collective-permute-done.2.b3
  36.5 0.0 copy-start.1
  36.5 1.0 %project_last.1 = (f32[96,128]{1,0:T(8,128)S(1)}, bf16[128,256]{1,0:T(8,128)(2,1)S(1)}, s32[1,128]{1,0:T(1,128)S(1)}) custom-call(bf16[896,256]{1,0:T(8,128)(2,1)S(1)} %get-tuple-element.19.rows_h, bf16[896,256]{1,0:T(8,128)(2,1)S(1)} %get-tuple-element.20.rows_l, f32[64,64]{1,0:T(8,128)S(1)} %bitcast.38, f32[16,256]{1,0:T(8,128)S(1)} %get-tuple-element.21.coef_in, ...), custom_call_target="tpu_custom_call" | custom-call | tf_op jit(solution)/shard_map/project_last/pallas_call | solution.py:497
  37.5 0.4 collective-permute-start.3
  37.9 0.9 %collective-permute-done.3.other = f32[96,128]{1,0:T(8,128)S(1)} collective-permute-done((f32[96,128]{1,0:T(8,128)S(1)}, f32[96,128]{1,0:T(8,128)S(1)}, u32[]{:S(2)}, u32[]{:S(2)}) %collective-permute-start.3) | collective-permute-done | bytes 49184 | tf_op jit(solution)/shard_map/ppermute | solution.py:556
  38.8 0.1 merge.1
  38.8 3.4 %collective-permute-start.4 = (f32[80,128]{1,0:T(8,128)S(1)}, f32[80,128]{1,0:T(8,128)S(1)}, u32[]{:S(2)}, u32[]{:S(2)}) collective-permute-start(f32[80,128]{1,0:T(8,128)S(1)} %get-tuple-element.23), channel_id=1, source_target_pairs={{0,248},{4,252},{8,16},{12,20},{16,8},{20,12},{24,32},{28,36},{32,... | collective-permute-start | bytes 122888 | tf_op jit(solution)/shard_map/ppermute | solution.py:559
  42.3 0.0 collective-permute-start.5
  42.3 0.5 put.1
  42.8 2.2 %collective-permute-done.4.second = f32[80,128]{1,0:T(8,128)S(1)} collective-permute-done((f32[80,128]{1,0:T(8,128)S(1)}, f32[80,128]{1,0:T(8,128)S(1)}, u32[]{:S(2)}, u32[]{:S(2)}) %collective-permute-start.4) | collective-permute-done | bytes 40992 | tf_op jit(solution)/shard_map/ppermute | solution.py:559
  45.1 0.4 collective-permute-done.5.first
  45.4 3.8 %back.1 = f32[448,128]{1,0:T(8,128)S(1)} custom-call(f32[864,256]{1,0:T(8,128)S(1)} %get-tuple-element.18.field, f32[96,128]{1,0:T(8,128)S(1)} %get-tuple-element.22.own, f32[96,128]{1,0:T(8,128)S(1)} %collective-permute-done.3.other, f32[80,128]{1,0:T(8,128)S(1)} %collective-permute-done.4.second, f32[80,128]{1,0:T(8,128)S(1)} %collective-permute-done.5.first, ...), custom_call_target="tpu_custom_call" | custom-call | tf_op jit(solution)/shard_map/back/pallas_call | solution.py:497
  49.2 17.6 %all_to_all.11 = f32[64,1,896]{2,1,0:T(1,128)S(1)} all-to-all(f32[64,1,896]{2,1,0:T(1,128)S(1)} %bitcast.33), channel_id=1, replica_groups=mesh['fft'=64,'band'=4] {'fft'}, dimensions={0} | all-to-all | bytes 458752 | tf_op jit(solution)/shard_map/all_to_all | solution.py:530
  66.8 1.6 %z_forward.1 = f32[1728,128]{1,0:T(8,128)} custom-call(f32[448,128]{1,0:T(8,128)S(1)} %bitcast.34, bf16[768,256]{1,0:T(8,128)(2,1)S(1)} %copy-done), custom_call_target="tpu_custom_call" | custom-call | tf_op jit(solution)/shard_map/z_forward/pallas_call | solution.py:497
  (18 shorter events, 0.0 us)
Async XLA Ops:
  0.1 0.7 copy-start.10
  0.1 0.7 copy-start.11
  0.8 6.4 %copy-start = (bf16[768,256]{1,0:T(8,128)(2,1)S(1)}, bf16[768,256]{1,0:T(8,128)(2,1)}, u32[]{:S(2)}) copy-start(bf16[768,256]{1,0:T(8,128)(2,1)} %constant.16.clone.wz.fz) | copy-start | bytes 1179652
  2.0 31.2 %copy-start.2 = (bf16[1024,512]{1,0:T(8,128)(2,1)S(1)}, bf16[1024,512]{1,0:T(8,128)(2,1)}, u32[]{:S(2)}) copy-start(bf16[1024,512]{1,0:T(8,128)(2,1)} %constant.18.clone.ix) | copy-start | bytes 3145732
  2.0 32.5 %collective-permute-start.1 = (f32[1032,128]{1,0:T(8,128)S(1)}, f32[1032,128]{1,0:T(8,128)S(1)}, u32[]{:S(2)}, u32[]{:S(2)}) collective-permute-start(f32[1032,128]{1,0:T(8,128)S(1)} %maximum_bitcast_fusion.b0), channel_id=1, source_target_pairs={{0,2},{1,3},{2,0},{3,1},{4,6},{5,7},{6,4},{7,5},{8,10},{9,11},{10,... | collective-permute-start | bytes 1585160 | tf_op jit(solution)/shard_map/ppermute | solution.py:521
  5.8 28.7 %collective-permute-start = (f32[1032,128]{1,0:T(8,128)S(1)}, f32[1032,128]{1,0:T(8,128)S(1)}, u32[]{:S(2)}, u32[]{:S(2)}) collective-permute-start(f32[1032,128]{1,0:T(8,128)S(1)} %maximum_bitcast_fusion.b0), channel_id=1, source_target_pairs={{0,3},{1,0},{2,1},{3,2},{4,7},{5,4},{6,5},{7,6},{8,11},{9,8},{10,9... | collective-permute-start | bytes 1585160 | tf_op jit(solution)/shard_map/ppermute | solution.py:521
  6.6 29.9 %collective-permute-start.2 = (f32[1032,128]{1,0:T(8,128)S(1)}, f32[1032,128]{1,0:T(8,128)S(1)}, u32[]{:S(2)}, u32[]{:S(2)}) collective-permute-start(f32[1032,128]{1,0:T(8,128)S(1)} %maximum_bitcast_fusion.b0), channel_id=1, source_target_pairs={{0,1},{1,2},{2,3},{3,0},{4,5},{5,6},{6,7},{7,4},{8,9},{9,10},{10,1... | collective-permute-start | bytes 1585160 | tf_op jit(solution)/shard_map/ppermute | solution.py:521
  7.3 1.2 %copy-start.3 = (f32[1,2,3,36864]{3,1,2,0:T(2,128)S(1)}, f32[1,2,3,36864]{3,1,2,0:T(2,128)}, u32[]{:S(2)}) copy-start(f32[1,2,3,36864]{3,1,2,0:T(2,128)} %param.14) | copy-start | bytes 2654212
  8.4 24.7 %copy-start.7 = (bf16[128,384]{1,0:T(8,128)(2,1)S(1)}, bf16[128,384]{1,0:T(8,128)(2,1)}, u32[]{:S(2)}) copy-start(bf16[128,384]{1,0:T(8,128)(2,1)} %constant.21.clone.u) | copy-start | bytes 294916
  9.1 24.1 %copy-start.6 = (bf16[768,256]{1,0:T(8,128)(2,1)S(1)}, bf16[768,256]{1,0:T(8,128)(2,1)}, u32[]{:S(2)}) copy-start(bf16[768,256]{1,0:T(8,128)(2,1)} %constant.17.clone.ey) | copy-start | bytes 1179652
  34.5 2.0 %copy-start.9 = (f32[64,8,8]{0,2,1:T(8,128)S(1)}, f32[64,8,8]{0,2,1:T(8,128)}, u32[]{:S(2)}) copy-start(f32[64,8,8]{0,2,1:T(8,128)} %param.19) | copy-start | bytes 49156
  34.5 7.8 %copy-start.4 = (f32[3,36864]{1,0:T(4,128)S(1)}, f32[3,36864]{1,0:T(4,128)}, u32[]{:S(2)}) copy-start(f32[3,36864]{1,0:T(4,128)} %param.15) | copy-start | bytes 1327108
  36.5 8.9 %copy-start.1 = (bf16[2048,256]{1,0:T(8,128)(2,1)S(1)}, bf16[2048,256]{1,0:T(8,128)(2,1)}, u32[]{:S(2)}) copy-start(bf16[2048,256]{1,0:T(8,128)(2,1)} %constant.19.clone.fx) | copy-start | bytes 3145732
  37.5 8.0 %copy-start.5 = (bf16[512,384]{1,0:T(8,128)(2,1)S(1)}, bf16[512,384]{1,0:T(8,128)(2,1)}, u32[]{:S(2)}) copy-start(bf16[512,384]{1,0:T(8,128)(2,1)} %constant.20.clone.fy) | copy-start | bytes 1179652
  37.5 1.3 %collective-permute-start.3 = (f32[96,128]{1,0:T(8,128)S(1)}, f32[96,128]{1,0:T(8,128)S(1)}, u32[]{:S(2)}, u32[]{:S(2)}) collective-permute-start(f32[96,128]{1,0:T(8,128)S(1)} %get-tuple-element.22.own), channel_id=1, source_target_pairs={{0,4},{4,0},{8,12},{12,8},{16,20},{20,16},{24,28},{28,24},{32,36},... | collective-permute-start | bytes 147464 | tf_op jit(solution)/shard_map/ppermute | solution.py:556
  38.8 6.2 %collective-permute-start.4 = (f32[80,128]{1,0:T(8,128)S(1)}, f32[80,128]{1,0:T(8,128)S(1)}, u32[]{:S(2)}, u32[]{:S(2)}) collective-permute-start(f32[80,128]{1,0:T(8,128)S(1)} %get-tuple-element.23), channel_id=1, source_target_pairs={{0,248},{4,252},{8,16},{12,20},{16,8},{20,12},{24,32},{28,36},{32,... | collective-permute-start | bytes 122888 | tf_op jit(solution)/shard_map/ppermute | solution.py:559
  42.3 3.1 %collective-permute-start.5 = (f32[80,128]{1,0:T(8,128)S(1)}, f32[80,128]{1,0:T(8,128)S(1)}, u32[]{:S(2)}, u32[]{:S(2)}) collective-permute-start(f32[80,128]{1,0:T(8,128)S(1)} %get-tuple-element.24), channel_id=1, source_target_pairs={{0,8},{4,12},{8,0},{12,4},{16,24},{20,28},{24,16},{28,20},{32,40},... | collective-permute-start | bytes 122888 | tf_op jit(solution)/shard_map/ppermute | solution.py:558
  42.3 3.1 %copy-start.8 = (bf16[384,128]{1,0:T(8,128)(2,1)S(1)}, bf16[384,128]{1,0:T(8,128)(2,1)}, u32[]{:S(2)}) copy-start(bf16[384,128]{1,0:T(8,128)(2,1)} %constant.22.clone.ut) | copy-start | bytes 294916

commit v11 on v10

--- a/solution.py
+++ b/solution.py
@@ -516,15 +516,14 @@
     }
     psi = psi_g[0].transpose(1, 0, 2).reshape(3, 2, 288, 128).transpose(0, 2, 1, 3)
     psi = psi.reshape(1728, 128)
-    def gathered(x):
-        return [x] + [
-            lax.ppermute(x, "band", [(i, (i + k) % 4) for i in range(4)]) for k in (3, 2, 1)
-        ]
+    def from_band(x, k):
+        return lax.ppermute(x, "band", [(i, (i + k) % 4) for i in range(4)])
 
     ids = jnp.concatenate([blk_slot[None], blk_tile[None], jnp.zeros((6, 128), jnp.int32)], 0)
     own = jnp.concatenate([beta, ids.astype(F32)[None]], 0).reshape(1032, 128)
     (send,) = call(kernel_z_inverse, "z_inverse", [(448, 128)], (psi, t["wz"]))
-    betas = gathered(own)
+    own_later, send = lax.optimization_barrier((own, send))
+    betas = [own, from_band(own, 3), from_band(own, 2), from_band(own_later, 1)]
 
     def exchange(x):
         x = lax.all_to_all(x.reshape(64, 1, 896), "fft", 0, 0, tiled=True)

time: 68.7 us -> 68.7 us (level)
  no operation moved by 1% of the time
where the time goes in v11:
time: 68.7 us; the launch traced here: 68.4 us
  blocking collectives  41.5 us (60%)
  Pallas kernels  10.9 us (16%)
  starting transfers between devices  9.27 us (13%)
  waiting for transfers between devices  3.49 us (5%)
  local copies, waits for them, and re-layouts  1.97 us (3%)
  other arithmetic  1.2 us (2%)
    all_to_all x2, blocking collectives, exchange(): x = lax.all_to_all(x.reshape(64, 1, 896), 'fft', 0, 0, tiled=True)  41.5 us
    pallas_call x8, Pallas kernels, call(): pl.pallas_call(kernel, name=name, out_shape=shapes, in_specs=specs, out_s...  10.9 us
    ppermute x3, starting transfers between devices, from_band(): return lax.ppermute(x, 'band', [(i, (i + k) % 4) for i in range(4)])  5.37 us
    ppermute x1, starting transfers between devices, body(): lax.ppermute(second, 'fft', [(i, ((i + 2) % 64 ^ 2) - 2 & 63) for i in ra...  3.49 us
    ppermute x1, waiting for transfers between devices, body(): lax.ppermute(second, 'fft', [(i, ((i + 2) % 64 ^ 2) - 2 & 63) for i in ra...  2.18 us
    unnamed x24, local copies, waits for them, and re-layouts  1.89 us
  transfers between devices with their start and end apart: 6, of which 3 were waited for; matrix products, arithmetic and copies ran while one was open for 0% of the time, Pallas kernels for 6%

profile of v11, /device:TPU:1, one launch (start us, length us, event | category | flops | bytes accessed | tf_op | source)
XLA Modules:
  0.0 68.4 jit_solution(2498704842499212632)
XLA Ops:
  0.0 0.1 pad.4.clone
  0.1 0.7 copy-done.10
  0.7 0.0 copy-done.11
  0.8 0.1 add_convert_fusion
  0.8 1.1 %maximum_bitcast_fusion.b0 = f32[1032,128]{1,0:T(8,128)S(1)} fusion(f32[1,8,128]{2,1,0:T(8,128)S(1)} %add_convert_fusion, f32[128,8,128]{2,1,0:T(8,128)} %param.16), kind=kLoop, calls=%fused_computation | loop fusion | flops 132096 | bytes 1056768 | tf_op jit(solution)/shard_map/reshape | solution.py:523
  2.0 0.0 copy-start.2
  2.0 3.8 %collective-permute-start.1 = (f32[1032,128]{1,0:T(8,128)S(1)}, f32[1032,128]{1,0:T(8,128)S(1)}, u32[]{:S(2)}, u32[]{:S(2)}) collective-permute-start(f32[1032,128]{1,0:T(8,128)S(1)} %maximum_bitcast_fusion.b0), channel_id=1, source_target_pairs={{0,2},{1,3},{2,0},{3,1},{4,6},{5,7},{6,4},{7,5},{8,10},{9,11},{10,... | collective-permute-start | bytes 1585160 | tf_op jit(solution)/shard_map/ppermute | solution.py:520
  5.8 0.8 %collective-permute-start = (f32[1032,128]{1,0:T(8,128)S(1)}, f32[1032,128]{1,0:T(8,128)S(1)}, u32[]{:S(2)}, u32[]{:S(2)}) collective-permute-start(f32[1032,128]{1,0:T(8,128)S(1)} %maximum_bitcast_fusion.b0), channel_id=1, source_target_pairs={{0,3},{1,0},{2,1},{3,2},{4,7},{5,4},{6,5},{7,6},{8,11},{9,8},{10,9... | collective-permute-start | bytes 1585160 | tf_op jit(solution)/shard_map/ppermute | solution.py:520
  6.6 1.2 %copy-done.3 = f32[1,2,3,36864]{3,1,2,0:T(2,128)S(1)} copy-done((f32[1,2,3,36864]{3,1,2,0:T(2,128)S(1)}, f32[1,2,3,36864]{3,1,2,0:T(2,128)}, u32[]{:S(2)}) %copy-start.3) | copy-done | bytes 884760
  7.7 0.6 z_inverse.1
  8.4 0.0 copy-start.6
  8.4 0.8 %collective-permute-start.2 = (f32[1032,128]{1,0:T(8,128)S(1)}, f32[1032,128]{1,0:T(8,128)S(1)}, u32[]{:S(2)}, u32[]{:S(2)}) collective-permute-start(f32[1032,128]{1,0:T(8,128)S(1)} %maximum_bitcast_fusion.b0), channel_id=1, source_target_pairs={{0,1},{1,2},{2,3},{3,0},{4,5},{5,6},{6,7},{7,4},{8,9},{9,10},{10,1... | collective-permute-start | bytes 1585160 | tf_op jit(solution)/shard_map/ppermute | solution.py:520
  9.2 23.9 %all_to_all.10 = f32[64,1,896]{2,1,0:T(1,128)S(1)} all-to-all(f32[64,1,896]{2,1,0:T(1,128)S(1)} %bitcast.34), channel_id=1, replica_groups=mesh['fft'=64,'band'=4] {'fft'}, dimensions={0} | all-to-all | bytes 458752 | tf_op jit(solution)/shard_map/all_to_all | solution.py:529
  33.1 1.3 %field.1 = (f32[864,256]{1,0:T(8,128)S(1)}, bf16[896,256]{1,0:T(8,128)(2,1)S(1)}, bf16[896,256]{1,0:T(8,128)(2,1)S(1)}) custom-call(f32[448,128]{1,0:T(8,128)S(1)} %bitcast.32, bf16[768,256]{1,0:T(8,128)(2,1)S(1)} %copy-done.6, bf16[1024,512]{1,0:T(8,128)(2,1)S(1)} %copy-done.2, bf16[128,384]{1,0:T(8,128)(2,1)S(1)} %copy-done.7), custom_call_target="tpu_custom_call" | custom-call | tf_op jit(solution)/shard_map/field/pallas_call | solution.py:497
  34.4 0.0 collective-permute-done.1.b2
  34.4 0.0 collective-permute-done.b1
  34.4 0.0 copy-start.9
  34.4 0.0 copy-start.4
  34.4 2.0 %project.1 = (f32[16,256]{1,0:T(8,128)S(1)}, bf16[384,256]{1,0:T(8,128)(2,1)S(1)}, s32[1,384]{1,0:T(1,128)S(1)}) custom-call(bf16[896,256]{1,0:T(8,128)(2,1)S(1)} %get-tuple-element.22.rows_h, bf16[896,256]{1,0:T(8,128)(2,1)S(1)} %get-tuple-element.23.rows_l, f32[1032,128]{1,0:T(8,128)S(1)} %maximum_bitcast_fusion.b0, ...), custom_call_target="tpu_custom_call" | custom-call | tf_op jit(solution)/shard_map/project/pallas_call | solution.py:497
  36.4 0.0 collective-permute-done.2.b3
  36.4 0.0 copy-start.1
  36.5 1.0 %project_last.1 = (f32[96,128]{1,0:T(8,128)S(1)}, bf16[128,256]{1,0:T(8,128)(2,1)S(1)}, s32[1,128]{1,0:T(1,128)S(1)}) custom-call(bf16[896,256]{1,0:T(8,128)(2,1)S(1)} %get-tuple-element.22.rows_h, bf16[896,256]{1,0:T(8,128)(2,1)S(1)} %get-tuple-element.23.rows_l, f32[64,64]{1,0:T(8,128)S(1)} %bitcast.38, f32[16,256]{1,0:T(8,128)S(1)} %get-tuple-element.24.coef_in, ...), custom_call_target="tpu_custom_call" | custom-call | tf_op jit(solution)/shard_map/project_last/pallas_call | solution.py:497
  37.4 0.4 collective-permute-start.3
  37.8 0.9 %collective-permute-done.3.other = f32[96,128]{1,0:T(8,128)S(1)} collective-permute-done((f32[96,128]{1,0:T(8,128)S(1)}, f32[96,128]{1,0:T(8,128)S(1)}, u32[]{:S(2)}, u32[]{:S(2)}) %collective-permute-start.3) | collective-permute-done | bytes 49184 | tf_op jit(solution)/shard_map/ppermute | solution.py:555
  38.7 0.1 merge.1
  38.8 3.5 %collective-permute-start.4 = (f32[80,128]{1,0:T(8,128)S(1)}, f32[80,128]{1,0:T(8,128)S(1)}, u32[]{:S(2)}, u32[]{:S(2)}) collective-permute-start(f32[80,128]{1,0:T(8,128)S(1)} %get-tuple-element.27), channel_id=1, source_target_pairs={{0,248},{4,252},{8,16},{12,20},{16,8},{20,12},{24,32},{28,36},{32,... | collective-permute-start | bytes 122888 | tf_op jit(solution)/shard_map/ppermute | solution.py:558
  42.3 0.5 put.1
  42.8 2.2 %collective-permute-done.4.second = f32[80,128]{1,0:T(8,128)S(1)} collective-permute-done((f32[80,128]{1,0:T(8,128)S(1)}, f32[80,128]{1,0:T(8,128)S(1)}, u32[]{:S(2)}, u32[]{:S(2)}) %collective-permute-start.4) | collective-permute-done | bytes 40992 | tf_op jit(solution)/shard_map/ppermute | solution.py:558
  45.0 0.4 collective-permute-done.5.first
  45.4 3.8 %back.1 = f32[448,128]{1,0:T(8,128)S(1)} custom-call(f32[864,256]{1,0:T(8,128)S(1)} %get-tuple-element.21.field, f32[96,128]{1,0:T(8,128)S(1)} %get-tuple-element.26.own, f32[96,128]{1,0:T(8,128)S(1)} %collective-permute-done.3.other, f32[80,128]{1,0:T(8,128)S(1)} %collective-permute-done.4.second, f32[80,128]{1,0:T(8,128)S(1)} %collective-permute-done.5.first, ...), custom_call_target="tpu_custom_call" | custom-call | tf_op jit(solution)/shard_map/back/pallas_call | solution.py:497
  49.2 17.6 %all_to_all.11 = f32[64,1,896]{2,1,0:T(1,128)S(1)} all-to-all(f32[64,1,896]{2,1,0:T(1,128)S(1)} %bitcast.33), channel_id=1, replica_groups=mesh['fft'=64,'band'=4] {'fft'}, dimensions={0} | all-to-all | bytes 458752 | tf_op jit(solution)/shard_map/all_to_all | solution.py:529
  66.8 1.6 %z_forward.1 = f32[1728,128]{1,0:T(8,128)} custom-call(f32[448,128]{1,0:T(8,128)S(1)} %bitcast.35, bf16[768,256]{1,0:T(8,128)(2,1)S(1)} %copy-done), custom_call_target="tpu_custom_call" | custom-call | tf_op jit(solution)/shard_map/z_forward/pallas_call | solution.py:497
  (18 shorter events, 0.0 us)
Async XLA Ops:
  0.1 0.7 copy-start.10
  0.1 0.7 copy-start.11
  0.8 5.8 %copy-start = (bf16[768,256]{1,0:T(8,128)(2,1)S(1)}, bf16[768,256]{1,0:T(8,128)(2,1)}, u32[]{:S(2)}) copy-start(bf16[768,256]{1,0:T(8,128)(2,1)} %constant.16.clone.wz.fz) | copy-start | bytes 1179652
  2.0 31.1 %copy-start.2 = (bf16[1024,512]{1,0:T(8,128)(2,1)S(1)}, bf16[1024,512]{1,0:T(8,128)(2,1)}, u32[]{:S(2)}) copy-start(bf16[1024,512]{1,0:T(8,128)(2,1)} %constant.18.clone.ix) | copy-start | bytes 3145732
  2.0 32.4 %collective-permute-start.1 = (f32[1032,128]{1,0:T(8,128)S(1)}, f32[1032,128]{1,0:T(8,128)S(1)}, u32[]{:S(2)}, u32[]{:S(2)}) collective-permute-start(f32[1032,128]{1,0:T(8,128)S(1)} %maximum_bitcast_fusion.b0), channel_id=1, source_target_pairs={{0,2},{1,3},{2,0},{3,1},{4,6},{5,7},{6,4},{7,5},{8,10},{9,11},{10,... | collective-permute-start | bytes 1585160 | tf_op jit(solution)/shard_map/ppermute | solution.py:520
  5.8 28.6 %collective-permute-start = (f32[1032,128]{1,0:T(8,128)S(1)}, f32[1032,128]{1,0:T(8,128)S(1)}, u32[]{:S(2)}, u32[]{:S(2)}) collective-permute-start(f32[1032,128]{1,0:T(8,128)S(1)} %maximum_bitcast_fusion.b0), channel_id=1, source_target_pairs={{0,3},{1,0},{2,1},{3,2},{4,7},{5,4},{6,5},{7,6},{8,11},{9,8},{10,9... | collective-permute-start | bytes 1585160 | tf_op jit(solution)/shard_map/ppermute | solution.py:520
  6.6 1.2 %copy-start.3 = (f32[1,2,3,36864]{3,1,2,0:T(2,128)S(1)}, f32[1,2,3,36864]{3,1,2,0:T(2,128)}, u32[]{:S(2)}) copy-start(f32[1,2,3,36864]{3,1,2,0:T(2,128)} %param.14) | copy-start | bytes 2654212
  7.7 25.3 %copy-start.7 = (bf16[128,384]{1,0:T(8,128)(2,1)S(1)}, bf16[128,384]{1,0:T(8,128)(2,1)}, u32[]{:S(2)}) copy-start(bf16[128,384]{1,0:T(8,128)(2,1)} %constant.21.clone.u) | copy-start | bytes 294916
  8.4 24.7 %copy-start.6 = (bf16[768,256]{1,0:T(8,128)(2,1)S(1)}, bf16[768,256]{1,0:T(8,128)(2,1)}, u32[]{:S(2)}) copy-start(bf16[768,256]{1,0:T(8,128)(2,1)} %constant.17.clone.ey) | copy-start | bytes 1179652
  8.4 28.1 %collective-permute-start.2 = (f32[1032,128]{1,0:T(8,128)S(1)}, f32[1032,128]{1,0:T(8,128)S(1)}, u32[]{:S(2)}, u32[]{:S(2)}) collective-permute-start(f32[1032,128]{1,0:T(8,128)S(1)} %maximum_bitcast_fusion.b0), channel_id=1, source_target_pairs={{0,1},{1,2},{2,3},{3,0},{4,5},{5,6},{6,7},{7,4},{8,9},{9,10},{10,1... | collective-permute-start | bytes 1585160 | tf_op jit(solution)/shard_map/ppermute | solution.py:520
  34.4 2.0 %copy-start.9 = (f32[64,8,8]{0,2,1:T(8,128)S(1)}, f32[64,8,8]{0,2,1:T(8,128)}, u32[]{:S(2)}) copy-start(f32[64,8,8]{0,2,1:T(8,128)} %param.19) | copy-start | bytes 49156
  34.4 7.9 %copy-start.4 = (f32[3,36864]{1,0:T(4,128)S(1)}, f32[3,36864]{1,0:T(4,128)}, u32[]{:S(2)}) copy-start(f32[3,36864]{1,0:T(4,128)} %param.15) | copy-start | bytes 1327108
  36.4 9.0 %copy-start.1 = (bf16[2048,256]{1,0:T(8,128)(2,1)S(1)}, bf16[2048,256]{1,0:T(8,128)(2,1)}, u32[]{:S(2)}) copy-start(bf16[2048,256]{1,0:T(8,128)(2,1)} %constant.19.clone.fx) | copy-start | bytes 3145732
  37.4 8.0 %copy-start.5 = (bf16[512,384]{1,0:T(8,128)(2,1)S(1)}, bf16[512,384]{1,0:T(8,128)(2,1)}, u32[]{:S(2)}) copy-start(bf16[512,384]{1,0:T(8,128)(2,1)} %constant.20.clone.fy) | copy-start | bytes 1179652
  37.4 1.3 %collective-permute-start.3 = (f32[96,128]{1,0:T(8,128)S(1)}, f32[96,128]{1,0:T(8,128)S(1)}, u32[]{:S(2)}, u32[]{:S(2)}) collective-permute-start(f32[96,128]{1,0:T(8,128)S(1)} %get-tuple-element.26.own), channel_id=1, source_target_pairs={{0,4},{4,0},{8,12},{12,8},{16,20},{20,16},{24,28},{28,24},{32,36},... | collective-permute-start | bytes 147464 | tf_op jit(solution)/shard_map/ppermute | solution.py:555
  38.8 6.2 %collective-permute-start.4 = (f32[80,128]{1,0:T(8,128)S(1)}, f32[80,128]{1,0:T(8,128)S(1)}, u32[]{:S(2)}, u32[]{:S(2)}) collective-permute-start(f32[80,128]{1,0:T(8,128)S(1)} %get-tuple-element.27), channel_id=1, source_target_pairs={{0,248},{4,252},{8,16},{12,20},{16,8},{20,12},{24,32},{28,36},{32,... | collective-permute-start | bytes 122888 | tf_op jit(solution)/shard_map/ppermute | solution.py:558
  42.3 3.1 %collective-permute-start.5 = (f32[80,128]{1,0:T(8,128)S(1)}, f32[80,128]{1,0:T(8,128)S(1)}, u32[]{:S(2)}, u32[]{:S(2)}) collective-permute-start(f32[80,128]{1,0:T(8,128)S(1)} %get-tuple-element.28), channel_id=1, source_target_pairs={{0,8},{4,12},{8,0},{12,4},{16,24},{20,28},{24,16},{28,20},{32,40},... | collective-permute-start | bytes 122888 | tf_op jit(solution)/shard_map/ppermute | solution.py:557
  42.3 3.1 %copy-start.8 = (bf16[384,128]{1,0:T(8,128)(2,1)S(1)}, bf16[384,128]{1,0:T(8,128)(2,1)}, u32[]{:S(2)}) copy-start(bf16[384,128]{1,0:T(8,128)(2,1)} %constant.22.clone.ut) | copy-start | bytes 294916

commit v12 on v11

--- a/solution.py
+++ b/solution.py
@@ -523,7 +523,7 @@
     own = jnp.concatenate([beta, ids.astype(F32)[None]], 0).reshape(1032, 128)
     (send,) = call(kernel_z_inverse, "z_inverse", [(448, 128)], (psi, t["wz"]))
     own_later, send = lax.optimization_barrier((own, send))
-    betas = [own, from_band(own, 3), from_band(own, 2), from_band(own_later, 1)]
+    betas = [own, from_band(own, 2), from_band(own, 3), from_band(own_later, 1)]
 
     def exchange(x):
         x = lax.all_to_all(x.reshape(64, 1, 896), "fft", 0, 0, tiled=True)

time: 68.7 us -> 69 us (level)
    ppermute x1, starting transfers between devices: 3.49 us -> 4.42 us  [body(): lax.ppermute(second, 'fft', [(i, ((i + 2) % 64 ^ 2) - 2 & 63) for i in ra...]
    ppermute x1, waiting for transfers between devices: 2.18 us -> 1.24 us  [body(): lax.ppermute(second, 'fft', [(i, ((i + 2) % 64 ^ 2) - 2 & 63) for i in ra...]
where the time goes in v12:
time: 69 us; the launch traced here: 68.8 us
  blocking collectives  41.8 us (61%)
  Pallas kernels  10.9 us (16%)
  starting transfers between devices  9.59 us (14%)
  waiting for transfers between devices  3.24 us (5%)
  local copies, waits for them, and re-layouts  1.97 us (3%)
  other arithmetic  1.2 us (2%)
    all_to_all x2, blocking collectives, exchange(): x = lax.all_to_all(x.reshape(64, 1, 896), 'fft', 0, 0, tiled=True)  41.8 us
    pallas_call x8, Pallas kernels, call(): pl.pallas_call(kernel, name=name, out_shape=shapes, in_specs=specs, out_s...  10.9 us
    ppermute x3, starting transfers between devices, from_band(): return lax.ppermute(x, 'band', [(i, (i + k) % 4) for i in range(4)])  4.76 us
    ppermute x1, starting transfers between devices, body(): lax.ppermute(second, 'fft', [(i, ((i + 2) % 64 ^ 2) - 2 & 63) for i in ra...  4.42 us
    unnamed x24, local copies, waits for them, and re-layouts  1.89 us
  transfers between devices with their start and end apart: 6, of which 3 were waited for; matrix products, arithmetic and copies ran while one was open for 0% of the time, Pallas kernels for 6%

profile of v12, /device:TPU:1, one launch (start us, length us, event | category | flops | bytes accessed | tf_op | source)
XLA Modules:
  0.0 68.8 jit_solution(5490055523378726816)
XLA Ops:
  0.0 0.1 pad.4.clone
  0.1 0.7 copy-done.10
  0.7 0.0 copy-done.11
  0.8 0.1 add_convert_fusion
  0.8 1.1 %maximum_bitcast_fusion.b0 = f32[1032,128]{1,0:T(8,128)S(1)} fusion(f32[1,8,128]{2,1,0:T(8,128)S(1)} %add_convert_fusion, f32[128,8,128]{2,1,0:T(8,128)} %param.16), kind=kLoop, calls=%fused_computation | loop fusion | flops 132096 | bytes 1056768 | tf_op jit(solution)/shard_map/reshape | solution.py:523
  2.0 0.0 copy-start.2
  2.0 3.6 %collective-permute-start.1 = (f32[1032,128]{1,0:T(8,128)S(1)}, f32[1032,128]{1,0:T(8,128)S(1)}, u32[]{:S(2)}, u32[]{:S(2)}) collective-permute-start(f32[1032,128]{1,0:T(8,128)S(1)} %maximum_bitcast_fusion.b0), channel_id=1, source_target_pairs={{0,3},{1,0},{2,1},{3,2},{4,7},{5,4},{6,5},{7,6},{8,11},{9,8},{10,9... | collective-permute-start | bytes 1585160 | tf_op jit(solution)/shard_map/ppermute | solution.py:520
  5.6 0.3 collective-permute-start
  6.0 1.2 %copy-done.3 = f32[1,2,3,36864]{3,1,2,0:T(2,128)S(1)} copy-done((f32[1,2,3,36864]{3,1,2,0:T(2,128)S(1)}, f32[1,2,3,36864]{3,1,2,0:T(2,128)}, u32[]{:S(2)}) %copy-start.3) | copy-done | bytes 884760
  7.1 0.6 z_inverse.1
  7.8 0.0 copy-start.6
  7.8 0.8 %collective-permute-start.2 = (f32[1032,128]{1,0:T(8,128)S(1)}, f32[1032,128]{1,0:T(8,128)S(1)}, u32[]{:S(2)}, u32[]{:S(2)}) collective-permute-start(f32[1032,128]{1,0:T(8,128)S(1)} %maximum_bitcast_fusion.b0), channel_id=1, source_target_pairs={{0,1},{1,2},{2,3},{3,0},{4,5},{5,6},{6,7},{7,4},{8,9},{9,10},{10,1... | collective-permute-start | bytes 1585160 | tf_op jit(solution)/shard_map/ppermute | solution.py:520
  8.5 23.9 %all_to_all.10 = f32[64,1,896]{2,1,0:T(1,128)S(1)} all-to-all(f32[64,1,896]{2,1,0:T(1,128)S(1)} %bitcast.34), channel_id=1, replica_groups=mesh['fft'=64,'band'=4] {'fft'}, dimensions={0} | all-to-all | bytes 458752 | tf_op jit(solution)/shard_map/all_to_all | solution.py:529
  32.5 1.3 %field.1 = (f32[864,256]{1,0:T(8,128)S(1)}, bf16[896,256]{1,0:T(8,128)(2,1)S(1)}, bf16[896,256]{1,0:T(8,128)(2,1)S(1)}) custom-call(f32[448,128]{1,0:T(8,128)S(1)} %bitcast.32, bf16[768,256]{1,0:T(8,128)(2,1)S(1)} %copy-done.6, bf16[1024,512]{1,0:T(8,128)(2,1)S(1)} %copy-done.2, bf16[128,384]{1,0:T(8,128)(2,1)S(1)} %copy-done.7), custom_call_target="tpu_custom_call" | custom-call | tf_op jit(solution)/shard_map/field/pallas_call | solution.py:497
  33.8 0.0 collective-permute-done.1.b2
  33.8 0.0 collective-permute-done.b1
  33.8 0.0 copy-start.9
  33.8 0.0 copy-start.4
  33.8 2.0 %project.1 = (f32[16,256]{1,0:T(8,128)S(1)}, bf16[384,256]{1,0:T(8,128)(2,1)S(1)}, s32[1,384]{1,0:T(1,128)S(1)}) custom-call(bf16[896,256]{1,0:T(8,128)(2,1)S(1)} %get-tuple-element.22.rows_h, bf16[896,256]{1,0:T(8,128)(2,1)S(1)} %get-tuple-element.23.rows_l, f32[1032,128]{1,0:T(8,128)S(1)} %maximum_bitcast_fusion.b0, ...), custom_call_target="tpu_custom_call" | custom-call | tf_op jit(solution)/shard_map/project/pallas_call | solution.py:497
  35.8 0.0 copy-start.1
  35.8 1.0 %project_last.1 = (f32[96,128]{1,0:T(8,128)S(1)}, bf16[128,256]{1,0:T(8,128)(2,1)S(1)}, s32[1,128]{1,0:T(1,128)S(1)}) custom-call(bf16[896,256]{1,0:T(8,128)(2,1)S(1)} %get-tuple-element.22.rows_h, bf16[896,256]{1,0:T(8,128)(2,1)S(1)} %get-tuple-element.23.rows_l, f32[64,64]{1,0:T(8,128)S(1)} %bitcast.38, f32[16,256]{1,0:T(8,128)S(1)} %get-tuple-element.24.coef_in, ...), custom_call_target="tpu_custom_call" | custom-call | tf_op jit(solution)/shard_map/project_last/pallas_call | solution.py:497
  36.8 0.4 collective-permute-start.3
  37.2 0.9 %collective-permute-done.3.other = f32[96,128]{1,0:T(8,128)S(1)} collective-permute-done((f32[96,128]{1,0:T(8,128)S(1)}, f32[96,128]{1,0:T(8,128)S(1)}, u32[]{:S(2)}, u32[]{:S(2)}) %collective-permute-start.3) | collective-permute-done | bytes 49184 | tf_op jit(solution)/shard_map/ppermute | solution.py:555
  38.1 0.1 merge.1
  38.2 4.4 %collective-permute-start.4 = (f32[80,128]{1,0:T(8,128)S(1)}, f32[80,128]{1,0:T(8,128)S(1)}, u32[]{:S(2)}, u32[]{:S(2)}) collective-permute-start(f32[80,128]{1,0:T(8,128)S(1)} %get-tuple-element.27), channel_id=1, source_target_pairs={{0,248},{4,252},{8,16},{12,20},{16,8},{20,12},{24,32},{28,36},{32,... | collective-permute-start | bytes 122888 | tf_op jit(solution)/shard_map/ppermute | solution.py:558
  42.6 0.0 collective-permute-start.5
  42.6 0.5 put.1
  43.1 1.2 %collective-permute-done.4.second = f32[80,128]{1,0:T(8,128)S(1)} collective-permute-done((f32[80,128]{1,0:T(8,128)S(1)}, f32[80,128]{1,0:T(8,128)S(1)}, u32[]{:S(2)}, u32[]{:S(2)}) %collective-permute-start.4) | collective-permute-done | bytes 40992 | tf_op jit(solution)/shard_map/ppermute | solution.py:558
  44.4 1.1 %collective-permute-done.5.first = f32[80,128]{1,0:T(8,128)S(1)} collective-permute-done((f32[80,128]{1,0:T(8,128)S(1)}, f32[80,128]{1,0:T(8,128)S(1)}, u32[]{:S(2)}, u32[]{:S(2)}) %collective-permute-start.5) | collective-permute-done | bytes 40992 | tf_op jit(solution)/shard_map/ppermute | solution.py:557
  45.5 3.8 %back.1 = f32[448,128]{1,0:T(8,128)S(1)} custom-call(f32[864,256]{1,0:T(8,128)S(1)} %get-tuple-element.21.field, f32[96,128]{1,0:T(8,128)S(1)} %get-tuple-element.26.own, f32[96,128]{1,0:T(8,128)S(1)} %collective-permute-done.3.other, f32[80,128]{1,0:T(8,128)S(1)} %collective-permute-done.4.second, f32[80,128]{1,0:T(8,128)S(1)} %collective-permute-done.5.first, ...), custom_call_target="tpu_custom_call" | custom-call | tf_op jit(solution)/shard_map/back/pallas_call | solution.py:497
  49.3 17.9 %all_to_all.11 = f32[64,1,896]{2,1,0:T(1,128)S(1)} all-to-all(f32[64,1,896]{2,1,0:T(1,128)S(1)} %bitcast.33), channel_id=1, replica_groups=mesh['fft'=64,'band'=4] {'fft'}, dimensions={0} | all-to-all | bytes 458752 | tf_op jit(solution)/shard_map/all_to_all | solution.py:529
  67.1 1.6 %z_forward.1 = f32[1728,128]{1,0:T(8,128)} custom-call(f32[448,128]{1,0:T(8,128)S(1)} %bitcast.35, bf16[768,256]{1,0:T(8,128)(2,1)S(1)} %copy-done), custom_call_target="tpu_custom_call" | custom-call | tf_op jit(solution)/shard_map/z_forward/pallas_call | solution.py:497
  (18 shorter events, 0.0 us)
Async XLA Ops:
  0.1 0.7 copy-start.10
  0.1 0.7 copy-start.11
  0.8 5.1 %copy-start = (bf16[768,256]{1,0:T(8,128)(2,1)S(1)}, bf16[768,256]{1,0:T(8,128)(2,1)}, u32[]{:S(2)}) copy-start(bf16[768,256]{1,0:T(8,128)(2,1)} %constant.16.clone.wz.fz) | copy-start | bytes 1179652
  2.0 30.5 %copy-start.2 = (bf16[1024,512]{1,0:T(8,128)(2,1)S(1)}, bf16[1024,512]{1,0:T(8,128)(2,1)}, u32[]{:S(2)}) copy-start(bf16[1024,512]{1,0:T(8,128)(2,1)} %constant.18.clone.ix) | copy-start | bytes 3145732
  2.0 31.8 %collective-permute-start.1 = (f32[1032,128]{1,0:T(8,128)S(1)}, f32[1032,128]{1,0:T(8,128)S(1)}, u32[]{:S(2)}, u32[]{:S(2)}) collective-permute-start(f32[1032,128]{1,0:T(8,128)S(1)} %maximum_bitcast_fusion.b0), channel_id=1, source_target_pairs={{0,3},{1,0},{2,1},{3,2},{4,7},{5,4},{6,5},{7,6},{8,11},{9,8},{10,9... | collective-permute-start | bytes 1585160 | tf_op jit(solution)/shard_map/ppermute | solution.py:520
  5.6 28.2 %collective-permute-start = (f32[1032,128]{1,0:T(8,128)S(1)}, f32[1032,128]{1,0:T(8,128)S(1)}, u32[]{:S(2)}, u32[]{:S(2)}) collective-permute-start(f32[1032,128]{1,0:T(8,128)S(1)} %maximum_bitcast_fusion.b0), channel_id=1, source_target_pairs={{0,2},{1,3},{2,0},{3,1},{4,6},{5,7},{6,4},{7,5},{8,10},{9,11},{10,... | collective-permute-start | bytes 1585160 | tf_op jit(solution)/shard_map/ppermute | solution.py:520
  6.0 1.2 %copy-start.3 = (f32[1,2,3,36864]{3,1,2,0:T(2,128)S(1)}, f32[1,2,3,36864]{3,1,2,0:T(2,128)}, u32[]{:S(2)}) copy-start(f32[1,2,3,36864]{3,1,2,0:T(2,128)} %param.14) | copy-start | bytes 2654212
  7.1 25.3 %copy-start.7 = (bf16[128,384]{1,0:T(8,128)(2,1)S(1)}, bf16[128,384]{1,0:T(8,128)(2,1)}, u32[]{:S(2)}) copy-start(bf16[128,384]{1,0:T(8,128)(2,1)} %constant.21.clone.u) | copy-start | bytes 294916
  7.8 24.7 %copy-start.6 = (bf16[768,256]{1,0:T(8,128)(2,1)S(1)}, bf16[768,256]{1,0:T(8,128)(2,1)}, u32[]{:S(2)}) copy-start(bf16[768,256]{1,0:T(8,128)(2,1)} %constant.17.clone.ey) | copy-start | bytes 1179652
  7.8 28.1 %collective-permute-start.2 = (f32[1032,128]{1,0:T(8,128)S(1)}, f32[1032,128]{1,0:T(8,128)S(1)}, u32[]{:S(2)}, u32[]{:S(2)}) collective-permute-start(f32[1032,128]{1,0:T(8,128)S(1)} %maximum_bitcast_fusion.b0), channel_id=1, source_target_pairs={{0,1},{1,2},{2,3},{3,0},{4,5},{5,6},{6,7},{7,4},{8,9},{9,10},{10,1... | collective-permute-start | bytes 1585160 | tf_op jit(solution)/shard_map/ppermute | solution.py:520
  33.8 2.0 %copy-start.9 = (f32[64,8,8]{0,2,1:T(8,128)S(1)}, f32[64,8,8]{0,2,1:T(8,128)}, u32[]{:S(2)}) copy-start(f32[64,8,8]{0,2,1:T(8,128)} %param.19) | copy-start | bytes 49156
  33.8 8.8 %copy-start.4 = (f32[3,36864]{1,0:T(4,128)S(1)}, f32[3,36864]{1,0:T(4,128)}, u32[]{:S(2)}) copy-start(f32[3,36864]{1,0:T(4,128)} %param.15) | copy-start | bytes 1327108
  35.8 9.7 %copy-start.1 = (bf16[2048,256]{1,0:T(8,128)(2,1)S(1)}, bf16[2048,256]{1,0:T(8,128)(2,1)}, u32[]{:S(2)}) copy-start(bf16[2048,256]{1,0:T(8,128)(2,1)} %constant.19.clone.fx) | copy-start | bytes 3145732
  36.8 8.7 %copy-start.5 = (bf16[512,384]{1,0:T(8,128)(2,1)S(1)}, bf16[512,384]{1,0:T(8,128)(2,1)}, u32[]{:S(2)}) copy-start(bf16[512,384]{1,0:T(8,128)(2,1)} %constant.20.clone.fy) | copy-start | bytes 1179652
  36.8 1.3 %collective-permute-start.3 = (f32[96,128]{1,0:T(8,128)S(1)}, f32[96,128]{1,0:T(8,128)S(1)}, u32[]{:S(2)}, u32[]{:S(2)}) collective-permute-start(f32[96,128]{1,0:T(8,128)S(1)} %get-tuple-element.26.own), channel_id=1, source_target_pairs={{0,4},{4,0},{8,12},{12,8},{16,20},{20,16},{24,28},{28,24},{32,36},... | collective-permute-start | bytes 147464 | tf_op jit(solution)/shard_map/ppermute | solution.py:555
  38.2 6.2 %collective-permute-start.4 = (f32[80,128]{1,0:T(8,128)S(1)}, f32[80,128]{1,0:T(8,128)S(1)}, u32[]{:S(2)}, u32[]{:S(2)}) collective-permute-start(f32[80,128]{1,0:T(8,128)S(1)} %get-tuple-element.27), channel_id=1, source_target_pairs={{0,248},{4,252},{8,16},{12,20},{16,8},{20,12},{24,32},{28,36},{32,... | collective-permute-start | bytes 122888 | tf_op jit(solution)/shard_map/ppermute | solution.py:558
  42.6 2.9 %collective-permute-start.5 = (f32[80,128]{1,0:T(8,128)S(1)}, f32[80,128]{1,0:T(8,128)S(1)}, u32[]{:S(2)}, u32[]{:S(2)}) collective-permute-start(f32[80,128]{1,0:T(8,128)S(1)} %get-tuple-element.28), channel_id=1, source_target_pairs={{0,8},{4,12},{8,0},{12,4},{16,24},{20,28},{24,16},{28,20},{32,40},... | collective-permute-start | bytes 122888 | tf_op jit(solution)/shard_map/ppermute | solution.py:557
  42.6 2.9 %copy-start.8 = (bf16[384,128]{1,0:T(8,128)(2,1)S(1)}, bf16[384,128]{1,0:T(8,128)(2,1)}, u32[]{:S(2)}) copy-start(bf16[384,128]{1,0:T(8,128)(2,1)} %constant.22.clone.ut) | copy-start | bytes 294916

commit v13 on v12

--- a/solution.py
+++ b/solution.py
@@ -522,8 +522,7 @@
     ids = jnp.concatenate([blk_slot[None], blk_tile[None], jnp.zeros((6, 128), jnp.int32)], 0)
     own = jnp.concatenate([beta, ids.astype(F32)[None]], 0).reshape(1032, 128)
     (send,) = call(kernel_z_inverse, "z_inverse", [(448, 128)], (psi, t["wz"]))
-    own_later, send = lax.optimization_barrier((own, send))
-    betas = [own, from_band(own, 2), from_band(own, 3), from_band(own_later, 1)]
+    betas = [own, from_band(own, 2), from_band(own, 3), from_band(own, 1)]
 
     def exchange(x):
         x = lax.all_to_all(x.reshape(64, 1, 896), "fft", 0, 0, tiled=True)

time: 69 us -> 69 us (level)
  no operation moved by 1% of the time
where the time goes in v13:
time: 69 us; the launch traced here: 68.8 us
  blocking collectives  41.9 us (61%)
  Pallas kernels  10.9 us (16%)
  starting transfers between devices  9.45 us (14%)
  waiting for transfers between devices  3.29 us (5%)
  local copies, waits for them, and re-layouts  1.97 us (3%)
  other arithmetic  1.2 us (2%)
    all_to_all x2, blocking collectives, exchange(): x = lax.all_to_all(x.reshape(64, 1, 896), 'fft', 0, 0, tiled=True)  41.9 us
    pallas_call x8, Pallas kernels, call(): pl.pallas_call(kernel, name=name, out_shape=shapes, in_specs=specs, out_s...  10.9 us
    ppermute x3, starting transfers between devices, from_band(): return lax.ppermute(x, 'band', [(i, (i + k) % 4) for i in range(4)])  4.68 us
    ppermute x1, starting transfers between devices, body(): lax.ppermute(second, 'fft', [(i, ((i + 2) % 64 ^ 2) - 2 & 63) for i in ra...  4.36 us
    unnamed x24, local copies, waits for them, and re-layouts  1.89 us
  transfers between devices with their start and end apart: 6, of which 3 were waited for; matrix products, arithmetic and copies ran while one was open for 0% of the time, Pallas kernels for 6%

profile of v13, /device:TPU:1, one launch (start us, length us, event | category | flops | bytes accessed | tf_op | source)
XLA Modules:
  0.0 68.8 jit_solution(4891073123479083007)
XLA Ops:
  0.0 0.1 pad.4.clone
  0.1 0.7 copy-done.10
  0.7 0.0 copy-done.11
  0.8 0.1 add_convert_fusion
  0.8 1.1 %maximum_bitcast_fusion.b0 = f32[1032,128]{1,0:T(8,128)S(1)} fusion(f32[1,8,128]{2,1,0:T(8,128)S(1)} %add_convert_fusion, f32[128,8,128]{2,1,0:T(8,128)} %param.16), kind=kLoop, calls=%fused_computation | loop fusion | flops 132096 | bytes 1056768 | tf_op jit(solution)/shard_map/reshape | solution.py:523
  2.0 0.0 copy-start.2
  2.0 3.6 %collective-permute-start.1 = (f32[1032,128]{1,0:T(8,128)S(1)}, f32[1032,128]{1,0:T(8,128)S(1)}, u32[]{:S(2)}, u32[]{:S(2)}) collective-permute-start(f32[1032,128]{1,0:T(8,128)S(1)} %maximum_bitcast_fusion.b0), channel_id=1, source_target_pairs={{0,3},{1,0},{2,1},{3,2},{4,7},{5,4},{6,5},{7,6},{8,11},{9,8},{10,9... | collective-permute-start | bytes 1585160 | tf_op jit(solution)/shard_map/ppermute | solution.py:520
  5.6 0.3 collective-permute-start
  6.0 0.7 %collective-permute-start.2 = (f32[1032,128]{1,0:T(8,128)S(1)}, f32[1032,128]{1,0:T(8,128)S(1)}, u32[]{:S(2)}, u32[]{:S(2)}) collective-permute-start(f32[1032,128]{1,0:T(8,128)S(1)} %maximum_bitcast_fusion.b0), channel_id=1, source_target_pairs={{0,1},{1,2},{2,3},{3,0},{4,5},{5,6},{6,7},{7,4},{8,9},{9,10},{10,1... | collective-permute-start | bytes 1585160 | tf_op jit(solution)/shard_map/ppermute | solution.py:520
  6.7 1.2 %copy-done.3 = f32[1,2,3,36864]{3,1,2,0:T(2,128)S(1)} copy-done((f32[1,2,3,36864]{3,1,2,0:T(2,128)S(1)}, f32[1,2,3,36864]{3,1,2,0:T(2,128)}, u32[]{:S(2)}) %copy-start.3) | copy-done | bytes 884760
  7.8 0.6 z_inverse.1
  8.4 0.0 copy-start.6
  8.5 24.1 %all_to_all.10 = f32[64,1,896]{2,1,0:T(1,128)S(1)} all-to-all(f32[64,1,896]{2,1,0:T(1,128)S(1)} %bitcast.35), channel_id=1, replica_groups=mesh['fft'=64,'band'=4] {'fft'}, dimensions={0} | all-to-all | bytes 458752 | tf_op jit(solution)/shard_map/all_to_all | solution.py:528
  32.5 1.3 %field.1 = (f32[864,256]{1,0:T(8,128)S(1)}, bf16[896,256]{1,0:T(8,128)(2,1)S(1)}, bf16[896,256]{1,0:T(8,128)(2,1)S(1)}) custom-call(f32[448,128]{1,0:T(8,128)S(1)} %bitcast.32, bf16[768,256]{1,0:T(8,128)(2,1)S(1)} %copy-done.6, bf16[1024,512]{1,0:T(8,128)(2,1)S(1)} %copy-done.2, bf16[128,384]{1,0:T(8,128)(2,1)S(1)} %copy-done.7), custom_call_target="tpu_custom_call" | custom-call | tf_op jit(solution)/shard_map/field/pallas_call | solution.py:497
  33.8 0.0 collective-permute-done.1.b2
  33.9 0.0 collective-permute-done.b1
  33.9 0.0 copy-start.9
  33.9 0.0 copy-start.4
  33.9 2.0 %project.1 = (f32[16,256]{1,0:T(8,128)S(1)}, bf16[384,256]{1,0:T(8,128)(2,1)S(1)}, s32[1,384]{1,0:T(1,128)S(1)}) custom-call(bf16[896,256]{1,0:T(8,128)(2,1)S(1)} %get-tuple-element.19.rows_h, bf16[896,256]{1,0:T(8,128)(2,1)S(1)} %get-tuple-element.20.rows_l, f32[1032,128]{1,0:T(8,128)S(1)} %maximum_bitcast_fusion.b0, ...), custom_call_target="tpu_custom_call" | custom-call | tf_op jit(solution)/shard_map/project/pallas_call | solution.py:497
  35.9 0.0 copy-start.1
  35.9 1.0 %project_last.1 = (f32[96,128]{1,0:T(8,128)S(1)}, bf16[128,256]{1,0:T(8,128)(2,1)S(1)}, s32[1,128]{1,0:T(1,128)S(1)}) custom-call(bf16[896,256]{1,0:T(8,128)(2,1)S(1)} %get-tuple-element.19.rows_h, bf16[896,256]{1,0:T(8,128)(2,1)S(1)} %get-tuple-element.20.rows_l, f32[64,64]{1,0:T(8,128)S(1)} %bitcast.38, f32[16,256]{1,0:T(8,128)S(1)} %get-tuple-element.21.coef_in, ...), custom_call_target="tpu_custom_call" | custom-call | tf_op jit(solution)/shard_map/project_last/pallas_call | solution.py:497
  36.9 0.4 collective-permute-start.3
  37.3 0.9 %collective-permute-done.3.other = f32[96,128]{1,0:T(8,128)S(1)} collective-permute-done((f32[96,128]{1,0:T(8,128)S(1)}, f32[96,128]{1,0:T(8,128)S(1)}, u32[]{:S(2)}, u32[]{:S(2)}) %collective-permute-start.3) | collective-permute-done | bytes 49184 | tf_op jit(solution)/shard_map/ppermute | solution.py:554
  38.2 0.1 merge.1
  38.2 4.4 %collective-permute-start.4 = (f32[80,128]{1,0:T(8,128)S(1)}, f32[80,128]{1,0:T(8,128)S(1)}, u32[]{:S(2)}, u32[]{:S(2)}) collective-permute-start(f32[80,128]{1,0:T(8,128)S(1)} %get-tuple-element.23), channel_id=1, source_target_pairs={{0,248},{4,252},{8,16},{12,20},{16,8},{20,12},{24,32},{28,36},{32,... | collective-permute-start | bytes 122888 | tf_op jit(solution)/shard_map/ppermute | solution.py:557
  42.6 0.0 collective-permute-start.5
  42.6 0.5 put.1
  43.1 1.3 %collective-permute-done.4.second = f32[80,128]{1,0:T(8,128)S(1)} collective-permute-done((f32[80,128]{1,0:T(8,128)S(1)}, f32[80,128]{1,0:T(8,128)S(1)}, u32[]{:S(2)}, u32[]{:S(2)}) %collective-permute-start.4) | collective-permute-done | bytes 40992 | tf_op jit(solution)/shard_map/ppermute | solution.py:557
  44.4 1.1 %collective-permute-done.5.first = f32[80,128]{1,0:T(8,128)S(1)} collective-permute-done((f32[80,128]{1,0:T(8,128)S(1)}, f32[80,128]{1,0:T(8,128)S(1)}, u32[]{:S(2)}, u32[]{:S(2)}) %collective-permute-start.5) | collective-permute-done | bytes 40992 | tf_op jit(solution)/shard_map/ppermute | solution.py:556
  45.6 3.8 %back.1 = f32[448,128]{1,0:T(8,128)S(1)} custom-call(f32[864,256]{1,0:T(8,128)S(1)} %get-tuple-element.18.field, f32[96,128]{1,0:T(8,128)S(1)} %get-tuple-element.22.own, f32[96,128]{1,0:T(8,128)S(1)} %collective-permute-done.3.other, f32[80,128]{1,0:T(8,128)S(1)} %collective-permute-done.4.second, f32[80,128]{1,0:T(8,128)S(1)} %collective-permute-done.5.first, ...), custom_call_target="tpu_custom_call" | custom-call | tf_op jit(solution)/shard_map/back/pallas_call | solution.py:497
  49.3 17.8 %all_to_all.11 = f32[64,1,896]{2,1,0:T(1,128)S(1)} all-to-all(f32[64,1,896]{2,1,0:T(1,128)S(1)} %bitcast.33), channel_id=1, replica_groups=mesh['fft'=64,'band'=4] {'fft'}, dimensions={0} | all-to-all | bytes 458752 | tf_op jit(solution)/shard_map/all_to_all | solution.py:528
  67.1 1.6 %z_forward.1 = f32[1728,128]{1,0:T(8,128)} custom-call(f32[448,128]{1,0:T(8,128)S(1)} %bitcast.34, bf16[768,256]{1,0:T(8,128)(2,1)S(1)} %copy-done), custom_call_target="tpu_custom_call" | custom-call | tf_op jit(solution)/shard_map/z_forward/pallas_call | solution.py:497
  (18 shorter events, 0.0 us)
Async XLA Ops:
  0.1 0.7 copy-start.10
  0.1 0.7 copy-start.11
  0.8 5.8 %copy-start = (bf16[768,256]{1,0:T(8,128)(2,1)S(1)}, bf16[768,256]{1,0:T(8,128)(2,1)}, u32[]{:S(2)}) copy-start(bf16[768,256]{1,0:T(8,128)(2,1)} %constant.16.clone.wz.fz) | copy-start | bytes 1179652
  2.0 30.6 %copy-start.2 = (bf16[1024,512]{1,0:T(8,128)(2,1)S(1)}, bf16[1024,512]{1,0:T(8,128)(2,1)}, u32[]{:S(2)}) copy-start(bf16[1024,512]{1,0:T(8,128)(2,1)} %constant.18.clone.ix) | copy-start | bytes 3145732
  2.0 31.9 %collective-permute-start.1 = (f32[1032,128]{1,0:T(8,128)S(1)}, f32[1032,128]{1,0:T(8,128)S(1)}, u32[]{:S(2)}, u32[]{:S(2)}) collective-permute-start(f32[1032,128]{1,0:T(8,128)S(1)} %maximum_bitcast_fusion.b0), channel_id=1, source_target_pairs={{0,3},{1,0},{2,1},{3,2},{4,7},{5,4},{6,5},{7,6},{8,11},{9,8},{10,9... | collective-permute-start | bytes 1585160 | tf_op jit(solution)/shard_map/ppermute | solution.py:520
  5.6 28.2 %collective-permute-start = (f32[1032,128]{1,0:T(8,128)S(1)}, f32[1032,128]{1,0:T(8,128)S(1)}, u32[]{:S(2)}, u32[]{:S(2)}) collective-permute-start(f32[1032,128]{1,0:T(8,128)S(1)} %maximum_bitcast_fusion.b0), channel_id=1, source_target_pairs={{0,2},{1,3},{2,0},{3,1},{4,6},{5,7},{6,4},{7,5},{8,10},{9,11},{10,... | collective-permute-start | bytes 1585160 | tf_op jit(solution)/shard_map/ppermute | solution.py:520
  6.0 29.9 %collective-permute-start.2 = (f32[1032,128]{1,0:T(8,128)S(1)}, f32[1032,128]{1,0:T(8,128)S(1)}, u32[]{:S(2)}, u32[]{:S(2)}) collective-permute-start(f32[1032,128]{1,0:T(8,128)S(1)} %maximum_bitcast_fusion.b0), channel_id=1, source_target_pairs={{0,1},{1,2},{2,3},{3,0},{4,5},{5,6},{6,7},{7,4},{8,9},{9,10},{10,1... | collective-permute-start | bytes 1585160 | tf_op jit(solution)/shard_map/ppermute | solution.py:520
  6.7 1.2 %copy-start.3 = (f32[1,2,3,36864]{3,1,2,0:T(2,128)S(1)}, f32[1,2,3,36864]{3,1,2,0:T(2,128)}, u32[]{:S(2)}) copy-start(f32[1,2,3,36864]{3,1,2,0:T(2,128)} %param.14) | copy-start | bytes 2654212
  7.8 24.7 %copy-start.7 = (bf16[128,384]{1,0:T(8,128)(2,1)S(1)}, bf16[128,384]{1,0:T(8,128)(2,1)}, u32[]{:S(2)}) copy-start(bf16[128,384]{1,0:T(8,128)(2,1)} %constant.21.clone.u) | copy-start | bytes 294916
  8.4 24.1 %copy-start.6 = (bf16[768,256]{1,0:T(8,128)(2,1)S(1)}, bf16[768,256]{1,0:T(8,128)(2,1)}, u32[]{:S(2)}) copy-start(bf16[768,256]{1,0:T(8,128)(2,1)} %constant.17.clone.ey) | copy-start | bytes 1179652
  33.9 2.0 %copy-start.9 = (f32[64,8,8]{0,2,1:T(8,128)S(1)}, f32[64,8,8]{0,2,1:T(8,128)}, u32[]{:S(2)}) copy-start(f32[64,8,8]{0,2,1:T(8,128)} %param.19) | copy-start | bytes 49156
  33.9 8.7 %copy-start.4 = (f32[3,36864]{1,0:T(4,128)S(1)}, f32[3,36864]{1,0:T(4,128)}, u32[]{:S(2)}) copy-start(f32[3,36864]{1,0:T(4,128)} %param.15) | copy-start | bytes 1327108
  35.9 9.7 %copy-start.1 = (bf16[2048,256]{1,0:T(8,128)(2,1)S(1)}, bf16[2048,256]{1,0:T(8,128)(2,1)}, u32[]{:S(2)}) copy-start(bf16[2048,256]{1,0:T(8,128)(2,1)} %constant.19.clone.fx) | copy-start | bytes 3145732
  36.9 8.7 %copy-start.5 = (bf16[512,384]{1,0:T(8,128)(2,1)S(1)}, bf16[512,384]{1,0:T(8,128)(2,1)}, u32[]{:S(2)}) copy-start(bf16[512,384]{1,0:T(8,128)(2,1)} %constant.20.clone.fy) | copy-start | bytes 1179652
  36.9 1.3 %collective-permute-start.3 = (f32[96,128]{1,0:T(8,128)S(1)}, f32[96,128]{1,0:T(8,128)S(1)}, u32[]{:S(2)}, u32[]{:S(2)}) collective-permute-start(f32[96,128]{1,0:T(8,128)S(1)} %get-tuple-element.22.own), channel_id=1, source_target_pairs={{0,4},{4,0},{8,12},{12,8},{16,20},{20,16},{24,28},{28,24},{32,36},... | collective-permute-start | bytes 147464 | tf_op jit(solution)/shard_map/ppermute | solution.py:554
  38.2 6.2 %collective-permute-start.4 = (f32[80,128]{1,0:T(8,128)S(1)}, f32[80,128]{1,0:T(8,128)S(1)}, u32[]{:S(2)}, u32[]{:S(2)}) collective-permute-start(f32[80,128]{1,0:T(8,128)S(1)} %get-tuple-element.23), channel_id=1, source_target_pairs={{0,248},{4,252},{8,16},{12,20},{16,8},{20,12},{24,32},{28,36},{32,... | collective-permute-start | bytes 122888 | tf_op jit(solution)/shard_map/ppermute | solution.py:557
  42.6 2.9 %collective-permute-start.5 = (f32[80,128]{1,0:T(8,128)S(1)}, f32[80,128]{1,0:T(8,128)S(1)}, u32[]{:S(2)}, u32[]{:S(2)}) collective-permute-start(f32[80,128]{1,0:T(8,128)S(1)} %get-tuple-element.24), channel_id=1, source_target_pairs={{0,8},{4,12},{8,0},{12,4},{16,24},{20,28},{24,16},{28,20},{32,40},... | collective-permute-start | bytes 122888 | tf_op jit(solution)/shard_map/ppermute | solution.py:556
  42.6 2.9 %copy-start.8 = (bf16[384,128]{1,0:T(8,128)(2,1)S(1)}, bf16[384,128]{1,0:T(8,128)(2,1)}, u32[]{:S(2)}) copy-start(bf16[384,128]{1,0:T(8,128)(2,1)} %constant.22.clone.ut) | copy-start | bytes 294916

commit v14 on v13

--- a/solution.py
+++ b/solution.py
@@ -522,7 +522,7 @@
     ids = jnp.concatenate([blk_slot[None], blk_tile[None], jnp.zeros((6, 128), jnp.int32)], 0)
     own = jnp.concatenate([beta, ids.astype(F32)[None]], 0).reshape(1032, 128)
     (send,) = call(kernel_z_inverse, "z_inverse", [(448, 128)], (psi, t["wz"]))
-    betas = [own, from_band(own, 2), from_band(own, 3), from_band(own, 1)]
+    betas = [own, from_band(own, 2), from_band(own, 1), from_band(own, 3)]
 
     def exchange(x):
         x = lax.all_to_all(x.reshape(64, 1, 896), "fft", 0, 0, tiled=True)

time: 69 us -> 69.2 us (level)
    ppermute x3, starting transfers between devices: 4.68 us -> 5.89 us  [from_band(): return lax.ppermute(x, 'band', [(i, (i + k) % 4) for i in range(4)])]
    ppermute x1, starting transfers between devices: 4.36 us -> 3.38 us  [body(): lax.ppermute(second, 'fft', [(i, ((i + 2) % 64 ^ 2) - 2 & 63) for i in ra...]
    ppermute x1, waiting for transfers between devices: 1.3 us -> 2.28 us  [body(): lax.ppermute(second, 'fft', [(i, ((i + 2) % 64 ^ 2) - 2 & 63) for i in ra...]
    ppermute x1, waiting for transfers between devices: 1.1 us -> 0.32 us  [body(): first = lax.ppermute(first, 'fft', [(i, i ^ 2) for i in range(64)])]
where the time goes in v14:
time: 69.2 us; the launch traced here: 69 us
  blocking collectives  41.7 us (60%)
  Pallas kernels  10.9 us (16%)
  starting transfers between devices  9.68 us (14%)
  waiting for transfers between devices  3.49 us (5%)
  local copies, waits for them, and re-layouts  1.97 us (3%)
  other arithmetic  1.2 us (2%)
    all_to_all x2, blocking collectives, exchange(): x = lax.all_to_all(x.reshape(64, 1, 896), 'fft', 0, 0, tiled=True)  41.7 us
    pallas_call x8, Pallas kernels, call(): pl.pallas_call(kernel, name=name, out_shape=shapes, in_specs=specs, out_s...  10.9 us
    ppermute x3, starting transfers between devices, from_band(): return lax.ppermute(x, 'band', [(i, (i + k) % 4) for i in range(4)])  5.89 us
    ppermute x1, starting transfers between devices, body(): lax.ppermute(second, 'fft', [(i, ((i + 2) % 64 ^ 2) - 2 & 63) for i in ra...  3.38 us
    ppermute x1, waiting for transfers between devices, body(): lax.ppermute(second, 'fft', [(i, ((i + 2) % 64 ^ 2) - 2 & 63) for i in ra...  2.28 us
    unnamed x24, local copies, waits for them, and re-layouts  1.89 us
  transfers between devices with their start and end apart: 6, of which 3 were waited for; matrix products, arithmetic and copies ran while one was open for 0% of the time, Pallas kernels for 6%

profile of v14, /device:TPU:1, one launch (start us, length us, event | category | flops | bytes accessed | tf_op | source)
XLA Modules:
  0.0 69.0 jit_solution(16711558248935799321)
XLA Ops:
  0.0 0.1 pad.4.clone
  0.1 0.7 copy-done.10
  0.7 0.0 copy-done.11
  0.8 0.1 add_convert_fusion
  0.8 1.1 %maximum_bitcast_fusion.b0 = f32[1032,128]{1,0:T(8,128)S(1)} fusion(f32[1,8,128]{2,1,0:T(8,128)S(1)} %add_convert_fusion, f32[128,8,128]{2,1,0:T(8,128)} %param.16), kind=kLoop, calls=%fused_computation | loop fusion | flops 132096 | bytes 1056768 | tf_op jit(solution)/shard_map/reshape | solution.py:523
  2.0 0.0 copy-start.2
  2.0 2.2 %collective-permute-start.1 = (f32[1032,128]{1,0:T(8,128)S(1)}, f32[1032,128]{1,0:T(8,128)S(1)}, u32[]{:S(2)}, u32[]{:S(2)}) collective-permute-start(f32[1032,128]{1,0:T(8,128)S(1)} %maximum_bitcast_fusion.b0), channel_id=1, source_target_pairs={{0,1},{1,2},{2,3},{3,0},{4,5},{5,6},{6,7},{7,4},{8,9},{9,10},{10,1... | collective-permute-start | bytes 1585160 | tf_op jit(solution)/shard_map/ppermute | solution.py:520
  4.2 2.6 %collective-permute-start = (f32[1032,128]{1,0:T(8,128)S(1)}, f32[1032,128]{1,0:T(8,128)S(1)}, u32[]{:S(2)}, u32[]{:S(2)}) collective-permute-start(f32[1032,128]{1,0:T(8,128)S(1)} %maximum_bitcast_fusion.b0), channel_id=1, source_target_pairs={{0,2},{1,3},{2,0},{3,1},{4,6},{5,7},{6,4},{7,5},{8,10},{9,11},{10,... | collective-permute-start | bytes 1585160 | tf_op jit(solution)/shard_map/ppermute | solution.py:520
  6.8 1.1 %collective-permute-start.2 = (f32[1032,128]{1,0:T(8,128)S(1)}, f32[1032,128]{1,0:T(8,128)S(1)}, u32[]{:S(2)}, u32[]{:S(2)}) collective-permute-start(f32[1032,128]{1,0:T(8,128)S(1)} %maximum_bitcast_fusion.b0), channel_id=1, source_target_pairs={{0,3},{1,0},{2,1},{3,2},{4,7},{5,4},{6,5},{7,6},{8,11},{9,8},{10,9... | collective-permute-start | bytes 1585160 | tf_op jit(solution)/shard_map/ppermute | solution.py:520
  7.9 1.2 %copy-done.3 = f32[1,2,3,36864]{3,1,2,0:T(2,128)S(1)} copy-done((f32[1,2,3,36864]{3,1,2,0:T(2,128)S(1)}, f32[1,2,3,36864]{3,1,2,0:T(2,128)}, u32[]{:S(2)}) %copy-start.3) | copy-done | bytes 884760
  9.0 0.6 z_inverse.1
  9.7 0.0 copy-start.6
  9.7 24.1 %all_to_all.10 = f32[64,1,896]{2,1,0:T(1,128)S(1)} all-to-all(f32[64,1,896]{2,1,0:T(1,128)S(1)} %bitcast.35), channel_id=1, replica_groups=mesh['fft'=64,'band'=4] {'fft'}, dimensions={0} | all-to-all | bytes 458752 | tf_op jit(solution)/shard_map/all_to_all | solution.py:528
  33.7 1.3 %field.1 = (f32[864,256]{1,0:T(8,128)S(1)}, bf16[896,256]{1,0:T(8,128)(2,1)S(1)}, bf16[896,256]{1,0:T(8,128)(2,1)S(1)}) custom-call(f32[448,128]{1,0:T(8,128)S(1)} %bitcast.32, bf16[768,256]{1,0:T(8,128)(2,1)S(1)} %copy-done.6, bf16[1024,512]{1,0:T(8,128)(2,1)S(1)} %copy-done.2, bf16[128,384]{1,0:T(8,128)(2,1)S(1)} %copy-done.7), custom_call_target="tpu_custom_call" | custom-call | tf_op jit(solution)/shard_map/field/pallas_call | solution.py:497
  35.1 0.0 collective-permute-done.1.b2
  35.1 0.0 copy-start.9
  35.1 0.0 copy-start.4
  35.1 2.0 %project.1 = (f32[16,256]{1,0:T(8,128)S(1)}, bf16[384,256]{1,0:T(8,128)(2,1)S(1)}, s32[1,384]{1,0:T(1,128)S(1)}) custom-call(bf16[896,256]{1,0:T(8,128)(2,1)S(1)} %get-tuple-element.19.rows_h, bf16[896,256]{1,0:T(8,128)(2,1)S(1)} %get-tuple-element.20.rows_l, f32[1032,128]{1,0:T(8,128)S(1)} %maximum_bitcast_fusion.b0, ...), custom_call_target="tpu_custom_call" | custom-call | tf_op jit(solution)/shard_map/project/pallas_call | solution.py:497
  37.1 0.0 collective-permute-done.2.b3
  37.1 0.0 copy-start.1
  37.1 1.0 %project_last.1 = (f32[96,128]{1,0:T(8,128)S(1)}, bf16[128,256]{1,0:T(8,128)(2,1)S(1)}, s32[1,128]{1,0:T(1,128)S(1)}) custom-call(bf16[896,256]{1,0:T(8,128)(2,1)S(1)} %get-tuple-element.19.rows_h, bf16[896,256]{1,0:T(8,128)(2,1)S(1)} %get-tuple-element.20.rows_l, f32[64,64]{1,0:T(8,128)S(1)} %bitcast.38, f32[16,256]{1,0:T(8,128)S(1)} %get-tuple-element.21.coef_in, ...), custom_call_target="tpu_custom_call" | custom-call | tf_op jit(solution)/shard_map/project_last/pallas_call | solution.py:497
  38.1 0.4 collective-permute-start.3
  38.5 0.9 %collective-permute-done.3.other = f32[96,128]{1,0:T(8,128)S(1)} collective-permute-done((f32[96,128]{1,0:T(8,128)S(1)}, f32[96,128]{1,0:T(8,128)S(1)}, u32[]{:S(2)}, u32[]{:S(2)}) %collective-permute-start.3) | collective-permute-done | bytes 49184 | tf_op jit(solution)/shard_map/ppermute | solution.py:554
  39.4 0.1 merge.1
  39.4 3.4 %collective-permute-start.4 = (f32[80,128]{1,0:T(8,128)S(1)}, f32[80,128]{1,0:T(8,128)S(1)}, u32[]{:S(2)}, u32[]{:S(2)}) collective-permute-start(f32[80,128]{1,0:T(8,128)S(1)} %get-tuple-element.23), channel_id=1, source_target_pairs={{0,248},{4,252},{8,16},{12,20},{16,8},{20,12},{24,32},{28,36},{32,... | collective-permute-start | bytes 122888 | tf_op jit(solution)/shard_map/ppermute | solution.py:557
  42.8 0.0 collective-permute-start.5
  42.8 0.5 put.1
  43.4 2.3 %collective-permute-done.4.second = f32[80,128]{1,0:T(8,128)S(1)} collective-permute-done((f32[80,128]{1,0:T(8,128)S(1)}, f32[80,128]{1,0:T(8,128)S(1)}, u32[]{:S(2)}, u32[]{:S(2)}) %collective-permute-start.4) | collective-permute-done | bytes 40992 | tf_op jit(solution)/shard_map/ppermute | solution.py:557
  45.7 0.3 collective-permute-done.5.first
  46.0 3.8 %back.1 = f32[448,128]{1,0:T(8,128)S(1)} custom-call(f32[864,256]{1,0:T(8,128)S(1)} %get-tuple-element.18.field, f32[96,128]{1,0:T(8,128)S(1)} %get-tuple-element.22.own, f32[96,128]{1,0:T(8,128)S(1)} %collective-permute-done.3.other, f32[80,128]{1,0:T(8,128)S(1)} %collective-permute-done.4.second, f32[80,128]{1,0:T(8,128)S(1)} %collective-permute-done.5.first, ...), custom_call_target="tpu_custom_call" | custom-call | tf_op jit(solution)/shard_map/back/pallas_call | solution.py:497
  49.7 17.6 %all_to_all.11 = f32[64,1,896]{2,1,0:T(1,128)S(1)} all-to-all(f32[64,1,896]{2,1,0:T(1,128)S(1)} %bitcast.33), channel_id=1, replica_groups=mesh['fft'=64,'band'=4] {'fft'}, dimensions={0} | all-to-all | bytes 458752 | tf_op jit(solution)/shard_map/all_to_all | solution.py:528
  67.4 1.6 %z_forward.1 = f32[1728,128]{1,0:T(8,128)} custom-call(f32[448,128]{1,0:T(8,128)S(1)} %bitcast.34, bf16[768,256]{1,0:T(8,128)(2,1)S(1)} %copy-done), custom_call_target="tpu_custom_call" | custom-call | tf_op jit(solution)/shard_map/z_forward/pallas_call | solution.py:497
  (18 shorter events, 0.0 us)
Async XLA Ops:
  0.1 0.7 copy-start.10
  0.1 0.7 copy-start.11
  0.8 7.0 %copy-start = (bf16[768,256]{1,0:T(8,128)(2,1)S(1)}, bf16[768,256]{1,0:T(8,128)(2,1)}, u32[]{:S(2)}) copy-start(bf16[768,256]{1,0:T(8,128)(2,1)} %constant.16.clone.wz.fz) | copy-start | bytes 1179652
  2.0 31.8 %copy-start.2 = (bf16[1024,512]{1,0:T(8,128)(2,1)S(1)}, bf16[1024,512]{1,0:T(8,128)(2,1)}, u32[]{:S(2)}) copy-start(bf16[1024,512]{1,0:T(8,128)(2,1)} %constant.18.clone.ix) | copy-start | bytes 3145732
  2.0 33.1 %collective-permute-start.1 = (f32[1032,128]{1,0:T(8,128)S(1)}, f32[1032,128]{1,0:T(8,128)S(1)}, u32[]{:S(2)}, u32[]{:S(2)}) collective-permute-start(f32[1032,128]{1,0:T(8,128)S(1)} %maximum_bitcast_fusion.b0), channel_id=1, source_target_pairs={{0,1},{1,2},{2,3},{3,0},{4,5},{5,6},{6,7},{7,4},{8,9},{9,10},{10,1... | collective-permute-start | bytes 1585160 | tf_op jit(solution)/shard_map/ppermute | solution.py:520
  4.2 30.9 %collective-permute-start = (f32[1032,128]{1,0:T(8,128)S(1)}, f32[1032,128]{1,0:T(8,128)S(1)}, u32[]{:S(2)}, u32[]{:S(2)}) collective-permute-start(f32[1032,128]{1,0:T(8,128)S(1)} %maximum_bitcast_fusion.b0), channel_id=1, source_target_pairs={{0,2},{1,3},{2,0},{3,1},{4,6},{5,7},{6,4},{7,5},{8,10},{9,11},{10,... | collective-permute-start | bytes 1585160 | tf_op jit(solution)/shard_map/ppermute | solution.py:520
  6.8 30.3 %collective-permute-start.2 = (f32[1032,128]{1,0:T(8,128)S(1)}, f32[1032,128]{1,0:T(8,128)S(1)}, u32[]{:S(2)}, u32[]{:S(2)}) collective-permute-start(f32[1032,128]{1,0:T(8,128)S(1)} %maximum_bitcast_fusion.b0), channel_id=1, source_target_pairs={{0,3},{1,0},{2,1},{3,2},{4,7},{5,4},{6,5},{7,6},{8,11},{9,8},{10,9... | collective-permute-start | bytes 1585160 | tf_op jit(solution)/shard_map/ppermute | solution.py:520
  7.9 1.2 %copy-start.3 = (f32[1,2,3,36864]{3,1,2,0:T(2,128)S(1)}, f32[1,2,3,36864]{3,1,2,0:T(2,128)}, u32[]{:S(2)}) copy-start(f32[1,2,3,36864]{3,1,2,0:T(2,128)} %param.14) | copy-start | bytes 2654212
  9.0 24.7 %copy-start.7 = (bf16[128,384]{1,0:T(8,128)(2,1)S(1)}, bf16[128,384]{1,0:T(8,128)(2,1)}, u32[]{:S(2)}) copy-start(bf16[128,384]{1,0:T(8,128)(2,1)} %constant.21.clone.u) | copy-start | bytes 294916
  9.7 24.1 %copy-start.6 = (bf16[768,256]{1,0:T(8,128)(2,1)S(1)}, bf16[768,256]{1,0:T(8,128)(2,1)}, u32[]{:S(2)}) copy-start(bf16[768,256]{1,0:T(8,128)(2,1)} %constant.17.clone.ey) | copy-start | bytes 1179652
  35.1 2.0 %copy-start.9 = (f32[64,8,8]{0,2,1:T(8,128)S(1)}, f32[64,8,8]{0,2,1:T(8,128)}, u32[]{:S(2)}) copy-start(f32[64,8,8]{0,2,1:T(8,128)} %param.19) | copy-start | bytes 49156
  35.1 7.7 %copy-start.4 = (f32[3,36864]{1,0:T(4,128)S(1)}, f32[3,36864]{1,0:T(4,128)}, u32[]{:S(2)}) copy-start(f32[3,36864]{1,0:T(4,128)} %param.15) | copy-start | bytes 1327108
  37.1 8.9 %copy-start.1 = (bf16[2048,256]{1,0:T(8,128)(2,1)S(1)}, bf16[2048,256]{1,0:T(8,128)(2,1)}, u32[]{:S(2)}) copy-start(bf16[2048,256]{1,0:T(8,128)(2,1)} %constant.19.clone.fx) | copy-start | bytes 3145732
  38.1 7.9 %copy-start.5 = (bf16[512,384]{1,0:T(8,128)(2,1)S(1)}, bf16[512,384]{1,0:T(8,128)(2,1)}, u32[]{:S(2)}) copy-start(bf16[512,384]{1,0:T(8,128)(2,1)} %constant.20.clone.fy) | copy-start | bytes 1179652
  38.1 1.3 %collective-permute-start.3 = (f32[96,128]{1,0:T(8,128)S(1)}, f32[96,128]{1,0:T(8,128)S(1)}, u32[]{:S(2)}, u32[]{:S(2)}) collective-permute-start(f32[96,128]{1,0:T(8,128)S(1)} %get-tuple-element.22.own), channel_id=1, source_target_pairs={{0,4},{4,0},{8,12},{12,8},{16,20},{20,16},{24,28},{28,24},{32,36},... | collective-permute-start | bytes 147464 | tf_op jit(solution)/shard_map/ppermute | solution.py:554
  39.4 6.2 %collective-permute-start.4 = (f32[80,128]{1,0:T(8,128)S(1)}, f32[80,128]{1,0:T(8,128)S(1)}, u32[]{:S(2)}, u32[]{:S(2)}) collective-permute-start(f32[80,128]{1,0:T(8,128)S(1)} %get-tuple-element.23), channel_id=1, source_target_pairs={{0,248},{4,252},{8,16},{12,20},{16,8},{20,12},{24,32},{28,36},{32,... | collective-permute-start | bytes 122888 | tf_op jit(solution)/shard_map/ppermute | solution.py:557
  42.8 3.1 %collective-permute-start.5 = (f32[80,128]{1,0:T(8,128)S(1)}, f32[80,128]{1,0:T(8,128)S(1)}, u32[]{:S(2)}, u32[]{:S(2)}) collective-permute-start(f32[80,128]{1,0:T(8,128)S(1)} %get-tuple-element.24), channel_id=1, source_target_pairs={{0,8},{4,12},{8,0},{12,4},{16,24},{20,28},{24,16},{28,20},{32,40},... | collective-permute-start | bytes 122888 | tf_op jit(solution)/shard_map/ppermute | solution.py:556
  42.8 3.1 %copy-start.8 = (bf16[384,128]{1,0:T(8,128)(2,1)S(1)}, bf16[384,128]{1,0:T(8,128)(2,1)}, u32[]{:S(2)}) copy-start(bf16[384,128]{1,0:T(8,128)(2,1)} %constant.22.clone.ut) | copy-start | bytes 294916

commit v15 on v11

--- a/solution.py
+++ b/solution.py
@@ -318,7 +318,7 @@
     second[...] = jnp.where(even, down, up)
 
 
-def kernel_put(tiles, tiles_last, vloc_in, put, vloc_out, vloc, sems):
+def kernel_put(tiles, tiles_last, field, vloc_in, put, local, vloc, sems):
     copies = [
         pltpu.make_async_copy(vloc_in.at[:, zi, :], vloc.at[zi], sems.at[zi]) for zi in range(3)
     ]
@@ -331,12 +331,13 @@
     for k in range(3):
         for zi in range(3):
             at = 288 * k + 96 * zi
-            vloc_out[at : at + 96, :] = vloc[zi, pl.ds(k, 96, stride=3), :]
+            factor = vloc[zi, pl.ds(k, 96, stride=3), :]
+            local[at : at + 96, :] = field[at : at + 96, :] * jnp.concatenate([factor, factor], 1)
 
 
 def kernel_back(
-    field, own, other, second, first, slots, slots_last, put, b0, b1, b2, b3,
-    vloc, fx, fy, ut, send, scr, rows,
+    local, own, other, second, first, slots, slots_last, put, b0, b1, b2, b3,
+    fx, fy, ut, send, scr, rows,
 ):
     core, even, a, b = chip_of(own, other)
     above = jnp.where(even, first[...], second[...])
@@ -364,11 +365,8 @@
     left = jnp.where(core == 0, left, jnp.where(low_lane, left_turned, right_turned))
     right = jnp.where(low_lane, jnp.where(core == 0, right, right_turned), 0.0)
     high, low = split(jnp.concatenate([left, right], 1))
-    weight = jnp.concatenate(
-        [mm_nt(hot[...], high) + mm_nt(hot[...], low) for hot in (slots, slots_last)], 0
-    )
-    high, low = split(weight)
-    weight = jnp.concatenate([high, low], 1)
+    parts = jnp.concatenate([high, low], 0)
+    weight = jnp.concatenate([mm_nt(hot[...], parts) for hot in (slots, slots_last)], 0).astype(BF)
     for k, beta in enumerate(betas):
         span = slice(128 * k, 128 * k + 128)
         terms = jnp.zeros((128, 256), F32)
@@ -384,8 +382,7 @@
     kinds = []
     for k in range(3):
         at = slice(288 * k, 288 * k + 288)
-        factor = vloc[at, :]
-        kinds.append(split(field[at, :] * jnp.concatenate([factor, factor], 1) + nonloc[at, :]))
+        kinds.append(split(local[at, :] + nonloc[at, :]))
     g = []
     for parity in range(2):
         table = [fx[1024 * parity + 512 * i : 1024 * parity + 512 * i + 512, :] for i in range(2)]
@@ -556,20 +553,20 @@
     first, second = call(kernel_merge, "merge", [(80, 128), (80, 128)], (near, other))
     first = lax.ppermute(first, "fft", [(i, i ^ 2) for i in range(64)])
     second = lax.ppermute(second, "fft", [(i, (((i + 2) % 64) ^ 2) - 2 & 63) for i in range(64)])
-    put, vloc_rows = call(
+    put, local = call(
         kernel_put,
         "put",
-        [((864, 512), BF), (864, 128)],
-        (tiles, tiles_last, vloc_tiles),
+        [((864, 512), BF), (864, 256)],
+        (tiles, tiles_last, field, vloc_tiles),
         [pltpu.VMEM((3, 288, 128), F32), pltpu.SemaphoreType.DMA((3,))],
-        anywhere=(2,),
+        anywhere=(3,),
         cost=pl.CostEstimate(flops=2000000, bytes_accessed=3000000, transcendentals=0),
     )
     (send,) = call(
         kernel_back,
         "back",
         [(448, 128)],
-        (field, near, other, second, first, slots, slots_last, put, *betas, vloc_rows, t["fx"], t["fy"], t["ut"]),
+        (local, near, other, second, first, slots, slots_last, put, *betas, t["fx"], t["fy"], t["ut"]),
         [
             pltpu.VMEM((16, 256), F32),
             pltpu.VMEM((512, 512), BF),

time: 68.7 us -> 68.8 us (level)
    ppermute x1, waiting for transfers between devices: 2.18 us -> 1.18 us  [body(): lax.ppermute(second, 'fft', [(i, ((i + 2) % 64 ^ 2) - 2 & 63) for i in ra...]
    ppermute x1, starting transfers between devices: 3.49 us -> 4.43 us  [body(): lax.ppermute(second, 'fft', [(i, ((i + 2) % 64 ^ 2) - 2 & 63) for i in ra...]
  transfers between devices with their start and end apart: 6 -> 6, of which waited for: 3 -> 3; matrix products, arithmetic and copies ran while one was open for 0% -> 0% of each run, Pallas kernels for 6% -> 7%
where the time goes in v15:
time: 68.8 us; the launch traced here: 68.6 us
  blocking collectives  41.8 us (61%)
  Pallas kernels  10.8 us (16%)
  starting transfers between devices  9.61 us (14%)
  waiting for transfers between devices  3.17 us (5%)
  local copies, waits for them, and re-layouts  1.96 us (3%)
  other arithmetic  1.2 us (2%)
    all_to_all x2, blocking collectives, exchange(): x = lax.all_to_all(x.reshape(64, 1, 896), 'fft', 0, 0, tiled=True)  41.8 us
    pallas_call x8, Pallas kernels, call(): pl.pallas_call(kernel, name=name, out_shape=shapes, in_specs=specs, out_s...  10.8 us
    ppermute x3, starting transfers between devices, from_band(): return lax.ppermute(x, 'band', [(i, (i + k) % 4) for i in range(4)])  4.76 us
    ppermute x1, starting transfers between devices, body(): lax.ppermute(second, 'fft', [(i, ((i + 2) % 64 ^ 2) - 2 & 63) for i in ra...  4.43 us
    unnamed x24, local copies, waits for them, and re-layouts  1.89 us
  transfers between devices with their start and end apart: 6, of which 3 were waited for; matrix products, arithmetic and copies ran while one was open for 0% of the time, Pallas kernels for 7%

profile of v15, /device:TPU:1, one launch (start us, length us, event | category | flops | bytes accessed | tf_op | source)
XLA Modules:
  0.0 68.6 jit_solution(16806386322478544788)
XLA Ops:
  0.0 0.1 pad.4.clone
  0.1 0.7 copy-done.10
  0.7 0.0 copy-done.11
  0.8 0.1 add_convert_fusion
  0.8 1.1 %maximum_bitcast_fusion.b0 = f32[1032,128]{1,0:T(8,128)S(1)} fusion(f32[1,8,128]{2,1,0:T(8,128)S(1)} %add_convert_fusion, f32[128,8,128]{2,1,0:T(8,128)} %param.16), kind=kLoop, calls=%fused_computation | loop fusion | flops 132096 | bytes 1056768 | tf_op jit(solution)/shard_map/reshape | solution.py:520
  2.0 0.0 copy-start.1
  2.0 3.6 %collective-permute-start = (f32[1032,128]{1,0:T(8,128)S(1)}, f32[1032,128]{1,0:T(8,128)S(1)}, u32[]{:S(2)}, u32[]{:S(2)}) collective-permute-start(f32[1032,128]{1,0:T(8,128)S(1)} %maximum_bitcast_fusion.b0), channel_id=1, source_target_pairs={{0,3},{1,0},{2,1},{3,2},{4,7},{5,4},{6,5},{7,6},{8,11},{9,8},{10,9... | collective-permute-start | bytes 1585160 | tf_op jit(solution)/shard_map/ppermute | solution.py:517
  5.6 0.3 collective-permute-start.1
  6.0 1.2 %copy-done.3 = f32[1,2,3,36864]{3,1,2,0:T(2,128)S(1)} copy-done((f32[1,2,3,36864]{3,1,2,0:T(2,128)S(1)}, f32[1,2,3,36864]{3,1,2,0:T(2,128)}, u32[]{:S(2)}) %copy-start.3) | copy-done | bytes 884760
  7.1 0.6 z_inverse.1
  7.8 0.0 copy-start.6
  7.8 0.8 %collective-permute-start.2 = (f32[1032,128]{1,0:T(8,128)S(1)}, f32[1032,128]{1,0:T(8,128)S(1)}, u32[]{:S(2)}, u32[]{:S(2)}) collective-permute-start(f32[1032,128]{1,0:T(8,128)S(1)} %maximum_bitcast_fusion.b0), channel_id=1, source_target_pairs={{0,1},{1,2},{2,3},{3,0},{4,5},{5,6},{6,7},{7,4},{8,9},{9,10},{10,1... | collective-permute-start | bytes 1585160 | tf_op jit(solution)/shard_map/ppermute | solution.py:517
  8.5 23.9 %all_to_all.10 = f32[64,1,896]{2,1,0:T(1,128)S(1)} all-to-all(f32[64,1,896]{2,1,0:T(1,128)S(1)} %bitcast.34), channel_id=1, replica_groups=mesh['fft'=64,'band'=4] {'fft'}, dimensions={0} | all-to-all | bytes 458752 | tf_op jit(solution)/shard_map/all_to_all | solution.py:526
  32.5 1.3 %field.1 = (f32[864,256]{1,0:T(8,128)S(1)}, bf16[896,256]{1,0:T(8,128)(2,1)S(1)}, bf16[896,256]{1,0:T(8,128)(2,1)S(1)}) custom-call(f32[448,128]{1,0:T(8,128)S(1)} %bitcast.32, bf16[768,256]{1,0:T(8,128)(2,1)S(1)} %copy-done.6, bf16[1024,512]{1,0:T(8,128)(2,1)S(1)} %copy-done.1, bf16[128,384]{1,0:T(8,128)(2,1)S(1)} %copy-done.7), custom_call_target="tpu_custom_call" | custom-call | tf_op jit(solution)/shard_map/field/pallas_call | solution.py:494
  33.8 0.0 collective-permute-done.b1
  33.8 0.0 collective-permute-done.1.b2
  33.8 0.0 copy-start.9
  33.8 2.0 %project.1 = (f32[16,256]{1,0:T(8,128)S(1)}, bf16[384,256]{1,0:T(8,128)(2,1)S(1)}, s32[1,384]{1,0:T(1,128)S(1)}) custom-call(bf16[896,256]{1,0:T(8,128)(2,1)S(1)} %get-tuple-element.21.rows_h, bf16[896,256]{1,0:T(8,128)(2,1)S(1)} %get-tuple-element.22.rows_l, f32[1032,128]{1,0:T(8,128)S(1)} %maximum_bitcast_fusion.b0, ...), custom_call_target="tpu_custom_call" | custom-call | tf_op jit(solution)/shard_map/project/pallas_call | solution.py:494
  35.8 0.0 collective-permute-done.2.b3
  35.8 0.0 copy-start.4
  35.8 1.0 %project_last.1 = (f32[96,128]{1,0:T(8,128)S(1)}, bf16[128,256]{1,0:T(8,128)(2,1)S(1)}, s32[1,128]{1,0:T(1,128)S(1)}) custom-call(bf16[896,256]{1,0:T(8,128)(2,1)S(1)} %get-tuple-element.21.rows_h, bf16[896,256]{1,0:T(8,128)(2,1)S(1)} %get-tuple-element.22.rows_l, f32[64,64]{1,0:T(8,128)S(1)} %bitcast.38, f32[16,256]{1,0:T(8,128)S(1)} %get-tuple-element.24.coef_in, ...), custom_call_target="tpu_custom_call" | custom-call | tf_op jit(solution)/shard_map/project_last/pallas_call | solution.py:494
  36.8 0.4 collective-permute-start.3
  37.2 0.9 %collective-permute-done.3.other = f32[96,128]{1,0:T(8,128)S(1)} collective-permute-done((f32[96,128]{1,0:T(8,128)S(1)}, f32[96,128]{1,0:T(8,128)S(1)}, u32[]{:S(2)}, u32[]{:S(2)}) %collective-permute-start.3) | collective-permute-done | bytes 49184 | tf_op jit(solution)/shard_map/ppermute | solution.py:552
  38.1 0.1 merge.1
  38.2 4.4 %collective-permute-start.4 = (f32[80,128]{1,0:T(8,128)S(1)}, f32[80,128]{1,0:T(8,128)S(1)}, u32[]{:S(2)}, u32[]{:S(2)}) collective-permute-start(f32[80,128]{1,0:T(8,128)S(1)} %get-tuple-element.30), channel_id=1, source_target_pairs={{0,248},{4,252},{8,16},{12,20},{16,8},{20,12},{24,32},{28,36},{32,... | collective-permute-start | bytes 122888 | tf_op jit(solution)/shard_map/ppermute | solution.py:555
  42.6 0.0 collective-permute-start.5
  42.6 0.6 put.1
  43.2 1.2 %collective-permute-done.4.second = f32[80,128]{1,0:T(8,128)S(1)} collective-permute-done((f32[80,128]{1,0:T(8,128)S(1)}, f32[80,128]{1,0:T(8,128)S(1)}, u32[]{:S(2)}, u32[]{:S(2)}) %collective-permute-start.4) | collective-permute-done | bytes 40992 | tf_op jit(solution)/shard_map/ppermute | solution.py:555
  44.4 1.1 %collective-permute-done.5.first = f32[80,128]{1,0:T(8,128)S(1)} collective-permute-done((f32[80,128]{1,0:T(8,128)S(1)}, f32[80,128]{1,0:T(8,128)S(1)}, u32[]{:S(2)}, u32[]{:S(2)}) %collective-permute-start.5) | collective-permute-done | bytes 40992 | tf_op jit(solution)/shard_map/ppermute | solution.py:554
  45.5 3.6 %back.1 = f32[448,128]{1,0:T(8,128)S(1)} custom-call(f32[864,256]{1,0:T(8,128)S(1)} %get-tuple-element.28.local, f32[96,128]{1,0:T(8,128)S(1)} %get-tuple-element.29.own, f32[96,128]{1,0:T(8,128)S(1)} %collective-permute-done.3.other, f32[80,128]{1,0:T(8,128)S(1)} %collective-permute-done.4.second, f32[80,128]{1,0:T(8,128)S(1)} %collective-permute-done.5.first, ...), custom_call_target="tpu_custom_call" | custom-call | tf_op jit(solution)/shard_map/back/pallas_call | solution.py:494
  49.1 17.9 %all_to_all.11 = f32[64,1,896]{2,1,0:T(1,128)S(1)} all-to-all(f32[64,1,896]{2,1,0:T(1,128)S(1)} %bitcast.33), channel_id=1, replica_groups=mesh['fft'=64,'band'=4] {'fft'}, dimensions={0} | all-to-all | bytes 458752 | tf_op jit(solution)/shard_map/all_to_all | solution.py:526
  67.0 1.6 %z_forward.1 = f32[1728,128]{1,0:T(8,128)} custom-call(f32[448,128]{1,0:T(8,128)S(1)} %bitcast.35, bf16[768,256]{1,0:T(8,128)(2,1)S(1)} %copy-done), custom_call_target="tpu_custom_call" | custom-call | tf_op jit(solution)/shard_map/z_forward/pallas_call | solution.py:494
  (18 shorter events, 0.0 us)
Async XLA Ops:
  0.1 0.7 copy-start.10
  0.1 0.7 copy-start.11
  0.8 5.1 %copy-start = (bf16[768,256]{1,0:T(8,128)(2,1)S(1)}, bf16[768,256]{1,0:T(8,128)(2,1)}, u32[]{:S(2)}) copy-start(bf16[768,256]{1,0:T(8,128)(2,1)} %constant.16.clone.wz.fz) | copy-start | bytes 1179652
  2.0 30.5 %copy-start.1 = (bf16[1024,512]{1,0:T(8,128)(2,1)S(1)}, bf16[1024,512]{1,0:T(8,128)(2,1)}, u32[]{:S(2)}) copy-start(bf16[1024,512]{1,0:T(8,128)(2,1)} %constant.18.clone.ix) | copy-start | bytes 3145732
  2.0 31.8 %collective-permute-start = (f32[1032,128]{1,0:T(8,128)S(1)}, f32[1032,128]{1,0:T(8,128)S(1)}, u32[]{:S(2)}, u32[]{:S(2)}) collective-permute-start(f32[1032,128]{1,0:T(8,128)S(1)} %maximum_bitcast_fusion.b0), channel_id=1, source_target_pairs={{0,3},{1,0},{2,1},{3,2},{4,7},{5,4},{6,5},{7,6},{8,11},{9,8},{10,9... | collective-permute-start | bytes 1585160 | tf_op jit(solution)/shard_map/ppermute | solution.py:517
  5.6 28.2 %collective-permute-start.1 = (f32[1032,128]{1,0:T(8,128)S(1)}, f32[1032,128]{1,0:T(8,128)S(1)}, u32[]{:S(2)}, u32[]{:S(2)}) collective-permute-start(f32[1032,128]{1,0:T(8,128)S(1)} %maximum_bitcast_fusion.b0), channel_id=1, source_target_pairs={{0,2},{1,3},{2,0},{3,1},{4,6},{5,7},{6,4},{7,5},{8,10},{9,11},{10,... | collective-permute-start | bytes 1585160 | tf_op jit(solution)/shard_map/ppermute | solution.py:517
  6.0 1.2 %copy-start.3 = (f32[1,2,3,36864]{3,1,2,0:T(2,128)S(1)}, f32[1,2,3,36864]{3,1,2,0:T(2,128)}, u32[]{:S(2)}) copy-start(f32[1,2,3,36864]{3,1,2,0:T(2,128)} %param.14) | copy-start | bytes 2654212
  7.1 25.3 %copy-start.7 = (bf16[128,384]{1,0:T(8,128)(2,1)S(1)}, bf16[128,384]{1,0:T(8,128)(2,1)}, u32[]{:S(2)}) copy-start(bf16[128,384]{1,0:T(8,128)(2,1)} %constant.21.clone.u) | copy-start | bytes 294916
  7.8 24.7 %copy-start.6 = (bf16[768,256]{1,0:T(8,128)(2,1)S(1)}, bf16[768,256]{1,0:T(8,128)(2,1)}, u32[]{:S(2)}) copy-start(bf16[768,256]{1,0:T(8,128)(2,1)} %constant.17.clone.ey) | copy-start | bytes 1179652
  7.8 28.0 %collective-permute-start.2 = (f32[1032,128]{1,0:T(8,128)S(1)}, f32[1032,128]{1,0:T(8,128)S(1)}, u32[]{:S(2)}, u32[]{:S(2)}) collective-permute-start(f32[1032,128]{1,0:T(8,128)S(1)} %maximum_bitcast_fusion.b0), channel_id=1, source_target_pairs={{0,1},{1,2},{2,3},{3,0},{4,5},{5,6},{6,7},{7,4},{8,9},{9,10},{10,1... | collective-permute-start | bytes 1585160 | tf_op jit(solution)/shard_map/ppermute | solution.py:517
  33.8 2.0 %copy-start.9 = (f32[64,8,8]{0,2,1:T(8,128)S(1)}, f32[64,8,8]{0,2,1:T(8,128)}, u32[]{:S(2)}) copy-start(f32[64,8,8]{0,2,1:T(8,128)} %param.19) | copy-start | bytes 49156
  35.8 6.8 %copy-start.4 = (f32[3,36864]{1,0:T(4,128)S(1)}, f32[3,36864]{1,0:T(4,128)}, u32[]{:S(2)}) copy-start(f32[3,36864]{1,0:T(4,128)} %param.15) | copy-start | bytes 1327108
  36.8 8.7 %copy-start.2 = (bf16[2048,256]{1,0:T(8,128)(2,1)S(1)}, bf16[2048,256]{1,0:T(8,128)(2,1)}, u32[]{:S(2)}) copy-start(bf16[2048,256]{1,0:T(8,128)(2,1)} %constant.19.clone.fx) | copy-start | bytes 3145732
  36.8 1.3 %collective-permute-start.3 = (f32[96,128]{1,0:T(8,128)S(1)}, f32[96,128]{1,0:T(8,128)S(1)}, u32[]{:S(2)}, u32[]{:S(2)}) collective-permute-start(f32[96,128]{1,0:T(8,128)S(1)} %get-tuple-element.29.own), channel_id=1, source_target_pairs={{0,4},{4,0},{8,12},{12,8},{16,20},{20,16},{24,28},{28,24},{32,36},... | collective-permute-start | bytes 147464 | tf_op jit(solution)/shard_map/ppermute | solution.py:552
  38.2 6.2 %collective-permute-start.4 = (f32[80,128]{1,0:T(8,128)S(1)}, f32[80,128]{1,0:T(8,128)S(1)}, u32[]{:S(2)}, u32[]{:S(2)}) collective-permute-start(f32[80,128]{1,0:T(8,128)S(1)} %get-tuple-element.30), channel_id=1, source_target_pairs={{0,248},{4,252},{8,16},{12,20},{16,8},{20,12},{24,32},{28,36},{32,... | collective-permute-start | bytes 122888 | tf_op jit(solution)/shard_map/ppermute | solution.py:555
  42.6 2.9 %collective-permute-start.5 = (f32[80,128]{1,0:T(8,128)S(1)}, f32[80,128]{1,0:T(8,128)S(1)}, u32[]{:S(2)}, u32[]{:S(2)}) collective-permute-start(f32[80,128]{1,0:T(8,128)S(1)} %get-tuple-element.31), channel_id=1, source_target_pairs={{0,8},{4,12},{8,0},{12,4},{16,24},{20,28},{24,16},{28,20},{32,40},... | collective-permute-start | bytes 122888 | tf_op jit(solution)/shard_map/ppermute | solution.py:554
  42.6 2.9 %copy-start.5 = (bf16[512,384]{1,0:T(8,128)(2,1)S(1)}, bf16[512,384]{1,0:T(8,128)(2,1)}, u32[]{:S(2)}) copy-start(bf16[512,384]{1,0:T(8,128)(2,1)} %constant.20.clone.fy) | copy-start | bytes 1179652
  42.6 2.9 %copy-start.8 = (bf16[384,128]{1,0:T(8,128)(2,1)S(1)}, bf16[384,128]{1,0:T(8,128)(2,1)}, u32[]{:S(2)}) copy-start(bf16[384,128]{1,0:T(8,128)(2,1)} %constant.22.clone.ut) | copy-start | bytes 294916

commit v16 on v15

--- a/solution.py
+++ b/solution.py
@@ -519,8 +519,7 @@
     ids = jnp.concatenate([blk_slot[None], blk_tile[None], jnp.zeros((6, 128), jnp.int32)], 0)
     own = jnp.concatenate([beta, ids.astype(F32)[None]], 0).reshape(1032, 128)
     (send,) = call(kernel_z_inverse, "z_inverse", [(448, 128)], (psi, t["wz"]))
-    own_later, send = lax.optimization_barrier((own, send))
-    betas = [own, from_band(own, 3), from_band(own, 2), from_band(own_later, 1)]
+    betas = [own, from_band(own, 2), from_band(own, 3), from_band(own, 1)]
 
     def exchange(x):
         x = lax.all_to_all(x.reshape(64, 1, 896), "fft", 0, 0, tiled=True)

time: 68.8 us -> 68.5 us (level)
    ppermute x1, waiting for transfers between devices: 1.18 us -> 2.17 us  [body(): lax.ppermute(second, 'fft', [(i, ((i + 2) % 64 ^ 2) - 2 & 63) for i in ra...]
    ppermute x1, starting transfers between devices: 4.43 us -> 3.43 us  [body(): lax.ppermute(second, 'fft', [(i, ((i + 2) % 64 ^ 2) - 2 & 63) for i in ra...]
    ppermute x1, waiting for transfers between devices: 1.1 us -> 0.37 us  [body(): first = lax.ppermute(first, 'fft', [(i, i ^ 2) for i in range(64)])]
where the time goes in v16:
time: 68.5 us; the launch traced here: 68.3 us
  blocking collectives  41.7 us (61%)
  Pallas kernels  10.8 us (16%)
  starting transfers between devices  9.13 us (13%)
  waiting for transfers between devices  3.44 us (5%)
  local copies, waits for them, and re-layouts  1.96 us (3%)
  other arithmetic  1.2 us (2%)
    all_to_all x2, blocking collectives, exchange(): x = lax.all_to_all(x.reshape(64, 1, 896), 'fft', 0, 0, tiled=True)  41.7 us
    pallas_call x8, Pallas kernels, call(): pl.pallas_call(kernel, name=name, out_shape=shapes, in_specs=specs, out_s...  10.8 us
    ppermute x3, starting transfers between devices, from_band(): return lax.ppermute(x, 'band', [(i, (i + k) % 4) for i in range(4)])  5.3 us
    ppermute x1, starting transfers between devices, body(): lax.ppermute(second, 'fft', [(i, ((i + 2) % 64 ^ 2) - 2 & 63) for i in ra...  3.43 us
    ppermute x1, waiting for transfers between devices, body(): lax.ppermute(second, 'fft', [(i, ((i + 2) % 64 ^ 2) - 2 & 63) for i in ra...  2.17 us
    unnamed x24, local copies, waits for them, and re-layouts  1.89 us
  transfers between devices with their start and end apart: 6, of which 3 were waited for; matrix products, arithmetic and copies ran while one was open for 0% of the time, Pallas kernels for 7%

profile of v16, /device:TPU:1, one launch (start us, length us, event | category | flops | bytes accessed | tf_op | source)
XLA Modules:
  0.0 68.3 jit_solution(6313472382680225333)
XLA Ops:
  0.0 0.1 pad.4.clone
  0.1 0.7 copy-done.10
  0.7 0.0 copy-done.11
  0.8 0.1 add_convert_fusion
  0.8 1.1 %maximum_bitcast_fusion.b0 = f32[1032,128]{1,0:T(8,128)S(1)} fusion(f32[1,8,128]{2,1,0:T(8,128)S(1)} %add_convert_fusion, f32[128,8,128]{2,1,0:T(8,128)} %param.16), kind=kLoop, calls=%fused_computation | loop fusion | flops 132096 | bytes 1056768 | tf_op jit(solution)/shard_map/reshape | solution.py:520
  2.0 0.0 copy-start.1
  2.0 3.8 %collective-permute-start = (f32[1032,128]{1,0:T(8,128)S(1)}, f32[1032,128]{1,0:T(8,128)S(1)}, u32[]{:S(2)}, u32[]{:S(2)}) collective-permute-start(f32[1032,128]{1,0:T(8,128)S(1)} %maximum_bitcast_fusion.b0), channel_id=1, source_target_pairs={{0,2},{1,3},{2,0},{3,1},{4,6},{5,7},{6,4},{7,5},{8,10},{9,11},{10,... | collective-permute-start | bytes 1585160 | tf_op jit(solution)/shard_map/ppermute | solution.py:517
  5.8 0.8 %collective-permute-start.1 = (f32[1032,128]{1,0:T(8,128)S(1)}, f32[1032,128]{1,0:T(8,128)S(1)}, u32[]{:S(2)}, u32[]{:S(2)}) collective-permute-start(f32[1032,128]{1,0:T(8,128)S(1)} %maximum_bitcast_fusion.b0), channel_id=1, source_target_pairs={{0,3},{1,0},{2,1},{3,2},{4,7},{5,4},{6,5},{7,6},{8,11},{9,8},{10,9... | collective-permute-start | bytes 1585160 | tf_op jit(solution)/shard_map/ppermute | solution.py:517
  6.6 0.7 %collective-permute-start.2 = (f32[1032,128]{1,0:T(8,128)S(1)}, f32[1032,128]{1,0:T(8,128)S(1)}, u32[]{:S(2)}, u32[]{:S(2)}) collective-permute-start(f32[1032,128]{1,0:T(8,128)S(1)} %maximum_bitcast_fusion.b0), channel_id=1, source_target_pairs={{0,1},{1,2},{2,3},{3,0},{4,5},{5,6},{6,7},{7,4},{8,9},{9,10},{10,1... | collective-permute-start | bytes 1585160 | tf_op jit(solution)/shard_map/ppermute | solution.py:517
  7.3 1.2 %copy-done.3 = f32[1,2,3,36864]{3,1,2,0:T(2,128)S(1)} copy-done((f32[1,2,3,36864]{3,1,2,0:T(2,128)S(1)}, f32[1,2,3,36864]{3,1,2,0:T(2,128)}, u32[]{:S(2)}) %copy-start.3) | copy-done | bytes 884760
  8.4 0.6 z_inverse.1
  9.1 0.0 copy-start.6
  9.1 24.1 %all_to_all.10 = f32[64,1,896]{2,1,0:T(1,128)S(1)} all-to-all(f32[64,1,896]{2,1,0:T(1,128)S(1)} %bitcast.35), channel_id=1, replica_groups=mesh['fft'=64,'band'=4] {'fft'}, dimensions={0} | all-to-all | bytes 458752 | tf_op jit(solution)/shard_map/all_to_all | solution.py:525
  33.1 1.3 %field.1 = (f32[864,256]{1,0:T(8,128)S(1)}, bf16[896,256]{1,0:T(8,128)(2,1)S(1)}, bf16[896,256]{1,0:T(8,128)(2,1)S(1)}) custom-call(f32[448,128]{1,0:T(8,128)S(1)} %bitcast.32, bf16[768,256]{1,0:T(8,128)(2,1)S(1)} %copy-done.6, bf16[1024,512]{1,0:T(8,128)(2,1)S(1)} %copy-done.1, bf16[128,384]{1,0:T(8,128)(2,1)S(1)} %copy-done.7), custom_call_target="tpu_custom_call" | custom-call | tf_op jit(solution)/shard_map/field/pallas_call | solution.py:494
  34.5 0.0 collective-permute-done.b1
  34.5 0.0 collective-permute-done.1.b2
  34.5 0.0 copy-start.9
  34.5 2.0 %project.1 = (f32[16,256]{1,0:T(8,128)S(1)}, bf16[384,256]{1,0:T(8,128)(2,1)S(1)}, s32[1,384]{1,0:T(1,128)S(1)}) custom-call(bf16[896,256]{1,0:T(8,128)(2,1)S(1)} %get-tuple-element.18.rows_h, bf16[896,256]{1,0:T(8,128)(2,1)S(1)} %get-tuple-element.19.rows_l, f32[1032,128]{1,0:T(8,128)S(1)} %maximum_bitcast_fusion.b0, ...), custom_call_target="tpu_custom_call" | custom-call | tf_op jit(solution)/shard_map/project/pallas_call | solution.py:494
  36.5 0.0 collective-permute-done.2.b3
  36.5 0.0 copy-start.4
  36.5 1.0 %project_last.1 = (f32[96,128]{1,0:T(8,128)S(1)}, bf16[128,256]{1,0:T(8,128)(2,1)S(1)}, s32[1,128]{1,0:T(1,128)S(1)}) custom-call(bf16[896,256]{1,0:T(8,128)(2,1)S(1)} %get-tuple-element.18.rows_h, bf16[896,256]{1,0:T(8,128)(2,1)S(1)} %get-tuple-element.19.rows_l, f32[64,64]{1,0:T(8,128)S(1)} %bitcast.38, f32[16,256]{1,0:T(8,128)S(1)} %get-tuple-element.21.coef_in, ...), custom_call_target="tpu_custom_call" | custom-call | tf_op jit(solution)/shard_map/project_last/pallas_call | solution.py:494
  37.5 0.4 collective-permute-start.3
  37.9 0.9 %collective-permute-done.3.other = f32[96,128]{1,0:T(8,128)S(1)} collective-permute-done((f32[96,128]{1,0:T(8,128)S(1)}, f32[96,128]{1,0:T(8,128)S(1)}, u32[]{:S(2)}, u32[]{:S(2)}) %collective-permute-start.3) | collective-permute-done | bytes 49184 | tf_op jit(solution)/shard_map/ppermute | solution.py:551
  38.8 0.1 merge.1
  38.8 3.4 %collective-permute-start.4 = (f32[80,128]{1,0:T(8,128)S(1)}, f32[80,128]{1,0:T(8,128)S(1)}, u32[]{:S(2)}, u32[]{:S(2)}) collective-permute-start(f32[80,128]{1,0:T(8,128)S(1)} %get-tuple-element.26), channel_id=1, source_target_pairs={{0,248},{4,252},{8,16},{12,20},{16,8},{20,12},{24,32},{28,36},{32,... | collective-permute-start | bytes 122888 | tf_op jit(solution)/shard_map/ppermute | solution.py:554
  42.3 0.0 collective-permute-start.5
  42.3 0.6 put.1
  42.9 2.2 %collective-permute-done.4.second = f32[80,128]{1,0:T(8,128)S(1)} collective-permute-done((f32[80,128]{1,0:T(8,128)S(1)}, f32[80,128]{1,0:T(8,128)S(1)}, u32[]{:S(2)}, u32[]{:S(2)}) %collective-permute-start.4) | collective-permute-done | bytes 40992 | tf_op jit(solution)/shard_map/ppermute | solution.py:554
  45.0 0.4 collective-permute-done.5.first
  45.4 3.6 %back.1 = f32[448,128]{1,0:T(8,128)S(1)} custom-call(f32[864,256]{1,0:T(8,128)S(1)} %get-tuple-element.24.local, f32[96,128]{1,0:T(8,128)S(1)} %get-tuple-element.25.own, f32[96,128]{1,0:T(8,128)S(1)} %collective-permute-done.3.other, f32[80,128]{1,0:T(8,128)S(1)} %collective-permute-done.4.second, f32[80,128]{1,0:T(8,128)S(1)} %collective-permute-done.5.first, ...), custom_call_target="tpu_custom_call" | custom-call | tf_op jit(solution)/shard_map/back/pallas_call | solution.py:494
  49.0 17.6 %all_to_all.11 = f32[64,1,896]{2,1,0:T(1,128)S(1)} all-to-all(f32[64,1,896]{2,1,0:T(1,128)S(1)} %bitcast.33), channel_id=1, replica_groups=mesh['fft'=64,'band'=4] {'fft'}, dimensions={0} | all-to-all | bytes 458752 | tf_op jit(solution)/shard_map/all_to_all | solution.py:525
  66.6 1.6 %z_forward.1 = f32[1728,128]{1,0:T(8,128)} custom-call(f32[448,128]{1,0:T(8,128)S(1)} %bitcast.34, bf16[768,256]{1,0:T(8,128)(2,1)S(1)} %copy-done), custom_call_target="tpu_custom_call" | custom-call | tf_op jit(solution)/shard_map/z_forward/pallas_call | solution.py:494
  (18 shorter events, 0.0 us)
Async XLA Ops:
  0.1 0.7 copy-start.10
  0.1 0.7 copy-start.11
  0.8 6.4 %copy-start = (bf16[768,256]{1,0:T(8,128)(2,1)S(1)}, bf16[768,256]{1,0:T(8,128)(2,1)}, u32[]{:S(2)}) copy-start(bf16[768,256]{1,0:T(8,128)(2,1)} %constant.16.clone.wz.fz) | copy-start | bytes 1179652
  2.0 31.2 %copy-start.1 = (bf16[1024,512]{1,0:T(8,128)(2,1)S(1)}, bf16[1024,512]{1,0:T(8,128)(2,1)}, u32[]{:S(2)}) copy-start(bf16[1024,512]{1,0:T(8,128)(2,1)} %constant.18.clone.ix) | copy-start | bytes 3145732
  2.0 32.5 %collective-permute-start = (f32[1032,128]{1,0:T(8,128)S(1)}, f32[1032,128]{1,0:T(8,128)S(1)}, u32[]{:S(2)}, u32[]{:S(2)}) collective-permute-start(f32[1032,128]{1,0:T(8,128)S(1)} %maximum_bitcast_fusion.b0), channel_id=1, source_target_pairs={{0,2},{1,3},{2,0},{3,1},{4,6},{5,7},{6,4},{7,5},{8,10},{9,11},{10,... | collective-permute-start | bytes 1585160 | tf_op jit(solution)/shard_map/ppermute | solution.py:517
  5.8 28.7 %collective-permute-start.1 = (f32[1032,128]{1,0:T(8,128)S(1)}, f32[1032,128]{1,0:T(8,128)S(1)}, u32[]{:S(2)}, u32[]{:S(2)}) collective-permute-start(f32[1032,128]{1,0:T(8,128)S(1)} %maximum_bitcast_fusion.b0), channel_id=1, source_target_pairs={{0,3},{1,0},{2,1},{3,2},{4,7},{5,4},{6,5},{7,6},{8,11},{9,8},{10,9... | collective-permute-start | bytes 1585160 | tf_op jit(solution)/shard_map/ppermute | solution.py:517
  6.6 29.9 %collective-permute-start.2 = (f32[1032,128]{1,0:T(8,128)S(1)}, f32[1032,128]{1,0:T(8,128)S(1)}, u32[]{:S(2)}, u32[]{:S(2)}) collective-permute-start(f32[1032,128]{1,0:T(8,128)S(1)} %maximum_bitcast_fusion.b0), channel_id=1, source_target_pairs={{0,1},{1,2},{2,3},{3,0},{4,5},{5,6},{6,7},{7,4},{8,9},{9,10},{10,1... | collective-permute-start | bytes 1585160 | tf_op jit(solution)/shard_map/ppermute | solution.py:517
  7.3 1.2 %copy-start.3 = (f32[1,2,3,36864]{3,1,2,0:T(2,128)S(1)}, f32[1,2,3,36864]{3,1,2,0:T(2,128)}, u32[]{:S(2)}) copy-start(f32[1,2,3,36864]{3,1,2,0:T(2,128)} %param.14) | copy-start | bytes 2654212
  8.4 24.7 %copy-start.7 = (bf16[128,384]{1,0:T(8,128)(2,1)S(1)}, bf16[128,384]{1,0:T(8,128)(2,1)}, u32[]{:S(2)}) copy-start(bf16[128,384]{1,0:T(8,128)(2,1)} %constant.21.clone.u) | copy-start | bytes 294916
  9.1 24.1 %copy-start.6 = (bf16[768,256]{1,0:T(8,128)(2,1)S(1)}, bf16[768,256]{1,0:T(8,128)(2,1)}, u32[]{:S(2)}) copy-start(bf16[768,256]{1,0:T(8,128)(2,1)} %constant.17.clone.ey) | copy-start | bytes 1179652
  34.5 2.0 %copy-start.9 = (f32[64,8,8]{0,2,1:T(8,128)S(1)}, f32[64,8,8]{0,2,1:T(8,128)}, u32[]{:S(2)}) copy-start(f32[64,8,8]{0,2,1:T(8,128)} %param.19) | copy-start | bytes 49156
  36.5 5.8 %copy-start.4 = (f32[3,36864]{1,0:T(4,128)S(1)}, f32[3,36864]{1,0:T(4,128)}, u32[]{:S(2)}) copy-start(f32[3,36864]{1,0:T(4,128)} %param.15) | copy-start | bytes 1327108
  37.5 7.9 %copy-start.2 = (bf16[2048,256]{1,0:T(8,128)(2,1)S(1)}, bf16[2048,256]{1,0:T(8,128)(2,1)}, u32[]{:S(2)}) copy-start(bf16[2048,256]{1,0:T(8,128)(2,1)} %constant.19.clone.fx) | copy-start | bytes 3145732
  37.5 1.3 %collective-permute-start.3 = (f32[96,128]{1,0:T(8,128)S(1)}, f32[96,128]{1,0:T(8,128)S(1)}, u32[]{:S(2)}, u32[]{:S(2)}) collective-permute-start(f32[96,128]{1,0:T(8,128)S(1)} %get-tuple-element.25.own), channel_id=1, source_target_pairs={{0,4},{4,0},{8,12},{12,8},{16,20},{20,16},{24,28},{28,24},{32,36},... | collective-permute-start | bytes 147464 | tf_op jit(solution)/shard_map/ppermute | solution.py:551
  38.8 6.2 %collective-permute-start.4 = (f32[80,128]{1,0:T(8,128)S(1)}, f32[80,128]{1,0:T(8,128)S(1)}, u32[]{:S(2)}, u32[]{:S(2)}) collective-permute-start(f32[80,128]{1,0:T(8,128)S(1)} %get-tuple-element.26), channel_id=1, source_target_pairs={{0,248},{4,252},{8,16},{12,20},{16,8},{20,12},{24,32},{28,36},{32,... | collective-permute-start | bytes 122888 | tf_op jit(solution)/shard_map/ppermute | solution.py:554
  42.3 3.1 %collective-permute-start.5 = (f32[80,128]{1,0:T(8,128)S(1)}, f32[80,128]{1,0:T(8,128)S(1)}, u32[]{:S(2)}, u32[]{:S(2)}) collective-permute-start(f32[80,128]{1,0:T(8,128)S(1)} %get-tuple-element.27), channel_id=1, source_target_pairs={{0,8},{4,12},{8,0},{12,4},{16,24},{20,28},{24,16},{28,20},{32,40},... | collective-permute-start | bytes 122888 | tf_op jit(solution)/shard_map/ppermute | solution.py:553
  42.3 3.1 %copy-start.5 = (bf16[512,384]{1,0:T(8,128)(2,1)S(1)}, bf16[512,384]{1,0:T(8,128)(2,1)}, u32[]{:S(2)}) copy-start(bf16[512,384]{1,0:T(8,128)(2,1)} %constant.20.clone.fy) | copy-start | bytes 1179652
  42.3 3.1 %copy-start.8 = (bf16[384,128]{1,0:T(8,128)(2,1)S(1)}, bf16[384,128]{1,0:T(8,128)(2,1)}, u32[]{:S(2)}) copy-start(bf16[384,128]{1,0:T(8,128)(2,1)} %constant.22.clone.ut) | copy-start | bytes 294916

commit v17 on v15

--- a/solution.py
+++ b/solution.py
@@ -520,7 +520,7 @@
     own = jnp.concatenate([beta, ids.astype(F32)[None]], 0).reshape(1032, 128)
     (send,) = call(kernel_z_inverse, "z_inverse", [(448, 128)], (psi, t["wz"]))
     own_later, send = lax.optimization_barrier((own, send))
-    betas = [own, from_band(own, 3), from_band(own, 2), from_band(own_later, 1)]
+    betas = [own, from_band(own, 2), from_band(own, 3), from_band(own_later, 1)]
 
     def exchange(x):
         x = lax.all_to_all(x.reshape(64, 1, 896), "fft", 0, 0, tiled=True)

time: 68.8 us -> 68.5 us (level)
    ppermute x1, waiting for transfers between devices: 1.18 us -> 2.12 us  [body(): lax.ppermute(second, 'fft', [(i, ((i + 2) % 64 ^ 2) - 2 & 63) for i in ra...]
    ppermute x1, starting transfers between devices: 4.43 us -> 3.49 us  [body(): lax.ppermute(second, 'fft', [(i, ((i + 2) % 64 ^ 2) - 2 & 63) for i in ra...]
where the time goes in v17:
time: 68.5 us; the launch traced here: 68.3 us
  blocking collectives  41.5 us (61%)
  Pallas kernels  10.8 us (16%)
  starting transfers between devices  9.28 us (14%)
  waiting for transfers between devices  3.44 us (5%)
  local copies, waits for them, and re-layouts  1.96 us (3%)
  other arithmetic  1.2 us (2%)
    all_to_all x2, blocking collectives, exchange(): x = lax.all_to_all(x.reshape(64, 1, 896), 'fft', 0, 0, tiled=True)  41.5 us
    pallas_call x8, Pallas kernels, call(): pl.pallas_call(kernel, name=name, out_shape=shapes, in_specs=specs, out_s...  10.8 us
    ppermute x3, starting transfers between devices, from_band(): return lax.ppermute(x, 'band', [(i, (i + k) % 4) for i in range(4)])  5.37 us
    ppermute x1, starting transfers between devices, body(): lax.ppermute(second, 'fft', [(i, ((i + 2) % 64 ^ 2) - 2 & 63) for i in ra...  3.49 us
    ppermute x1, waiting for transfers between devices, body(): lax.ppermute(second, 'fft', [(i, ((i + 2) % 64 ^ 2) - 2 & 63) for i in ra...  2.12 us
    unnamed x24, local copies, waits for them, and re-layouts  1.89 us
  transfers between devices with their start and end apart: 6, of which 3 were waited for; matrix products, arithmetic and copies ran while one was open for 0% of the time, Pallas kernels for 7%

profile of v17, /device:TPU:1, one launch (start us, length us, event | category | flops | bytes accessed | tf_op | source)
XLA Modules:
  0.0 68.3 jit_solution(2933066537650027907)
XLA Ops:
  0.0 0.1 pad.4.clone
  0.1 0.7 copy-done.10
  0.7 0.0 copy-done.11
  0.8 0.1 add_convert_fusion
  0.8 1.1 %maximum_bitcast_fusion.b0 = f32[1032,128]{1,0:T(8,128)S(1)} fusion(f32[1,8,128]{2,1,0:T(8,128)S(1)} %add_convert_fusion, f32[128,8,128]{2,1,0:T(8,128)} %param.16), kind=kLoop, calls=%fused_computation | loop fusion | flops 132096 | bytes 1056768 | tf_op jit(solution)/shard_map/reshape | solution.py:520
  2.0 0.0 copy-start.1
  2.0 3.8 %collective-permute-start = (f32[1032,128]{1,0:T(8,128)S(1)}, f32[1032,128]{1,0:T(8,128)S(1)}, u32[]{:S(2)}, u32[]{:S(2)}) collective-permute-start(f32[1032,128]{1,0:T(8,128)S(1)} %maximum_bitcast_fusion.b0), channel_id=1, source_target_pairs={{0,2},{1,3},{2,0},{3,1},{4,6},{5,7},{6,4},{7,5},{8,10},{9,11},{10,... | collective-permute-start | bytes 1585160 | tf_op jit(solution)/shard_map/ppermute | solution.py:517
  5.8 0.8 %collective-permute-start.1 = (f32[1032,128]{1,0:T(8,128)S(1)}, f32[1032,128]{1,0:T(8,128)S(1)}, u32[]{:S(2)}, u32[]{:S(2)}) collective-permute-start(f32[1032,128]{1,0:T(8,128)S(1)} %maximum_bitcast_fusion.b0), channel_id=1, source_target_pairs={{0,3},{1,0},{2,1},{3,2},{4,7},{5,4},{6,5},{7,6},{8,11},{9,8},{10,9... | collective-permute-start | bytes 1585160 | tf_op jit(solution)/shard_map/ppermute | solution.py:517
  6.6 1.2 %copy-done.3 = f32[1,2,3,36864]{3,1,2,0:T(2,128)S(1)} copy-done((f32[1,2,3,36864]{3,1,2,0:T(2,128)S(1)}, f32[1,2,3,36864]{3,1,2,0:T(2,128)}, u32[]{:S(2)}) %copy-start.3) | copy-done | bytes 884760
  7.7 0.6 z_inverse.1
  8.4 0.0 copy-start.6
  8.4 0.8 %collective-permute-start.2 = (f32[1032,128]{1,0:T(8,128)S(1)}, f32[1032,128]{1,0:T(8,128)S(1)}, u32[]{:S(2)}, u32[]{:S(2)}) collective-permute-start(f32[1032,128]{1,0:T(8,128)S(1)} %maximum_bitcast_fusion.b0), channel_id=1, source_target_pairs={{0,1},{1,2},{2,3},{3,0},{4,5},{5,6},{6,7},{7,4},{8,9},{9,10},{10,1... | collective-permute-start | bytes 1585160 | tf_op jit(solution)/shard_map/ppermute | solution.py:517
  9.2 23.9 %all_to_all.10 = f32[64,1,896]{2,1,0:T(1,128)S(1)} all-to-all(f32[64,1,896]{2,1,0:T(1,128)S(1)} %bitcast.34), channel_id=1, replica_groups=mesh['fft'=64,'band'=4] {'fft'}, dimensions={0} | all-to-all | bytes 458752 | tf_op jit(solution)/shard_map/all_to_all | solution.py:526
  33.1 1.3 %field.1 = (f32[864,256]{1,0:T(8,128)S(1)}, bf16[896,256]{1,0:T(8,128)(2,1)S(1)}, bf16[896,256]{1,0:T(8,128)(2,1)S(1)}) custom-call(f32[448,128]{1,0:T(8,128)S(1)} %bitcast.32, bf16[768,256]{1,0:T(8,128)(2,1)S(1)} %copy-done.6, bf16[1024,512]{1,0:T(8,128)(2,1)S(1)} %copy-done.1, bf16[128,384]{1,0:T(8,128)(2,1)S(1)} %copy-done.7), custom_call_target="tpu_custom_call" | custom-call | tf_op jit(solution)/shard_map/field/pallas_call | solution.py:494
  34.4 0.0 collective-permute-done.b1
  34.4 0.0 collective-permute-done.1.b2
  34.4 0.0 copy-start.9
  34.4 2.0 %project.1 = (f32[16,256]{1,0:T(8,128)S(1)}, bf16[384,256]{1,0:T(8,128)(2,1)S(1)}, s32[1,384]{1,0:T(1,128)S(1)}) custom-call(bf16[896,256]{1,0:T(8,128)(2,1)S(1)} %get-tuple-element.21.rows_h, bf16[896,256]{1,0:T(8,128)(2,1)S(1)} %get-tuple-element.22.rows_l, f32[1032,128]{1,0:T(8,128)S(1)} %maximum_bitcast_fusion.b0, ...), custom_call_target="tpu_custom_call" | custom-call | tf_op jit(solution)/shard_map/project/pallas_call | solution.py:494
  36.4 0.0 collective-permute-done.2.b3
  36.4 0.0 copy-start.4
  36.4 1.0 %project_last.1 = (f32[96,128]{1,0:T(8,128)S(1)}, bf16[128,256]{1,0:T(8,128)(2,1)S(1)}, s32[1,128]{1,0:T(1,128)S(1)}) custom-call(bf16[896,256]{1,0:T(8,128)(2,1)S(1)} %get-tuple-element.21.rows_h, bf16[896,256]{1,0:T(8,128)(2,1)S(1)} %get-tuple-element.22.rows_l, f32[64,64]{1,0:T(8,128)S(1)} %bitcast.38, f32[16,256]{1,0:T(8,128)S(1)} %get-tuple-element.24.coef_in, ...), custom_call_target="tpu_custom_call" | custom-call | tf_op jit(solution)/shard_map/project_last/pallas_call | solution.py:494
  37.4 0.4 collective-permute-start.3
  37.8 0.9 %collective-permute-done.3.other = f32[96,128]{1,0:T(8,128)S(1)} collective-permute-done((f32[96,128]{1,0:T(8,128)S(1)}, f32[96,128]{1,0:T(8,128)S(1)}, u32[]{:S(2)}, u32[]{:S(2)}) %collective-permute-start.3) | collective-permute-done | bytes 49184 | tf_op jit(solution)/shard_map/ppermute | solution.py:552
  38.7 0.1 merge.1
  38.8 3.5 %collective-permute-start.4 = (f32[80,128]{1,0:T(8,128)S(1)}, f32[80,128]{1,0:T(8,128)S(1)}, u32[]{:S(2)}, u32[]{:S(2)}) collective-permute-start(f32[80,128]{1,0:T(8,128)S(1)} %get-tuple-element.30), channel_id=1, source_target_pairs={{0,248},{4,252},{8,16},{12,20},{16,8},{20,12},{24,32},{28,36},{32,... | collective-permute-start | bytes 122888 | tf_op jit(solution)/shard_map/ppermute | solution.py:555
  42.3 0.0 collective-permute-start.5
  42.3 0.6 put.1
  42.9 2.1 %collective-permute-done.4.second = f32[80,128]{1,0:T(8,128)S(1)} collective-permute-done((f32[80,128]{1,0:T(8,128)S(1)}, f32[80,128]{1,0:T(8,128)S(1)}, u32[]{:S(2)}, u32[]{:S(2)}) %collective-permute-start.4) | collective-permute-done | bytes 40992 | tf_op jit(solution)/shard_map/ppermute | solution.py:555
  45.0 0.4 collective-permute-done.5.first
  45.4 3.6 %back.1 = f32[448,128]{1,0:T(8,128)S(1)} custom-call(f32[864,256]{1,0:T(8,128)S(1)} %get-tuple-element.28.local, f32[96,128]{1,0:T(8,128)S(1)} %get-tuple-element.29.own, f32[96,128]{1,0:T(8,128)S(1)} %collective-permute-done.3.other, f32[80,128]{1,0:T(8,128)S(1)} %collective-permute-done.4.second, f32[80,128]{1,0:T(8,128)S(1)} %collective-permute-done.5.first, ...), custom_call_target="tpu_custom_call" | custom-call | tf_op jit(solution)/shard_map/back/pallas_call | solution.py:494
  49.0 17.6 %all_to_all.11 = f32[64,1,896]{2,1,0:T(1,128)S(1)} all-to-all(f32[64,1,896]{2,1,0:T(1,128)S(1)} %bitcast.33), channel_id=1, replica_groups=mesh['fft'=64,'band'=4] {'fft'}, dimensions={0} | all-to-all | bytes 458752 | tf_op jit(solution)/shard_map/all_to_all | solution.py:526
  66.6 1.6 %z_forward.1 = f32[1728,128]{1,0:T(8,128)} custom-call(f32[448,128]{1,0:T(8,128)S(1)} %bitcast.35, bf16[768,256]{1,0:T(8,128)(2,1)S(1)} %copy-done), custom_call_target="tpu_custom_call" | custom-call | tf_op jit(solution)/shard_map/z_forward/pallas_call | solution.py:494
  (18 shorter events, 0.0 us)
Async XLA Ops:
  0.1 0.7 copy-start.10
  0.1 0.7 copy-start.11
  0.8 5.8 %copy-start = (bf16[768,256]{1,0:T(8,128)(2,1)S(1)}, bf16[768,256]{1,0:T(8,128)(2,1)}, u32[]{:S(2)}) copy-start(bf16[768,256]{1,0:T(8,128)(2,1)} %constant.16.clone.wz.fz) | copy-start | bytes 1179652
  2.0 31.1 %copy-start.1 = (bf16[1024,512]{1,0:T(8,128)(2,1)S(1)}, bf16[1024,512]{1,0:T(8,128)(2,1)}, u32[]{:S(2)}) copy-start(bf16[1024,512]{1,0:T(8,128)(2,1)} %constant.18.clone.ix) | copy-start | bytes 3145732
  2.0 32.4 %collective-permute-start = (f32[1032,128]{1,0:T(8,128)S(1)}, f32[1032,128]{1,0:T(8,128)S(1)}, u32[]{:S(2)}, u32[]{:S(2)}) collective-permute-start(f32[1032,128]{1,0:T(8,128)S(1)} %maximum_bitcast_fusion.b0), channel_id=1, source_target_pairs={{0,2},{1,3},{2,0},{3,1},{4,6},{5,7},{6,4},{7,5},{8,10},{9,11},{10,... | collective-permute-start | bytes 1585160 | tf_op jit(solution)/shard_map/ppermute | solution.py:517
  5.8 28.6 %collective-permute-start.1 = (f32[1032,128]{1,0:T(8,128)S(1)}, f32[1032,128]{1,0:T(8,128)S(1)}, u32[]{:S(2)}, u32[]{:S(2)}) collective-permute-start(f32[1032,128]{1,0:T(8,128)S(1)} %maximum_bitcast_fusion.b0), channel_id=1, source_target_pairs={{0,3},{1,0},{2,1},{3,2},{4,7},{5,4},{6,5},{7,6},{8,11},{9,8},{10,9... | collective-permute-start | bytes 1585160 | tf_op jit(solution)/shard_map/ppermute | solution.py:517
  6.6 1.2 %copy-start.3 = (f32[1,2,3,36864]{3,1,2,0:T(2,128)S(1)}, f32[1,2,3,36864]{3,1,2,0:T(2,128)}, u32[]{:S(2)}) copy-start(f32[1,2,3,36864]{3,1,2,0:T(2,128)} %param.14) | copy-start | bytes 2654212
  7.7 25.3 %copy-start.7 = (bf16[128,384]{1,0:T(8,128)(2,1)S(1)}, bf16[128,384]{1,0:T(8,128)(2,1)}, u32[]{:S(2)}) copy-start(bf16[128,384]{1,0:T(8,128)(2,1)} %constant.21.clone.u) | copy-start | bytes 294916
  8.4 24.7 %copy-start.6 = (bf16[768,256]{1,0:T(8,128)(2,1)S(1)}, bf16[768,256]{1,0:T(8,128)(2,1)}, u32[]{:S(2)}) copy-start(bf16[768,256]{1,0:T(8,128)(2,1)} %constant.17.clone.ey) | copy-start | bytes 1179652
  8.4 28.0 %collective-permute-start.2 = (f32[1032,128]{1,0:T(8,128)S(1)}, f32[1032,128]{1,0:T(8,128)S(1)}, u32[]{:S(2)}, u32[]{:S(2)}) collective-permute-start(f32[1032,128]{1,0:T(8,128)S(1)} %maximum_bitcast_fusion.b0), channel_id=1, source_target_pairs={{0,1},{1,2},{2,3},{3,0},{4,5},{5,6},{6,7},{7,4},{8,9},{9,10},{10,1... | collective-permute-start | bytes 1585160 | tf_op jit(solution)/shard_map/ppermute | solution.py:517
  34.4 2.0 %copy-start.9 = (f32[64,8,8]{0,2,1:T(8,128)S(1)}, f32[64,8,8]{0,2,1:T(8,128)}, u32[]{:S(2)}) copy-start(f32[64,8,8]{0,2,1:T(8,128)} %param.19) | copy-start | bytes 49156
  36.4 5.8 %copy-start.4 = (f32[3,36864]{1,0:T(4,128)S(1)}, f32[3,36864]{1,0:T(4,128)}, u32[]{:S(2)}) copy-start(f32[3,36864]{1,0:T(4,128)} %param.15) | copy-start | bytes 1327108
  37.4 8.0 %copy-start.2 = (bf16[2048,256]{1,0:T(8,128)(2,1)S(1)}, bf16[2048,256]{1,0:T(8,128)(2,1)}, u32[]{:S(2)}) copy-start(bf16[2048,256]{1,0:T(8,128)(2,1)} %constant.19.clone.fx) | copy-start | bytes 3145732
  37.4 1.3 %collective-permute-start.3 = (f32[96,128]{1,0:T(8,128)S(1)}, f32[96,128]{1,0:T(8,128)S(1)}, u32[]{:S(2)}, u32[]{:S(2)}) collective-permute-start(f32[96,128]{1,0:T(8,128)S(1)} %get-tuple-element.29.own), channel_id=1, source_target_pairs={{0,4},{4,0},{8,12},{12,8},{16,20},{20,16},{24,28},{28,24},{32,36},... | collective-permute-start | bytes 147464 | tf_op jit(solution)/shard_map/ppermute | solution.py:552
  38.8 6.2 %collective-permute-start.4 = (f32[80,128]{1,0:T(8,128)S(1)}, f32[80,128]{1,0:T(8,128)S(1)}, u32[]{:S(2)}, u32[]{:S(2)}) collective-permute-start(f32[80,128]{1,0:T(8,128)S(1)} %get-tuple-element.30), channel_id=1, source_target_pairs={{0,248},{4,252},{8,16},{12,20},{16,8},{20,12},{24,32},{28,36},{32,... | collective-permute-start | bytes 122888 | tf_op jit(solution)/shard_map/ppermute | solution.py:555
  42.3 3.1 %collective-permute-start.5 = (f32[80,128]{1,0:T(8,128)S(1)}, f32[80,128]{1,0:T(8,128)S(1)}, u32[]{:S(2)}, u32[]{:S(2)}) collective-permute-start(f32[80,128]{1,0:T(8,128)S(1)} %get-tuple-element.31), channel_id=1, source_target_pairs={{0,8},{4,12},{8,0},{12,4},{16,24},{20,28},{24,16},{28,20},{32,40},... | collective-permute-start | bytes 122888 | tf_op jit(solution)/shard_map/ppermute | solution.py:554
  42.3 3.1 %copy-start.5 = (bf16[512,384]{1,0:T(8,128)(2,1)S(1)}, bf16[512,384]{1,0:T(8,128)(2,1)}, u32[]{:S(2)}) copy-start(bf16[512,384]{1,0:T(8,128)(2,1)} %constant.20.clone.fy) | copy-start | bytes 1179652
  42.3 3.1 %copy-start.8 = (bf16[384,128]{1,0:T(8,128)(2,1)S(1)}, bf16[384,128]{1,0:T(8,128)(2,1)}, u32[]{:S(2)}) copy-start(bf16[384,128]{1,0:T(8,128)(2,1)} %constant.22.clone.ut) | copy-start | bytes 294916

commit v18 on v16

--- a/solution.py
+++ b/solution.py
@@ -519,7 +519,7 @@
     ids = jnp.concatenate([blk_slot[None], blk_tile[None], jnp.zeros((6, 128), jnp.int32)], 0)
     own = jnp.concatenate([beta, ids.astype(F32)[None]], 0).reshape(1032, 128)
     (send,) = call(kernel_z_inverse, "z_inverse", [(448, 128)], (psi, t["wz"]))
-    betas = [own, from_band(own, 2), from_band(own, 3), from_band(own, 1)]
+    betas = [own, from_band(own, 2), from_band(own, 1), from_band(own, 3)]
 
     def exchange(x):
         x = lax.all_to_all(x.reshape(64, 1, 896), "fft", 0, 0, tiled=True)

time: 68.5 us -> 69.4 us (1.013)
    ppermute x3, starting transfers between devices: 5.3 us -> 6.51 us  [from_band(): return lax.ppermute(x, 'band', [(i, (i + k) % 4) for i in range(4)])]
    ppermute x1, waiting for transfers between devices: 2.17 us -> 3.01 us  [body(): lax.ppermute(second, 'fft', [(i, ((i + 2) % 64 ^ 2) - 2 & 63) for i in ra...]
    ppermute x1, starting transfers between devices: 3.43 us -> 2.59 us  [body(): lax.ppermute(second, 'fft', [(i, ((i + 2) % 64 ^ 2) - 2 & 63) for i in ra...]
  transfers between devices with their start and end apart: 6 -> 6, of which waited for: 3 -> 2; matrix products, arithmetic and copies ran while one was open for 0% -> 0% of each run, Pallas kernels for 7% -> 7%
where the time goes in v18:
time: 69.4 us; the launch traced here: 69.1 us
  blocking collectives  41.7 us (60%)
  Pallas kernels  10.8 us (16%)
  starting transfers between devices  9.51 us (14%)
  waiting for transfers between devices  3.9 us (6%)
  local copies, waits for them, and re-layouts  1.96 us (3%)
  other arithmetic  1.2 us (2%)
    all_to_all x2, blocking collectives, exchange(): x = lax.all_to_all(x.reshape(64, 1, 896), 'fft', 0, 0, tiled=True)  41.7 us
    pallas_call x8, Pallas kernels, call(): pl.pallas_call(kernel, name=name, out_shape=shapes, in_specs=specs, out_s...  10.8 us
    ppermute x3, starting transfers between devices, from_band(): return lax.ppermute(x, 'band', [(i, (i + k) % 4) for i in range(4)])  6.51 us
    ppermute x1, waiting for transfers between devices, body(): lax.ppermute(second, 'fft', [(i, ((i + 2) % 64 ^ 2) - 2 & 63) for i in ra...  3.01 us
    ppermute x1, starting transfers between devices, body(): lax.ppermute(second, 'fft', [(i, ((i + 2) % 64 ^ 2) - 2 & 63) for i in ra...  2.59 us
    unnamed x24, local copies, waits for them, and re-layouts  1.89 us
  transfers between devices with their start and end apart: 6, of which 2 were waited for; matrix products, arithmetic and copies ran while one was open for 0% of the time, Pallas kernels for 7%

profile of v18, /device:TPU:1, one launch (start us, length us, event | category | flops | bytes accessed | tf_op | source)
XLA Modules:
  0.0 69.1 jit_solution(17842846262911201086)
XLA Ops:
  0.0 0.1 pad.4.clone
  0.1 0.7 copy-done.10
  0.7 0.0 copy-done.11
  0.8 0.1 add_convert_fusion
  0.8 1.1 %maximum_bitcast_fusion.b0 = f32[1032,128]{1,0:T(8,128)S(1)} fusion(f32[1,8,128]{2,1,0:T(8,128)S(1)} %add_convert_fusion, f32[128,8,128]{2,1,0:T(8,128)} %param.16), kind=kLoop, calls=%fused_computation | loop fusion | flops 132096 | bytes 1056768 | tf_op jit(solution)/shard_map/reshape | solution.py:520
  2.0 0.0 copy-start.1
  2.0 3.8 %collective-permute-start = (f32[1032,128]{1,0:T(8,128)S(1)}, f32[1032,128]{1,0:T(8,128)S(1)}, u32[]{:S(2)}, u32[]{:S(2)}) collective-permute-start(f32[1032,128]{1,0:T(8,128)S(1)} %maximum_bitcast_fusion.b0), channel_id=1, source_target_pairs={{0,2},{1,3},{2,0},{3,1},{4,6},{5,7},{6,4},{7,5},{8,10},{9,11},{10,... | collective-permute-start | bytes 1585160 | tf_op jit(solution)/shard_map/ppermute | solution.py:517
  5.8 0.4 collective-permute-start.1
  6.2 2.3 %collective-permute-start.2 = (f32[1032,128]{1,0:T(8,128)S(1)}, f32[1032,128]{1,0:T(8,128)S(1)}, u32[]{:S(2)}, u32[]{:S(2)}) collective-permute-start(f32[1032,128]{1,0:T(8,128)S(1)} %maximum_bitcast_fusion.b0), channel_id=1, source_target_pairs={{0,3},{1,0},{2,1},{3,2},{4,7},{5,4},{6,5},{7,6},{8,11},{9,8},{10,9... | collective-permute-start | bytes 1585160 | tf_op jit(solution)/shard_map/ppermute | solution.py:517
  8.5 1.2 %copy-done.3 = f32[1,2,3,36864]{3,1,2,0:T(2,128)S(1)} copy-done((f32[1,2,3,36864]{3,1,2,0:T(2,128)S(1)}, f32[1,2,3,36864]{3,1,2,0:T(2,128)}, u32[]{:S(2)}) %copy-start.3) | copy-done | bytes 884760
  9.7 0.6 z_inverse.1
  10.3 0.0 copy-start.6
  10.3 24.1 %all_to_all.10 = f32[64,1,896]{2,1,0:T(1,128)S(1)} all-to-all(f32[64,1,896]{2,1,0:T(1,128)S(1)} %bitcast.35), channel_id=1, replica_groups=mesh['fft'=64,'band'=4] {'fft'}, dimensions={0} | all-to-all | bytes 458752 | tf_op jit(solution)/shard_map/all_to_all | solution.py:525
  34.4 1.3 %field.1 = (f32[864,256]{1,0:T(8,128)S(1)}, bf16[896,256]{1,0:T(8,128)(2,1)S(1)}, bf16[896,256]{1,0:T(8,128)(2,1)S(1)}) custom-call(f32[448,128]{1,0:T(8,128)S(1)} %bitcast.32, bf16[768,256]{1,0:T(8,128)(2,1)S(1)} %copy-done.6, bf16[1024,512]{1,0:T(8,128)(2,1)S(1)} %copy-done.1, bf16[128,384]{1,0:T(8,128)(2,1)S(1)} %copy-done.7), custom_call_target="tpu_custom_call" | custom-call | tf_op jit(solution)/shard_map/field/pallas_call | solution.py:494
  35.7 0.0 collective-permute-done.b1
  35.7 0.0 collective-permute-done.1.b2
  35.7 0.0 copy-start.9
  35.7 2.0 %project.1 = (f32[16,256]{1,0:T(8,128)S(1)}, bf16[384,256]{1,0:T(8,128)(2,1)S(1)}, s32[1,384]{1,0:T(1,128)S(1)}) custom-call(bf16[896,256]{1,0:T(8,128)(2,1)S(1)} %get-tuple-element.18.rows_h, bf16[896,256]{1,0:T(8,128)(2,1)S(1)} %get-tuple-element.19.rows_l, f32[1032,128]{1,0:T(8,128)S(1)} %maximum_bitcast_fusion.b0, ...), custom_call_target="tpu_custom_call" | custom-call | tf_op jit(solution)/shard_map/project/pallas_call | solution.py:494
  37.7 0.0 collective-permute-done.2.b3
  37.7 0.0 copy-start.4
  37.7 1.0 %project_last.1 = (f32[96,128]{1,0:T(8,128)S(1)}, bf16[128,256]{1,0:T(8,128)(2,1)S(1)}, s32[1,128]{1,0:T(1,128)S(1)}) custom-call(bf16[896,256]{1,0:T(8,128)(2,1)S(1)} %get-tuple-element.18.rows_h, bf16[896,256]{1,0:T(8,128)(2,1)S(1)} %get-tuple-element.19.rows_l, f32[64,64]{1,0:T(8,128)S(1)} %bitcast.38, f32[16,256]{1,0:T(8,128)S(1)} %get-tuple-element.21.coef_in, ...), custom_call_target="tpu_custom_call" | custom-call | tf_op jit(solution)/shard_map/project_last/pallas_call | solution.py:494
  38.7 0.4 collective-permute-start.3
  39.1 0.9 %collective-permute-done.3.other = f32[96,128]{1,0:T(8,128)S(1)} collective-permute-done((f32[96,128]{1,0:T(8,128)S(1)}, f32[96,128]{1,0:T(8,128)S(1)}, u32[]{:S(2)}, u32[]{:S(2)}) %collective-permute-start.3) | collective-permute-done | bytes 49184 | tf_op jit(solution)/shard_map/ppermute | solution.py:551
  40.0 0.1 merge.1
  40.1 2.6 %collective-permute-start.4 = (f32[80,128]{1,0:T(8,128)S(1)}, f32[80,128]{1,0:T(8,128)S(1)}, u32[]{:S(2)}, u32[]{:S(2)}) collective-permute-start(f32[80,128]{1,0:T(8,128)S(1)} %get-tuple-element.26), channel_id=1, source_target_pairs={{0,248},{4,252},{8,16},{12,20},{16,8},{20,12},{24,32},{28,36},{32,... | collective-permute-start | bytes 122888 | tf_op jit(solution)/shard_map/ppermute | solution.py:554
  42.6 0.0 collective-permute-start.5
  42.7 0.6 put.1
  43.2 3.0 %collective-permute-done.4.second = f32[80,128]{1,0:T(8,128)S(1)} collective-permute-done((f32[80,128]{1,0:T(8,128)S(1)}, f32[80,128]{1,0:T(8,128)S(1)}, u32[]{:S(2)}, u32[]{:S(2)}) %collective-permute-start.4) | collective-permute-done | bytes 40992 | tf_op jit(solution)/shard_map/ppermute | solution.py:554
  46.3 0.0 collective-permute-done.5.first
  46.3 3.6 %back.1 = f32[448,128]{1,0:T(8,128)S(1)} custom-call(f32[864,256]{1,0:T(8,128)S(1)} %get-tuple-element.24.local, f32[96,128]{1,0:T(8,128)S(1)} %get-tuple-element.25.own, f32[96,128]{1,0:T(8,128)S(1)} %collective-permute-done.3.other, f32[80,128]{1,0:T(8,128)S(1)} %collective-permute-done.4.second, f32[80,128]{1,0:T(8,128)S(1)} %collective-permute-done.5.first, ...), custom_call_target="tpu_custom_call" | custom-call | tf_op jit(solution)/shard_map/back/pallas_call | solution.py:494
  49.9 17.6 %all_to_all.11 = f32[64,1,896]{2,1,0:T(1,128)S(1)} all-to-all(f32[64,1,896]{2,1,0:T(1,128)S(1)} %bitcast.33), channel_id=1, replica_groups=mesh['fft'=64,'band'=4] {'fft'}, dimensions={0} | all-to-all | bytes 458752 | tf_op jit(solution)/shard_map/all_to_all | solution.py:525
  67.5 1.6 %z_forward.1 = f32[1728,128]{1,0:T(8,128)} custom-call(f32[448,128]{1,0:T(8,128)S(1)} %bitcast.34, bf16[768,256]{1,0:T(8,128)(2,1)S(1)} %copy-done), custom_call_target="tpu_custom_call" | custom-call | tf_op jit(solution)/shard_map/z_forward/pallas_call | solution.py:494
  (18 shorter events, 0.0 us)
Async XLA Ops:
  0.1 0.7 copy-start.10
  0.1 0.7 copy-start.11
  0.8 7.7 %copy-start = (bf16[768,256]{1,0:T(8,128)(2,1)S(1)}, bf16[768,256]{1,0:T(8,128)(2,1)}, u32[]{:S(2)}) copy-start(bf16[768,256]{1,0:T(8,128)(2,1)} %constant.16.clone.wz.fz) | copy-start | bytes 1179652
  2.0 32.4 %copy-start.1 = (bf16[1024,512]{1,0:T(8,128)(2,1)S(1)}, bf16[1024,512]{1,0:T(8,128)(2,1)}, u32[]{:S(2)}) copy-start(bf16[1024,512]{1,0:T(8,128)(2,1)} %constant.18.clone.ix) | copy-start | bytes 3145732
  2.0 33.7 %collective-permute-start = (f32[1032,128]{1,0:T(8,128)S(1)}, f32[1032,128]{1,0:T(8,128)S(1)}, u32[]{:S(2)}, u32[]{:S(2)}) collective-permute-start(f32[1032,128]{1,0:T(8,128)S(1)} %maximum_bitcast_fusion.b0), channel_id=1, source_target_pairs={{0,2},{1,3},{2,0},{3,1},{4,6},{5,7},{6,4},{7,5},{8,10},{9,11},{10,... | collective-permute-start | bytes 1585160 | tf_op jit(solution)/shard_map/ppermute | solution.py:517
  5.8 29.9 %collective-permute-start.1 = (f32[1032,128]{1,0:T(8,128)S(1)}, f32[1032,128]{1,0:T(8,128)S(1)}, u32[]{:S(2)}, u32[]{:S(2)}) collective-permute-start(f32[1032,128]{1,0:T(8,128)S(1)} %maximum_bitcast_fusion.b0), channel_id=1, source_target_pairs={{0,1},{1,2},{2,3},{3,0},{4,5},{5,6},{6,7},{7,4},{8,9},{9,10},{10,1... | collective-permute-start | bytes 1585160 | tf_op jit(solution)/shard_map/ppermute | solution.py:517
  6.2 31.5 %collective-permute-start.2 = (f32[1032,128]{1,0:T(8,128)S(1)}, f32[1032,128]{1,0:T(8,128)S(1)}, u32[]{:S(2)}, u32[]{:S(2)}) collective-permute-start(f32[1032,128]{1,0:T(8,128)S(1)} %maximum_bitcast_fusion.b0), channel_id=1, source_target_pairs={{0,3},{1,0},{2,1},{3,2},{4,7},{5,4},{6,5},{7,6},{8,11},{9,8},{10,9... | collective-permute-start | bytes 1585160 | tf_op jit(solution)/shard_map/ppermute | solution.py:517
  8.5 1.2 %copy-start.3 = (f32[1,2,3,36864]{3,1,2,0:T(2,128)S(1)}, f32[1,2,3,36864]{3,1,2,0:T(2,128)}, u32[]{:S(2)}) copy-start(f32[1,2,3,36864]{3,1,2,0:T(2,128)} %param.14) | copy-start | bytes 2654212
  9.6 24.7 %copy-start.7 = (bf16[128,384]{1,0:T(8,128)(2,1)S(1)}, bf16[128,384]{1,0:T(8,128)(2,1)}, u32[]{:S(2)}) copy-start(bf16[128,384]{1,0:T(8,128)(2,1)} %constant.21.clone.u) | copy-start | bytes 294916
  10.3 24.1 %copy-start.6 = (bf16[768,256]{1,0:T(8,128)(2,1)S(1)}, bf16[768,256]{1,0:T(8,128)(2,1)}, u32[]{:S(2)}) copy-start(bf16[768,256]{1,0:T(8,128)(2,1)} %constant.17.clone.ey) | copy-start | bytes 1179652
  35.7 2.0 %copy-start.9 = (f32[64,8,8]{0,2,1:T(8,128)S(1)}, f32[64,8,8]{0,2,1:T(8,128)}, u32[]{:S(2)}) copy-start(f32[64,8,8]{0,2,1:T(8,128)} %param.19) | copy-start | bytes 49156
  37.7 4.9 %copy-start.4 = (f32[3,36864]{1,0:T(4,128)S(1)}, f32[3,36864]{1,0:T(4,128)}, u32[]{:S(2)}) copy-start(f32[3,36864]{1,0:T(4,128)} %param.15) | copy-start | bytes 1327108
  38.7 7.6 %copy-start.2 = (bf16[2048,256]{1,0:T(8,128)(2,1)S(1)}, bf16[2048,256]{1,0:T(8,128)(2,1)}, u32[]{:S(2)}) copy-start(bf16[2048,256]{1,0:T(8,128)(2,1)} %constant.19.clone.fx) | copy-start | bytes 3145732
  38.7 1.3 %collective-permute-start.3 = (f32[96,128]{1,0:T(8,128)S(1)}, f32[96,128]{1,0:T(8,128)S(1)}, u32[]{:S(2)}, u32[]{:S(2)}) collective-permute-start(f32[96,128]{1,0:T(8,128)S(1)} %get-tuple-element.25.own), channel_id=1, source_target_pairs={{0,4},{4,0},{8,12},{12,8},{16,20},{20,16},{24,28},{28,24},{32,36},... | collective-permute-start | bytes 147464 | tf_op jit(solution)/shard_map/ppermute | solution.py:551
  40.1 6.2 %collective-permute-start.4 = (f32[80,128]{1,0:T(8,128)S(1)}, f32[80,128]{1,0:T(8,128)S(1)}, u32[]{:S(2)}, u32[]{:S(2)}) collective-permute-start(f32[80,128]{1,0:T(8,128)S(1)} %get-tuple-element.26), channel_id=1, source_target_pairs={{0,248},{4,252},{8,16},{12,20},{16,8},{20,12},{24,32},{28,36},{32,... | collective-permute-start | bytes 122888 | tf_op jit(solution)/shard_map/ppermute | solution.py:554
  42.6 3.6 %collective-permute-start.5 = (f32[80,128]{1,0:T(8,128)S(1)}, f32[80,128]{1,0:T(8,128)S(1)}, u32[]{:S(2)}, u32[]{:S(2)}) collective-permute-start(f32[80,128]{1,0:T(8,128)S(1)} %get-tuple-element.27), channel_id=1, source_target_pairs={{0,8},{4,12},{8,0},{12,4},{16,24},{20,28},{24,16},{28,20},{32,40},... | collective-permute-start | bytes 122888 | tf_op jit(solution)/shard_map/ppermute | solution.py:553
  42.7 3.6 %copy-start.5 = (bf16[512,384]{1,0:T(8,128)(2,1)S(1)}, bf16[512,384]{1,0:T(8,128)(2,1)}, u32[]{:S(2)}) copy-start(bf16[512,384]{1,0:T(8,128)(2,1)} %constant.20.clone.fy) | copy-start | bytes 1179652
  42.7 3.6 %copy-start.8 = (bf16[384,128]{1,0:T(8,128)(2,1)S(1)}, bf16[384,128]{1,0:T(8,128)(2,1)}, u32[]{:S(2)}) copy-start(bf16[384,128]{1,0:T(8,128)(2,1)} %constant.22.clone.ut) | copy-start | bytes 294916
